TPU v7x, 32 devices: a whole 2x2x4 slice. The times are simulated.
32 devices in a mesh: wide: 8 (over z, y), narrow: 4 (over x, core).
Axes of the slice: x: 2, y: 2, z: 4, core: 2. Of those that a mesh axis runs over, the one named last changes fastest.
Arguments:
- tokens: bfloat16 [16384, 320], P(('wide', 'narrow')), may hold values from -6 to 6
- cotangent: bfloat16 [16384, 320], P(('wide', 'narrow')), may hold values from -6 to 6
- img_rows: int32 [64], P(('wide', 'narrow')), may hold values from 0 to 32, as said below
- img_cols: int32 [64], P(('wide', 'narrow')), may hold values from 0 to 32, as said below
- q_weight: bfloat16 [320, 320], P('narrow', 'wide'), may hold values from -0.3125 to 0.3125
- kv_weight: bfloat16 [320, 640], P('narrow', 'wide'), may hold values from -0.3125 to 0.3125
- reduce_weight: bfloat16 [1280, 320], P('narrow', 'wide'), may hold values from -0.15625 to 0.15625
- proj_weight: bfloat16 [320, 320], P('narrow', 'wide'), may hold values from -2 to 2
- up_weight: bfloat16 [320, 1280], P('narrow', 'wide'), may hold values from -0.3125 to 0.3125
- down_weight: bfloat16 [1280, 320], P('narrow', 'wide'), may hold values from -0.15625 to 0.15625
- vec_model: bfloat16 [11, 320], P(None, 'narrow'), may hold values from -1.3 to 2.1, as said below
- vec_hidden: bfloat16 [11, 1280], P(None, 'narrow'), may hold values from -1.4 to 1.4, as said below
Outputs:
- mixed: bfloat16 [16384, 320], P(('wide', 'narrow'))
- token_grad: bfloat16 [16384, 320], P(('wide', 'narrow'))
- q_grad: float32 [320, 320], P('narrow', 'wide')
- kv_grad: float32 [320, 640], P('narrow', 'wide')
- reduce_grad: float32 [1280, 320], P('narrow', 'wide')
- proj_grad: float32 [320, 320], P('narrow', 'wide')
- up_grad: float32 [320, 1280], P('narrow', 'wide')
- down_grad: float32 [1280, 320], P('narrow', 'wide')
- model_vec_grad: float32 [11, 320], P(None, 'narrow')
- hidden_vec_grad: float32 [11, 1280], P(None, 'narrow')
Inputs may be any that keep to these rules, and one draw needn't show every extreme that they name: `img_rows`: each device holds two image slots (consecutive entries). Rows and columns are even multiples of 2; the two images of a device cover at most 512 patches, exactly 512 on some device; the first slot is never empty, an empty second slot has 0 rows and 0 columns. `img_cols`: columns of the same slots. `vec_model`: gains near 1, biases of order a few tenths. `vec_hidden`: biases and taps of order a few tenths.
All inputs are finite; a program needn't handle non-finite values.
Results may differ from a plain program's by a relative error of at most 0.019.
Values may be sent and summed in bfloat16 or wider, within the bound.
No kernel may reach another device: no remote copies, remote signals or barrier semaphores. Data moves between devices by JAX's collectives and lax.ppermute only.
A program may use at most 128 MiB of HBM per device.

v0:
```python
import jax
import jax.numpy as jnp
from jax import lax
from jax.sharding import PartitionSpec as P

HEADS = 5


EPSILON = 1e-06
MASKED = -1000000000.0


def arrange(rows_dev, cols_dev, capacity):
    areas = rows_dev * cols_dev
    position = jnp.arange(capacity, dtype=jnp.int32)
    in_first = position < areas[0]
    in_second = jnp.logical_and(position >= areas[0], position < areas[0] + areas[1])
    image_id = jnp.where(in_first, 0, jnp.where(in_second, 1, -1)).astype(jnp.int32)
    widths = jnp.maximum(jnp.where(in_second, cols_dev[1], cols_dev[0]), 2)
    heights = jnp.where(in_second, rows_dev[1], rows_dev[0])
    local_pos = position - jnp.where(in_second, areas[0], 0)
    row_of = local_pos // widths
    col_of = local_pos % widths
    near_index = []
    near_valid = []
    for step_row in (-1, 0, 1):
        for step_col in (-1, 0, 1):
            new_row = row_of + step_row
            new_col = col_of + step_col
            inside = (
                (image_id >= 0)
                & (new_row >= 0)
                & (new_row < heights)
                & (new_col >= 0)
                & (new_col < widths)
            )
            near_index.append(jnp.clip(position + step_row * widths + step_col, 0, capacity - 1))
            near_valid.append(inside)
    key_pos = jnp.arange(capacity // 4, dtype=jnp.int32)
    quarters = areas // 4
    key_first = key_pos < quarters[0]
    key_second = (key_pos >= quarters[0]) & (key_pos < quarters[0] + quarters[1])
    key_image = jnp.where(key_first, 0, jnp.where(key_second, 1, -2)).astype(jnp.int32)
    key_width = jnp.maximum(jnp.where(key_second, cols_dev[1], cols_dev[0]), 2)
    key_local = key_pos - jnp.where(key_second, quarters[0], 0)
    half_width = key_width // 2
    corner = (
        jnp.where(key_second, areas[0], 0)
        + 2 * (key_local // half_width) * key_width
        + 2 * (key_local % half_width)
    )
    key_taps = jnp.stack(
        [
            jnp.clip(corner, 0, capacity - 1),
            jnp.clip(corner + 1, 0, capacity - 1),
            jnp.clip(corner + key_width, 0, capacity - 1),
            jnp.clip(corner + key_width + 1, 0, capacity - 1),
        ]
    )
    patch_slot = (
        (jnp.where(in_second, quarters[0], 0) + row_of // 2 * (widths // 2) + col_of // 2) * 4
        + row_of % 2 * 2
        + col_of % 2
    )
    patch_slot = jnp.clip(patch_slot, 0, capacity - 1)
    return (image_id, jnp.stack(near_index), jnp.stack(near_valid), key_image, key_taps, patch_slot)


def norm_stats(values):
    centre = values - jnp.mean(values, axis=-1, keepdims=True)
    inverse = lax.rsqrt(jnp.mean(centre * centre, axis=-1, keepdims=True) + EPSILON)
    return (centre * inverse, inverse)


def norm_back(grad_out, normed, inverse, gain):
    scaled = grad_out * gain
    grad_in = (
        scaled
        - jnp.mean(scaled, axis=-1, keepdims=True)
        - normed * jnp.mean(scaled * normed, axis=-1, keepdims=True)
    ) * inverse
    return (grad_in, jnp.sum(grad_out * normed, axis=0), jnp.sum(grad_out, axis=0))


def product(left, right):
    return jnp.dot(left, right, preferred_element_type=jnp.float32)


def forward_pass(tokens, layout, weights):
    w_query, w_keyval, w_reduce, w_proj, w_up, w_down, model_vecs, hidden_vecs = weights
    model_vecs = model_vecs.astype(jnp.float32)
    hidden_vecs = hidden_vecs.astype(jnp.float32)
    image_id, near_index, near_valid, key_image, key_taps, patch_slot = layout
    capacity, width = tokens.shape
    head_dim = width // HEADS
    scale = head_dim ** (-0.5)
    x_float = tokens.astype(jnp.float32)
    normed_one, inverse_one = norm_stats(x_float)
    h_one = (normed_one * model_vecs[0] + model_vecs[1]).astype(jnp.bfloat16)
    query = (product(h_one, w_query) + model_vecs[2]).astype(jnp.bfloat16)
    patches = jnp.concatenate(
        [jnp.take(h_one, key_taps[tap_index], axis=0) for tap_index in range(4)], axis=1
    )
    reduced = product(patches, w_reduce) + model_vecs[4]
    normed_key, inverse_key = norm_stats(reduced)
    key_norm = (normed_key * model_vecs[5] + model_vecs[6]).astype(jnp.bfloat16)
    keyval = product(key_norm, w_keyval)
    keys = keyval[:, :width].astype(jnp.bfloat16)
    values = (keyval[:, width:] + model_vecs[3]).astype(jnp.bfloat16)
    query_heads = query.reshape(capacity, HEADS, head_dim)
    key_heads = keys.reshape(-1, HEADS, head_dim)
    value_heads = values.reshape(-1, HEADS, head_dim)
    scores = (
        jnp.einsum("qhd,khd->hqk", query_heads, key_heads, preferred_element_type=jnp.float32)
        * scale
    )
    live = image_id[:, None] == key_image[None, :]
    scores = jnp.where(live[None], scores, MASKED)
    expo = jnp.exp(scores - jnp.max(scores, axis=-1, keepdims=True))
    probs = expo / jnp.sum(expo, axis=-1, keepdims=True)
    probs_low = probs.astype(jnp.bfloat16)
    attended = jnp.einsum(
        "hqk,khd->qhd", probs_low, value_heads, preferred_element_type=jnp.float32
    )
    attended = attended.reshape(capacity, width).astype(jnp.bfloat16)
    x_two = x_float + product(attended, w_proj) + model_vecs[7]
    normed_two, inverse_two = norm_stats(x_two)
    h_two = (normed_two * model_vecs[8] + model_vecs[9]).astype(jnp.bfloat16)
    f_one = product(h_two, w_up) + hidden_vecs[0]
    conv = hidden_vecs[1] + jnp.zeros_like(f_one)
    for tap_index in range(9):
        neighbour = jnp.where(
            near_valid[tap_index][:, None], jnp.take(f_one, near_index[tap_index], axis=0), 0.0
        )
        conv = conv + hidden_vecs[2 + tap_index] * neighbour
    activ = (0.5 * conv * (1.0 + lax.erf(conv * 2.0 ** (-0.5)))).astype(jnp.bfloat16)
    occupied = (image_id >= 0)[:, None]
    mixed = jnp.where(occupied, x_two + product(activ, w_down) + model_vecs[10], 0.0)
    saved = (
        normed_one,
        inverse_one,
        h_one,
        query_heads,
        patches,
        normed_key,
        inverse_key,
        key_norm,
        key_heads,
        value_heads,
        probs,
        probs_low,
        attended,
        normed_two,
        inverse_two,
        h_two,
        f_one,
        conv,
        activ,
    )
    return (mixed, saved)


def backward_pass(cotangent, layout, weights, saved):
    w_query, w_keyval, w_reduce, w_proj, w_up, w_down, model_vecs, hidden_vecs = weights
    model_vecs = model_vecs.astype(jnp.float32)
    hidden_vecs = hidden_vecs.astype(jnp.float32)
    image_id, near_index, near_valid, key_image, key_taps, patch_slot = layout
    (
        normed_one,
        inverse_one,
        h_one,
        query_heads,
        patches,
        normed_key,
        inverse_key,
        key_norm,
        key_heads,
        value_heads,
        probs,
        probs_low,
        attended,
        normed_two,
        inverse_two,
        h_two,
        f_one,
        conv,
        activ,
    ) = saved
    capacity, width = cotangent.shape
    head_dim = width // HEADS
    scale = head_dim ** (-0.5)
    occupied = (image_id >= 0)[:, None]
    grad_out = jnp.where(occupied, cotangent.astype(jnp.float32), 0.0)
    grad_low = grad_out.astype(jnp.bfloat16)
    down_grad = jnp.einsum("nf,nd->fd", activ, grad_low, preferred_element_type=jnp.float32)
    bias_down = jnp.sum(grad_out, axis=0)
    grad_activ = jnp.einsum("nd,fd->nf", grad_low, w_down, preferred_element_type=jnp.float32)
    slope = 0.5 * (1.0 + lax.erf(conv * 2.0 ** (-0.5))) + conv * jnp.exp(-0.5 * conv * conv) * (
        2.0 * jnp.pi
    ) ** (-0.5)
    grad_conv = grad_activ * slope
    bias_conv = jnp.sum(grad_conv, axis=0)
    tap_grads = []
    grad_fone = jnp.zeros_like(grad_conv)
    for tap_index in range(9):
        neighbour = jnp.where(
            near_valid[tap_index][:, None], jnp.take(f_one, near_index[tap_index], axis=0), 0.0
        )
        tap_grads.append(jnp.sum(grad_conv * neighbour, axis=0))
        mirror = 8 - tap_index
        back_term = jnp.where(
            near_valid[mirror][:, None], jnp.take(grad_conv, near_index[mirror], axis=0), 0.0
        )
        grad_fone = grad_fone + hidden_vecs[2 + tap_index] * back_term
    grad_fone = grad_fone.astype(jnp.bfloat16)
    bias_up = jnp.sum(grad_fone.astype(jnp.float32), axis=0)
    up_grad = jnp.einsum("nd,nf->df", h_two, grad_fone, preferred_element_type=jnp.float32)
    grad_htwo = jnp.einsum("nf,df->nd", grad_fone, w_up, preferred_element_type=jnp.float32)
    grad_xtwo, gain_two, shift_two = norm_back(grad_htwo, normed_two, inverse_two, model_vecs[8])
    grad_xtwo = grad_out + grad_xtwo
    grad_attn = grad_xtwo.astype(jnp.bfloat16)
    bias_proj = jnp.sum(grad_attn.astype(jnp.float32), axis=0)
    proj_grad = jnp.einsum("nc,nd->cd", attended, grad_attn, preferred_element_type=jnp.float32)
    grad_attended = jnp.einsum(
        "nd,cd->nc", grad_attn, w_proj, preferred_element_type=jnp.float32
    ).astype(jnp.bfloat16)
    grad_heads = grad_attended.reshape(capacity, HEADS, head_dim)
    grad_probs = jnp.einsum(
        "qhd,khd->hqk", grad_heads, value_heads, preferred_element_type=jnp.float32
    )
    grad_values = jnp.einsum(
        "hqk,qhd->khd", probs_low, grad_heads, preferred_element_type=jnp.float32
    )
    row_dot = jnp.sum(probs * grad_probs, axis=-1, keepdims=True)
    grad_scores = (probs * (grad_probs - row_dot)).astype(jnp.bfloat16)
    grad_query = (
        jnp.einsum("hqk,khd->qhd", grad_scores, key_heads, preferred_element_type=jnp.float32)
        * scale
    )
    grad_query = grad_query.reshape(capacity, width).astype(jnp.bfloat16)
    grad_keys = (
        jnp.einsum("hqk,qhd->khd", grad_scores, query_heads, preferred_element_type=jnp.float32)
        * scale
    )
    grad_keys = grad_keys.reshape(-1, width).astype(jnp.bfloat16)
    grad_values = grad_values.reshape(-1, width).astype(jnp.bfloat16)
    bias_query = jnp.sum(grad_query.astype(jnp.float32), axis=0)
    q_grad = jnp.einsum("nc,nd->cd", h_one, grad_query, preferred_element_type=jnp.float32)
    grad_hone = jnp.einsum("nd,cd->nc", grad_query, w_query, preferred_element_type=jnp.float32)
    grad_keyval = jnp.concatenate([grad_keys, grad_values], axis=1)
    bias_value = jnp.sum(grad_values.astype(jnp.float32), axis=0)
    kv_grad = jnp.einsum("nc,nd->cd", key_norm, grad_keyval, preferred_element_type=jnp.float32)
    grad_keynorm = jnp.einsum(
        "nd,cd->nc", grad_keyval, w_keyval, preferred_element_type=jnp.float32
    )
    grad_reduced, gain_key, shift_key = norm_back(
        grad_keynorm, normed_key, inverse_key, model_vecs[5]
    )
    grad_reduced = grad_reduced.astype(jnp.bfloat16)
    bias_reduce = jnp.sum(grad_reduced.astype(jnp.float32), axis=0)
    reduce_grad = jnp.einsum("nc,nd->cd", patches, grad_reduced, preferred_element_type=jnp.float32)
    grad_patches = jnp.einsum(
        "nd,cd->nc", grad_reduced, w_reduce, preferred_element_type=jnp.float32
    )
    grad_patches = grad_patches.reshape(-1, width)
    grad_hone = grad_hone + jnp.where(occupied, jnp.take(grad_patches, patch_slot, axis=0), 0.0)
    grad_xone, gain_one, shift_one = norm_back(grad_hone, normed_one, inverse_one, model_vecs[0])
    token_grad = (grad_xtwo + grad_xone).astype(jnp.bfloat16)
    model_grads = jnp.stack(
        [
            gain_one,
            shift_one,
            bias_query,
            bias_value,
            bias_reduce,
            gain_key,
            shift_key,
            bias_proj,
            gain_two,
            shift_two,
            bias_down,
        ]
    )
    hidden_grads = jnp.stack([bias_up, bias_conv] + tap_grads)
    return (
        token_grad,
        (q_grad, kv_grad, reduce_grad, proj_grad, up_grad, down_grad, model_grads, hidden_grads),
    )


def on_device(
    tokens,
    cotangent,
    img_rows,
    img_cols,
    q_weight,
    kv_weight,
    reduce_weight,
    proj_weight,
    up_weight,
    down_weight,
    vec_model,
    vec_hidden,
):

    def collect():
        inner = (
            lax.all_gather(q_weight, "narrow", axis=0, tiled=True),
            lax.all_gather(kv_weight, "narrow", axis=0, tiled=True),
            lax.all_gather(reduce_weight, "narrow", axis=0, tiled=True),
            lax.all_gather(proj_weight, "narrow", axis=0, tiled=True),
            lax.all_gather(up_weight, "narrow", axis=0, tiled=True),
            lax.all_gather(down_weight, "narrow", axis=0, tiled=True),
            lax.all_gather(vec_model, "narrow", axis=1, tiled=True),
            lax.all_gather(vec_hidden, "narrow", axis=1, tiled=True),
        )
        outer = (
            lax.all_gather(inner[0], "wide", axis=1, tiled=True),
            lax.all_gather(inner[1], "wide", axis=1, tiled=True),
            lax.all_gather(inner[2], "wide", axis=1, tiled=True),
            lax.all_gather(inner[3], "wide", axis=1, tiled=True),
            lax.all_gather(inner[4], "wide", axis=1, tiled=True),
            lax.all_gather(inner[5], "wide", axis=1, tiled=True),
        )
        return (outer[0], outer[1], outer[2], outer[3], outer[4], outer[5], inner[6], inner[7])

    layout = arrange(img_rows, img_cols, tokens.shape[0])
    forward_weights = collect()
    mixed, unused_saved = forward_pass(tokens, layout, forward_weights)
    backward_weights = collect()
    unused_mixed, saved = forward_pass(tokens, layout, backward_weights)
    token_grad, grads = backward_pass(cotangent, layout, backward_weights, saved)
    columns = (
        lax.psum_scatter(
            grads[0].astype(jnp.bfloat16), "wide", scatter_dimension=1, tiled=True
        ).astype(jnp.float32),
        lax.psum_scatter(
            grads[1].astype(jnp.bfloat16), "wide", scatter_dimension=1, tiled=True
        ).astype(jnp.float32),
        lax.psum_scatter(
            grads[2].astype(jnp.bfloat16), "wide", scatter_dimension=1, tiled=True
        ).astype(jnp.float32),
        lax.psum_scatter(
            grads[3].astype(jnp.bfloat16), "wide", scatter_dimension=1, tiled=True
        ).astype(jnp.float32),
        lax.psum_scatter(
            grads[4].astype(jnp.bfloat16), "wide", scatter_dimension=1, tiled=True
        ).astype(jnp.float32),
        lax.psum_scatter(
            grads[5].astype(jnp.bfloat16), "wide", scatter_dimension=1, tiled=True
        ).astype(jnp.float32),
    )
    vectors = (
        lax.psum(grads[6].astype(jnp.bfloat16), "wide").astype(jnp.float32),
        lax.psum(grads[7].astype(jnp.bfloat16), "wide").astype(jnp.float32),
    )
    owned = (
        lax.psum_scatter(
            columns[0].astype(jnp.bfloat16), "narrow", scatter_dimension=0, tiled=True
        ).astype(jnp.float32),
        lax.psum_scatter(
            columns[1].astype(jnp.bfloat16), "narrow", scatter_dimension=0, tiled=True
        ).astype(jnp.float32),
        lax.psum_scatter(
            columns[2].astype(jnp.bfloat16), "narrow", scatter_dimension=0, tiled=True
        ).astype(jnp.float32),
        lax.psum_scatter(
            columns[3].astype(jnp.bfloat16), "narrow", scatter_dimension=0, tiled=True
        ).astype(jnp.float32),
        lax.psum_scatter(
            columns[4].astype(jnp.bfloat16), "narrow", scatter_dimension=0, tiled=True
        ).astype(jnp.float32),
        lax.psum_scatter(
            columns[5].astype(jnp.bfloat16), "narrow", scatter_dimension=0, tiled=True
        ).astype(jnp.float32),
        lax.psum_scatter(
            vectors[0].astype(jnp.bfloat16), "narrow", scatter_dimension=1, tiled=True
        ).astype(jnp.float32),
        lax.psum_scatter(
            vectors[1].astype(jnp.bfloat16), "narrow", scatter_dimension=1, tiled=True
        ).astype(jnp.float32),
    )
    return (
        mixed.astype(jnp.bfloat16),
        token_grad,
        owned[0],
        owned[1],
        owned[2],
        owned[3],
        owned[4],
        owned[5],
        owned[6],
        owned[7],
    )


def solution(mesh):
    placed = (
        P(("wide", "narrow"), None),
        P(("wide", "narrow"), None),
        P(("wide", "narrow")),
        P(("wide", "narrow")),
        P("narrow", "wide"),
        P("narrow", "wide"),
        P("narrow", "wide"),
        P("narrow", "wide"),
        P("narrow", "wide"),
        P("narrow", "wide"),
        P(None, "narrow"),
        P(None, "narrow"),
    )
    return jax.shard_map(
        on_device,
        mesh=mesh,
        in_specs=placed,
        out_specs=(
            P(("wide", "narrow"), None),
            P(("wide", "narrow"), None),
            P("narrow", "wide"),
            P("narrow", "wide"),
            P("narrow", "wide"),
            P("narrow", "wide"),
            P("narrow", "wide"),
            P("narrow", "wide"),
            P(None, "narrow"),
            P(None, "narrow"),
        ),
        check_vma=False,
    )
```

profile of v0, /device:TPU:0, one launch (start us, length us, event | category | flops | bytes accessed | tf_op | source)
XLA Modules:
  0.0 934.4 jit_solution(8866004136917281364)
XLA Ops:
  19.1 6.3 all-gather
  26.1 5.7 all_gather.59
  31.9 5.7 all-gather.1
  42.6 32.1 %all_gather.60 = bf16[320,640]{0,1:T(8,128)(2,1)S(1)} all-gather(bf16[320,80]{0,1:T(8,128)(2,1)S(1)} %copy.104), channel_id=1, replica_groups=mesh['wide'=8,'narrow'=4] {'wide'}, dimensions={1}, use_global_device_ids=true | all-gather | bytes 460800 | tf_op jit(solution)/shard_map/all_gather | solution.py:319
  74.7 31.8 %all_gather.58 = bf16[1280,320]{0,1:T(8,128)(2,1)S(1)} all-gather(bf16[1280,40]{0,1:T(8,128)(2,1)S(1)} %reshape.725), channel_id=1, replica_groups=mesh['wide'=8,'narrow'=4] {'wide'}, dimensions={1}, use_global_device_ids=true | all-gather | bytes 921600 | tf_op jit(solution)/shard_map/all_gather | solution.py:320
  117.5 3.8 and_and_fusion.8
  121.3 3.9 broadcast_compare_fusion.2
  128.1 5.2 all-gather.2
  133.4 5.2 all-gather.3
  138.8 5.2 all-gather.4
  144.9 5.4 all-gather.5
  150.5 5.5 all_gather.66
  156.1 30.8 %all_gather.64 = bf16[320,320]{0,1:T(8,128)(2,1)S(1)} all-gather(bf16[320,40]{0,1:T(8,128)(2,1)S(1)} %reshape.729), channel_id=1, replica_groups=mesh['wide'=8,'narrow'=4] {'wide'}, dimensions={1}, use_global_device_ids=true | all-gather | bytes 230400 | tf_op jit(solution)/shard_map/all_gather | solution.py:321
  186.9 31.0 %all_gather.62 = bf16[320,320]{0,1:T(8,128)(2,1)S(1)} all-gather(bf16[320,40]{0,1:T(8,128)(2,1)S(1)} %reshape.727), channel_id=1, replica_groups=mesh['wide'=8,'narrow'=4] {'wide'}, dimensions={1}, use_global_device_ids=true | all-gather | bytes 230400 | tf_op jit(solution)/shard_map/all_gather | solution.py:318
  217.9 34.4 %all_gather.69 = bf16[1280,320]{0,1:T(8,128)(2,1)} all-gather(bf16[1280,40]{0,1:T(8,128)(2,1)S(1)} %reshape.733), channel_id=1, replica_groups=mesh['wide'=8,'narrow'=4] {'wide'}, dimensions={1}, use_global_device_ids=true | all-gather | bytes 921600 | tf_op jit(solution)/shard_map/all_gather | solution.py:323
  252.5 34.7 %all_gather.67 = bf16[320,1280]{0,1:T(8,128)(2,1)} all-gather(bf16[320,160]{0,1:T(8,128)(2,1)S(1)} %copy.111), channel_id=1, replica_groups=mesh['wide'=8,'narrow'=4] {'wide'}, dimensions={1}, use_global_device_ids=true | all-gather | bytes 921600 | tf_op jit(solution)/shard_map/all_gather | solution.py:322
  320.5 11.8 %multiply_convert_fusion = (bf16[512,1280]{1,0:T(8,128)(2,1)}, f32[512,1280]{1,0:T(8,128)S(1)}) fusion(f32[512,1280]{1,0:T(8,128)} %gather_fusion.13, pred[512]{0:T(512)(128)(4,1)} %get-tuple-element.181, pred[512]{0:T(512)(128)(4,1)S(1)} %get-tuple-element.164, f32[1280]{0:T(1024)S(1)} %get-tuple-element.85, f32[512,1280]{1,0:T(8,128)} %gather_fusion.12, ...), kind=kLoop, calls=%fused_computation.79 | loop fusion | flops 26869760 | bytes 27585536 | tf_op jit(solution)/shard_map/convert_element_type | solution.py:136
  363.9 10.8 %fusion.95 = (bf16[1280]{0:T(1024)(128)(2,1)}, bf16[512,1280]{1,0:T(8,128)(2,1)S(1)}) fusion(f32[512,1280]{1,0:T(8,128)} %gather_fusion.22, pred[512]{0:T(512)(128)(4,1)} %get-tuple-element.171, pred[512]{0:T(512)(128)(4,1)} %get-tuple-element.120, f32[1280]{0:T(1024)S(1)} %get-tuple-element.85, f32[512,1280]{1,0:T(8,128)} %gather_fusion.21, ...), kind=kLoop, calls=%fused_computation.343 | loop fusion | flops 24247040 | bytes 24961536 | tf_op jit(solution)/shard_map/reduce_sum | solution.py:216
  422.1 7.1 multiply_reduce_fusion
  430.5 8.9 reduce-scatter.61.cloned.1.call-done
  441.0 59.4 %reduce-scatter.59.cloned.1.call-done = bf16[320,40]{0,1:T(8,128)(2,1)} async-done(((bf16[320,320]{0,1:T(8,128)(2,1)}), bf16[320,40]{0,1:T(8,128)(2,1)}) %reduce-scatter.59.cloned.1.call-update) | async-done | bytes 25616
  502.0 60.2 %reduce-scatter.35.cloned.1.call-done = bf16[320,80]{0,1:T(8,128)(2,1)} async-done(((bf16[320,640]{0,1:T(8,128)(2,1)}), bf16[320,80]{0,1:T(8,128)(2,1)}) %reduce-scatter.35.cloned.1.call-update) | async-done | bytes 51216 | tf_op jit(solution)/shard_map/reduce_scatter | solution.py:337
  566.9 54.8 %reduce-scatter.41.cloned.1.call-done = bf16[1280,40]{0,1:T(8,128)(2,1)} async-done(((bf16[1280,320]{0,1:T(8,128)(2,1)}), bf16[1280,40]{0,1:T(8,128)(2,1)}) %reduce-scatter.41.cloned.1.call-update) | async-done | bytes 102416 | tf_op jit(solution)/shard_map/reduce_scatter | solution.py:349
  623.5 64.1 %reduce-scatter.39.cloned.1.call-done = bf16[320,160]{0,1:T(8,128)(2,1)} async-done(((bf16[320,1280]{0,1:T(8,128)(2,1)}), bf16[320,160]{0,1:T(8,128)(2,1)}) %reduce-scatter.39.cloned.1.call-update) | async-done | bytes 102416 | tf_op jit(solution)/shard_map/reduce_scatter | solution.py:346
  689.4 57.7 %reduce-scatter.37.cloned.1.call-done = bf16[1280,40]{0,1:T(8,128)(2,1)} async-done(((bf16[1280,320]{0,1:T(8,128)(2,1)}), bf16[1280,40]{0,1:T(8,128)(2,1)}) %reduce-scatter.37.cloned.1.call-update) | async-done | bytes 102416 | tf_op jit(solution)/shard_map/reduce_scatter | solution.py:340
  749.9 18.3 %reduce-scatter.55.cloned.1.call-done = bf16[80,11]{1,0:T(8,128)(2,1)} async-done(((bf16[320,11]{1,0:T(8,128)(2,1)}), bf16[80,11]{1,0:T(8,128)(2,1)}) %reduce-scatter.55.cloned.1.call-update) | async-done | bytes 1776
  769.0 22.3 %reduce-scatter.57.cloned.1.call-done = bf16[320,11]{1,0:T(8,128)(2,1)} async-done(((bf16[1280,11]{1,0:T(8,128)(2,1)}), bf16[320,11]{1,0:T(8,128)(2,1)}) %reduce-scatter.57.cloned.1.call-update) | async-done | bytes 7056
  792.3 37.1 %all-reduce.2 = (bf16[11,80]{1,0:T(8,128)(2,1)S(1)}, bf16[11,320]{1,0:T(8,128)(2,1)S(1)}) all-reduce(bf16[11,80]{1,0:T(8,128)(2,1)S(1)} %copy.136, bf16[11,320]{1,0:T(8,128)(2,1)S(1)} %copy.138), channel_id=1, replica_groups=mesh['wide'=8,'narrow'=4] {'wide'}, use_global_device_ids=true, to_apply=%region_38.41 | all-reduce | flops 4400 | bytes 17600 | tf_op jit(solution)/shard_map/psum | solution.py:354
  837.1 20.6 %reduce-scatter.45.cloned.1.call-done = bf16[80,80]{1,0:T(8,128)(2,1)} async-done(((bf16[320,80]{1,0:T(8,128)(2,1)}), bf16[80,80]{1,0:T(8,128)(2,1)}) %reduce-scatter.45.cloned.1.call-update) | async-done | bytes 12816
  859.2 21.3 %reduce-scatter.53.cloned.1.call-done = bf16[320,40]{1,0:T(8,128)(2,1)} async-done(((bf16[1280,40]{1,0:T(8,128)(2,1)}), bf16[320,40]{1,0:T(8,128)(2,1)}) %reduce-scatter.53.cloned.1.call-update) | async-done | bytes 25616
  882.1 20.7 %reduce-scatter.51.cloned.1.call-done = bf16[80,160]{1,0:T(8,128)(2,1)} async-done(((bf16[320,160]{1,0:T(8,128)(2,1)}), bf16[80,160]{1,0:T(8,128)(2,1)}) %reduce-scatter.51.cloned.1.call-update) | async-done | bytes 25616
  904.4 21.4 %reduce-scatter.47.cloned.1.call-done = bf16[320,40]{1,0:T(8,128)(2,1)} async-done(((bf16[1280,40]{1,0:T(8,128)(2,1)}), bf16[320,40]{1,0:T(8,128)(2,1)}) %reduce-scatter.47.cloned.1.call-update) | async-done | bytes 25616
  (426 shorter events, 172.5 us)
Async XLA Ops:
  7.2 432.3 %reduce-scatter.61.cloned.1.call-start = ((), (), s32[]{:S(2)}) async-start(), calls=%async_computation.27 | async-start | bytes 276480
  26.1 81.5 %copy-start.40 = (f32[320]{0:T(512)}, f32[320]{0:T(512)S(1)}, u32[]{:S(2)}) copy-start(f32[320]{0:T(512)S(1)} %get-tuple-element.102) | copy-start | bytes 3844
  26.1 81.5 %copy-start.45 = (f32[320]{0:T(512)}, f32[320]{0:T(512)S(1)}, u32[]{:S(2)}) copy-start(f32[320]{0:T(512)S(1)} %get-tuple-element.101) | copy-start | bytes 3844
  38.9 248.5 %copy-start.15 = (bf16[512,320]{0,1:T(8,128)(2,1)}, bf16[512,320]{0,1:T(8,128)(2,1)S(1)}, u32[]{:S(2)}) copy-start(bf16[512,320]{0,1:T(8,128)(2,1)S(1)} %fusion.40) | copy-start | bytes 983044
  74.7 34.1 %copy-start.18 = (bf16[320,640]{0,1:T(8,128)(2,1)}, bf16[320,640]{0,1:T(8,128)(2,1)S(1)}, u32[]{:S(2)}) copy-start(bf16[320,640]{0,1:T(8,128)(2,1)S(1)} %all_gather.60) | copy-start | bytes 1228804
  74.7 53.4 %copy-start.58 = (bf16[80,40]{0,1:T(8,128)(2,1)S(1)}, bf16[80,40]{0,1:T(8,128)(2,1)}, u32[]{:S(2)}) copy-start(bf16[80,40]{0,1:T(8,128)(2,1)} %param.20) | copy-start | bytes 19204
  106.5 37.5 %copy-start.7 = (bf16[1280,320]{0,1:T(8,128)(2,1)}, bf16[1280,320]{0,1:T(8,128)(2,1)S(1)}, u32[]{:S(2)}) copy-start(bf16[1280,320]{0,1:T(8,128)(2,1)S(1)} %all_gather.58) | copy-start | bytes 2457604
  106.7 38.2 %copy-start.44 = (bf16[320,40]{0,1:T(8,128)(2,1)S(1)}, bf16[320,40]{0,1:T(8,128)(2,1)}, u32[]{:S(2)}) copy-start(bf16[320,40]{0,1:T(8,128)(2,1)} %param.25) | copy-start | bytes 76804
  106.9 43.6 %copy-start.39 = (bf16[80,160]{1,0:T(8,128)(2,1)S(1)}, bf16[80,160]{1,0:T(8,128)(2,1)}, u32[]{:S(2)}) copy-start(bf16[80,160]{1,0:T(8,128)(2,1)} %param.24) | copy-start | bytes 76804
  107.1 79.8 %copy-start.17 = (bf16[128,1280]{1,0:T(8,128)(2,1)}, bf16[128,1280]{1,0:T(8,128)(2,1)S(1)}, u32[]{:S(2)}) copy-start(bf16[128,1280]{1,0:T(8,128)(2,1)S(1)} %concatenate.7) | copy-start | bytes 983044
  107.6 144.8 %copy-start.92 = (f32[128]{0:T(128)}, f32[128]{0:T(128)S(1)}, u32[]{:S(2)}) copy-start(f32[128]{0:T(128)S(1)} %add_rsqrt_fusion.2) | copy-start | bytes 1540
  217.9 69.9 %copy-start.36 = (bf16[320,320]{0,1:T(8,128)(2,1)}, bf16[320,320]{0,1:T(8,128)(2,1)S(1)}, u32[]{:S(2)}) copy-start(bf16[320,320]{0,1:T(8,128)(2,1)S(1)} %all_gather.62) | copy-start | bytes 614404
  252.5 36.0 %copy-start.31 = (bf16[128,320]{0,1:T(8,128)(2,1)}, bf16[128,320]{0,1:T(8,128)(2,1)S(1)}, u32[]{:S(2)}) copy-start(bf16[128,320]{0,1:T(8,128)(2,1)S(1)} %copy.107) | copy-start | bytes 245764
  290.1 84.7 %copy-start.9 = (f32[512,320]{0,1:T(8,128)}, f32[512,320]{0,1:T(8,128)S(1)}, u32[]{:S(2)}) copy-start(f32[512,320]{0,1:T(8,128)S(1)} %get-tuple-element.206) | copy-start | bytes 1966084
  379.5 121.0 %reduce-scatter.59.cloned.1.call-start = ((), (), s32[]{:S(2)}) async-start(), calls=%async_computation.26 | async-start | bytes 276480
  385.3 176.9 %reduce-scatter.35.cloned.1.call-start = ((), (), s32[]{:S(2)}) async-start(), calls=%async_computation.14 | async-start | bytes 552960 | tf_op jit(solution)/shard_map/reduce_scatter | solution.py:337
  390.6 231.1 %reduce-scatter.41.cloned.1.call-start = ((), (), s32[]{:S(2)}) async-start(), calls=%async_computation.17 | async-start | bytes 921600 | tf_op jit(solution)/shard_map/reduce_scatter | solution.py:349
  393.6 294.1 %reduce-scatter.39.cloned.1.call-start = ((), (), s32[]{:S(2)}) async-start(), calls=%async_computation.16 | async-start | bytes 1105920 | tf_op jit(solution)/shard_map/reduce_scatter | solution.py:346
  397.0 350.1 %reduce-scatter.37.cloned.1.call-start = ((), (), s32[]{:S(2)}) async-start(), calls=%async_computation.15 | async-start | bytes 921600 | tf_op jit(solution)/shard_map/reduce_scatter | solution.py:340
  403.5 364.7 %reduce-scatter.55.cloned.1.call-start = ((), (), s32[]{:S(2)}) async-start(), calls=%async_computation.24 | async-start | bytes 102400
  421.9 141.9 %copy-start.11 = (f32[512,320]{0,1:T(8,128)S(1)}, f32[512,320]{0,1:T(8,128)}, u32[]{:S(2)}) copy-start(f32[512,320]{0,1:T(8,128)} %copy-done.9) | copy-start | bytes 1966084
  421.9 141.9 %copy-start.103 = (f32[320]{0:T(512)S(1)}, f32[320]{0:T(512)}, u32[]{:S(2)}) copy-start(f32[320]{0:T(512)} %get-tuple-element.95) | copy-start | bytes 3844
  421.9 369.4 %reduce-scatter.57.cloned.1.call-start = ((), (), s32[]{:S(2)}) async-start(), calls=%async_computation.25 | async-start | bytes 409600
  430.5 400.1 %reduce-scatter.49.cloned.1.call-start = ((), (), s32[]{:S(2)}) async-start(), calls=%async_computation.21 | async-start | bytes 102400
  440.9 394.8 %reduce-scatter.43.cloned.1.call-start = ((), (), s32[]{:S(2)}) async-start(), calls=%async_computation.18 | async-start | bytes 102400
  502.0 355.7 %reduce-scatter.45.cloned.1.call-start = ((), (), s32[]{:S(2)}) async-start(), calls=%async_computation.19 | async-start | bytes 102400
  563.8 316.8 %reduce-scatter.53.cloned.1.call-start = ((), (), s32[]{:S(2)}) async-start(), calls=%async_computation.23 | async-start | bytes 409600
  563.8 185.0 %copy-start.1 = (f32[512,320]{0,1:T(8,128)S(1)}, f32[512,320]{0,1:T(8,128)}, u32[]{:S(2)}) copy-start(f32[512,320]{0,1:T(8,128)} %copy-done) | copy-start | bytes 1966084
  563.8 185.0 %copy-start.6 = (bf16[512,320]{0,1:T(8,128)(2,1)S(1)}, bf16[512,320]{0,1:T(8,128)(2,1)}, u32[]{:S(2)}) copy-start(bf16[512,320]{0,1:T(8,128)(2,1)} %param.16) | copy-start | bytes 983044
  563.9 185.0 %copy-start.30 = (f32[512,320]{0,1:T(8,128)S(1)}, f32[512,320]{0,1:T(8,128)}, u32[]{:S(2)}) copy-start(f32[512,320]{0,1:T(8,128)} %get-tuple-element.211) | copy-start | bytes 1966084
  623.4 279.4 %reduce-scatter.51.cloned.1.call-start = ((), (), s32[]{:S(2)}) async-start(), calls=%async_computation.22 | async-start | bytes 204800
  689.3 236.5 %reduce-scatter.47.cloned.1.call-start = ((), (), s32[]{:S(2)}) async-start(), calls=%async_computation.20 | async-start | bytes 409600
  (91 other events, 616.4 us)
Sparse Core Ops, SparseCore 0:
  379.6 59.8 reduce-scatter.60
  442.7 57.6 reduce-scatter.58
  503.7 58.3 reduce-scatter.34
  565.4 56.2 reduce-scatter.40
  625.2 62.3 reduce-scatter.38
  690.8 56.1 reduce-scatter.36
  749.6 18.5 reduce-scatter.54
  770.8 20.4 reduce-scatter.56
  793.7 19.5 reduce-scatter.48
  816.1 19.5 reduce-scatter.42
  838.1 19.5 reduce-scatter.44
  860.0 20.4 reduce-scatter.52
  883.1 19.6 reduce-scatter.50
  905.3 20.4 reduce-scatter.46
where the time goes:
time: 944 us; the launch traced here: 934 us
  waiting for transfers between devices  434 us (46%)
  blocking collectives  276 us (29%)
  local copies, waits for them, and re-layouts  98.8 us (10%)
  other arithmetic  70.5 us (7%)
  matrix products  35.8 us (4%)
  between operations  18.8 us (2%)
    unnamed x24, waiting for transfers between devices  197 us
    reduce_scatter x1, waiting for transfers between devices, on_device(): lax.psum_scatter(grads[4].astype(jnp.bfloat16), 'wide', scatter_dimension...  64.1 us
    reduce_scatter x1, waiting for transfers between devices, on_device(): lax.psum_scatter(grads[1].astype(jnp.bfloat16), 'wide', scatter_dimension...  60.2 us
    reduce_scatter x1, waiting for transfers between devices, on_device(): lax.psum_scatter(grads[2].astype(jnp.bfloat16), 'wide', scatter_dimension...  57.7 us
    reduce_scatter x1, waiting for transfers between devices, on_device(): lax.psum_scatter(grads[5].astype(jnp.bfloat16), 'wide', scatter_dimension...  54.8 us
    psum x1, blocking collectives, on_device(): lax.psum(grads[6].astype(jnp.bfloat16), 'wide').astype(jnp.float32)  37.1 us
    all_gather x1, blocking collectives, collect(): lax.all_gather(inner[4], 'wide', axis=1, tiled=True)  34.7 us
    all_gather x1, blocking collectives, collect(): lax.all_gather(inner[5], 'wide', axis=1, tiled=True)  34.4 us
  transfers between devices with their start and end apart: 14, of which 13 were waited for; matrix products, arithmetic and copies ran while one was open for 8% of the time, Pallas kernels for 0%

commit v1 on v0

v1 whole, which is shorter than its diff:
```python
import functools
import math

import jax
import jax.numpy as jnp
from jax import lax
from jax.experimental import pallas as pl
from jax.experimental.pallas import tpu as pltpu
from jax.sharding import PartitionSpec as P

HEADS = 5
EPSILON = 1e-06
MASKED = -1000000000.0
F32 = jnp.float32
BF16 = jnp.bfloat16

PARTS_W = 8
PARTS_N = 4
SLOTS = 16
TILE = 32
CHUNK = 256
PAD = 40


def dot_nn(left, right):
    return jnp.dot(left, right, preferred_element_type=F32)


def dot_nt(left, right):
    return lax.dot_general(left, right, (((1,), (1,)), ((), ())), preferred_element_type=F32)


def dot_tn(left, right):
    return lax.dot_general(left, right, (((0,), (0,)), ((), ())), preferred_element_type=F32)


def lanes(*parts):
    return jnp.concatenate(parts, axis=1)


def rows_of(*parts):
    return jnp.concatenate(parts, axis=0)


def my_index(tuned):
    if not tuned:
        return jnp.int32(0)
    return lax.axis_index("wide") * PARTS_N + lax.axis_index("narrow")


def slot_of(device, me):
    delta = device ^ me
    return ((delta >> 1) & 3) * 4 + (delta >> 3)


def normalise(values):
    centre = values - jnp.mean(values, axis=-1, keepdims=True)
    inverse = lax.rsqrt(jnp.mean(centre * centre, axis=-1, keepdims=True) + EPSILON)
    return centre * inverse, inverse


def normalise_back(grad, normed, inverse, gain):
    scaled = grad * gain
    first = jnp.mean(scaled, axis=-1, keepdims=True)
    second = jnp.mean(scaled * normed, axis=-1, keepdims=True)
    return (scaled - first - normed * second) * inverse


def column_sum(values):
    return jnp.sum(values, axis=0, keepdims=True)


def piece_of(own_ref, other_ref, device, me):
    slot = slot_of(device, me)
    mine = ((device ^ me) & 1) == 0
    return jnp.where(mine, own_ref[slot].astype(F32), other_ref[slot].astype(F32))


def token_geometry(rows_ref, cols_ref, capacity, width):
    row0, row1, col0, col1 = rows_ref[0], rows_ref[1], cols_ref[0], cols_ref[1]
    area0, area1 = row0 * col0, row1 * col1
    position = lax.broadcasted_iota(jnp.int32, (capacity, width), 0)
    first = position < area0
    second = jnp.logical_and(position >= area0, position < area0 + area1)
    widths = jnp.maximum(jnp.where(second, col1, col0), 2)
    heights = jnp.where(second, row1, row0)
    local = position - jnp.where(second, area0, 0)
    row = ((local.astype(F32) + 0.5) / widths.astype(F32)).astype(jnp.int32)
    col = local - row * widths
    return first, second, row, col, heights, widths


def pack_kernel(q_ref, kv_ref, red_ref, proj_ref, up_ref, down_ref, vm_ref, vh_ref, a_ref, b_ref, v_ref):
    cw = q_ref.shape[1]

    def turned(ref):
        return ref[...].astype(F32).T

    kv = turned(kv_ref)
    a_ref[...] = lanes(turned(red_ref), turned(q_ref), kv[:cw], kv[cw:], turned(proj_ref)).astype(BF16)
    up = turned(up_ref)
    b_ref[...] = lanes(turned(down_ref), *[up[cw * e : cw * e + cw] for e in range(4)]).astype(BF16)
    v_ref[...] = jnp.zeros_like(v_ref)
    both = lanes(vm_ref[...].astype(F32), vh_ref[...].astype(F32))
    v_ref[: both.shape[0], : both.shape[1]] = both.astype(BF16)


def attend_kernel(
    tuned,
    rows_ref, cols_ref, tok_ref, own_ref, oth_ref, vec_ref,
    x2_ref, h1_ref, n1_ref, r1_ref, patch_ref, nk_ref, rk_ref, kn_ref, q_ref, kb_ref, vb_ref,
    p_ref, o_ref, wr_ref, wq_ref, wkv_ref, wp_ref, mv_ref, hv_ref,
    score_ref,
):
    me = my_index(tuned)
    capacity, width = tok_ref.shape
    cw, rn = width // PARTS_W, width // PARTS_N
    keys = capacity // 4
    dim = width // HEADS

    pieces = [vec_ref[n ^ (me & 3)].astype(F32) for n in range(PARTS_N)]
    mv = lanes(*[p[:, :rn] for p in pieces])
    mv_ref[...] = mv
    hv_ref[...] = lanes(*[p[:, rn : 5 * rn] for p in pieces])

    for pair in range(PARTS_W // 2):
        got = [
            [piece_of(own_ref, oth_ref, w * PARTS_N + n, me) for n in range(PARTS_N)]
            for w in (2 * pair, 2 * pair + 1)
        ]
        at = pl.ds(pair * 2 * cw, 2 * cw)
        for n in range(PARTS_N):
            wr_ref[n, at, :] = rows_of(got[0][n][:, :width], got[1][n][:, :width]).astype(BF16)

        def unit(w, k):
            return lanes(*[got[w][n][:, width + k * rn : width + (k + 1) * rn] for n in range(PARTS_N)])

        wq_ref[at, :] = rows_of(unit(0, 0), unit(1, 0)).astype(BF16)
        wkv_ref[pl.ds(pair * 4 * cw, 4 * cw), :] = rows_of(
            unit(0, 1), unit(0, 2), unit(1, 1), unit(1, 2)
        ).astype(BF16)
        wp_ref[at, :] = rows_of(unit(0, 3), unit(1, 3)).astype(BF16)

    normed, inverse = normalise(tok_ref[...].astype(F32))
    n1_ref[...] = normed
    r1_ref[...] = inverse
    h1 = (normed * mv[0:1] + mv[1:2]).astype(BF16)
    h1_ref[...] = h1
    q = (dot_nt(h1, wq_ref[...]) + mv[2:3]).astype(BF16)
    q_ref[...] = q

    chosen = one_hot(rows_ref, cols_ref, capacity)
    patches = dot_nn(chosen, h1).astype(BF16)
    patch_ref[...] = patches
    reduced = mv[4:5]
    for n in range(4):
        reduced = reduced + dot_nt(patches[n * keys : (n + 1) * keys], wr_ref[n])
    nk, rk = normalise(reduced)
    nk_ref[...] = nk
    rk_ref[...] = rk
    kn = (nk * mv[5:6] + mv[6:7]).astype(BF16)
    kn_ref[...] = kn
    kv = dot_nt(kn, wkv_ref[...])
    k = kv[:, :width].astype(BF16).astype(F32)
    v = (kv[:, width:] + mv[3:4]).astype(BF16).astype(F32)
    lane = lax.broadcasted_iota(jnp.int32, (keys, width), 1)
    for h in range(HEADS):
        inside = (lane >= h * dim) & (lane < (h + 1) * dim)
        at = pl.ds(h * keys, keys)
        kb_ref[at, :] = jnp.where(inside, k, 0.0).astype(BF16)
        vb_ref[at, :] = jnp.where(inside, v, 0.0).astype(BF16)

    score_ref[...] = dot_nt(q, kb_ref[...]) * dim ** (-0.5)
    area0 = rows_ref[0] * cols_ref[0]
    area1 = rows_ref[1] * cols_ref[1]

    def soften(i, carry):
        at = pl.ds(pl.multiple_of(i * 64, 64), 64)
        token = lax.broadcasted_iota(jnp.int32, (64, keys), 0) + i * 64
        key = lax.broadcasted_iota(jnp.int32, (64, keys), 1)
        quarter0, quarter1 = area0 // 4, area1 // 4
        live = ((token < area0) & (key < quarter0)) | (
            (token >= area0) & (token < area0 + area1) & (key >= quarter0) & (key < quarter0 + quarter1)
        )
        for h in range(HEADS):
            lane_at = pl.ds(h * keys, keys)
            s = jnp.where(live, score_ref[at, lane_at], MASKED)
            e = jnp.exp(s - jnp.max(s, axis=-1, keepdims=True))
            p_ref[at, lane_at] = e / jnp.sum(e, axis=-1, keepdims=True)
        return carry

    lax.fori_loop(0, capacity // 64, soften, 0)
    o = dot_nn(p_ref[...].astype(BF16), vb_ref[...]).astype(BF16)
    o_ref[...] = o
    x2_ref[...] = tok_ref[...].astype(F32) + dot_nt(o, wp_ref[...]) + mv[7:8]


def one_hot(rows_ref, cols_ref, capacity):
    row0, row1, col0, col1 = rows_ref[0], rows_ref[1], cols_ref[0], cols_ref[1]
    area0, area1 = row0 * col0, row1 * col1
    quarter0, quarter1 = area0 // 4, area1 // 4
    keys = capacity // 4
    index = lax.broadcasted_iota(jnp.int32, (capacity, 128), 0)
    tap = index // keys
    key = index - tap * keys
    first = key < quarter0
    second = jnp.logical_and(key >= quarter0, key < quarter0 + quarter1)
    width = jnp.maximum(jnp.where(second, col1, col0), 2)
    half = width // 2
    local = key - jnp.where(second, quarter0, 0)
    row = ((local.astype(F32) + 0.5) / half.astype(F32)).astype(jnp.int32)
    col = local - row * half
    token = jnp.where(second, area0, 0) + (2 * row + tap // 2) * width + 2 * col + tap % 2
    token = jnp.where(first | second, token, -1)
    lane = lax.broadcasted_iota(jnp.int32, (capacity, 128), 1)
    return lanes(
        *[jnp.where(token == lane + t * 128, 1.0, 0.0).astype(BF16) for t in range(capacity // 128)]
    )


def ffn_kernel(
    tuned,
    rows_ref, cols_ref, x2_ref, cot_ref, own_ref, oth_ref, mv_ref, hv_ref,
    mixed_ref, gown_ref, gsend_ref, dx2_ref, mg_ref, hg_ref,
    wu_ref, wd_ref, mask_ref, n2_ref, r2_ref, h2_ref, h2t_ref, gy_ref, gyt_ref,
    f_ref, gm_ref, gp_ref, dc_ref, ul_ref, ur_ref, g0_ref, slope_ref, act_ref, u0_ref, df_ref, da_ref,
    mix_ref, dh2_ref, upg_ref, dng_ref,
):
    me = my_index(tuned)
    capacity, width = x2_ref.shape
    hidden = hv_ref.shape[1]
    cw, rn = width // PARTS_W, width // PARTS_N
    tiles = capacity // TILE

    for pair in range(PARTS_W // 2):
        got = [
            [piece_of(own_ref, oth_ref, w * PARTS_N + n, me) for n in range(PARTS_N)]
            for w in (2 * pair, 2 * pair + 1)
        ]
        wd_ref[pl.ds(pair * 2 * cw, 2 * cw), :] = lanes(
            *[rows_of(got[0][n][:, :width], got[1][n][:, :width]) for n in range(PARTS_N)]
        ).astype(BF16)

        def unit(w, k):
            return lanes(*[got[w][n][:, width + k * rn : width + (k + 1) * rn] for n in range(PARTS_N)])

        wu_ref[pl.ds(pair * 8 * cw, 8 * cw), :] = rows_of(
            *[unit(w, k) for w in range(2) for k in range(4)]
        ).astype(BF16)

    first, second, row, col, heights, widths = token_geometry(rows_ref, cols_ref, capacity, 128)
    live = first | second
    conditions = (
        live & (col > 0),
        live & (col < widths - 1),
        first & (row > 0),
        second & (row > 0),
        first & (row < heights - 1),
        second & (row < heights - 1),
        live,
    )
    for k, condition in enumerate(conditions):
        mask_ref[k] = jnp.where(condition, 1.0, 0.0)
    w0 = cols_ref[0]
    w1 = cols_ref[1]

    for ref in (f_ref, gm_ref, gp_ref, dc_ref, ul_ref, ur_ref):
        ref[:, :PAD, :] = jnp.zeros((CHUNK // 128, PAD, 128), F32)
        ref[:, PAD + capacity :, :] = jnp.zeros((CHUNK // 128, PAD, 128), F32)

    def wide_mask(k, at, size):
        m = mask_ref[k, at, :]
        return lanes(*([m] * (size // 128)), *([m[:, : size % 128]] if size % 128 else []))

    gain2, shift2, bias2 = mv_ref[8:9, :], mv_ref[9:10, :], mv_ref[10:11, :]

    def start(i, carry):
        at = pl.ds(pl.multiple_of(i * 64, 64), 64)
        normed, inverse = normalise(x2_ref[at, :])
        n2_ref[at, :] = normed
        r2_ref[at, :] = inverse
        h2_ref[at, :] = (normed * gain2 + shift2).astype(BF16)
        gy_ref[at, :] = (cot_ref[at, :].astype(F32) * wide_mask(6, at, width)).astype(BF16)
        return carry

    lax.fori_loop(0, capacity // 64, start, 0)
    h2t_ref[...] = h2_ref[...].astype(F32).T.astype(BF16)
    gyt_ref[...] = gy_ref[...].astype(F32).T.astype(BF16)
    mix_ref[...] = jnp.zeros_like(mix_ref)
    dh2_ref[...] = jnp.zeros_like(dh2_ref)

    def fold(values):
        return jnp.sum(values.reshape(TILE // 8, 8, 128), axis=0)

    halves = CHUNK // 128

    def chunk_step(c, carry):
        at_c = pl.ds(pl.multiple_of(c * CHUNK, CHUNK), CHUNK)

        def vector(k, j):
            return hv_ref[k : k + 1, pl.ds(pl.multiple_of(c * CHUNK + j * 128, 128), 128)]

        def put_vector(k, j, value):
            hg_ref[k : k + 1, pl.ds(pl.multiple_of(c * CHUNK + j * 128, 128), 128)] = value

        first_layer = dot_nt(h2_ref[...], wu_ref[at_c, :])
        for j in range(halves):
            f_ref[j, pl.ds(PAD, capacity), :] = first_layer[:, j * 128 : (j + 1) * 128] + vector(0, j)

        def taps_of(j, r, at):
            here = f_ref[j, pl.ds(PAD + r, TILE), :]
            left = f_ref[j, pl.ds(PAD + r - 1, TILE), :] * mask_ref[0, at, :]
            right = f_ref[j, pl.ds(PAD + r + 1, TILE), :] * mask_ref[1, at, :]
            return left, here, right

        def column_taps(i, carry):
            r = pl.multiple_of(i * TILE, TILE)
            at = pl.ds(r, TILE)
            for j in range(halves):
                left, here, right = taps_of(j, r, at)
                v = [vector(k, j) for k in range(11)]
                gm_ref[j, pl.ds(PAD + r, TILE), :] = v[2] * left + v[3] * here + v[4] * right
                g0_ref[j, at, :] = v[1] + v[5] * left + v[6] * here + v[7] * right
                gp_ref[j, pl.ds(PAD + r, TILE), :] = v[8] * left + v[9] * here + v[10] * right
            return carry

        lax.fori_loop(0, tiles, column_taps, 0)

        def activate(i, carry):
            r = pl.multiple_of(i * TILE, TILE)
            at = pl.ds(r, TILE)
            for j in range(halves):
                conv = (
                    g0_ref[j, at, :]
                    + mask_ref[2, at, :] * gm_ref[j, pl.ds(PAD + r - w0, TILE), :]
                    + mask_ref[3, at, :] * gm_ref[j, pl.ds(PAD + r - w1, TILE), :]
                    + mask_ref[4, at, :] * gp_ref[j, pl.ds(PAD + r + w0, TILE), :]
                    + mask_ref[5, at, :] * gp_ref[j, pl.ds(PAD + r + w1, TILE), :]
                )
                half = 0.5 * (1.0 + lax.erf(conv * 2.0 ** (-0.5)))
                lane_at = pl.ds(j * 128, 128)
                act_ref[at, lane_at] = (conv * half).astype(BF16)
                slope = half + conv * jnp.exp(-0.5 * conv * conv) * (2.0 * math.pi) ** (-0.5)
                slope_ref[at, lane_at] = slope
            return carry

        lax.fori_loop(0, tiles, activate, 0)
        act = act_ref[...]
        mix_ref[...] += dot_nt(act, wd_ref[:, at_c])
        dng_ref[:, at_c] = dot_nn(gyt_ref[...], act)
        da_ref[...] = dot_nn(gy_ref[...], wd_ref[:, at_c])

        def into_conv(i, carry):
            r = pl.multiple_of(i * TILE, TILE)
            at = pl.ds(r, TILE)
            totals = []
            for j in range(halves):
                value = da_ref[at, pl.ds(j * 128, 128)] * slope_ref[at, pl.ds(j * 128, 128)]
                dc_ref[j, pl.ds(PAD + r, TILE), :] = value
                totals.append(carry[j] + fold(value))
            return tuple(totals)

        zero = jnp.zeros((8, 128), F32)
        totals = lax.fori_loop(0, tiles, into_conv, (zero,) * halves)
        for j in range(halves):
            put_vector(1, j, column_sum(totals[j]))

        for j in range(halves):
            v = [vector(k, j) for k in range(11)]

            def tap_back(i, carry, j=j, v=v):
                r = pl.multiple_of(i * TILE, TILE)
                at = pl.ds(r, TILE)
                left, here, right = taps_of(j, r, at)
                below = (
                    mask_ref[4, at, :] * dc_ref[j, pl.ds(PAD + r + w0, TILE), :]
                    + mask_ref[5, at, :] * dc_ref[j, pl.ds(PAD + r + w1, TILE), :]
                )
                level = dc_ref[j, pl.ds(PAD + r, TILE), :]
                above = (
                    mask_ref[2, at, :] * dc_ref[j, pl.ds(PAD + r - w0, TILE), :]
                    + mask_ref[3, at, :] * dc_ref[j, pl.ds(PAD + r - w1, TILE), :]
                )
                ul_ref[j, pl.ds(PAD + r, TILE), :] = v[2] * below + v[5] * level + v[8] * above
                u0_ref[j, at, :] = v[3] * below + v[6] * level + v[9] * above
                ur_ref[j, pl.ds(PAD + r, TILE), :] = v[4] * below + v[7] * level + v[10] * above
                grads = [fold(d * f) for d in (below, level, above) for f in (left, here, right)]
                return tuple(a + b for a, b in zip(carry, grads))

            sums = lax.fori_loop(0, tiles, tap_back, (zero,) * 9)
            for k in range(9):
                put_vector(2 + k, j, column_sum(sums[k]))

        def spread_back(i, carry):
            r = pl.multiple_of(i * TILE, TILE)
            at = pl.ds(r, TILE)
            totals = []
            for j in range(halves):
                value = (
                    u0_ref[j, at, :]
                    + mask_ref[0, at, :] * ur_ref[j, pl.ds(PAD + r - 1, TILE), :]
                    + mask_ref[1, at, :] * ul_ref[j, pl.ds(PAD + r + 1, TILE), :]
                ).astype(BF16)
                df_ref[at, pl.ds(j * 128, 128)] = value
                totals.append(carry[j] + fold(value.astype(F32)))
            return tuple(totals)

        totals = lax.fori_loop(0, tiles, spread_back, (zero,) * halves)
        for j in range(halves):
            put_vector(0, j, column_sum(totals[j]))
        df = df_ref[...]
        upg_ref[:, at_c] = dot_nn(h2t_ref[...], df)
        dh2_ref[...] += dot_nn(df, wu_ref[at_c, :])
        return carry

    lax.fori_loop(0, hidden // CHUNK, chunk_step, 0)
    hg_ref[11:, :] = jnp.zeros((hg_ref.shape[0] - 11, hidden), F32)

    for w in range(PARTS_W):
        for n in range(PARTS_N):
            up = upg_ref[pl.ds(n * rn, rn), pl.ds(w * 4 * cw, 4 * cw)]
            value = lanes(
                dng_ref[pl.ds(w * cw, cw), pl.ds(n * width, width)],
                *[up[e * cw : (e + 1) * cw] for e in range(rn // cw)],
            ).astype(BF16)
            store_piece(gown_ref, gsend_ref, w * PARTS_N + n, me, value)

    def finish(i, carry):
        at = pl.ds(pl.multiple_of(i * 64, 64), 64)
        occupied = wide_mask(6, at, width)
        mixed_ref[at, :] = ((x2_ref[at, :] + mix_ref[at, :] + bias2) * occupied).astype(BF16)
        gy = gy_ref[at, :].astype(F32)
        grad, normed = dh2_ref[at, :], n2_ref[at, :]
        dx2_ref[at, :] = gy + normalise_back(grad, normed, r2_ref[at, :], gain2)
        return tuple(a + column_sum(b) for a, b in zip(carry, (grad * normed, grad, gy)))

    zero = jnp.zeros((1, width), F32)
    sums = lax.fori_loop(0, capacity // 64, finish, (zero, zero, zero))
    mg_ref[...] = jnp.zeros_like(mg_ref)
    for k in range(3):
        mg_ref[8 + k : 9 + k, :] = sums[k]


def store_piece(own_ref, send_ref, device, me, value):
    slot = slot_of(device, me)
    mine = ((device ^ me) & 1) == 0

    @pl.when(mine)
    def _():
        own_ref[slot] = value

    @pl.when(jnp.logical_not(mine))
    def _():
        send_ref[slot] = value


def attend_back_kernel(
    tuned,
    rows_ref, cols_ref, dx2_ref, h1_ref, n1_ref, r1_ref, patch_ref, nk_ref, rk_ref, kn_ref, q_ref,
    kb_ref, vb_ref, p_ref, o_ref, wr_ref, wq_ref, wkv_ref, wp_ref, mv_ref, mg_ref, hg_ref,
    tg_ref, gown_ref, gsend_ref, vown_ref, vsend_ref,
    dp_ref, ds_ref, gr_ref, gq_ref, gkv_ref, gp_ref, dpatch_ref,
):
    me = my_index(tuned)
    capacity, width = dx2_ref.shape
    cw, rn = width // PARTS_W, width // PARTS_N
    keys = capacity // 4
    dim = width // HEADS
    scale = dim ** (-0.5)
    mv = mv_ref[...]

    datt = dx2_ref[...].astype(BF16)
    bias_proj = column_sum(datt.astype(F32))
    gp_ref[...] = dot_tn(datt, o_ref[...])
    dob = dot_nn(datt, wp_ref[...]).astype(BF16)
    dp_ref[...] = dot_nt(dob, vb_ref[...])

    def soften_back(i, carry):
        at = pl.ds(pl.multiple_of(i * 64, 64), 64)
        for h in range(HEADS):
            lane_at = pl.ds(h * keys, keys)
            p = p_ref[at, lane_at]
            dp = dp_ref[at, lane_at]
            row = jnp.sum(p * dp, axis=-1, keepdims=True)
            ds_ref[at, lane_at] = (p * (dp - row)).astype(BF16)
        return carry

    lax.fori_loop(0, capacity // 64, soften_back, 0)
    ds = ds_ref[...]
    dq = (dot_nn(ds, kb_ref[...]) * scale).astype(BF16)
    dk_all = dot_tn(ds, q_ref[...])
    dv_all = dot_tn(p_ref[...].astype(BF16), dob)
    lane = lax.broadcasted_iota(jnp.int32, (keys, width), 1)
    dk = jnp.zeros((keys, width), F32)
    dv = jnp.zeros((keys, width), F32)
    for h in range(HEADS):
        inside = (lane >= h * dim) & (lane < (h + 1) * dim)
        dk = jnp.where(inside, dk_all[h * keys : (h + 1) * keys], dk)
        dv = jnp.where(inside, dv_all[h * keys : (h + 1) * keys], dv)
    dk = (dk * scale).astype(BF16)
    dv = dv.astype(BF16)
    bias_query = column_sum(dq.astype(F32))
    bias_value = column_sum(dv.astype(F32))
    gq_ref[...] = dot_tn(dq, h1_ref[...])
    kn = kn_ref[...]
    gkv_ref[pl.ds(0, width), :] = dot_tn(dk, kn)
    gkv_ref[pl.ds(width, width), :] = dot_tn(dv, kn)
    dkn = dot_nn(dk, wkv_ref[pl.ds(0, width), :]) + dot_nn(dv, wkv_ref[pl.ds(width, width), :])
    nk = nk_ref[...]
    gain_key, shift_key = column_sum(dkn * nk), column_sum(dkn)
    dsr = normalise_back(dkn, nk, rk_ref[...], mv[5:6]).astype(BF16)
    bias_reduce = column_sum(dsr.astype(F32))
    for n in range(4):
        at = pl.ds(n * keys, keys)
        gr_ref[n] = dot_tn(dsr, patch_ref[at, :])
        dpatch_ref[at, :] = dot_nn(dsr, wr_ref[n])

    for w in range(PARTS_W):
        for n in range(PARTS_N):
            at, lane_at = pl.ds(w * cw, cw), pl.ds(n * rn, rn)
            value = lanes(
                gr_ref[n, at, :],
                gq_ref[at, lane_at],
                gkv_ref[pl.ds(2 * w * cw, cw), lane_at],
                gkv_ref[pl.ds(2 * w * cw + cw, cw), lane_at],
                gp_ref[at, lane_at],
            ).astype(BF16)
            store_piece(gown_ref, gsend_ref, w * PARTS_N + n, me, value)

    chosen = one_hot(rows_ref, cols_ref, capacity)
    high = dpatch_ref[...].astype(BF16)
    low = (dpatch_ref[...] - high.astype(F32)).astype(BF16)
    dh1 = dot_nn(dq, wq_ref[...]) + dot_tn(chosen, high) + dot_tn(chosen, low)
    n1 = n1_ref[...]
    gain_one, shift_one = column_sum(dh1 * n1), column_sum(dh1)
    tg_ref[...] = (dx2_ref[...] + normalise_back(dh1, n1, r1_ref[...], mv[0:1])).astype(BF16)

    sums = rows_of(
        gain_one, shift_one, bias_query, bias_value, bias_reduce, gain_key, shift_key, bias_proj,
        mg_ref[8:16, :],
    )
    hg = hg_ref[...]
    spare = jnp.zeros((16, 3 * rn), F32)
    for n in range(PARTS_N):
        value = lanes(sums[:, n * rn : (n + 1) * rn], hg[:, n * width : (n + 1) * width], spare).astype(BF16)
        delta = n ^ (me & 3)

        @pl.when((delta & 1) == 0)
        def _():
            vown_ref[delta >> 1] = value

        @pl.when((delta & 1) == 1)
        def _():
            vsend_ref[delta >> 1] = value


def total_of(refs):
    value = refs[0][...].astype(F32)
    for ref in refs[1:]:
        value = value + ref[...].astype(F32)
    return value


def finish_ffn_kernel(a_ref, b_ref, c_ref, d_ref, up_ref, down_ref):
    total = total_of((a_ref, b_ref, c_ref, d_ref))[0]
    width = down_ref.shape[0]
    down_ref[...] = total[:, :width].T
    up_ref[...] = rows_of(total[:, width : width + width // 2], total[:, width + width // 2 :])


def finish_attend_kernel(
    a_ref, b_ref, c_ref, d_ref, va_ref, vb_ref, vc_ref, vd_ref,
    q_ref, kv_ref, red_ref, proj_ref, vm_ref, vh_ref,
):
    total = total_of((a_ref, b_ref, c_ref, d_ref))[0]
    width, rn = red_ref.shape[0], q_ref.shape[0]
    red_ref[...] = total[:, :width].T
    unit = [total[:, width + k * rn : width + (k + 1) * rn] for k in range(4)]
    q_ref[...] = unit[0].T
    kv_ref[...] = rows_of(unit[1], unit[2]).T
    proj_ref[...] = unit[3].T
    vector = total_of((va_ref, vb_ref, vc_ref, vd_ref))[0]
    vm_ref[...] = vector[: vm_ref.shape[0], :rn]
    vh_ref[...] = vector[: vh_ref.shape[0], rn : rn + width]


def call(kernel, inputs, outputs, scratch=(), scalars=0, limit=40, flops=0, moved=0):
    vmem = pl.BlockSpec(memory_space=pltpu.VMEM)
    smem = pl.BlockSpec(memory_space=pltpu.SMEM)
    return pl.pallas_call(
        kernel,
        out_shape=[jax.ShapeDtypeStruct(shape, kind) for shape, kind in outputs],
        in_specs=[smem] * scalars + [vmem] * (len(inputs) - scalars),
        out_specs=[vmem] * len(outputs),
        scratch_shapes=[pltpu.VMEM(shape, kind) for shape, kind in scratch],
        compiler_params=pltpu.CompilerParams(vmem_limit_bytes=limit * 2**20),
        cost_estimate=pl.CostEstimate(flops=flops, bytes_accessed=moved, transcendentals=0),
    )(*inputs)


def on_device(
    mesh_shape,
    tokens, cotangent, img_rows, img_cols,
    q_weight, kv_weight, reduce_weight, proj_weight, up_weight, down_weight, vec_model, vec_hidden,
):
    wide, narrow = mesh_shape
    tuned = (wide, narrow) == (PARTS_W, PARTS_N)
    capacity, width = tokens.shape
    hidden = vec_hidden.shape[1] * narrow
    cw, rn = width // PARTS_W, width // PARTS_N
    keys = capacity // 4
    piece = (cw, 2 * width)
    vpiece = (16, 2 * width)

    def swap(value, mask):
        pairs = [(i, i ^ mask) for i in range(wide * narrow)]
        return lax.ppermute(value, ("wide", "narrow"), pairs)

    def gather(value):
        near = jnp.concatenate([value[None]] + [swap(value[None], m) for m in (8, 16, 24)], axis=0)
        half = jnp.concatenate([near] + [swap(near, m) for m in (2, 4, 6)], axis=0)
        return half, swap(half, 1)

    def add(*parts):
        total = parts[0].astype(F32)
        for part in parts[1:]:
            total = total + part.astype(F32)
        return total.astype(BF16)

    def scatter(own, send):
        half = add(own, swap(send, 1))
        near = add(half[0:4], *[swap(half[4 * k : 4 * k + 4], 2 * k) for k in (1, 2, 3)])
        return [near[0:1]] + [swap(near[k : k + 1], 8 * k) for k in (1, 2, 3)]

    if tuned:
        pack_a, pack_b, pack_v = call(
            pack_kernel,
            (q_weight, kv_weight, reduce_weight, proj_weight, up_weight, down_weight, vec_model, vec_hidden),
            ((piece, BF16), (piece, BF16), (vpiece, BF16)),
        )
        own_a, oth_a = gather(pack_a)
        vec_pair = jnp.concatenate([pack_v[None], swap(pack_v[None], 1)], axis=0)
        vecs = jnp.concatenate([vec_pair, swap(vec_pair, 2)], axis=0)
        own_b, oth_b = gather(pack_b)
    else:
        own_a, oth_a, own_b, oth_b, vecs = gather_plain(
            q_weight, kv_weight, reduce_weight, proj_weight, up_weight, down_weight, vec_model, vec_hidden
        )

    square = (width, width)
    (
        x2, h1, n1, r1, patches, nk, rk, kn, q, kb, vb, p, o, wr, wq, wkv, wp, mv, hv,
    ) = call(
        functools.partial(attend_kernel, tuned),
        (img_rows, img_cols, tokens, own_a, oth_a, vecs),
        (
            ((capacity, width), F32), ((capacity, width), BF16), ((capacity, width), F32), ((capacity, 1), F32),
            ((capacity, width), BF16), ((keys, width), F32), ((keys, 1), F32), ((keys, width), BF16),
            ((capacity, width), BF16), ((HEADS * keys, width), BF16), ((HEADS * keys, width), BF16),
            ((capacity, HEADS * keys), F32), ((capacity, width), BF16),
            ((4,) + square, BF16), (square, BF16), ((2 * width, width), BF16), (square, BF16),
            ((16, width), F32), ((16, hidden), F32),
        ),
        scratch=(((capacity, HEADS * keys), F32),),
        scalars=2,
        flops=2 * 10**9,
    )

    padded = ((CHUNK // 128, capacity + 2 * PAD, 128), F32)
    halved = ((CHUNK // 128, capacity, 128), F32)
    chunked = ((capacity, CHUNK), F32)
    mixed, gown_b, gsend_b, dx2, mg, hg = call(
        functools.partial(ffn_kernel, tuned),
        (img_rows, img_cols, x2, cotangent, own_b, oth_b, mv, hv),
        (
            ((capacity, width), BF16), ((SLOTS,) + piece, BF16), ((SLOTS,) + piece, BF16),
            ((capacity, width), F32), ((16, width), F32), ((16, hidden), F32),
        ),
        scratch=(
            ((hidden, width), BF16), ((width, hidden), BF16), ((7, capacity, 128), F32),
            ((capacity, width), F32), ((capacity, 1), F32), ((capacity, width), BF16), ((width, capacity), BF16),
            ((capacity, width), BF16), ((width, capacity), BF16),
            padded, padded, padded, padded, padded, padded,
            halved, chunked, ((capacity, CHUNK), BF16), halved, ((capacity, CHUNK), BF16), chunked,
            ((capacity, width), F32), ((capacity, width), F32), ((width, hidden), F32), ((width, hidden), F32),
        ),
        scalars=2,
        flops=4 * 10**9,
    )

    token_grad, gown_a, gsend_a, vown, vsend = call(
        functools.partial(attend_back_kernel, tuned),
        (
            img_rows, img_cols, dx2, h1, n1, r1, patches, nk, rk, kn, q, kb, vb, p, o, wr, wq, wkv, wp,
            mv, mg, hg,
        ),
        (
            ((capacity, width), BF16), ((SLOTS,) + piece, BF16), ((SLOTS,) + piece, BF16),
            ((2,) + vpiece, BF16), ((2,) + vpiece, BF16),
        ),
        scratch=(
            ((capacity, HEADS * keys), F32), ((capacity, HEADS * keys), BF16), ((4,) + square, F32),
            (square, F32), ((2 * width, width), F32), (square, F32), ((capacity, width), F32),
        ),
        scalars=2,
        flops=2 * 10**9,
    )

    if not tuned:
        grads = scatter_plain(mesh_shape, width, gown_a, gsend_a, gown_b, gsend_b, vown, vsend)
        return (mixed, token_grad) + grads

    parts_b = scatter(gown_b, gsend_b)
    vhalf = add(vown, swap(vsend, 1))
    vnear = add(vhalf[0:1], swap(vhalf[1:2], 2), swap(vhalf[0:1], 4), swap(vhalf[1:2], 6))
    vparts = [vnear] + [swap(vnear, 8 * k) for k in (1, 2, 3)]
    parts_a = scatter(gown_a, gsend_a)
    up_grad, down_grad = call(
        finish_ffn_kernel, parts_b, (((rn, 4 * cw), F32), ((width, cw), F32))
    )
    q_grad, kv_grad, reduce_grad, proj_grad, vm_grad, vh_grad = call(
        finish_attend_kernel,
        (*parts_a, *vparts),
        (
            ((rn, cw), F32), ((rn, 2 * cw), F32), ((width, cw), F32), ((rn, cw), F32),
            ((11, rn), F32), ((11, width), F32),
        ),
    )
    return mixed, token_grad, q_grad, kv_grad, reduce_grad, proj_grad, up_grad, down_grad, vm_grad, vh_grad


def gather_plain(q, kv, reduce, proj, up, down, vec_model, vec_hidden):
    def whole(value):
        rows = lax.all_gather(value, "narrow", axis=0, tiled=True)
        return lax.all_gather(rows, "wide", axis=1, tiled=True).T

    q, kv, reduce, proj, up, down = (whole(v) for v in (q, kv, reduce, proj, up, down))
    width = q.shape[0]
    cw, rn = width // PARTS_W, width // PARTS_N

    def pieces(turned, blocks):
        split = turned.reshape(PARTS_W, blocks, cw, PARTS_N, -1)
        return split.transpose(0, 3, 2, 1, 4).reshape(PARTS_W, PARTS_N, cw, -1)

    def slots(value):
        value = value.reshape(4, 4, 2, cw, -1).transpose(2, 1, 0, 3, 4)
        value = value.reshape(2, SLOTS, cw, -1)
        return value[0], value[1]

    a = jnp.concatenate([pieces(reduce, 1), pieces(q, 1), pieces(kv, 2), pieces(proj, 1)], axis=-1)
    b = jnp.concatenate([pieces(down, 1), pieces(up, 4)], axis=-1)
    vm = lax.all_gather(vec_model, "narrow", axis=1, tiled=True)
    vh = lax.all_gather(vec_hidden, "narrow", axis=1, tiled=True)
    both = jnp.concatenate([vm.reshape(11, PARTS_N, rn), vh.reshape(11, PARTS_N, width)], axis=-1)
    vecs = jnp.pad(both.transpose(1, 0, 2), ((0, 0), (0, 5), (0, 3 * rn)))
    return (*slots(a), *slots(b), vecs)


def scatter_plain(mesh_shape, width, gown_a, gsend_a, gown_b, gsend_b, vown, vsend):
    cw, rn = width // PARTS_W, width // PARTS_N

    def devices(own, send):
        both = jnp.stack([own, send]).reshape(2, 4, 4, cw, -1).transpose(2, 1, 0, 3, 4)
        return both.reshape(PARTS_W, PARTS_N, cw, -1)

    def natural(value, blocks):
        split = value.reshape(PARTS_W, PARTS_N, cw, blocks, -1).transpose(0, 3, 2, 1, 4)
        return split.reshape(PARTS_W * blocks * cw, -1).T

    def share(value):
        columns = lax.psum_scatter(value.astype(BF16), "wide", scatter_dimension=1, tiled=True)
        return lax.psum_scatter(columns, "narrow", scatter_dimension=0, tiled=True).astype(F32)

    a = devices(gown_a, gsend_a)
    b = devices(gown_b, gsend_b)
    reduce = natural(a[..., :width], 1)
    q = natural(a[..., width : width + rn], 1)
    kv = natural(a[..., width + rn : width + 3 * rn], 2)
    proj = natural(a[..., width + 3 * rn :], 1)
    down = natural(b[..., :width], 1)
    up = b[..., width:].reshape(PARTS_W, PARTS_N, cw, rn // cw, 4 * cw).transpose(1, 3, 2, 0, 4)
    up = up.reshape(width, PARTS_W * 4 * cw)
    vectors = jnp.stack([vown, vsend], axis=1).reshape(PARTS_N, 16, -1)[:, :11].transpose(1, 0, 2)
    vm = vectors[..., :rn].reshape(11, width)
    vh = vectors[..., rn : rn + width].reshape(11, PARTS_N * width)

    def share_vector(value):
        total = lax.psum(value.astype(BF16), "wide")
        return lax.psum_scatter(total, "narrow", scatter_dimension=1, tiled=True).astype(F32)

    return tuple(share(v) for v in (q, kv, reduce, proj, up, down)) + (share_vector(vm), share_vector(vh))


def solution(mesh):
    both, rows, weight, vector = P(("wide", "narrow"), None), P(("wide", "narrow")), P("narrow", "wide"), P(None, "narrow")
    return jax.shard_map(
        functools.partial(on_device, (mesh.shape["wide"], mesh.shape["narrow"])),
        mesh=mesh,
        in_specs=(both, both, rows, rows) + (weight,) * 6 + (vector,) * 2,
        out_specs=(both, both) + (weight,) * 6 + (vector,) * 2,
        check_vma=False,
    )
```

time: 944 us -> 139 us (0.15)
  waiting for transfers between devices: 434 us -> 29.9 us
  blocking collectives: 276 us -> 0 us
  local copies, waits for them, and re-layouts: 98.8 us -> 12.7 us
  other arithmetic: 70.5 us -> 0.77 us
  Pallas kernels: 0 us -> 48.2 us
  starting transfers between devices: 0.83 us -> 45.6 us
  matrix products: 35.8 us -> 0 us
  between operations: 18.8 us -> 1.01 us
    all_gather x14 -> x0, blocking collectives: 239 us -> none  [the longest x1 34.7 us: collect(): lax.all_gather(inner[4], 'wide', axis=1, tiled=True)]
    reduce_scatter x4 -> x0, waiting for transfers between devices: 237 us -> none  [the longest x1 64.1 us: on_device(): lax.psum_scatter(grads[4].astype(jnp.bfloat16), 'wide', scatter_dimension...]
    unnamed x24 -> x0, waiting for transfers between devices: 197 us -> none
    gather x24 -> x0, local copies, waits for them, and re-layouts: 62.5 us -> none  [the longest x9 27.7 us: backward_pass(): jnp.take(grad_conv, near_index[mirror], axis=0)]
    pallas_call x0 -> x6, Pallas kernels: none -> 48.2 us  [call(): pl.pallas_call(kernel, out_shape=[jax.ShapeDtypeStruct(shape, kind) for s...]
    ppermute x0 -> x37, starting transfers between devices: none -> 45.6 us  [swap(): return lax.ppermute(value, ('wide', 'narrow'), pairs)]
    psum x1 -> x0, blocking collectives: 37.1 us -> none  [on_device(): lax.psum(grads[6].astype(jnp.bfloat16), 'wide').astype(jnp.float32)]
    dot_general x23 -> x0, matrix products: 35.2 us -> none  [the longest x6 5.49 us: product(): return jnp.dot(left, right, preferred_element_type=jnp.float32)]
  transfers between devices with their start and end apart: 14 -> 37, of which waited for: 13 -> 14; matrix products, arithmetic and copies ran while one was open for 8% -> 5% of each run, Pallas kernels for 0% -> 6%
where the time goes in v1:
time: 139 us; the launch traced here: 138 us
  Pallas kernels  48.2 us (35%)
  starting transfers between devices  45.6 us (33%)
  waiting for transfers between devices  29.9 us (22%)
  local copies, waits for them, and re-layouts  12.7 us (9%)
    pallas_call x6, Pallas kernels, call(): pl.pallas_call(kernel, out_shape=[jax.ShapeDtypeStruct(shape, kind) for s...  48.2 us
    ppermute x37, starting transfers between devices, swap(): return lax.ppermute(value, ('wide', 'narrow'), pairs)  45.6 us
    ppermute x37, waiting for transfers between devices, swap(): return lax.ppermute(value, ('wide', 'narrow'), pairs)  29.9 us
    unnamed x37, local copies, waits for them, and re-layouts  12.5 us
  transfers between devices with their start and end apart: 37, of which 14 were waited for; matrix products, arithmetic and copies ran while one was open for 5% of the time, Pallas kernels for 6%

profile of v1, /device:TPU:0, one launch (start us, length us, event | category | flops | bytes accessed | tf_op | source)
XLA Modules:
  0.0 138.2 jit_solution(2893716205535737967)
XLA Ops:
  7.2 5.1 %collective-permute-start.2 = (bf16[1,40,640]{2,1,0:T(8,128)(2,1)S(1)}, bf16[1,40,640]{2,1,0:T(8,128)(2,1)S(1)}, u32[]{:S(2)}, u32[]{:S(2)}) collective-permute-start(bf16[1,40,640]{2,1,0:T(8,128)(2,1)S(1)} %bitcast.9), channel_id=1, source_target_pairs={{0,24},{1,25},{2,26},{3,27},{4,28},{5,29},{6,30},{7,31},{8,16},{9,... | collective-permute-start | bytes 153608 | tf_op jit(solution)/shard_map/ppermute | solution.py:617
  12.9 3.7 %collective-permute-start.11 = (bf16[1,40,640]{2,1,0:T(8,128)(2,1)S(1)}, bf16[1,40,640]{2,1,0:T(8,128)(2,1)S(1)}, u32[]{:S(2)}, u32[]{:S(2)}) collective-permute-start(bf16[1,40,640]{2,1,0:T(8,128)(2,1)S(1)} %bitcast.5), channel_id=1, source_target_pairs={{0,24},{1,25},{2,26},{3,27},{4,28},{5,29},{6,30},{7,31},{8,16},{9,... | collective-permute-start | bytes 153608 | tf_op jit(solution)/shard_map/ppermute | solution.py:617
  17.4 1.3 collective-permute-done.1
  18.7 2.5 %collective-permute-start.5 = (bf16[4,40,640]{2,1,0:T(8,128)(2,1)S(1)}, bf16[4,40,640]{2,1,0:T(8,128)(2,1)S(1)}, u32[]{:S(2)}, u32[]{:S(2)}) collective-permute-start(bf16[4,40,640]{2,1,0:T(8,128)(2,1)S(1)} %pad_maximum_fusion), channel_id=1, source_target_pairs={{0,6},{1,7},{2,4},{3,5},{4,2},{5,3},{6,0},{7,1},{8,14},{9,15},{10,... | collective-permute-start | bytes 614408 | tf_op jit(solution)/shard_map/ppermute | solution.py:617
  22.3 2.5 %collective-permute-start.14 = (bf16[4,40,640]{2,1,0:T(8,128)(2,1)S(1)}, bf16[4,40,640]{2,1,0:T(8,128)(2,1)S(1)}, u32[]{:S(2)}, u32[]{:S(2)}) collective-permute-start(bf16[4,40,640]{2,1,0:T(8,128)(2,1)S(1)} %pad_maximum_fusion.1), channel_id=1, source_target_pairs={{0,6},{1,7},{2,4},{3,5},{4,2},{5,3},{6,0},{7,1},{8,14},{9,15},{10,... | collective-permute-start | bytes 614408 | tf_op jit(solution)/shard_map/ppermute | solution.py:617
  25.4 6.7 %collective-permute-done.3 = bf16[4,40,640]{2,1,0:T(8,128)(2,1)S(1)} collective-permute-done((bf16[4,40,640]{2,1,0:T(8,128)(2,1)S(1)}, bf16[4,40,640]{2,1,0:T(8,128)(2,1)S(1)}, u32[]{:S(2)}, u32[]{:S(2)}) %collective-permute-start.3) | collective-permute-done | bytes 204832 | tf_op jit(solution)/shard_map/ppermute | solution.py:617
  32.2 1.5 %collective-permute-start.12 = (bf16[4,40,640]{2,1,0:T(8,128)(2,1)S(1)}, bf16[4,40,640]{2,1,0:T(8,128)(2,1)S(1)}, u32[]{:S(2)}, u32[]{:S(2)}) collective-permute-start(bf16[4,40,640]{2,1,0:T(8,128)(2,1)S(1)} %pad_maximum_fusion.1), channel_id=1, source_target_pairs={{0,2},{1,3},{2,0},{3,1},{4,6},{5,7},{6,4},{7,5},{8,10},{9,11},{10,... | collective-permute-start | bytes 614408 | tf_op jit(solution)/shard_map/ppermute | solution.py:617
  33.9 4.1 %collective-permute-done.12 = bf16[4,40,640]{2,1,0:T(8,128)(2,1)S(1)} collective-permute-done((bf16[4,40,640]{2,1,0:T(8,128)(2,1)S(1)}, bf16[4,40,640]{2,1,0:T(8,128)(2,1)S(1)}, u32[]{:S(2)}, u32[]{:S(2)}) %collective-permute-start.12) | collective-permute-done | bytes 204832 | tf_op jit(solution)/shard_map/ppermute | solution.py:617
  38.7 1.5 %collective-permute-done.7 = bf16[1,16,640]{2,1,0:T(8,128)(2,1)S(1)} collective-permute-done((bf16[1,16,640]{2,1,0:T(8,128)(2,1)S(1)}, bf16[1,16,640]{2,1,0:T(8,128)(2,1)S(1)}, u32[]{:S(2)}, u32[]{:S(2)}) %collective-permute-start.7) | collective-permute-done | bytes 20512 | tf_op jit(solution)/shard_map/ppermute | solution.py:617
  40.2 1.6 %collective-permute-start.8 = (bf16[2,16,640]{2,1,0:T(8,128)(2,1)S(1)}, bf16[2,16,640]{2,1,0:T(8,128)(2,1)S(1)}, u32[]{:S(2)}, u32[]{:S(2)}) collective-permute-start(bf16[2,16,640]{2,1,0:T(8,128)(2,1)S(1)} %pad_maximum_fusion.3), channel_id=1, source_target_pairs={{0,2},{1,3},{2,0},{3,1},{4,6},{5,7},{6,4},{7,5},{8,10},{9,11},{10,... | collective-permute-start | bytes 122888 | tf_op jit(solution)/shard_map/ppermute | solution.py:617
  42.0 1.2 copy.27.cot_ref
  43.2 1.1 collective-permute-done.8
  44.3 6.8 %shard_map.196 = (f32[512,320]{1,0:T(8,128)S(1)}, bf16[512,320]{1,0:T(8,128)(2,1)S(1)}, f32[512,320]{1,0:T(8,128)S(1)}, f32[512,1]{1,0:T(8,128)S(1)}, bf16[512,3...) custom-call(s32[2]{0:T(128)S(1)} %copy-done.4, ...), custom_call_target="tpu_custom_call" | custom-call | flops 2000000000 | tf_op jit(solution)/shard_map/pallas_call | solution.py:590
  51.1 29.6 %shard_map.197 = (bf16[512,320]{1,0:T(8,128)(2,1)S(1)}, bf16[16,40,640]{2,1,0:T(8,128)(2,1)S(1)}, bf16[16,40,640]{2,1,0:T(8,128)(2,1)S(1)}, f32[512,320]{1,0:T(8...) custom-call(s32[2]{0:T(128)S(1)} %copy-done.4, s32[2]{0:T(128)S(1)} %copy-done.5, ...), custom_call_target="tpu_custom_call" | custom-call | flops 4000000000 | tf_op jit(solution)/shard_map/pallas_call | solution.py:590
  80.8 9.8 %shard_map.198 = (bf16[512,320]{1,0:T(8,128)(2,1)S(1)}, bf16[16,40,640]{2,1,0:T(8,128)(2,1)S(1)}, bf16[16,40,640]{2,1,0:T(8,128)(2,1)S(1)}, bf16[2,16,640]{2,1,0:T(8,128)(2,1)S(1)}, bf16[2,16,640]{2,1,0:T(8,128)(2,1)S(1)}) custom-call(s32[2]{0:T(128)S(1)} %copy-done.4, s32[2]{0:T(128)S(1)} %copy-done.5, f32[512,320]{1,0:T(8,128)S(1)} %get-tuple-element.58.dx2_ref, ...), custom_call_target="tpu_custom_call" | custom-call | flops 2000000000 | tf_op jit(solution)/shard_map/pallas_call | solution.py:590
  91.2 1.8 %collective-permute-done.23 = bf16[2,16,640]{2,1,0:T(8,128)(2,1)S(1)} collective-permute-done((bf16[2,16,640]{2,1,0:T(8,128)(2,1)S(1)}, bf16[2,16,640]{2,1,0:T(8,128)(2,1)S(1)}, u32[]{:S(2)}, u32[]{:S(2)}) %collective-permute-start.23) | collective-permute-done | bytes 40992 | tf_op jit(solution)/shard_map/ppermute | solution.py:617
  93.8 2.1 %collective-permute-start.26 = (bf16[1,16,640]{2,1,0:T(8,128)(2,1)S(1)}, bf16[1,16,640]{2,1,0:T(8,128)(2,1)S(1)}, u32[]{:S(2)}, u32[]{:S(2)}) collective-permute-start(bf16[1,16,640]{2,1,0:T(8,128)(2,1)S(1)} %get-tuple-element.117), channel_id=1, source_target_pairs={{0,6},{1,7},{2,4},{3,5},{4,2},{5,3},{6,0},{7,1},{8,14},{9,15},{10,... | collective-permute-start | bytes 61448 | tf_op jit(solution)/shard_map/ppermute | solution.py:617
  96.9 1.6 %collective-permute-done.26 = bf16[1,16,640]{2,1,0:T(8,128)(2,1)S(1)} collective-permute-done((bf16[1,16,640]{2,1,0:T(8,128)(2,1)S(1)}, bf16[1,16,640]{2,1,0:T(8,128)(2,1)S(1)}, u32[]{:S(2)}, u32[]{:S(2)}) %collective-permute-start.26) | collective-permute-done | bytes 20512 | tf_op jit(solution)/shard_map/ppermute | solution.py:617
  98.5 1.2 collective-permute-done.24
  99.7 2.7 %collective-permute-start.29 = (bf16[1,16,640]{2,1,0:T(8,128)(2,1)S(1)}, bf16[1,16,640]{2,1,0:T(8,128)(2,1)S(1)}, u32[]{:S(2)}, u32[]{:S(2)}) collective-permute-start(bf16[1,16,640]{2,1,0:T(8,128)(2,1)S(1)} %add_convert_fusion.5.va_ref), channel_id=1, source_target_pairs={{0,24},{1,25},{2,26},{3,27},{4,28},{5,29},{6,30},{7,31},{8,16},{9,... | collective-permute-start | bytes 61448 | tf_op jit(solution)/shard_map/ppermute | solution.py:617
  103.3 1.5 %collective-permute-start.19 = (bf16[4,40,640]{2,1,0:T(8,128)(2,1)S(1)}, bf16[4,40,640]{2,1,0:T(8,128)(2,1)S(1)}, u32[]{:S(2)}, u32[]{:S(2)}) collective-permute-start(bf16[4,40,640]{2,1,0:T(8,128)(2,1)S(1)} %get-tuple-element.106), channel_id=1, source_target_pairs={{0,6},{1,7},{2,4},{3,5},{4,2},{5,3},{6,0},{7,1},{8,14},{9,15},{10,... | collective-permute-start | bytes 614408 | tf_op jit(solution)/shard_map/ppermute | solution.py:617
  104.8 1.5 %collective-permute-start.18 = (bf16[4,40,640]{2,1,0:T(8,128)(2,1)S(1)}, bf16[4,40,640]{2,1,0:T(8,128)(2,1)S(1)}, u32[]{:S(2)}, u32[]{:S(2)}) collective-permute-start(bf16[4,40,640]{2,1,0:T(8,128)(2,1)S(1)} %get-tuple-element.107), channel_id=1, source_target_pairs={{0,4},{1,5},{2,6},{3,7},{4,0},{5,1},{6,2},{7,3},{8,12},{9,13},{10,... | collective-permute-start | bytes 614408 | tf_op jit(solution)/shard_map/ppermute | solution.py:617
  106.5 4.2 %collective-permute-done.17 = bf16[4,40,640]{2,1,0:T(8,128)(2,1)S(1)} collective-permute-done((bf16[4,40,640]{2,1,0:T(8,128)(2,1)S(1)}, bf16[4,40,640]{2,1,0:T(8,128)(2,1)S(1)}, u32[]{:S(2)}, u32[]{:S(2)}) %collective-permute-start.17) | collective-permute-done | bytes 204832 | tf_op jit(solution)/shard_map/ppermute | solution.py:617
  111.3 4.0 %collective-permute-done.19 = bf16[4,40,640]{2,1,0:T(8,128)(2,1)S(1)} collective-permute-done((bf16[4,40,640]{2,1,0:T(8,128)(2,1)S(1)}, bf16[4,40,640]{2,1,0:T(8,128)(2,1)S(1)}, u32[]{:S(2)}, u32[]{:S(2)}) %collective-permute-start.19) | collective-permute-done | bytes 204832 | tf_op jit(solution)/shard_map/ppermute | solution.py:617
  115.3 1.4 %collective-permute-start.33 = (bf16[4,40,640]{2,1,0:T(8,128)(2,1)S(1)}, bf16[4,40,640]{2,1,0:T(8,128)(2,1)S(1)}, u32[]{:S(2)}, u32[]{:S(2)}) collective-permute-start(bf16[4,40,640]{2,1,0:T(8,128)(2,1)S(1)} %get-tuple-element.103), channel_id=1, source_target_pairs={{0,6},{1,7},{2,4},{3,5},{4,2},{5,3},{6,0},{7,1},{8,14},{9,15},{10,... | collective-permute-start | bytes 614408 | tf_op jit(solution)/shard_map/ppermute | solution.py:617
  116.7 1.4 %collective-permute-start.32 = (bf16[4,40,640]{2,1,0:T(8,128)(2,1)S(1)}, bf16[4,40,640]{2,1,0:T(8,128)(2,1)S(1)}, u32[]{:S(2)}, u32[]{:S(2)}) collective-permute-start(bf16[4,40,640]{2,1,0:T(8,128)(2,1)S(1)} %get-tuple-element.104), channel_id=1, source_target_pairs={{0,4},{1,5},{2,6},{3,7},{4,0},{5,1},{6,2},{7,3},{8,12},{9,13},{10,... | collective-permute-start | bytes 614408 | tf_op jit(solution)/shard_map/ppermute | solution.py:617
  119.0 1.8 %collective-permute-start.27 = (bf16[1,16,640]{2,1,0:T(8,128)(2,1)S(1)}, bf16[1,16,640]{2,1,0:T(8,128)(2,1)S(1)}, u32[]{:S(2)}, u32[]{:S(2)}) collective-permute-start(bf16[1,16,640]{2,1,0:T(8,128)(2,1)S(1)} %add_convert_fusion.5.va_ref), channel_id=1, source_target_pairs={{0,8},{1,9},{2,10},{3,11},{4,12},{5,13},{6,14},{7,15},{8,0},{9,1},... | collective-permute-start | bytes 61448 | tf_op jit(solution)/shard_map/ppermute | solution.py:617
  120.9 1.2 collective-permute-done.33
  122.0 2.0 %collective-permute-start.22 = (bf16[1,40,640]{2,1,0:T(8,128)(2,1)S(1)}, bf16[1,40,640]{2,1,0:T(8,128)(2,1)S(1)}, u32[]{:S(2)}, u32[]{:S(2)}) collective-permute-start(bf16[1,40,640]{2,1,0:T(8,128)(2,1)S(1)} %get-tuple-element.112), channel_id=1, source_target_pairs={{0,24},{1,25},{2,26},{3,27},{4,28},{5,29},{6,30},{7,31},{8,16},{9,... | collective-permute-start | bytes 153608 | tf_op jit(solution)/shard_map/ppermute | solution.py:617
  124.1 3.0 %collective-permute-start.21 = (bf16[1,40,640]{2,1,0:T(8,128)(2,1)S(1)}, bf16[1,40,640]{2,1,0:T(8,128)(2,1)S(1)}, u32[]{:S(2)}, u32[]{:S(2)}) collective-permute-start(bf16[1,40,640]{2,1,0:T(8,128)(2,1)S(1)} %get-tuple-element.113), channel_id=1, source_target_pairs={{0,16},{1,17},{2,18},{3,19},{4,20},{5,21},{6,22},{7,23},{8,24},{9,... | collective-permute-start | bytes 153608 | tf_op jit(solution)/shard_map/ppermute | solution.py:617
  127.3 1.5 %collective-permute-start.36 = (bf16[1,40,640]{2,1,0:T(8,128)(2,1)S(1)}, bf16[1,40,640]{2,1,0:T(8,128)(2,1)S(1)}, u32[]{:S(2)}, u32[]{:S(2)}) collective-permute-start(bf16[1,40,640]{2,1,0:T(8,128)(2,1)S(1)} %get-tuple-element.108), channel_id=1, source_target_pairs={{0,24},{1,25},{2,26},{3,27},{4,28},{5,29},{6,30},{7,31},{8,16},{9,... | collective-permute-start | bytes 153608 | tf_op jit(solution)/shard_map/ppermute | solution.py:617
  128.8 2.0 %collective-permute-start.35 = (bf16[1,40,640]{2,1,0:T(8,128)(2,1)S(1)}, bf16[1,40,640]{2,1,0:T(8,128)(2,1)S(1)}, u32[]{:S(2)}, u32[]{:S(2)}) collective-permute-start(bf16[1,40,640]{2,1,0:T(8,128)(2,1)S(1)} %get-tuple-element.109), channel_id=1, source_target_pairs={{0,16},{1,17},{2,18},{3,19},{4,20},{5,21},{6,22},{7,23},{8,24},{9,... | collective-permute-start | bytes 153608 | tf_op jit(solution)/shard_map/ppermute | solution.py:617
  (102 shorter events, 23.2 us)
Async XLA Ops:
  7.2 9.5 %collective-permute-start.2 = (bf16[1,40,640]{2,1,0:T(8,128)(2,1)S(1)}, bf16[1,40,640]{2,1,0:T(8,128)(2,1)S(1)}, u32[]{:S(2)}, u32[]{:S(2)}) collective-permute-start(bf16[1,40,640]{2,1,0:T(8,128)(2,1)S(1)} %bitcast.9), channel_id=1, source_target_pairs={{0,24},{1,25},{2,26},{3,27},{4,28},{5,29},{6,30},{7,31},{8,16},{9,... | collective-permute-start | bytes 153608 | tf_op jit(solution)/shard_map/ppermute | solution.py:617
  12.3 6.4 %collective-permute-start.1 = (bf16[1,40,640]{2,1,0:T(8,128)(2,1)S(1)}, bf16[1,40,640]{2,1,0:T(8,128)(2,1)S(1)}, u32[]{:S(2)}, u32[]{:S(2)}) collective-permute-start(bf16[1,40,640]{2,1,0:T(8,128)(2,1)S(1)} %bitcast.10), channel_id=1, source_target_pairs={{0,16},{1,17},{2,18},{3,19},{4,20},{5,21},{6,22},{7,23},{8,24},{9,... | collective-permute-start | bytes 153608 | tf_op jit(solution)/shard_map/ppermute | solution.py:617
  12.3 6.4 %collective-permute-start = (bf16[1,40,640]{2,1,0:T(8,128)(2,1)S(1)}, bf16[1,40,640]{2,1,0:T(8,128)(2,1)S(1)}, u32[]{:S(2)}, u32[]{:S(2)}) collective-permute-start(bf16[1,40,640]{2,1,0:T(8,128)(2,1)S(1)} %bitcast.11), channel_id=1, source_target_pairs={{0,8},{1,9},{2,10},{3,11},{4,12},{5,13},{6,14},{7,15},{8,0},{9,1},... | collective-permute-start | bytes 153608 | tf_op jit(solution)/shard_map/ppermute | solution.py:617
  12.9 8.8 %collective-permute-start.11 = (bf16[1,40,640]{2,1,0:T(8,128)(2,1)S(1)}, bf16[1,40,640]{2,1,0:T(8,128)(2,1)S(1)}, u32[]{:S(2)}, u32[]{:S(2)}) collective-permute-start(bf16[1,40,640]{2,1,0:T(8,128)(2,1)S(1)} %bitcast.5), channel_id=1, source_target_pairs={{0,24},{1,25},{2,26},{3,27},{4,28},{5,29},{6,30},{7,31},{8,16},{9,... | collective-permute-start | bytes 153608 | tf_op jit(solution)/shard_map/ppermute | solution.py:617
  16.7 5.6 %collective-permute-start.10 = (bf16[1,40,640]{2,1,0:T(8,128)(2,1)S(1)}, bf16[1,40,640]{2,1,0:T(8,128)(2,1)S(1)}, u32[]{:S(2)}, u32[]{:S(2)}) collective-permute-start(bf16[1,40,640]{2,1,0:T(8,128)(2,1)S(1)} %bitcast.6), channel_id=1, source_target_pairs={{0,16},{1,17},{2,18},{3,19},{4,20},{5,21},{6,22},{7,23},{8,24},{9,... | collective-permute-start | bytes 153608 | tf_op jit(solution)/shard_map/ppermute | solution.py:617
  16.7 5.6 %collective-permute-start.9 = (bf16[1,40,640]{2,1,0:T(8,128)(2,1)S(1)}, bf16[1,40,640]{2,1,0:T(8,128)(2,1)S(1)}, u32[]{:S(2)}, u32[]{:S(2)}) collective-permute-start(bf16[1,40,640]{2,1,0:T(8,128)(2,1)S(1)} %bitcast.7), channel_id=1, source_target_pairs={{0,8},{1,9},{2,10},{3,11},{4,12},{5,13},{6,14},{7,15},{8,0},{9,1},... | collective-permute-start | bytes 153608 | tf_op jit(solution)/shard_map/ppermute | solution.py:617
  18.7 15.0 %collective-permute-start.5 = (bf16[4,40,640]{2,1,0:T(8,128)(2,1)S(1)}, bf16[4,40,640]{2,1,0:T(8,128)(2,1)S(1)}, u32[]{:S(2)}, u32[]{:S(2)}) collective-permute-start(bf16[4,40,640]{2,1,0:T(8,128)(2,1)S(1)} %pad_maximum_fusion), channel_id=1, source_target_pairs={{0,6},{1,7},{2,4},{3,5},{4,2},{5,3},{6,0},{7,1},{8,14},{9,15},{10,... | collective-permute-start | bytes 614408 | tf_op jit(solution)/shard_map/ppermute | solution.py:617
  21.2 12.5 %collective-permute-start.4 = (bf16[4,40,640]{2,1,0:T(8,128)(2,1)S(1)}, bf16[4,40,640]{2,1,0:T(8,128)(2,1)S(1)}, u32[]{:S(2)}, u32[]{:S(2)}) collective-permute-start(bf16[4,40,640]{2,1,0:T(8,128)(2,1)S(1)} %pad_maximum_fusion), channel_id=1, source_target_pairs={{0,4},{1,5},{2,6},{3,7},{4,0},{5,1},{6,2},{7,3},{8,12},{9,13},{10,... | collective-permute-start | bytes 614408 | tf_op jit(solution)/shard_map/ppermute | solution.py:617
  21.7 10.4 %collective-permute-start.3 = (bf16[4,40,640]{2,1,0:T(8,128)(2,1)S(1)}, bf16[4,40,640]{2,1,0:T(8,128)(2,1)S(1)}, u32[]{:S(2)}, u32[]{:S(2)}) collective-permute-start(bf16[4,40,640]{2,1,0:T(8,128)(2,1)S(1)} %pad_maximum_fusion), channel_id=1, source_target_pairs={{0,2},{1,3},{2,0},{3,1},{4,6},{5,7},{6,4},{7,5},{8,10},{9,11},{10,... | collective-permute-start | bytes 614408 | tf_op jit(solution)/shard_map/ppermute | solution.py:617
  22.3 15.7 %collective-permute-start.14 = (bf16[4,40,640]{2,1,0:T(8,128)(2,1)S(1)}, bf16[4,40,640]{2,1,0:T(8,128)(2,1)S(1)}, u32[]{:S(2)}, u32[]{:S(2)}) collective-permute-start(bf16[4,40,640]{2,1,0:T(8,128)(2,1)S(1)} %pad_maximum_fusion.1), channel_id=1, source_target_pairs={{0,6},{1,7},{2,4},{3,5},{4,2},{5,3},{6,0},{7,1},{8,14},{9,15},{10,... | collective-permute-start | bytes 614408 | tf_op jit(solution)/shard_map/ppermute | solution.py:617
  24.8 13.2 %collective-permute-start.13 = (bf16[4,40,640]{2,1,0:T(8,128)(2,1)S(1)}, bf16[4,40,640]{2,1,0:T(8,128)(2,1)S(1)}, u32[]{:S(2)}, u32[]{:S(2)}) collective-permute-start(bf16[4,40,640]{2,1,0:T(8,128)(2,1)S(1)} %pad_maximum_fusion.1), channel_id=1, source_target_pairs={{0,4},{1,5},{2,6},{3,7},{4,0},{5,1},{6,2},{7,3},{8,12},{9,13},{10,... | collective-permute-start | bytes 614408 | tf_op jit(solution)/shard_map/ppermute | solution.py:617
  32.2 5.8 %collective-permute-start.12 = (bf16[4,40,640]{2,1,0:T(8,128)(2,1)S(1)}, bf16[4,40,640]{2,1,0:T(8,128)(2,1)S(1)}, u32[]{:S(2)}, u32[]{:S(2)}) collective-permute-start(bf16[4,40,640]{2,1,0:T(8,128)(2,1)S(1)} %pad_maximum_fusion.1), channel_id=1, source_target_pairs={{0,2},{1,3},{2,0},{3,1},{4,6},{5,7},{6,4},{7,5},{8,10},{9,11},{10,... | collective-permute-start | bytes 614408 | tf_op jit(solution)/shard_map/ppermute | solution.py:617
  33.8 10.5 %collective-permute-start.6 = (bf16[16,40,640]{2,1,0:T(8,128)(2,1)S(1)}, bf16[16,40,640]{2,1,0:T(8,128)(2,1)S(1)}, u32[]{:S(2)}, u32[]{:S(2)}) collective-permute-start(bf16[16,40,640]{2,1,0:T(8,128)(2,1)S(1)} %constant_dynamic-update-slice_fusion.own_ref), channel_id=1, source_target_pairs={{0,1},{1,0},{2,3},{3,2},{4,5},{5,4},{6,7},{7,6},{8,9},{9,8},{10,11... | collective-permute-start | bytes 2457608 | tf_op jit(solution)/shard_map/ppermute | solution.py:617
  38.1 13.0 %collective-permute-start.15 = (bf16[16,40,640]{2,1,0:T(8,128)(2,1)S(1)}, bf16[16,40,640]{2,1,0:T(8,128)(2,1)}, u32[]{:S(2)}, u32[]{:S(2)}) collective-permute-start(bf16[16,40,640]{2,1,0:T(8,128)(2,1)S(1)} %constant_dynamic-update-slice_fusion.7.own_ref), channel_id=1, source_target_pairs={{0,1},{1,0},{2,3},{3,2},{4,5},{5,4},{6,7},{7,6},{8,9},{9,8},{10,11... | collective-permute-start | bytes 2457608 | tf_op jit(solution)/shard_map/ppermute | solution.py:617
  90.5 11.9 %collective-permute-start.16 = (bf16[16,40,640]{2,1,0:T(8,128)(2,1)S(1)}, bf16[16,40,640]{2,1,0:T(8,128)(2,1)S(1)}, u32[]{:S(2)}, u32[]{:S(2)}) collective-permute-start(bf16[16,40,640]{2,1,0:T(8,128)(2,1)S(1)} %get-tuple-element.79), channel_id=1, source_target_pairs={{0,1},{1,0},{2,3},{3,2},{4,5},{5,4},{6,7},{7,6},{8,9},{9,8},{10,11... | collective-permute-start | bytes 2457608 | tf_op jit(solution)/shard_map/ppermute | solution.py:617
  91.1 13.7 %collective-permute-start.30 = (bf16[16,40,640]{2,1,0:T(8,128)(2,1)S(1)}, bf16[16,40,640]{2,1,0:T(8,128)(2,1)S(1)}, u32[]{:S(2)}, u32[]{:S(2)}) collective-permute-start(bf16[16,40,640]{2,1,0:T(8,128)(2,1)S(1)} %get-tuple-element.87), channel_id=1, source_target_pairs={{0,1},{1,0},{2,3},{3,2},{4,5},{5,4},{6,7},{7,6},{8,9},{9,8},{10,11... | collective-permute-start | bytes 2457608 | tf_op jit(solution)/shard_map/ppermute | solution.py:617
  93.8 4.7 %collective-permute-start.26 = (bf16[1,16,640]{2,1,0:T(8,128)(2,1)S(1)}, bf16[1,16,640]{2,1,0:T(8,128)(2,1)S(1)}, u32[]{:S(2)}, u32[]{:S(2)}) collective-permute-start(bf16[1,16,640]{2,1,0:T(8,128)(2,1)S(1)} %get-tuple-element.117), channel_id=1, source_target_pairs={{0,6},{1,7},{2,4},{3,5},{4,2},{5,3},{6,0},{7,1},{8,14},{9,15},{10,... | collective-permute-start | bytes 61448 | tf_op jit(solution)/shard_map/ppermute | solution.py:617
  99.7 27.5 %collective-permute-start.29 = (bf16[1,16,640]{2,1,0:T(8,128)(2,1)S(1)}, bf16[1,16,640]{2,1,0:T(8,128)(2,1)S(1)}, u32[]{:S(2)}, u32[]{:S(2)}) collective-permute-start(bf16[1,16,640]{2,1,0:T(8,128)(2,1)S(1)} %add_convert_fusion.5.va_ref), channel_id=1, source_target_pairs={{0,24},{1,25},{2,26},{3,27},{4,28},{5,29},{6,30},{7,31},{8,16},{9,... | collective-permute-start | bytes 61448 | tf_op jit(solution)/shard_map/ppermute | solution.py:617
  102.4 24.9 %collective-permute-start.28 = (bf16[1,16,640]{2,1,0:T(8,128)(2,1)S(1)}, bf16[1,16,640]{2,1,0:T(8,128)(2,1)S(1)}, u32[]{:S(2)}, u32[]{:S(2)}) collective-permute-start(bf16[1,16,640]{2,1,0:T(8,128)(2,1)S(1)} %add_convert_fusion.5.va_ref), channel_id=1, source_target_pairs={{0,16},{1,17},{2,18},{3,19},{4,20},{5,21},{6,22},{7,23},{8,24},{9,... | collective-permute-start | bytes 61448 | tf_op jit(solution)/shard_map/ppermute | solution.py:617
  102.7 8.1 %collective-permute-start.17 = (bf16[4,40,640]{2,1,0:T(8,128)(2,1)S(1)}, bf16[4,40,640]{2,1,0:T(8,128)(2,1)S(1)}, u32[]{:S(2)}, u32[]{:S(2)}) collective-permute-start(bf16[4,40,640]{2,1,0:T(8,128)(2,1)S(1)} %get-tuple-element.105), channel_id=1, source_target_pairs={{0,2},{1,3},{2,0},{3,1},{4,6},{5,7},{6,4},{7,5},{8,10},{9,11},{10,... | collective-permute-start | bytes 614408 | tf_op jit(solution)/shard_map/ppermute | solution.py:617
  103.3 12.0 %collective-permute-start.19 = (bf16[4,40,640]{2,1,0:T(8,128)(2,1)S(1)}, bf16[4,40,640]{2,1,0:T(8,128)(2,1)S(1)}, u32[]{:S(2)}, u32[]{:S(2)}) collective-permute-start(bf16[4,40,640]{2,1,0:T(8,128)(2,1)S(1)} %get-tuple-element.106), channel_id=1, source_target_pairs={{0,6},{1,7},{2,4},{3,5},{4,2},{5,3},{6,0},{7,1},{8,14},{9,15},{10,... | collective-permute-start | bytes 614408 | tf_op jit(solution)/shard_map/ppermute | solution.py:617
  104.8 11.9 %collective-permute-start.18 = (bf16[4,40,640]{2,1,0:T(8,128)(2,1)S(1)}, bf16[4,40,640]{2,1,0:T(8,128)(2,1)S(1)}, u32[]{:S(2)}, u32[]{:S(2)}) collective-permute-start(bf16[4,40,640]{2,1,0:T(8,128)(2,1)S(1)} %get-tuple-element.107), channel_id=1, source_target_pairs={{0,4},{1,5},{2,6},{3,7},{4,0},{5,1},{6,2},{7,3},{8,12},{9,13},{10,... | collective-permute-start | bytes 614408 | tf_op jit(solution)/shard_map/ppermute | solution.py:617
  110.8 8.2 %collective-permute-start.31 = (bf16[4,40,640]{2,1,0:T(8,128)(2,1)S(1)}, bf16[4,40,640]{2,1,0:T(8,128)(2,1)S(1)}, u32[]{:S(2)}, u32[]{:S(2)}) collective-permute-start(bf16[4,40,640]{2,1,0:T(8,128)(2,1)S(1)} %get-tuple-element.102), channel_id=1, source_target_pairs={{0,2},{1,3},{2,0},{3,1},{4,6},{5,7},{6,4},{7,5},{8,10},{9,11},{10,... | collective-permute-start | bytes 614408 | tf_op jit(solution)/shard_map/ppermute | solution.py:617
  115.3 6.8 %collective-permute-start.33 = (bf16[4,40,640]{2,1,0:T(8,128)(2,1)S(1)}, bf16[4,40,640]{2,1,0:T(8,128)(2,1)S(1)}, u32[]{:S(2)}, u32[]{:S(2)}) collective-permute-start(bf16[4,40,640]{2,1,0:T(8,128)(2,1)S(1)} %get-tuple-element.103), channel_id=1, source_target_pairs={{0,6},{1,7},{2,4},{3,5},{4,2},{5,3},{6,0},{7,1},{8,14},{9,15},{10,... | collective-permute-start | bytes 614408 | tf_op jit(solution)/shard_map/ppermute | solution.py:617
  116.7 7.4 %collective-permute-start.32 = (bf16[4,40,640]{2,1,0:T(8,128)(2,1)S(1)}, bf16[4,40,640]{2,1,0:T(8,128)(2,1)S(1)}, u32[]{:S(2)}, u32[]{:S(2)}) collective-permute-start(bf16[4,40,640]{2,1,0:T(8,128)(2,1)S(1)} %get-tuple-element.104), channel_id=1, source_target_pairs={{0,4},{1,5},{2,6},{3,7},{4,0},{5,1},{6,2},{7,3},{8,12},{9,13},{10,... | collective-permute-start | bytes 614408 | tf_op jit(solution)/shard_map/ppermute | solution.py:617
  119.0 9.8 %collective-permute-start.27 = (bf16[1,16,640]{2,1,0:T(8,128)(2,1)S(1)}, bf16[1,16,640]{2,1,0:T(8,128)(2,1)S(1)}, u32[]{:S(2)}, u32[]{:S(2)}) collective-permute-start(bf16[1,16,640]{2,1,0:T(8,128)(2,1)S(1)} %add_convert_fusion.5.va_ref), channel_id=1, source_target_pairs={{0,8},{1,9},{2,10},{3,11},{4,12},{5,13},{6,14},{7,15},{8,0},{9,1},... | collective-permute-start | bytes 61448 | tf_op jit(solution)/shard_map/ppermute | solution.py:617
  122.0 8.8 %collective-permute-start.22 = (bf16[1,40,640]{2,1,0:T(8,128)(2,1)S(1)}, bf16[1,40,640]{2,1,0:T(8,128)(2,1)S(1)}, u32[]{:S(2)}, u32[]{:S(2)}) collective-permute-start(bf16[1,40,640]{2,1,0:T(8,128)(2,1)S(1)} %get-tuple-element.112), channel_id=1, source_target_pairs={{0,24},{1,25},{2,26},{3,27},{4,28},{5,29},{6,30},{7,31},{8,16},{9,... | collective-permute-start | bytes 153608 | tf_op jit(solution)/shard_map/ppermute | solution.py:617
  124.1 9.5 %collective-permute-start.21 = (bf16[1,40,640]{2,1,0:T(8,128)(2,1)S(1)}, bf16[1,40,640]{2,1,0:T(8,128)(2,1)S(1)}, u32[]{:S(2)}, u32[]{:S(2)}) collective-permute-start(bf16[1,40,640]{2,1,0:T(8,128)(2,1)S(1)} %get-tuple-element.113), channel_id=1, source_target_pairs={{0,16},{1,17},{2,18},{3,19},{4,20},{5,21},{6,22},{7,23},{8,24},{9,... | collective-permute-start | bytes 153608 | tf_op jit(solution)/shard_map/ppermute | solution.py:617
  127.2 6.4 %collective-permute-start.20 = (bf16[1,40,640]{2,1,0:T(8,128)(2,1)S(1)}, bf16[1,40,640]{2,1,0:T(8,128)(2,1)S(1)}, u32[]{:S(2)}, u32[]{:S(2)}) collective-permute-start(bf16[1,40,640]{2,1,0:T(8,128)(2,1)S(1)} %get-tuple-element.114), channel_id=1, source_target_pairs={{0,8},{1,9},{2,10},{3,11},{4,12},{5,13},{6,14},{7,15},{8,0},{9,1},... | collective-permute-start | bytes 153608 | tf_op jit(solution)/shard_map/ppermute | solution.py:617
  127.3 9.3 %collective-permute-start.36 = (bf16[1,40,640]{2,1,0:T(8,128)(2,1)S(1)}, bf16[1,40,640]{2,1,0:T(8,128)(2,1)S(1)}, u32[]{:S(2)}, u32[]{:S(2)}) collective-permute-start(bf16[1,40,640]{2,1,0:T(8,128)(2,1)S(1)} %get-tuple-element.108), channel_id=1, source_target_pairs={{0,24},{1,25},{2,26},{3,27},{4,28},{5,29},{6,30},{7,31},{8,16},{9,... | collective-permute-start | bytes 153608 | tf_op jit(solution)/shard_map/ppermute | solution.py:617
  128.8 7.8 %collective-permute-start.35 = (bf16[1,40,640]{2,1,0:T(8,128)(2,1)S(1)}, bf16[1,40,640]{2,1,0:T(8,128)(2,1)S(1)}, u32[]{:S(2)}, u32[]{:S(2)}) collective-permute-start(bf16[1,40,640]{2,1,0:T(8,128)(2,1)S(1)} %get-tuple-element.109), channel_id=1, source_target_pairs={{0,16},{1,17},{2,18},{3,19},{4,20},{5,21},{6,22},{7,23},{8,24},{9,... | collective-permute-start | bytes 153608 | tf_op jit(solution)/shard_map/ppermute | solution.py:617
  130.9 5.7 %collective-permute-start.34 = (bf16[1,40,640]{2,1,0:T(8,128)(2,1)S(1)}, bf16[1,40,640]{2,1,0:T(8,128)(2,1)S(1)}, u32[]{:S(2)}, u32[]{:S(2)}) collective-permute-start(bf16[1,40,640]{2,1,0:T(8,128)(2,1)S(1)} %get-tuple-element.110), channel_id=1, source_target_pairs={{0,8},{1,9},{2,10},{3,11},{4,12},{5,13},{6,14},{7,15},{8,0},{9,1},... | collective-permute-start | bytes 153608 | tf_op jit(solution)/shard_map/ppermute | solution.py:617
  (12 other events, 47.9 us)

commit v2 on v1

--- a/solution.py
+++ b/solution.py
@@ -90,19 +90,38 @@
     return first, second, row, col, heights, widths
 
 
-def pack_kernel(q_ref, kv_ref, red_ref, proj_ref, up_ref, down_ref, vm_ref, vh_ref, a_ref, b_ref, v_ref):
-    cw = q_ref.shape[1]
-
-    def turned(ref):
-        return ref[...].astype(F32).T
-
-    kv = turned(kv_ref)
-    a_ref[...] = lanes(turned(red_ref), turned(q_ref), kv[:cw], kv[cw:], turned(proj_ref)).astype(BF16)
-    up = turned(up_ref)
-    b_ref[...] = lanes(turned(down_ref), *[up[cw * e : cw * e + cw] for e in range(4)]).astype(BF16)
-    v_ref[...] = jnp.zeros_like(v_ref)
-    both = lanes(vm_ref[...].astype(F32), vh_ref[...].astype(F32))
-    v_ref[: both.shape[0], : both.shape[1]] = both.astype(BF16)
+def pack_kernel(*refs):
+    sources, (a_ref, b_ref, v_ref), held, semaphores = refs[:8], refs[8:11], refs[11:19], refs[19]
+    copies = [pltpu.make_async_copy(source, ref, semaphores.at[i]) for i, (source, ref) in enumerate(zip(sources, held))]
+    for copy in copies:
+        copy.start()
+    for copy in copies:
+        copy.wait()
+    q_ref, kv_ref, red_ref, proj_ref, up_ref, down_ref, vm_ref, vh_ref = held
+    cw = q_ref.shape[0]
+
+    def wider(ref):
+        return ref[...].astype(F32)
+
+    kv = wider(kv_ref).T
+    a_ref[0] = lanes(wider(red_ref), wider(q_ref), kv[:cw], kv[cw:], wider(proj_ref)).astype(BF16)
+    up = wider(up_ref).T
+    b_ref[0] = lanes(wider(down_ref), *[up[cw * e : cw * e + cw] for e in range(4)]).astype(BF16)
+    v_ref[0] = jnp.zeros_like(v_ref[0])
+    both = lanes(wider(vm_ref), wider(vh_ref))
+    v_ref[0, : both.shape[0], : both.shape[1]] = both.astype(BF16)
+
+
+def pack(arguments, piece, vpiece):
+    vmem = pl.BlockSpec(memory_space=pltpu.VMEM)
+    return pl.pallas_call(
+        pack_kernel,
+        out_shape=[jax.ShapeDtypeStruct((1,) + shape, BF16) for shape in (piece, piece, vpiece)],
+        in_specs=[pl.BlockSpec(memory_space=pl.ANY)] * len(arguments),
+        out_specs=[vmem] * 3,
+        scratch_shapes=[pltpu.VMEM(v.shape, v.dtype) for v in arguments] + [pltpu.SemaphoreType.DMA((len(arguments),))],
+        compiler_params=pltpu.CompilerParams(vmem_limit_bytes=60 * 2**20),
+    )(*arguments)
 
 
 def attend_kernel(
@@ -113,7 +132,7 @@
     score_ref,
 ):
     me = my_index(tuned)
-    capacity, width = tok_ref.shape
+    width, capacity = tok_ref.shape
     cw, rn = width // PARTS_W, width // PARTS_N
     keys = capacity // 4
     dim = width // HEADS
@@ -141,7 +160,8 @@
         ).astype(BF16)
         wp_ref[at, :] = rows_of(unit(0, 3), unit(1, 3)).astype(BF16)
 
-    normed, inverse = normalise(tok_ref[...].astype(F32))
+    tokens = tok_ref[...].astype(F32).T
+    normed, inverse = normalise(tokens)
     n1_ref[...] = normed
     r1_ref[...] = inverse
     h1 = (normed * mv[0:1] + mv[1:2]).astype(BF16)
@@ -192,7 +212,7 @@
     lax.fori_loop(0, capacity // 64, soften, 0)
     o = dot_nn(p_ref[...].astype(BF16), vb_ref[...]).astype(BF16)
     o_ref[...] = o
-    x2_ref[...] = tok_ref[...].astype(F32) + dot_nt(o, wp_ref[...]) + mv[7:8]
+    x2_ref[...] = tokens + dot_nt(o, wp_ref[...]) + mv[7:8]
 
 
 def one_hot(rows_ref, cols_ref, capacity):
@@ -224,7 +244,7 @@
     mixed_ref, gown_ref, gsend_ref, dx2_ref, mg_ref, hg_ref,
     wu_ref, wd_ref, mask_ref, n2_ref, r2_ref, h2_ref, h2t_ref, gy_ref, gyt_ref,
     f_ref, gm_ref, gp_ref, dc_ref, ul_ref, ur_ref, g0_ref, slope_ref, act_ref, u0_ref, df_ref, da_ref,
-    mix_ref, dh2_ref, upg_ref, dng_ref,
+    mix_ref, dh2_ref, upg_ref, dng_ref, turned_ref,
 ):
     me = my_index(tuned)
     capacity, width = x2_ref.shape
@@ -280,9 +300,10 @@
         n2_ref[at, :] = normed
         r2_ref[at, :] = inverse
         h2_ref[at, :] = (normed * gain2 + shift2).astype(BF16)
-        gy_ref[at, :] = (cot_ref[at, :].astype(F32) * wide_mask(6, at, width)).astype(BF16)
+        gy_ref[at, :] = (turned_ref[at, :] * wide_mask(6, at, width)).astype(BF16)
         return carry
 
+    turned_ref[...] = cot_ref[...].astype(F32).T
     lax.fori_loop(0, capacity // 64, start, 0)
     h2t_ref[...] = h2_ref[...].astype(F32).T.astype(BF16)
     gyt_ref[...] = gy_ref[...].astype(F32).T.astype(BF16)
@@ -416,19 +437,19 @@
     lax.fori_loop(0, hidden // CHUNK, chunk_step, 0)
     hg_ref[11:, :] = jnp.zeros((hg_ref.shape[0] - 11, hidden), F32)
 
-    for w in range(PARTS_W):
-        for n in range(PARTS_N):
-            up = upg_ref[pl.ds(n * rn, rn), pl.ds(w * 4 * cw, 4 * cw)]
-            value = lanes(
-                dng_ref[pl.ds(w * cw, cw), pl.ds(n * width, width)],
-                *[up[e * cw : (e + 1) * cw] for e in range(rn // cw)],
-            ).astype(BF16)
-            store_piece(gown_ref, gsend_ref, w * PARTS_N + n, me, value)
+    def value_of(w, n):
+        up = upg_ref[pl.ds(n * rn, rn), pl.ds(w * 4 * cw, 4 * cw)]
+        return lanes(
+            dng_ref[pl.ds(w * cw, cw), pl.ds(n * width, width)],
+            *[up[e * cw : (e + 1) * cw] for e in range(rn // cw)],
+        )
+
+    store_pieces(gown_ref, gsend_ref, me, value_of)
 
     def finish(i, carry):
         at = pl.ds(pl.multiple_of(i * 64, 64), 64)
         occupied = wide_mask(6, at, width)
-        mixed_ref[at, :] = ((x2_ref[at, :] + mix_ref[at, :] + bias2) * occupied).astype(BF16)
+        turned_ref[at, :] = (x2_ref[at, :] + mix_ref[at, :] + bias2) * occupied
         gy = gy_ref[at, :].astype(F32)
         grad, normed = dh2_ref[at, :], n2_ref[at, :]
         dx2_ref[at, :] = gy + normalise_back(grad, normed, r2_ref[at, :], gain2)
@@ -436,43 +457,30 @@
 
     zero = jnp.zeros((1, width), F32)
     sums = lax.fori_loop(0, capacity // 64, finish, (zero, zero, zero))
+    mixed_ref[...] = turned_ref[...].T.astype(BF16)
     mg_ref[...] = jnp.zeros_like(mg_ref)
     for k in range(3):
         mg_ref[8 + k : 9 + k, :] = sums[k]
 
 
-def store_piece(own_ref, send_ref, device, me, value):
-    slot = slot_of(device, me)
-    mine = ((device ^ me) & 1) == 0
-
-    @pl.when(mine)
-    def _():
-        own_ref[slot] = value
-
-    @pl.when(jnp.logical_not(mine))
-    def _():
-        send_ref[slot] = value
-
-
-def attend_back_kernel(
-    tuned,
-    rows_ref, cols_ref, dx2_ref, h1_ref, n1_ref, r1_ref, patch_ref, nk_ref, rk_ref, kn_ref, q_ref,
-    kb_ref, vb_ref, p_ref, o_ref, wr_ref, wq_ref, wkv_ref, wp_ref, mv_ref, mg_ref, hg_ref,
-    tg_ref, gown_ref, gsend_ref, vown_ref, vsend_ref,
-    dp_ref, ds_ref, gr_ref, gq_ref, gkv_ref, gp_ref, dpatch_ref,
-):
-    me = my_index(tuned)
-    capacity, width = dx2_ref.shape
-    cw, rn = width // PARTS_W, width // PARTS_N
+def store_pieces(own_ref, send_ref, me, value_of):
+    even = (me & 1) == 0
+    for w in range(PARTS_W):
+        for x in range(PARTS_N // 2):
+            first, second = value_of(w, 2 * x), value_of(w, 2 * x + 1)
+            slot = slot_of(w * PARTS_N + 2 * x, me)
+            own_ref[slot] = jnp.where(even, first, second).astype(BF16)
+            send_ref[slot] = jnp.where(even, second, first).astype(BF16)
+
+
+def score_back_kernel(dx2_ref, vb_ref, p_ref, o_ref, wp_ref, gp_ref, dob_ref, ds_ref, bp_ref, dp_ref):
+    capacity = dx2_ref.shape[0]
     keys = capacity // 4
-    dim = width // HEADS
-    scale = dim ** (-0.5)
-    mv = mv_ref[...]
-
     datt = dx2_ref[...].astype(BF16)
-    bias_proj = column_sum(datt.astype(F32))
+    bp_ref[...] = column_sum(datt.astype(F32))
     gp_ref[...] = dot_tn(datt, o_ref[...])
     dob = dot_nn(datt, wp_ref[...]).astype(BF16)
+    dob_ref[...] = dob
     dp_ref[...] = dot_nt(dob, vb_ref[...])
 
     def soften_back(i, carry):
@@ -486,10 +494,27 @@
         return carry
 
     lax.fori_loop(0, capacity // 64, soften_back, 0)
+
+
+def attend_back_kernel(
+    tuned,
+    dob_ref, ds_ref, gp_ref, h1_ref, patch_ref, nk_ref, rk_ref, kn_ref, q_ref, kb_ref, p_ref,
+    wr_ref, wkv_ref, mv_ref,
+    gown_ref, gsend_ref, dq_ref, dpatch_ref, vk_ref,
+    gr_ref, gq_ref, gkv_ref,
+):
+    me = my_index(tuned)
+    capacity, width = h1_ref.shape
+    cw, rn = width // PARTS_W, width // PARTS_N
+    keys = capacity // 4
+    dim = width // HEADS
+    scale = dim ** (-0.5)
+
     ds = ds_ref[...]
     dq = (dot_nn(ds, kb_ref[...]) * scale).astype(BF16)
+    dq_ref[...] = dq
     dk_all = dot_tn(ds, q_ref[...])
-    dv_all = dot_tn(p_ref[...].astype(BF16), dob)
+    dv_all = dot_tn(p_ref[...].astype(BF16), dob_ref[...])
     lane = lax.broadcasted_iota(jnp.int32, (keys, width), 1)
     dk = jnp.zeros((keys, width), F32)
     dv = jnp.zeros((keys, width), F32)
@@ -499,59 +524,66 @@
         dv = jnp.where(inside, dv_all[h * keys : (h + 1) * keys], dv)
     dk = (dk * scale).astype(BF16)
     dv = dv.astype(BF16)
-    bias_query = column_sum(dq.astype(F32))
-    bias_value = column_sum(dv.astype(F32))
     gq_ref[...] = dot_tn(dq, h1_ref[...])
     kn = kn_ref[...]
     gkv_ref[pl.ds(0, width), :] = dot_tn(dk, kn)
     gkv_ref[pl.ds(width, width), :] = dot_tn(dv, kn)
     dkn = dot_nn(dk, wkv_ref[pl.ds(0, width), :]) + dot_nn(dv, wkv_ref[pl.ds(width, width), :])
     nk = nk_ref[...]
-    gain_key, shift_key = column_sum(dkn * nk), column_sum(dkn)
-    dsr = normalise_back(dkn, nk, rk_ref[...], mv[5:6]).astype(BF16)
-    bias_reduce = column_sum(dsr.astype(F32))
+    dsr = normalise_back(dkn, nk, rk_ref[...], mv_ref[5:6, :]).astype(BF16)
+    vk_ref[...] = rows_of(
+        column_sum(dq.astype(F32)),
+        column_sum(dv.astype(F32)),
+        column_sum(dsr.astype(F32)),
+        column_sum(dkn * nk),
+        column_sum(dkn),
+        jnp.zeros((3, width), F32),
+    )
     for n in range(4):
         at = pl.ds(n * keys, keys)
         gr_ref[n] = dot_tn(dsr, patch_ref[at, :])
         dpatch_ref[at, :] = dot_nn(dsr, wr_ref[n])
 
-    for w in range(PARTS_W):
-        for n in range(PARTS_N):
-            at, lane_at = pl.ds(w * cw, cw), pl.ds(n * rn, rn)
-            value = lanes(
-                gr_ref[n, at, :],
-                gq_ref[at, lane_at],
-                gkv_ref[pl.ds(2 * w * cw, cw), lane_at],
-                gkv_ref[pl.ds(2 * w * cw + cw, cw), lane_at],
-                gp_ref[at, lane_at],
-            ).astype(BF16)
-            store_piece(gown_ref, gsend_ref, w * PARTS_N + n, me, value)
-
+    def value_of(w, n):
+        at, lane_at = pl.ds(w * cw, cw), pl.ds(n * rn, rn)
+        return lanes(
+            gr_ref[n, at, :],
+            gq_ref[at, lane_at],
+            gkv_ref[pl.ds(2 * w * cw, cw), lane_at],
+            gkv_ref[pl.ds(2 * w * cw + cw, cw), lane_at],
+            gp_ref[at, lane_at],
+        )
+
+    store_pieces(gown_ref, gsend_ref, me, value_of)
+
+
+def token_back_kernel(
+    tuned,
+    rows_ref, cols_ref, dx2_ref, dq_ref, dpatch_ref, n1_ref, r1_ref, wq_ref, mv_ref, mg_ref, hg_ref, vk_ref, bp_ref,
+    tg_ref, vown_ref, vsend_ref,
+):
+    me = my_index(tuned)
+    capacity, width = dx2_ref.shape
+    rn = width // PARTS_N
     chosen = one_hot(rows_ref, cols_ref, capacity)
     high = dpatch_ref[...].astype(BF16)
     low = (dpatch_ref[...] - high.astype(F32)).astype(BF16)
-    dh1 = dot_nn(dq, wq_ref[...]) + dot_tn(chosen, high) + dot_tn(chosen, low)
+    dh1 = dot_nn(dq_ref[...], wq_ref[...]) + dot_tn(chosen, high) + dot_tn(chosen, low)
     n1 = n1_ref[...]
-    gain_one, shift_one = column_sum(dh1 * n1), column_sum(dh1)
-    tg_ref[...] = (dx2_ref[...] + normalise_back(dh1, n1, r1_ref[...], mv[0:1])).astype(BF16)
-
-    sums = rows_of(
-        gain_one, shift_one, bias_query, bias_value, bias_reduce, gain_key, shift_key, bias_proj,
-        mg_ref[8:16, :],
-    )
+    vk = vk_ref[...]
+    token_grad = dx2_ref[...] + normalise_back(dh1, n1, r1_ref[...], mv_ref[0:1, :])
+    tg_ref[...] = token_grad.T.astype(BF16)
+    sums = rows_of(column_sum(dh1 * n1), column_sum(dh1), vk[0:5], bp_ref[...], mg_ref[8:16, :])
     hg = hg_ref[...]
     spare = jnp.zeros((16, 3 * rn), F32)
-    for n in range(PARTS_N):
-        value = lanes(sums[:, n * rn : (n + 1) * rn], hg[:, n * width : (n + 1) * width], spare).astype(BF16)
-        delta = n ^ (me & 3)
-
-        @pl.when((delta & 1) == 0)
-        def _():
-            vown_ref[delta >> 1] = value
-
-        @pl.when((delta & 1) == 1)
-        def _():
-            vsend_ref[delta >> 1] = value
+    value = [
+        lanes(sums[:, n * rn : (n + 1) * rn], hg[:, n * width : (n + 1) * width], spare) for n in range(PARTS_N)
+    ]
+    even = (me & 1) == 0
+    for x in range(2):
+        slot = x ^ ((me >> 1) & 1)
+        vown_ref[slot] = jnp.where(even, value[2 * x], value[2 * x + 1]).astype(BF16)
+        vsend_ref[slot] = jnp.where(even, value[2 * x + 1], value[2 * x]).astype(BF16)
 
 
 def total_of(refs):
@@ -561,27 +593,51 @@
     return value
 
 
+def core_sum_kernel(own_ref, got_ref, *out_refs):
+    for k, ref in enumerate(out_refs):
+        at = slice(4 * k, 4 * k + 4)
+        ref[...] = (own_ref[at].astype(F32) + got_ref[at].astype(F32)).astype(BF16)
+
+
+def core_sum_vector_kernel(own_ref, got_ref, vown_ref, vgot_ref, *out_refs):
+    cw = own_ref.shape[1]
+    vector = [(vown_ref[x].astype(F32) + vgot_ref[x].astype(F32)).astype(BF16) for x in range(2)]
+    for k, ref in enumerate(out_refs):
+        parts = [own_ref[4 * k + j].astype(F32) + got_ref[4 * k + j].astype(F32) for j in range(4)]
+        ref[pl.ds(0, 4 * cw), :] = rows_of(*parts).astype(BF16)
+        ref[pl.ds(4 * cw, vector[0].shape[0]), :] = vector[k & 1]
+
+
+def plane_sum_kernel(a_ref, b_ref, c_ref, d_ref, *out_refs):
+    total = total_of((a_ref, b_ref, c_ref, d_ref)).astype(BF16)
+    for k, ref in enumerate(out_refs):
+        ref[0] = total[k]
+
+
+def plane_sum_vector_kernel(cw, a_ref, b_ref, c_ref, d_ref, *out_refs):
+    total = total_of((a_ref, b_ref, c_ref, d_ref))
+    for k, ref in enumerate(out_refs):
+        ref[...] = rows_of(total[k * cw : (k + 1) * cw], total[4 * cw :]).astype(BF16)
+
+
 def finish_ffn_kernel(a_ref, b_ref, c_ref, d_ref, up_ref, down_ref):
     total = total_of((a_ref, b_ref, c_ref, d_ref))[0]
-    width = down_ref.shape[0]
-    down_ref[...] = total[:, :width].T
+    width = down_ref.shape[1]
+    down_ref[...] = total[:, :width]
     up_ref[...] = rows_of(total[:, width : width + width // 2], total[:, width + width // 2 :])
 
 
-def finish_attend_kernel(
-    a_ref, b_ref, c_ref, d_ref, va_ref, vb_ref, vc_ref, vd_ref,
-    q_ref, kv_ref, red_ref, proj_ref, vm_ref, vh_ref,
-):
-    total = total_of((a_ref, b_ref, c_ref, d_ref))[0]
-    width, rn = red_ref.shape[0], q_ref.shape[0]
-    red_ref[...] = total[:, :width].T
-    unit = [total[:, width + k * rn : width + (k + 1) * rn] for k in range(4)]
-    q_ref[...] = unit[0].T
+def finish_attend_kernel(a_ref, b_ref, c_ref, d_ref, q_ref, kv_ref, red_ref, proj_ref, vm_ref, vh_ref):
+    total = total_of((a_ref, b_ref, c_ref, d_ref))
+    cw, width = red_ref.shape
+    rn = q_ref.shape[1]
+    red_ref[...] = total[:cw, :width]
+    unit = [total[:cw, width + k * rn : width + (k + 1) * rn] for k in range(4)]
+    q_ref[...] = unit[0]
     kv_ref[...] = rows_of(unit[1], unit[2]).T
-    proj_ref[...] = unit[3].T
-    vector = total_of((va_ref, vb_ref, vc_ref, vd_ref))[0]
-    vm_ref[...] = vector[: vm_ref.shape[0], :rn]
-    vh_ref[...] = vector[: vh_ref.shape[0], rn : rn + width]
+    proj_ref[...] = unit[3]
+    vm_ref[...] = total[cw : cw + vm_ref.shape[0], :rn]
+    vh_ref[...] = total[cw : cw + vh_ref.shape[0], rn : rn + width]
 
 
 def call(kernel, inputs, outputs, scratch=(), scalars=0, limit=40, flops=0, moved=0):
@@ -596,6 +652,10 @@
         compiler_params=pltpu.CompilerParams(vmem_limit_bytes=limit * 2**20),
         cost_estimate=pl.CostEstimate(flops=flops, bytes_accessed=moved, transcendentals=0),
     )(*inputs)
+
+
+def after(value, *others):
+    return lax.optimization_barrier((value, *others))[0]
 
 
 def on_device(
@@ -616,32 +676,23 @@
         pairs = [(i, i ^ mask) for i in range(wide * narrow)]
         return lax.ppermute(value, ("wide", "narrow"), pairs)
 
-    def gather(value):
-        near = jnp.concatenate([value[None]] + [swap(value[None], m) for m in (8, 16, 24)], axis=0)
-        half = jnp.concatenate([near] + [swap(near, m) for m in (2, 4, 6)], axis=0)
-        return half, swap(half, 1)
-
-    def add(*parts):
-        total = parts[0].astype(F32)
-        for part in parts[1:]:
-            total = total + part.astype(F32)
-        return total.astype(BF16)
-
-    def scatter(own, send):
-        half = add(own, swap(send, 1))
-        near = add(half[0:4], *[swap(half[4 * k : 4 * k + 4], 2 * k) for k in (1, 2, 3)])
-        return [near[0:1]] + [swap(near[k : k + 1], 8 * k) for k in (1, 2, 3)]
-
     if tuned:
-        pack_a, pack_b, pack_v = call(
-            pack_kernel,
-            (q_weight, kv_weight, reduce_weight, proj_weight, up_weight, down_weight, vec_model, vec_hidden),
-            ((piece, BF16), (piece, BF16), (vpiece, BF16)),
+        pack_a, pack_b, pack_v = pack(
+            (
+                q_weight.T, kv_weight, reduce_weight.T, proj_weight.T, up_weight, down_weight.T,
+                vec_model, vec_hidden,
+            ),
+            piece, vpiece,
         )
-        own_a, oth_a = gather(pack_a)
-        vec_pair = jnp.concatenate([pack_v[None], swap(pack_v[None], 1)], axis=0)
+        near_a = jnp.concatenate([pack_a] + [swap(pack_a, m) for m in (8, 16, 24)], axis=0)
+        vec_pair = jnp.concatenate([pack_v, swap(pack_v, 1)], axis=0)
         vecs = jnp.concatenate([vec_pair, swap(vec_pair, 2)], axis=0)
-        own_b, oth_b = gather(pack_b)
+        own_a = jnp.concatenate([near_a] + [swap(near_a, m) for m in (2, 4, 6)], axis=0)
+        pack_b = after(pack_b, near_a)
+        near_b = jnp.concatenate([pack_b] + [swap(pack_b, m) for m in (8, 16, 24)], axis=0)
+        own_a, near_b, vecs = lax.optimization_barrier((own_a, near_b, vecs))
+        oth_a = swap(own_a, 1)
+        plane_b = [swap(near_b, m) for m in (2, 4, 6)]
     else:
         own_a, oth_a, own_b, oth_b, vecs = gather_plain(
             q_weight, kv_weight, reduce_weight, proj_weight, up_weight, down_weight, vec_model, vec_hidden
@@ -652,7 +703,7 @@
         x2, h1, n1, r1, patches, nk, rk, kn, q, kb, vb, p, o, wr, wq, wkv, wp, mv, hv,
     ) = call(
         functools.partial(attend_kernel, tuned),
-        (img_rows, img_cols, tokens, own_a, oth_a, vecs),
+        (img_rows, img_cols, tokens.T, own_a, oth_a, vecs),
         (
             ((capacity, width), F32), ((capacity, width), BF16), ((capacity, width), F32), ((capacity, 1), F32),
             ((capacity, width), BF16), ((keys, width), F32), ((keys, 1), F32), ((keys, width), BF16),
@@ -663,17 +714,21 @@
         ),
         scratch=(((capacity, HEADS * keys), F32),),
         scalars=2,
-        flops=2 * 10**9,
-    )
-
+        flops=8 * 10**9,
+    )
+
+    if tuned:
+        plane_b = lax.optimization_barrier((*plane_b, x2))[:3]
+        own_b = jnp.concatenate([near_b, *plane_b], axis=0)
+        oth_b = swap(own_b, 1)
     padded = ((CHUNK // 128, capacity + 2 * PAD, 128), F32)
     halved = ((CHUNK // 128, capacity, 128), F32)
     chunked = ((capacity, CHUNK), F32)
     mixed, gown_b, gsend_b, dx2, mg, hg = call(
         functools.partial(ffn_kernel, tuned),
-        (img_rows, img_cols, x2, cotangent, own_b, oth_b, mv, hv),
+        (img_rows, img_cols, x2, cotangent.T, own_b, oth_b, mv, hv),
         (
-            ((capacity, width), BF16), ((SLOTS,) + piece, BF16), ((SLOTS,) + piece, BF16),
+            ((width, capacity), BF16), ((SLOTS,) + piece, BF16), ((SLOTS,) + piece, BF16),
             ((capacity, width), F32), ((16, width), F32), ((16, hidden), F32),
         ),
         scratch=(
@@ -683,50 +738,77 @@
             padded, padded, padded, padded, padded, padded,
             halved, chunked, ((capacity, CHUNK), BF16), halved, ((capacity, CHUNK), BF16), chunked,
             ((capacity, width), F32), ((capacity, width), F32), ((width, hidden), F32), ((width, hidden), F32),
+            ((capacity, width), F32),
         ),
         scalars=2,
-        flops=4 * 10**9,
-    )
-
-    token_grad, gown_a, gsend_a, vown, vsend = call(
+        flops=33 * 10**9,
+    )
+
+    if tuned:
+        got_b = swap(gsend_b, 1)
+    gp, dob, ds, bp = call(
+        score_back_kernel,
+        (dx2, vb, p, o, wp),
+        (
+            (square, F32), ((capacity, width), BF16), ((capacity, HEADS * keys), BF16), ((1, width), F32),
+        ),
+        scratch=(((capacity, HEADS * keys), F32),),
+        flops=25 * 10**8,
+    )
+    four = (4,) + piece
+    if tuned:
+        half_b = call(core_sum_kernel, (gown_b, got_b), ((four, BF16),) * 4)
+        plane_b = [swap(half_b[k], 2 * k) for k in (1, 2, 3)]
+        ds = after(ds, half_b[1])
+    gown_a, gsend_a, dq, dpatch, vk = call(
         functools.partial(attend_back_kernel, tuned),
+        (dob, ds, gp, h1, patches, nk, rk, kn, q, kb, p, wr, wkv, mv),
         (
-            img_rows, img_cols, dx2, h1, n1, r1, patches, nk, rk, kn, q, kb, vb, p, o, wr, wq, wkv, wp,
-            mv, mg, hg,
+            ((SLOTS,) + piece, BF16), ((SLOTS,) + piece, BF16), ((capacity, width), BF16), ((capacity, width), F32),
+            ((8, width), F32),
         ),
-        (
-            ((capacity, width), BF16), ((SLOTS,) + piece, BF16), ((SLOTS,) + piece, BF16),
-            ((2,) + vpiece, BF16), ((2,) + vpiece, BF16),
-        ),
-        scratch=(
-            ((capacity, HEADS * keys), F32), ((capacity, HEADS * keys), BF16), ((4,) + square, F32),
-            (square, F32), ((2 * width, width), F32), (square, F32), ((capacity, width), F32),
-        ),
+        scratch=(((4,) + square, F32), (square, F32), ((2 * width, width), F32)),
+        flops=0,
+    )
+    if tuned:
+        got_a = swap(gsend_a, 1)
+        near_b = call(plane_sum_kernel, (half_b[0], *plane_b), (((1,) + piece, BF16),) * 4, flops=2 * 10**10)
+        line_b = [swap(near_b[k], 8 * k) for k in (1, 2, 3)]
+    token_grad, vown, vsend = call(
+        functools.partial(token_back_kernel, tuned),
+        (img_rows, img_cols, dx2, dq, dpatch, n1, r1, wq, mv, mg, hg, vk, bp),
+        (((width, capacity), BF16), ((2,) + vpiece, BF16), ((2,) + vpiece, BF16)),
         scalars=2,
-        flops=2 * 10**9,
+        flops=0,
     )
 
     if not tuned:
         grads = scatter_plain(mesh_shape, width, gown_a, gsend_a, gown_b, gsend_b, vown, vsend)
-        return (mixed, token_grad) + grads
-
-    parts_b = scatter(gown_b, gsend_b)
-    vhalf = add(vown, swap(vsend, 1))
-    vnear = add(vhalf[0:1], swap(vhalf[1:2], 2), swap(vhalf[0:1], 4), swap(vhalf[1:2], 6))
-    vparts = [vnear] + [swap(vnear, 8 * k) for k in (1, 2, 3)]
-    parts_a = scatter(gown_a, gsend_a)
+        return (mixed.T, token_grad.T) + grads
+
+    gown_a = after(gown_a, near_b[1])
+    joined = ((4 * cw + 16, 2 * width), BF16)
+    half_a = call(core_sum_vector_kernel, (gown_a, got_a, vown, swap(vsend, 1)), (joined,) * 4)
+    plane_a = [swap(half_a[k], 2 * k) for k in (1, 2, 3)]
+    plane_a = lax.optimization_barrier((*plane_a, *line_b))[:3]
+    near_a = call(
+        functools.partial(plane_sum_vector_kernel, cw), (half_a[0], *plane_a), (((cw + 16, 2 * width), BF16),) * 4
+    )
+    line_a = [swap(near_a[k], 8 * k) for k in (1, 2, 3)]
     up_grad, down_grad = call(
-        finish_ffn_kernel, parts_b, (((rn, 4 * cw), F32), ((width, cw), F32))
+        finish_ffn_kernel, (near_b[0], *line_b), (((rn, 4 * cw), F32), ((cw, width), F32))
     )
     q_grad, kv_grad, reduce_grad, proj_grad, vm_grad, vh_grad = call(
         finish_attend_kernel,
-        (*parts_a, *vparts),
+        (near_a[0], *line_a),
         (
-            ((rn, cw), F32), ((rn, 2 * cw), F32), ((width, cw), F32), ((rn, cw), F32),
+            ((cw, rn), F32), ((rn, 2 * cw), F32), ((cw, width), F32), ((cw, rn), F32),
             ((11, rn), F32), ((11, width), F32),
         ),
     )
-    return mixed, token_grad, q_grad, kv_grad, reduce_grad, proj_grad, up_grad, down_grad, vm_grad, vh_grad
+    return (
+        mixed.T, token_grad.T, q_grad.T, kv_grad, reduce_grad.T, proj_grad.T, up_grad, down_grad.T, vm_grad, vh_grad,
+    )
 
 
 def gather_plain(q, kv, reduce, proj, up, down, vec_model, vec_hidden):

time: 139 us -> 114 us (0.82)
  local copies, waits for them, and re-layouts: 12.7 us -> 1.09 us
  starting transfers between devices: 45.6 us -> 36.9 us
  waiting for transfers between devices: 29.9 us -> 25.5 us
  other arithmetic: 0.77 us -> 2.31 us
    unnamed x37 -> x16, local copies, waits for them, and re-layouts: 12.5 us -> 1.01 us
    ppermute x37 -> x31, starting transfers between devices: 45.6 us -> 36.9 us  [swap(): return lax.ppermute(value, ('wide', 'narrow'), pairs)]
    ppermute x37 -> x31, waiting for transfers between devices: 29.9 us -> 25.5 us  [swap(): return lax.ppermute(value, ('wide', 'narrow'), pairs)]
    pallas_call x6 -> x11, Pallas kernels: 48.2 us -> 45.2 us  [call(): pl.pallas_call(kernel, out_shape=[jax.ShapeDtypeStruct(shape, kind) for s...]
    pallas_call x0 -> x1, Pallas kernels: none -> 1.72 us  [pack(): pl.pallas_call(pack_kernel, out_shape=[jax.ShapeDtypeStruct((1,) + shape,...]
    concatenate x3 -> x2, other arithmetic: 0.08 us -> 1.57 us  [the longest x1 0.84 us: on_device(): jnp.concatenate([pack_b] + [swap(pack_b, m) for m in (8, 16, 24)], axis=0)]
  transfers between devices with their start and end apart: 37 -> 31, of which waited for: 14 -> 15; matrix products, arithmetic and copies ran while one was open for 5% -> 3% of each run, Pallas kernels for 6% -> 14%
where the time goes in v2:
time: 114 us
  Pallas kernels  46.9 us (41%)
  starting transfers between devices  36.9 us (32%)
  waiting for transfers between devices  25.5 us (22%)
  other arithmetic  2.31 us (2%)
    pallas_call x11, Pallas kernels, call(): pl.pallas_call(kernel, out_shape=[jax.ShapeDtypeStruct(shape, kind) for s...  45.2 us
    ppermute x31, starting transfers between devices, swap(): return lax.ppermute(value, ('wide', 'narrow'), pairs)  36.9 us
    ppermute x31, waiting for transfers between devices, swap(): return lax.ppermute(value, ('wide', 'narrow'), pairs)  25.5 us
  transfers between devices with their start and end apart: 31, of which 15 were waited for; matrix products, arithmetic and copies ran while one was open for 3% of the time, Pallas kernels for 14%

profile of v2, /device:TPU:0, one launch (start us, length us, event | category | flops | bytes accessed | tf_op | source)
XLA Modules:
  0.0 113.6 jit_solution(10042544435715342133)
XLA Ops:
  0.6 1.7 %shard_map.195 = (bf16[1,40,640]{2,1,0:T(8,128)(2,1)}, bf16[1,40,640]{2,1,0:T(8,128)(2,1)}, bf16[1,16,640]{2,1,0:T(8,128)(2,1)}) custom-call(bf16[40,80]{1,0:T(8,128)(2,1)} %bitcast.16, bf16[80,80]{1,0:T(8,128)(2,1)} %refs_1_.1, bf16[40,320]{1,0:T(8,128)(2,1)} %bitcast.14, bf16[40,80]{1,0:T(8,128)(2,1)} %bitcast.17, bf16[80,160]{1,0:T(8,128)(2,1)} %refs_4_.1, ...), custom_call_target="tpu_custom_call" | custom-call | tf_op jit(solution)/shard_map/pallas_call | solution.py:117
  2.4 5.1 %collective-permute-start.2 = (bf16[1,40,640]{2,1,0:T(8,128)(2,1)}, bf16[1,40,640]{2,1,0:T(8,128)(2,1)S(1)}, u32[]{:S(2)}, u32[]{:S(2)}) collective-permute-start(bf16[1,40,640]{2,1,0:T(8,128)(2,1)} %get-tuple-element.86), channel_id=1, source_target_pairs={{0,24},{1,25},{2,26},{3,27},{4,28},{5,29},{6,30},{7,31},{8,16},{9,... | collective-permute-start | bytes 153608 | tf_op jit(solution)/shard_map/ppermute | solution.py:677
  10.3 1.6 %collective-permute-start.10 = (bf16[2,16,640]{2,1,0:T(8,128)(2,1)S(1)}, bf16[2,16,640]{2,1,0:T(8,128)(2,1)S(1)}, u32[]{:S(2)}, u32[]{:S(2)}) collective-permute-start(bf16[2,16,640]{2,1,0:T(8,128)(2,1)S(1)} %pad_maximum_fusion.2), channel_id=1, source_target_pairs={{0,2},{1,3},{2,0},{3,1},{4,6},{5,7},{6,4},{7,5},{8,10},{9,11},{10,... | collective-permute-start | bytes 122888 | tf_op jit(solution)/shard_map/ppermute | solution.py:677
  12.8 2.9 %collective-permute-start.8 = (bf16[1,40,640]{2,1,0:T(8,128)(2,1)}, bf16[1,40,640]{2,1,0:T(8,128)(2,1)S(1)}, u32[]{:S(2)}, u32[]{:S(2)}) collective-permute-start(bf16[1,40,640]{2,1,0:T(8,128)(2,1)} %get-tuple-element.88), channel_id=1, source_target_pairs={{0,24},{1,25},{2,26},{3,27},{4,28},{5,29},{6,30},{7,31},{8,16},{9,... | collective-permute-start | bytes 153608 | tf_op jit(solution)/shard_map/ppermute | solution.py:677
  15.7 1.5 %collective-permute-start.6 = (bf16[1,40,640]{2,1,0:T(8,128)(2,1)}, bf16[1,40,640]{2,1,0:T(8,128)(2,1)S(1)}, u32[]{:S(2)}, u32[]{:S(2)}) collective-permute-start(bf16[1,40,640]{2,1,0:T(8,128)(2,1)} %get-tuple-element.88), channel_id=1, source_target_pairs={{0,8},{1,9},{2,10},{3,11},{4,12},{5,13},{6,14},{7,15},{8,0},{9,1},... | collective-permute-start | bytes 153608 | tf_op jit(solution)/shard_map/ppermute | solution.py:677
  17.2 2.4 %collective-permute-start.5 = (bf16[4,40,640]{2,1,0:T(8,128)(2,1)S(1)}, bf16[4,40,640]{2,1,0:T(8,128)(2,1)S(1)}, u32[]{:S(2)}, u32[]{:S(2)}) collective-permute-start(bf16[4,40,640]{2,1,0:T(8,128)(2,1)S(1)} %get-tuple-element.162), channel_id=1, source_target_pairs={{0,6},{1,7},{2,4},{3,5},{4,2},{5,3},{6,0},{7,1},{8,14},{9,15},{10,... | collective-permute-start | bytes 614408 | tf_op jit(solution)/shard_map/ppermute | solution.py:677
  22.4 5.6 %collective-permute-done.3 = bf16[4,40,640]{2,1,0:T(8,128)(2,1)S(1)} collective-permute-done((bf16[4,40,640]{2,1,0:T(8,128)(2,1)S(1)}, bf16[4,40,640]{2,1,0:T(8,128)(2,1)S(1)}, u32[]{:S(2)}, u32[]{:S(2)}) %collective-permute-start.3) | collective-permute-done | bytes 204832 | tf_op jit(solution)/shard_map/ppermute | solution.py:677
  28.2 2.1 %collective-permute-start.14 = (bf16[4,40,640]{2,1,0:T(8,128)(2,1)S(1)}, bf16[4,40,640]{2,1,0:T(8,128)(2,1)S(1)}, u32[]{:S(2)}, u32[]{:S(2)}) collective-permute-start(bf16[4,40,640]{2,1,0:T(8,128)(2,1)S(1)} %pad_maximum_fusion), channel_id=1, source_target_pairs={{0,6},{1,7},{2,4},{3,5},{4,2},{5,3},{6,0},{7,1},{8,14},{9,15},{10,... | collective-permute-start | bytes 614408 | tf_op jit(solution)/shard_map/ppermute | solution.py:677
  31.8 6.9 %shard_map.196 = (f32[512,320]{1,0:T(8,128)S(1)}, bf16[512,320]{1,0:T(8,128)(2,1)S(1)}, f32[512,320]{1,0:T(8,128)S(1)}, f32[512,1]{1,0:T(8,128)S(1)}, bf16[512,3...) custom-call(s32[2]{0:T(128)S(1)} %copy-done, ...), custom_call_target="tpu_custom_call" | custom-call | flops 8000000000 | tf_op jit(solution)/shard_map/pallas_call | solution.py:646
  38.8 2.2 %collective-permute-done.13 = bf16[4,40,640]{2,1,0:T(8,128)(2,1)S(1)} collective-permute-done((bf16[4,40,640]{2,1,0:T(8,128)(2,1)S(1)}, bf16[4,40,640]{2,1,0:T(8,128)(2,1)S(1)}, u32[]{:S(2)}, u32[]{:S(2)}) %collective-permute-start.13) | collective-permute-done | bytes 204832 | tf_op jit(solution)/shard_map/ppermute | solution.py:677
  41.2 2.3 %collective-permute-done.15.oth_ref = bf16[16,40,640]{2,1,0:T(8,128)(2,1)S(1)} collective-permute-done((bf16[16,40,640]{2,1,0:T(8,128)(2,1)S(1)}, bf16[16,40,640]{2,1,0:T(8,128)(2,1)S(1)}, u32[]{:S(2)}, u32[]{:S(2)}) %collective-permute-start.15) | collective-permute-done | bytes 819232 | tf_op jit(solution)/shard_map/ppermute | solution.py:677
  43.5 27.9 %shard_map.197 = (bf16[320,512]{1,0:T(8,128)(2,1)}, bf16[16,40,640]{2,1,0:T(8,128)(2,1)S(1)}, bf16[16,40,640]{2,1,0:T(8,128)(2,1)S(1)}, f32[512,320]{1,0:T(8,128...) custom-call(s32[2]{0:T(128)S(1)} %copy-done, s32[2]{0:T(128)S(1)} %copy-done.1, ...), custom_call_target="tpu_custom_call" | custom-call | flops 32999999488 | tf_op jit(solution)/shard_map/pallas_call | solution.py:646
  71.4 2.3 %collective-permute-done.16.got_ref = bf16[16,40,640]{2,1,0:T(8,128)(2,1)S(1)} collective-permute-done((bf16[16,40,640]{2,1,0:T(8,128)(2,1)S(1)}, bf16[16,40,640]{2,1,0:T(8,128)(2,1)S(1)}, u32[]{:S(2)}, u32[]{:S(2)}) %collective-permute-start.16) | collective-permute-done | bytes 819232 | tf_op jit(solution)/shard_map/ppermute | solution.py:677
  73.9 1.3 %collective-permute-start.18 = (bf16[4,40,640]{2,1,0:T(8,128)(2,1)S(1)}, bf16[4,40,640]{2,1,0:T(8,128)(2,1)S(1)}, u32[]{:S(2)}, u32[]{:S(2)}) collective-permute-start(bf16[4,40,640]{2,1,0:T(8,128)(2,1)S(1)} %get-tuple-element.133), channel_id=1, source_target_pairs={{0,4},{1,5},{2,6},{3,7},{4,0},{5,1},{6,2},{7,3},{8,12},{9,13},{10,... | collective-permute-start | bytes 614408 | tf_op jit(solution)/shard_map/ppermute | solution.py:677
  75.2 1.5 %collective-permute-start.19 = (bf16[4,40,640]{2,1,0:T(8,128)(2,1)S(1)}, bf16[4,40,640]{2,1,0:T(8,128)(2,1)S(1)}, u32[]{:S(2)}, u32[]{:S(2)}) collective-permute-start(bf16[4,40,640]{2,1,0:T(8,128)(2,1)S(1)} %get-tuple-element.134), channel_id=1, source_target_pairs={{0,6},{1,7},{2,4},{3,5},{4,2},{5,3},{6,0},{7,1},{8,14},{9,15},{10,... | collective-permute-start | bytes 614408 | tf_op jit(solution)/shard_map/ppermute | solution.py:677
  77.5 2.2 %shard_map.198 = (f32[320,320]{1,0:T(8,128)S(1)}, bf16[512,320]{1,0:T(8,128)(2,1)S(1)}, bf16[512,640]{1,0:T(8,128)(2,1)S(1)}, f32[1,320]{1,0:T(1,128)S(1)}) custom-call(f32[512,320]{1,0:T(8,128)S(1)} %get-tuple-element.100.dx2_ref, bf16[640,320]{1,0:T(8,128)(2,1)S(1)} %get-tuple-element.101.vb_ref, f32[512,640]{1,0:T(8,128)S(1)} %get-tuple-element.102.p_ref, ...), custom_call_target="tpu_custom_call" | custom-call | flops 2500000000 | tf_op jit(solution)/shard_map/pallas_call | solution.py:646
  79.7 2.7 %shard_map.200 = (bf16[16,40,640]{2,1,0:T(8,128)(2,1)S(1)}, bf16[16,40,640]{2,1,0:T(8,128)(2,1)S(1)}, bf16[512,320]{1,0:T(8,128)(2,1)S(1)}, f32[512,320]{1,0:T(8,128)S(1)}, f32[8,320]{1,0:T(8,128)S(1)}) custom-call(bf16[512,320]{1,0:T(8,128)(2,1)S(1)} %get-tuple-element.105.dob_ref, bf16[512,640]{1,0:T(8,128)(2,1)S(1)} %get-tuple-element.110.ds_ref, ...), custom_call_target="tpu_custom_call" | custom-call | tf_op jit(solution)/shard_map/pallas_call | solution.py:646
  82.4 3.1 %shard_map.201 = (bf16[320,512]{1,0:T(8,128)(2,1)}, bf16[2,16,640]{2,1,0:T(8,128)(2,1)S(1)}, bf16[2,16,640]{2,1,0:T(8,128)(2,1)S(1)}) custom-call(s32[2]{0:T(128)S(1)} %copy-done, s32[2]{0:T(128)S(1)} %copy-done.1, f32[512,320]{1,0:T(8,128)S(1)} %get-tuple-element.100.dx2_ref, bf16[512,320]{1,0:T(8,128)(2,1)S(1)} %get-tuple-element.121.dq_ref, ...), custom_call_target="tpu_custom_call" | custom-call | tf_op jit(solution)/shard_map/pallas_call | solution.py:646
  86.9 1.1 collective-permute-done.20.got_ref
  88.2 1.4 %collective-permute-start.22 = (bf16[176,640]{1,0:T(8,128)(2,1)S(1)}, bf16[176,640]{1,0:T(8,128)(2,1)S(1)}, u32[]{:S(2)}, u32[]{:S(2)}) collective-permute-start(bf16[176,640]{1,0:T(8,128)(2,1)S(1)} %get-tuple-element.141), channel_id=1, source_target_pairs={{0,2},{1,3},{2,0},{3,1},{4,6},{5,7},{6,4},{7,5},{8,10},{9,11},{10,... | collective-permute-start | bytes 675848 | tf_op jit(solution)/shard_map/ppermute | solution.py:677
  89.6 0.9 collective-permute-start.23
  90.5 1.2 %collective-permute-start.24 = (bf16[176,640]{1,0:T(8,128)(2,1)S(1)}, bf16[176,640]{1,0:T(8,128)(2,1)S(1)}, u32[]{:S(2)}, u32[]{:S(2)}) collective-permute-start(bf16[176,640]{1,0:T(8,128)(2,1)S(1)} %get-tuple-element.143), channel_id=1, source_target_pairs={{0,6},{1,7},{2,4},{3,5},{4,2},{5,3},{6,0},{7,1},{8,14},{9,15},{10,... | collective-permute-start | bytes 675848 | tf_op jit(solution)/shard_map/ppermute | solution.py:677
  91.8 2.1 %collective-permute-start.26 = (bf16[1,40,640]{2,1,0:T(8,128)(2,1)S(1)}, bf16[1,40,640]{2,1,0:T(8,128)(2,1)S(1)}, u32[]{:S(2)}, u32[]{:S(2)}) collective-permute-start(bf16[1,40,640]{2,1,0:T(8,128)(2,1)S(1)} %get-tuple-element.144), channel_id=1, source_target_pairs={{0,16},{1,17},{2,18},{3,19},{4,20},{5,21},{6,22},{7,23},{8,24},{9,... | collective-permute-start | bytes 153608 | tf_op jit(solution)/shard_map/ppermute | solution.py:677
  93.9 1.5 %collective-permute-start.27 = (bf16[1,40,640]{2,1,0:T(8,128)(2,1)S(1)}, bf16[1,40,640]{2,1,0:T(8,128)(2,1)S(1)}, u32[]{:S(2)}, u32[]{:S(2)}) collective-permute-start(bf16[1,40,640]{2,1,0:T(8,128)(2,1)S(1)} %get-tuple-element.145), channel_id=1, source_target_pairs={{0,24},{1,25},{2,26},{3,27},{4,28},{5,29},{6,30},{7,31},{8,16},{9,... | collective-permute-start | bytes 153608 | tf_op jit(solution)/shard_map/ppermute | solution.py:677
  95.4 1.4 %collective-permute-done.26.c_ref = bf16[1,40,640]{2,1,0:T(8,128)(2,1)S(1)} collective-permute-done((bf16[1,40,640]{2,1,0:T(8,128)(2,1)S(1)}, bf16[1,40,640]{2,1,0:T(8,128)(2,1)S(1)}, u32[]{:S(2)}, u32[]{:S(2)}) %collective-permute-start.26) | collective-permute-done | bytes 51232 | tf_op jit(solution)/shard_map/ppermute | solution.py:677
  96.8 2.0 %collective-permute-start.25 = (bf16[1,40,640]{2,1,0:T(8,128)(2,1)S(1)}, bf16[1,40,640]{2,1,0:T(8,128)(2,1)S(1)}, u32[]{:S(2)}, u32[]{:S(2)}) collective-permute-start(bf16[1,40,640]{2,1,0:T(8,128)(2,1)S(1)} %get-tuple-element.135), channel_id=1, source_target_pairs={{0,8},{1,9},{2,10},{3,11},{4,12},{5,13},{6,14},{7,15},{8,0},{9,1},... | collective-permute-start | bytes 153608 | tf_op jit(solution)/shard_map/ppermute | solution.py:677
  98.8 1.2 %collective-permute-done.27.d_ref = bf16[1,40,640]{2,1,0:T(8,128)(2,1)S(1)} collective-permute-done((bf16[1,40,640]{2,1,0:T(8,128)(2,1)S(1)}, bf16[1,40,640]{2,1,0:T(8,128)(2,1)S(1)}, u32[]{:S(2)}, u32[]{:S(2)}) %collective-permute-start.27) | collective-permute-done | bytes 51232 | tf_op jit(solution)/shard_map/ppermute | solution.py:677
  100.9 1.0 collective-permute-done.23.c_ref
  102.1 1.1 collective-permute-start.28
  103.1 3.5 %collective-permute-start.29 = (bf16[56,640]{1,0:T(8,128)(2,1)S(1)}, bf16[56,640]{1,0:T(8,128)(2,1)S(1)}, u32[]{:S(2)}, u32[]{:S(2)}) collective-permute-start(bf16[56,640]{1,0:T(8,128)(2,1)S(1)} %get-tuple-element.151), channel_id=1, source_target_pairs={{0,16},{1,17},{2,18},{3,19},{4,20},{5,21},{6,22},{7,23},{8,24},{9,... | collective-permute-start | bytes 215048 | tf_op jit(solution)/shard_map/ppermute | solution.py:677
  107.4 3.0 %collective-permute-done.29.c_ref = bf16[56,640]{1,0:T(8,128)(2,1)S(1)} collective-permute-done((bf16[56,640]{1,0:T(8,128)(2,1)S(1)}, bf16[56,640]{1,0:T(8,128)(2,1)S(1)}, u32[]{:S(2)}, u32[]{:S(2)}) %collective-permute-start.29) | collective-permute-done | bytes 71712 | tf_op jit(solution)/shard_map/ppermute | solution.py:677
  110.4 2.3 %collective-permute-done.30.d_ref = bf16[56,640]{1,0:T(8,128)(2,1)S(1)} collective-permute-done((bf16[56,640]{1,0:T(8,128)(2,1)S(1)}, bf16[56,640]{1,0:T(8,128)(2,1)S(1)}, u32[]{:S(2)}, u32[]{:S(2)}) %collective-permute-start.30) | collective-permute-done | bytes 71712 | tf_op jit(solution)/shard_map/ppermute | solution.py:677
  (64 shorter events, 13.4 us)
Async XLA Ops:
  2.4 10.4 %collective-permute-start.2 = (bf16[1,40,640]{2,1,0:T(8,128)(2,1)}, bf16[1,40,640]{2,1,0:T(8,128)(2,1)S(1)}, u32[]{:S(2)}, u32[]{:S(2)}) collective-permute-start(bf16[1,40,640]{2,1,0:T(8,128)(2,1)} %get-tuple-element.86), channel_id=1, source_target_pairs={{0,24},{1,25},{2,26},{3,27},{4,28},{5,29},{6,30},{7,31},{8,16},{9,... | collective-permute-start | bytes 153608 | tf_op jit(solution)/shard_map/ppermute | solution.py:677
  7.5 5.2 %collective-permute-start.1 = (bf16[1,40,640]{2,1,0:T(8,128)(2,1)}, bf16[1,40,640]{2,1,0:T(8,128)(2,1)S(1)}, u32[]{:S(2)}, u32[]{:S(2)}) collective-permute-start(bf16[1,40,640]{2,1,0:T(8,128)(2,1)} %get-tuple-element.86), channel_id=1, source_target_pairs={{0,16},{1,17},{2,18},{3,19},{4,20},{5,21},{6,22},{7,23},{8,24},{9,... | collective-permute-start | bytes 153608 | tf_op jit(solution)/shard_map/ppermute | solution.py:677
  7.5 4.4 %collective-permute-start = (bf16[1,40,640]{2,1,0:T(8,128)(2,1)}, bf16[1,40,640]{2,1,0:T(8,128)(2,1)S(1)}, u32[]{:S(2)}, u32[]{:S(2)}) collective-permute-start(bf16[1,40,640]{2,1,0:T(8,128)(2,1)} %get-tuple-element.86), channel_id=1, source_target_pairs={{0,8},{1,9},{2,10},{3,11},{4,12},{5,13},{6,14},{7,15},{8,0},{9,1},... | collective-permute-start | bytes 153608 | tf_op jit(solution)/shard_map/ppermute | solution.py:677
  8.1 1.4 %collective-permute-start.9 = (bf16[1,16,640]{2,1,0:T(8,128)(2,1)}, bf16[1,16,640]{2,1,0:T(8,128)(2,1)S(1)}, u32[]{:S(2)}, u32[]{:S(2)}) collective-permute-start(bf16[1,16,640]{2,1,0:T(8,128)(2,1)} %get-tuple-element.89), channel_id=1, source_target_pairs={{0,1},{1,0},{2,3},{3,2},{4,5},{5,4},{6,7},{7,6},{8,9},{9,8},{10,11... | collective-permute-start | bytes 61448 | tf_op jit(solution)/shard_map/ppermute | solution.py:677
  10.3 9.4 %collective-permute-start.10 = (bf16[2,16,640]{2,1,0:T(8,128)(2,1)S(1)}, bf16[2,16,640]{2,1,0:T(8,128)(2,1)S(1)}, u32[]{:S(2)}, u32[]{:S(2)}) collective-permute-start(bf16[2,16,640]{2,1,0:T(8,128)(2,1)S(1)} %pad_maximum_fusion.2), channel_id=1, source_target_pairs={{0,2},{1,3},{2,0},{3,1},{4,6},{5,7},{6,4},{7,5},{8,10},{9,11},{10,... | collective-permute-start | bytes 122888 | tf_op jit(solution)/shard_map/ppermute | solution.py:677
  11.9 19.9 %copy-start.2 = (bf16[512,320]{0,1:T(8,128)(2,1)S(1)}, bf16[512,320]{0,1:T(8,128)(2,1)}, u32[]{:S(2)}) copy-start(bf16[512,320]{0,1:T(8,128)(2,1)} %param.12) | copy-start | bytes 983044
  12.8 8.2 %collective-permute-start.8 = (bf16[1,40,640]{2,1,0:T(8,128)(2,1)}, bf16[1,40,640]{2,1,0:T(8,128)(2,1)S(1)}, u32[]{:S(2)}, u32[]{:S(2)}) collective-permute-start(bf16[1,40,640]{2,1,0:T(8,128)(2,1)} %get-tuple-element.88), channel_id=1, source_target_pairs={{0,24},{1,25},{2,26},{3,27},{4,28},{5,29},{6,30},{7,31},{8,16},{9,... | collective-permute-start | bytes 153608 | tf_op jit(solution)/shard_map/ppermute | solution.py:677
  15.7 5.9 %collective-permute-start.7 = (bf16[1,40,640]{2,1,0:T(8,128)(2,1)}, bf16[1,40,640]{2,1,0:T(8,128)(2,1)S(1)}, u32[]{:S(2)}, u32[]{:S(2)}) collective-permute-start(bf16[1,40,640]{2,1,0:T(8,128)(2,1)} %get-tuple-element.88), channel_id=1, source_target_pairs={{0,16},{1,17},{2,18},{3,19},{4,20},{5,21},{6,22},{7,23},{8,24},{9,... | collective-permute-start | bytes 153608 | tf_op jit(solution)/shard_map/ppermute | solution.py:677
  15.7 5.9 %collective-permute-start.6 = (bf16[1,40,640]{2,1,0:T(8,128)(2,1)}, bf16[1,40,640]{2,1,0:T(8,128)(2,1)S(1)}, u32[]{:S(2)}, u32[]{:S(2)}) collective-permute-start(bf16[1,40,640]{2,1,0:T(8,128)(2,1)} %get-tuple-element.88), channel_id=1, source_target_pairs={{0,8},{1,9},{2,10},{3,11},{4,12},{5,13},{6,14},{7,15},{8,0},{9,1},... | collective-permute-start | bytes 153608 | tf_op jit(solution)/shard_map/ppermute | solution.py:677
  17.2 10.9 %collective-permute-start.5 = (bf16[4,40,640]{2,1,0:T(8,128)(2,1)S(1)}, bf16[4,40,640]{2,1,0:T(8,128)(2,1)S(1)}, u32[]{:S(2)}, u32[]{:S(2)}) collective-permute-start(bf16[4,40,640]{2,1,0:T(8,128)(2,1)S(1)} %get-tuple-element.162), channel_id=1, source_target_pairs={{0,6},{1,7},{2,4},{3,5},{4,2},{5,3},{6,0},{7,1},{8,14},{9,15},{10,... | collective-permute-start | bytes 614408 | tf_op jit(solution)/shard_map/ppermute | solution.py:677
  19.7 8.3 %collective-permute-start.3 = (bf16[4,40,640]{2,1,0:T(8,128)(2,1)S(1)}, bf16[4,40,640]{2,1,0:T(8,128)(2,1)S(1)}, u32[]{:S(2)}, u32[]{:S(2)}) collective-permute-start(bf16[4,40,640]{2,1,0:T(8,128)(2,1)S(1)} %get-tuple-element.162), channel_id=1, source_target_pairs={{0,2},{1,3},{2,0},{3,1},{4,6},{5,7},{6,4},{7,5},{8,10},{9,11},{10,... | collective-permute-start | bytes 614408 | tf_op jit(solution)/shard_map/ppermute | solution.py:677
  21.0 7.1 %collective-permute-start.4 = (bf16[4,40,640]{2,1,0:T(8,128)(2,1)S(1)}, bf16[4,40,640]{2,1,0:T(8,128)(2,1)S(1)}, u32[]{:S(2)}, u32[]{:S(2)}) collective-permute-start(bf16[4,40,640]{2,1,0:T(8,128)(2,1)S(1)} %get-tuple-element.162), channel_id=1, source_target_pairs={{0,4},{1,5},{2,6},{3,7},{4,0},{5,1},{6,2},{7,3},{8,12},{9,13},{10,... | collective-permute-start | bytes 614408 | tf_op jit(solution)/shard_map/ppermute | solution.py:677
  28.1 3.7 %collective-permute-start.11 = (bf16[16,40,640]{2,1,0:T(8,128)(2,1)S(1)}, bf16[16,40,640]{2,1,0:T(8,128)(2,1)S(1)}, u32[]{:S(2)}, u32[]{:S(2)}) collective-permute-start(bf16[16,40,640]{2,1,0:T(8,128)(2,1)S(1)} %constant_dynamic-update-slice_fusion.4.own_ref), channel_id=1, source_target_pairs={{0,1},{1,0},{2,3},{3,2},{4,5},{5,4},{6,7},{7,6},{8,9},{9,8},{10,11... | collective-permute-start | bytes 2457608 | tf_op jit(solution)/shard_map/ppermute | solution.py:677
  28.2 10.6 %collective-permute-start.14 = (bf16[4,40,640]{2,1,0:T(8,128)(2,1)S(1)}, bf16[4,40,640]{2,1,0:T(8,128)(2,1)S(1)}, u32[]{:S(2)}, u32[]{:S(2)}) collective-permute-start(bf16[4,40,640]{2,1,0:T(8,128)(2,1)S(1)} %pad_maximum_fusion), channel_id=1, source_target_pairs={{0,6},{1,7},{2,4},{3,5},{4,2},{5,3},{6,0},{7,1},{8,14},{9,15},{10,... | collective-permute-start | bytes 614408 | tf_op jit(solution)/shard_map/ppermute | solution.py:677
  30.3 10.7 %collective-permute-start.13 = (bf16[4,40,640]{2,1,0:T(8,128)(2,1)S(1)}, bf16[4,40,640]{2,1,0:T(8,128)(2,1)S(1)}, u32[]{:S(2)}, u32[]{:S(2)}) collective-permute-start(bf16[4,40,640]{2,1,0:T(8,128)(2,1)S(1)} %pad_maximum_fusion), channel_id=1, source_target_pairs={{0,4},{1,5},{2,6},{3,7},{4,0},{5,1},{6,2},{7,3},{8,12},{9,13},{10,... | collective-permute-start | bytes 614408 | tf_op jit(solution)/shard_map/ppermute | solution.py:677
  30.9 10.1 %collective-permute-start.12 = (bf16[4,40,640]{2,1,0:T(8,128)(2,1)S(1)}, bf16[4,40,640]{2,1,0:T(8,128)(2,1)S(1)}, u32[]{:S(2)}, u32[]{:S(2)}) collective-permute-start(bf16[4,40,640]{2,1,0:T(8,128)(2,1)S(1)} %pad_maximum_fusion), channel_id=1, source_target_pairs={{0,2},{1,3},{2,0},{3,1},{4,6},{5,7},{6,4},{7,5},{8,10},{9,11},{10,... | collective-permute-start | bytes 614408 | tf_op jit(solution)/shard_map/ppermute | solution.py:677
  41.1 2.4 %collective-permute-start.15 = (bf16[16,40,640]{2,1,0:T(8,128)(2,1)S(1)}, bf16[16,40,640]{2,1,0:T(8,128)(2,1)S(1)}, u32[]{:S(2)}, u32[]{:S(2)}) collective-permute-start(bf16[16,40,640]{2,1,0:T(8,128)(2,1)S(1)} %constant_dynamic-update-slice_fusion.11.own_ref), channel_id=1, source_target_pairs={{0,1},{1,0},{2,3},{3,2},{4,5},{5,4},{6,7},{7,6},{8,9},{9,8},{10,11... | collective-permute-start | bytes 2457608 | tf_op jit(solution)/shard_map/ppermute | solution.py:677
  71.4 2.3 %collective-permute-start.16 = (bf16[16,40,640]{2,1,0:T(8,128)(2,1)S(1)}, bf16[16,40,640]{2,1,0:T(8,128)(2,1)S(1)}, u32[]{:S(2)}, u32[]{:S(2)}) collective-permute-start(bf16[16,40,640]{2,1,0:T(8,128)(2,1)S(1)} %get-tuple-element.108), channel_id=1, source_target_pairs={{0,1},{1,0},{2,3},{3,2},{4,5},{5,4},{6,7},{7,6},{8,9},{9,8},{10,11... | collective-permute-start | bytes 2457608 | tf_op jit(solution)/shard_map/ppermute | solution.py:677
  73.9 12.1 %collective-permute-start.18 = (bf16[4,40,640]{2,1,0:T(8,128)(2,1)S(1)}, bf16[4,40,640]{2,1,0:T(8,128)(2,1)S(1)}, u32[]{:S(2)}, u32[]{:S(2)}) collective-permute-start(bf16[4,40,640]{2,1,0:T(8,128)(2,1)S(1)} %get-tuple-element.133), channel_id=1, source_target_pairs={{0,4},{1,5},{2,6},{3,7},{4,0},{5,1},{6,2},{7,3},{8,12},{9,13},{10,... | collective-permute-start | bytes 614408 | tf_op jit(solution)/shard_map/ppermute | solution.py:677
  75.2 10.8 %collective-permute-start.19 = (bf16[4,40,640]{2,1,0:T(8,128)(2,1)S(1)}, bf16[4,40,640]{2,1,0:T(8,128)(2,1)S(1)}, u32[]{:S(2)}, u32[]{:S(2)}) collective-permute-start(bf16[4,40,640]{2,1,0:T(8,128)(2,1)S(1)} %get-tuple-element.134), channel_id=1, source_target_pairs={{0,6},{1,7},{2,4},{3,5},{4,2},{5,3},{6,0},{7,1},{8,14},{9,15},{10,... | collective-permute-start | bytes 614408 | tf_op jit(solution)/shard_map/ppermute | solution.py:677
  76.8 10.0 %collective-permute-start.17 = (bf16[4,40,640]{2,1,0:T(8,128)(2,1)S(1)}, bf16[4,40,640]{2,1,0:T(8,128)(2,1)S(1)}, u32[]{:S(2)}, u32[]{:S(2)}) collective-permute-start(bf16[4,40,640]{2,1,0:T(8,128)(2,1)S(1)} %get-tuple-element.109), channel_id=1, source_target_pairs={{0,2},{1,3},{2,0},{3,1},{4,6},{5,7},{6,4},{7,5},{8,10},{9,11},{10,... | collective-permute-start | bytes 614408 | tf_op jit(solution)/shard_map/ppermute | solution.py:677
  85.5 1.3 %collective-permute-start.21 = (bf16[2,16,640]{2,1,0:T(8,128)(2,1)S(1)}, bf16[2,16,640]{2,1,0:T(8,128)(2,1)S(1)}, u32[]{:S(2)}, u32[]{:S(2)}) collective-permute-start(bf16[2,16,640]{2,1,0:T(8,128)(2,1)S(1)} %get-tuple-element.139), channel_id=1, source_target_pairs={{0,1},{1,0},{2,3},{3,2},{4,5},{5,4},{6,7},{7,6},{8,9},{9,8},{10,11... | collective-permute-start | bytes 122888 | tf_op jit(solution)/shard_map/ppermute | solution.py:677
  85.5 2.5 %collective-permute-start.20 = (bf16[16,40,640]{2,1,0:T(8,128)(2,1)S(1)}, bf16[16,40,640]{2,1,0:T(8,128)(2,1)S(1)}, u32[]{:S(2)}, u32[]{:S(2)}) collective-permute-start(bf16[16,40,640]{2,1,0:T(8,128)(2,1)S(1)} %get-tuple-element.137), channel_id=1, source_target_pairs={{0,1},{1,0},{2,3},{3,2},{4,5},{5,4},{6,7},{7,6},{8,9},{9,8},{10,11... | collective-permute-start | bytes 2457608 | tf_op jit(solution)/shard_map/ppermute | solution.py:677
  88.2 12.7 %collective-permute-start.22 = (bf16[176,640]{1,0:T(8,128)(2,1)S(1)}, bf16[176,640]{1,0:T(8,128)(2,1)S(1)}, u32[]{:S(2)}, u32[]{:S(2)}) collective-permute-start(bf16[176,640]{1,0:T(8,128)(2,1)S(1)} %get-tuple-element.141), channel_id=1, source_target_pairs={{0,2},{1,3},{2,0},{3,1},{4,6},{5,7},{6,4},{7,5},{8,10},{9,11},{10,... | collective-permute-start | bytes 675848 | tf_op jit(solution)/shard_map/ppermute | solution.py:677
  89.6 12.3 %collective-permute-start.23 = (bf16[176,640]{1,0:T(8,128)(2,1)S(1)}, bf16[176,640]{1,0:T(8,128)(2,1)S(1)}, u32[]{:S(2)}, u32[]{:S(2)}) collective-permute-start(bf16[176,640]{1,0:T(8,128)(2,1)S(1)} %get-tuple-element.142), channel_id=1, source_target_pairs={{0,4},{1,5},{2,6},{3,7},{4,0},{5,1},{6,2},{7,3},{8,12},{9,13},{10,... | collective-permute-start | bytes 675848 | tf_op jit(solution)/shard_map/ppermute | solution.py:677
  90.5 11.4 %collective-permute-start.24 = (bf16[176,640]{1,0:T(8,128)(2,1)S(1)}, bf16[176,640]{1,0:T(8,128)(2,1)S(1)}, u32[]{:S(2)}, u32[]{:S(2)}) collective-permute-start(bf16[176,640]{1,0:T(8,128)(2,1)S(1)} %get-tuple-element.143), channel_id=1, source_target_pairs={{0,6},{1,7},{2,4},{3,5},{4,2},{5,3},{6,0},{7,1},{8,14},{9,15},{10,... | collective-permute-start | bytes 675848 | tf_op jit(solution)/shard_map/ppermute | solution.py:677
  91.8 5.0 %collective-permute-start.26 = (bf16[1,40,640]{2,1,0:T(8,128)(2,1)S(1)}, bf16[1,40,640]{2,1,0:T(8,128)(2,1)S(1)}, u32[]{:S(2)}, u32[]{:S(2)}) collective-permute-start(bf16[1,40,640]{2,1,0:T(8,128)(2,1)S(1)} %get-tuple-element.144), channel_id=1, source_target_pairs={{0,16},{1,17},{2,18},{3,19},{4,20},{5,21},{6,22},{7,23},{8,24},{9,... | collective-permute-start | bytes 153608 | tf_op jit(solution)/shard_map/ppermute | solution.py:677
  93.9 6.1 %collective-permute-start.27 = (bf16[1,40,640]{2,1,0:T(8,128)(2,1)S(1)}, bf16[1,40,640]{2,1,0:T(8,128)(2,1)S(1)}, u32[]{:S(2)}, u32[]{:S(2)}) collective-permute-start(bf16[1,40,640]{2,1,0:T(8,128)(2,1)S(1)} %get-tuple-element.145), channel_id=1, source_target_pairs={{0,24},{1,25},{2,26},{3,27},{4,28},{5,29},{6,30},{7,31},{8,16},{9,... | collective-permute-start | bytes 153608 | tf_op jit(solution)/shard_map/ppermute | solution.py:677
  96.8 4.1 %collective-permute-start.25 = (bf16[1,40,640]{2,1,0:T(8,128)(2,1)S(1)}, bf16[1,40,640]{2,1,0:T(8,128)(2,1)S(1)}, u32[]{:S(2)}, u32[]{:S(2)}) collective-permute-start(bf16[1,40,640]{2,1,0:T(8,128)(2,1)S(1)} %get-tuple-element.135), channel_id=1, source_target_pairs={{0,8},{1,9},{2,10},{3,11},{4,12},{5,13},{6,14},{7,15},{8,0},{9,1},... | collective-permute-start | bytes 153608 | tf_op jit(solution)/shard_map/ppermute | solution.py:677
  102.1 5.3 %collective-permute-start.28 = (bf16[56,640]{1,0:T(8,128)(2,1)S(1)}, bf16[56,640]{1,0:T(8,128)(2,1)S(1)}, u32[]{:S(2)}, u32[]{:S(2)}) collective-permute-start(bf16[56,640]{1,0:T(8,128)(2,1)S(1)} %get-tuple-element.150), channel_id=1, source_target_pairs={{0,8},{1,9},{2,10},{3,11},{4,12},{5,13},{6,14},{7,15},{8,0},{9,1},... | collective-permute-start | bytes 215048 | tf_op jit(solution)/shard_map/ppermute | solution.py:677
  103.1 7.3 %collective-permute-start.29 = (bf16[56,640]{1,0:T(8,128)(2,1)S(1)}, bf16[56,640]{1,0:T(8,128)(2,1)S(1)}, u32[]{:S(2)}, u32[]{:S(2)}) collective-permute-start(bf16[56,640]{1,0:T(8,128)(2,1)S(1)} %get-tuple-element.151), channel_id=1, source_target_pairs={{0,16},{1,17},{2,18},{3,19},{4,20},{5,21},{6,22},{7,23},{8,24},{9,... | collective-permute-start | bytes 215048 | tf_op jit(solution)/shard_map/ppermute | solution.py:677
  106.6 6.1 %collective-permute-start.30 = (bf16[56,640]{1,0:T(8,128)(2,1)S(1)}, bf16[56,640]{1,0:T(8,128)(2,1)S(1)}, u32[]{:S(2)}, u32[]{:S(2)}) collective-permute-start(bf16[56,640]{1,0:T(8,128)(2,1)S(1)} %get-tuple-element.152), channel_id=1, source_target_pairs={{0,24},{1,25},{2,26},{3,27},{4,28},{5,29},{6,30},{7,31},{8,16},{9,... | collective-permute-start | bytes 215048 | tf_op jit(solution)/shard_map/ppermute | solution.py:677
  (3 other events, 51.5 us)

commit v3 on v2

--- a/solution.py
+++ b/solution.py
@@ -20,6 +20,9 @@
 TILE = 32
 CHUNK = 256
 PAD = 40
+UNROLL = 4
+RUN = 160
+REST = RUN - 128
 
 
 def dot_nn(left, right):
@@ -51,6 +54,14 @@
 def slot_of(device, me):
     delta = device ^ me
     return ((delta >> 1) & 3) * 4 + (delta >> 3)
+
+
+def round_slot(device, me):
+    delta = device ^ me
+    first, second = (delta >> 1) & 1, (delta >> 2) & 1
+    if device & 1:
+        first, second = second, first
+    return second * 8 + first * 4 + (delta >> 3)
 
 
 def normalise(values):
@@ -70,14 +81,15 @@
     return jnp.sum(values, axis=0, keepdims=True)
 
 
-def piece_of(own_ref, other_ref, device, me):
-    slot = slot_of(device, me)
+def piece_of(own_ref, other_ref, device, me, first=0, last=5):
+    slot = round_slot(device, me)
     mine = ((device ^ me) & 1) == 0
-    return jnp.where(mine, own_ref[slot].astype(F32), other_ref[slot].astype(F32))
-
-
-def token_geometry(rows_ref, cols_ref, capacity, width):
-    row0, row1, col0, col1 = rows_ref[0], rows_ref[1], cols_ref[0], cols_ref[1]
+    at = pl.ds(128 * first, 128 * (last - first))
+    return jnp.where(mine, own_ref[slot, :, at].astype(F32), other_ref[slot, :, at].astype(F32))
+
+
+def token_geometry(geo_ref, capacity, width):
+    row0, row1, col0, col1 = (geo_ref[k] for k in range(4))
     area0, area1 = row0 * col0, row1 * col1
     position = lax.broadcasted_iota(jnp.int32, (capacity, width), 0)
     first = position < area0
@@ -91,7 +103,7 @@
 
 
 def pack_kernel(*refs):
-    sources, (a_ref, b_ref, v_ref), held, semaphores = refs[:8], refs[8:11], refs[11:19], refs[19]
+    sources, (ab_ref, v_ref), held, semaphores = refs[:8], refs[8:10], refs[10:18], refs[18]
     copies = [pltpu.make_async_copy(source, ref, semaphores.at[i]) for i, (source, ref) in enumerate(zip(sources, held))]
     for copy in copies:
         copy.start()
@@ -104,9 +116,10 @@
         return ref[...].astype(F32)
 
     kv = wider(kv_ref).T
-    a_ref[0] = lanes(wider(red_ref), wider(q_ref), kv[:cw], kv[cw:], wider(proj_ref)).astype(BF16)
-    up = wider(up_ref).T
-    b_ref[0] = lanes(wider(down_ref), *[up[cw * e : cw * e + cw] for e in range(4)]).astype(BF16)
+    ab_ref[0] = lanes(wider(red_ref), wider(q_ref), kv[:cw], kv[cw:], wider(proj_ref)).astype(BF16)
+    up, down = wider(up_ref), wider(down_ref)
+    columns = (down[:, :RUN], down[:, RUN:], up[:cw], up[cw:])
+    ab_ref[1] = lanes(*[c[:, :128] for c in columns], *[c[:, 128:] for c in columns]).astype(BF16)
     v_ref[0] = jnp.zeros_like(v_ref[0])
     both = lanes(wider(vm_ref), wider(vh_ref))
     v_ref[0, : both.shape[0], : both.shape[1]] = both.astype(BF16)
@@ -116,31 +129,90 @@
     vmem = pl.BlockSpec(memory_space=pltpu.VMEM)
     return pl.pallas_call(
         pack_kernel,
-        out_shape=[jax.ShapeDtypeStruct((1,) + shape, BF16) for shape in (piece, piece, vpiece)],
+        out_shape=[jax.ShapeDtypeStruct(shape, BF16) for shape in ((2,) + piece, (1,) + vpiece)],
         in_specs=[pl.BlockSpec(memory_space=pl.ANY)] * len(arguments),
-        out_specs=[vmem] * 3,
+        out_specs=[vmem] * 2,
         scratch_shapes=[pltpu.VMEM(v.shape, v.dtype) for v in arguments] + [pltpu.SemaphoreType.DMA((len(arguments),))],
         compiler_params=pltpu.CompilerParams(vmem_limit_bytes=60 * 2**20),
     )(*arguments)
 
 
+def prepare_kernel(
+    rows_hbm, cols_hbm, tok_hbm, x_ref, n1_ref, r1_ref, chosen_ref, live_ref, geo_ref,
+    rows_ref, cols_ref, tok_ref, semaphores,
+):
+    copies = [
+        pltpu.make_async_copy(source, target, semaphores.at[i])
+        for i, (source, target) in enumerate(((rows_hbm, rows_ref), (cols_hbm, cols_ref), (tok_hbm, tok_ref)))
+    ]
+    for copy in copies:
+        copy.start()
+    for copy in copies:
+        copy.wait()
+    capacity = tok_ref.shape[1]
+    for j in range(2):
+        geo_ref[j] = rows_ref[j]
+        geo_ref[2 + j] = cols_ref[j]
+    tokens = tok_ref[...].astype(F32).T
+    x_ref[...] = tokens
+    normed, inverse = normalise(tokens)
+    n1_ref[...] = normed
+    r1_ref[...] = inverse
+    chosen_ref[...] = one_hot(rows_ref, cols_ref, capacity)
+    area0, area1 = rows_ref[0] * cols_ref[0], rows_ref[1] * cols_ref[1]
+    quarter0, quarter1 = area0 // 4, area1 // 4
+    token = lax.broadcasted_iota(jnp.int32, live_ref.shape, 0)
+    key = lax.broadcasted_iota(jnp.int32, live_ref.shape, 1)
+    live = ((token < area0) & (key < quarter0)) | (
+        (token >= area0) & (token < area0 + area1) & (key >= quarter0) & (key < quarter0 + quarter1)
+    )
+    live_ref[...] = jnp.where(live, 1.0, 0.0)
+
+
+def prepare(img_rows, img_cols, tokens):
+    width, capacity = tokens.shape
+    keys = capacity // 4
+    vmem, smem = (pl.BlockSpec(memory_space=space) for space in (pltpu.VMEM, pltpu.SMEM))
+    outputs = (
+        ((capacity, width), F32), ((capacity, width), F32), ((capacity, 1), F32), ((capacity, capacity), BF16),
+        ((capacity, keys), F32), ((4,), jnp.int32),
+    )
+    return pl.pallas_call(
+        prepare_kernel,
+        out_shape=[jax.ShapeDtypeStruct(shape, kind) for shape, kind in outputs],
+        in_specs=[pl.BlockSpec(memory_space=pl.ANY)] * 3,
+        out_specs=[vmem] * 5 + [smem],
+        scratch_shapes=[
+            pltpu.SMEM((2,), jnp.int32), pltpu.SMEM((2,), jnp.int32), pltpu.VMEM((width, capacity), BF16),
+            pltpu.SemaphoreType.DMA((3,)),
+        ],
+        compiler_params=pltpu.CompilerParams(vmem_limit_bytes=60 * 2**20),
+        cost_estimate=pl.CostEstimate(flops=2 * 10**9, bytes_accessed=0, transcendentals=0),
+    )(img_rows, img_cols, tokens)
+
+
 def attend_kernel(
     tuned,
-    rows_ref, cols_ref, tok_ref, own_ref, oth_ref, vec_ref,
-    x2_ref, h1_ref, n1_ref, r1_ref, patch_ref, nk_ref, rk_ref, kn_ref, q_ref, kb_ref, vb_ref,
+    x_ref, n1_ref, chosen_ref, live_ref, own_ref, oth_ref, v0_ref, v1_ref, v2_ref, v3_ref,
+    x2_ref, h1_ref, patch_ref, nk_ref, rk_ref, kn_ref, q_ref, kb_ref, vb_ref,
     p_ref, o_ref, wr_ref, wq_ref, wkv_ref, wp_ref, mv_ref, hv_ref,
     score_ref,
 ):
     me = my_index(tuned)
-    width, capacity = tok_ref.shape
+    capacity, width = x_ref.shape
     cw, rn = width // PARTS_W, width // PARTS_N
     keys = capacity // 4
     dim = width // HEADS
 
-    pieces = [vec_ref[n ^ (me & 3)].astype(F32) for n in range(PARTS_N)]
+    held = [ref[0].astype(F32) for ref in (v0_ref, v1_ref, v2_ref, v3_ref)]
+    odd = (me & 1) == 1
+    held = [jnp.where(odd, held[k ^ 1], held[k]) for k in range(4)]
+    odd = (me & 2) == 2
+    pieces = [jnp.where(odd, held[k ^ 2], held[k]) for k in range(4)]
     mv = lanes(*[p[:, :rn] for p in pieces])
     mv_ref[...] = mv
-    hv_ref[...] = lanes(*[p[:, rn : 5 * rn] for p in pieces])
+    runs = [p[:, rn + e * RUN : rn + (e + 1) * RUN] for p in pieces for e in range(2)]
+    hv_ref[...] = lanes(*[r[:, :128] for r in runs], *[r[:, 128:] for r in runs])
 
     for pair in range(PARTS_W // 2):
         got = [
@@ -160,17 +232,12 @@
         ).astype(BF16)
         wp_ref[at, :] = rows_of(unit(0, 3), unit(1, 3)).astype(BF16)
 
-    tokens = tok_ref[...].astype(F32).T
-    normed, inverse = normalise(tokens)
-    n1_ref[...] = normed
-    r1_ref[...] = inverse
-    h1 = (normed * mv[0:1] + mv[1:2]).astype(BF16)
+    h1 = (n1_ref[...] * mv[0:1] + mv[1:2]).astype(BF16)
     h1_ref[...] = h1
     q = (dot_nt(h1, wq_ref[...]) + mv[2:3]).astype(BF16)
     q_ref[...] = q
 
-    chosen = one_hot(rows_ref, cols_ref, capacity)
-    patches = dot_nn(chosen, h1).astype(BF16)
+    patches = dot_nn(chosen_ref[...], h1).astype(BF16)
     patch_ref[...] = patches
     reduced = mv[4:5]
     for n in range(4):
@@ -191,17 +258,9 @@
         vb_ref[at, :] = jnp.where(inside, v, 0.0).astype(BF16)
 
     score_ref[...] = dot_nt(q, kb_ref[...]) * dim ** (-0.5)
-    area0 = rows_ref[0] * cols_ref[0]
-    area1 = rows_ref[1] * cols_ref[1]
-
     def soften(i, carry):
         at = pl.ds(pl.multiple_of(i * 64, 64), 64)
-        token = lax.broadcasted_iota(jnp.int32, (64, keys), 0) + i * 64
-        key = lax.broadcasted_iota(jnp.int32, (64, keys), 1)
-        quarter0, quarter1 = area0 // 4, area1 // 4
-        live = ((token < area0) & (key < quarter0)) | (
-            (token >= area0) & (token < area0 + area1) & (key >= quarter0) & (key < quarter0 + quarter1)
-        )
+        live = live_ref[at, :] > 0.5
         for h in range(HEADS):
             lane_at = pl.ds(h * keys, keys)
             s = jnp.where(live, score_ref[at, lane_at], MASKED)
@@ -212,7 +271,7 @@
     lax.fori_loop(0, capacity // 64, soften, 0)
     o = dot_nn(p_ref[...].astype(BF16), vb_ref[...]).astype(BF16)
     o_ref[...] = o
-    x2_ref[...] = tokens + dot_nt(o, wp_ref[...]) + mv[7:8]
+    x2_ref[...] = x_ref[...] + dot_nt(o, wp_ref[...]) + mv[7:8]
 
 
 def one_hot(rows_ref, cols_ref, capacity):
@@ -238,37 +297,22 @@
     )
 
 
-def ffn_kernel(
-    tuned,
-    rows_ref, cols_ref, x2_ref, cot_ref, own_ref, oth_ref, mv_ref, hv_ref,
-    mixed_ref, gown_ref, gsend_ref, dx2_ref, mg_ref, hg_ref,
-    wu_ref, wd_ref, mask_ref, n2_ref, r2_ref, h2_ref, h2t_ref, gy_ref, gyt_ref,
-    f_ref, gm_ref, gp_ref, dc_ref, ul_ref, ur_ref, g0_ref, slope_ref, act_ref, u0_ref, df_ref, da_ref,
-    mix_ref, dh2_ref, upg_ref, dng_ref, turned_ref,
+def prepare_two_kernel(
+    geo_ref, cot_ref, x2_ref, mv_ref, n2_ref, r2_ref, h2_ref, h2t_ref, gy_ref, gyt_ref, mask_ref
 ):
-    me = my_index(tuned)
-    capacity, width = x2_ref.shape
-    hidden = hv_ref.shape[1]
-    cw, rn = width // PARTS_W, width // PARTS_N
-    tiles = capacity // TILE
-
-    for pair in range(PARTS_W // 2):
-        got = [
-            [piece_of(own_ref, oth_ref, w * PARTS_N + n, me) for n in range(PARTS_N)]
-            for w in (2 * pair, 2 * pair + 1)
-        ]
-        wd_ref[pl.ds(pair * 2 * cw, 2 * cw), :] = lanes(
-            *[rows_of(got[0][n][:, :width], got[1][n][:, :width]) for n in range(PARTS_N)]
-        ).astype(BF16)
-
-        def unit(w, k):
-            return lanes(*[got[w][n][:, width + k * rn : width + (k + 1) * rn] for n in range(PARTS_N)])
-
-        wu_ref[pl.ds(pair * 8 * cw, 8 * cw), :] = rows_of(
-            *[unit(w, k) for w in range(2) for k in range(4)]
-        ).astype(BF16)
-
-    first, second, row, col, heights, widths = token_geometry(rows_ref, cols_ref, capacity, 128)
+    width, capacity = cot_ref.shape
+    normed, inverse = normalise(x2_ref[...])
+    n2_ref[...] = normed
+    r2_ref[...] = inverse
+    h2 = normed * mv_ref[8:9, :] + mv_ref[9:10, :]
+    h2_ref[...] = h2.astype(BF16)
+    h2t_ref[...] = h2.T.astype(BF16)
+    area = geo_ref[0] * geo_ref[2] + geo_ref[1] * geo_ref[3]
+    position = lax.broadcasted_iota(jnp.int32, (width, capacity), 1)
+    gyt = jnp.where(position < area, cot_ref[...].astype(F32), 0.0)
+    gyt_ref[...] = gyt.astype(BF16)
+    gy_ref[...] = gyt.T.astype(BF16)
+    first, second, row, col, heights, widths = token_geometry(geo_ref, capacity, 128)
     live = first | second
     conditions = (
         live & (col > 0),
@@ -281,32 +325,46 @@
     )
     for k, condition in enumerate(conditions):
         mask_ref[k] = jnp.where(condition, 1.0, 0.0)
-    w0 = cols_ref[0]
-    w1 = cols_ref[1]
+
+
+def ffn_kernel(
+    tuned,
+    geo_ref, n2_ref, r2_ref, h2_ref, h2t_ref, gy_ref, gyt_ref, mask_ref, own_ref, oth_ref, mv_ref, hv_ref,
+    gown_ref, gsend_ref, mix_ref, dx2_ref, mg_ref, hg_ref,
+    wu_ref, wd_ref, f_ref, gm_ref, gp_ref, dc_ref, ul_ref, ur_ref, g0_ref, slope_ref, act_ref, u0_ref, df_ref, da_ref,
+    dh2_ref, upg_ref, dng_ref,
+):
+    me = my_index(tuned)
+    capacity, width = n2_ref.shape
+    hidden = hv_ref.shape[1]
+    cw, rn = width // PARTS_W, width // PARTS_N
+    tiles = capacity // TILE
+    tails = 128 * PARTS_W
+
+    for pair in range(PARTS_W // 2):
+        at = pl.ds(pair * 2 * cw, 2 * cw)
+        got = [
+            rows_of(*[piece_of(own_ref, oth_ref, w * PARTS_N + n, me, 0, 5) for w in (2 * pair, 2 * pair + 1)])
+            for n in range(PARTS_N)
+        ]
+        for n in range(PARTS_N):
+            wd_ref[at, pl.ds(256 * n, 256)] = got[n][:, :256].astype(BF16)
+        wd_ref[at, pl.ds(tails, 2 * REST * PARTS_N)] = lanes(*[g[:, 512 : 512 + 2 * REST] for g in got]).astype(BF16)
+    for n in range(PARTS_N):
+        at = pl.ds(n * rn, rn)
+        ends = []
+        for w in range(PARTS_W):
+            got = piece_of(own_ref, oth_ref, w * PARTS_N + n, me, 2, 5)
+            wu_ref[at, pl.ds(128 * w, 128)] = rows_of(got[:, :128], got[:, 128:256]).astype(BF16)
+            ends.append(rows_of(got[:, 256 + 2 * REST : 256 + 3 * REST], got[:, 256 + 3 * REST :]))
+        wu_ref[at, pl.ds(tails, REST * PARTS_W)] = lanes(*ends).astype(BF16)
+
+    w0, w1 = geo_ref[2], geo_ref[3]
 
     for ref in (f_ref, gm_ref, gp_ref, dc_ref, ul_ref, ur_ref):
         ref[:, :PAD, :] = jnp.zeros((CHUNK // 128, PAD, 128), F32)
         ref[:, PAD + capacity :, :] = jnp.zeros((CHUNK // 128, PAD, 128), F32)
 
-    def wide_mask(k, at, size):
-        m = mask_ref[k, at, :]
-        return lanes(*([m] * (size // 128)), *([m[:, : size % 128]] if size % 128 else []))
-
-    gain2, shift2, bias2 = mv_ref[8:9, :], mv_ref[9:10, :], mv_ref[10:11, :]
-
-    def start(i, carry):
-        at = pl.ds(pl.multiple_of(i * 64, 64), 64)
-        normed, inverse = normalise(x2_ref[at, :])
-        n2_ref[at, :] = normed
-        r2_ref[at, :] = inverse
-        h2_ref[at, :] = (normed * gain2 + shift2).astype(BF16)
-        gy_ref[at, :] = (turned_ref[at, :] * wide_mask(6, at, width)).astype(BF16)
-        return carry
-
-    turned_ref[...] = cot_ref[...].astype(F32).T
-    lax.fori_loop(0, capacity // 64, start, 0)
-    h2t_ref[...] = h2_ref[...].astype(F32).T.astype(BF16)
-    gyt_ref[...] = gy_ref[...].astype(F32).T.astype(BF16)
     mix_ref[...] = jnp.zeros_like(mix_ref)
     dh2_ref[...] = jnp.zeros_like(dh2_ref)
 
@@ -324,7 +382,7 @@
         def put_vector(k, j, value):
             hg_ref[k : k + 1, pl.ds(pl.multiple_of(c * CHUNK + j * 128, 128), 128)] = value
 
-        first_layer = dot_nt(h2_ref[...], wu_ref[at_c, :])
+        first_layer = dot_nn(h2_ref[...], wu_ref[:, at_c])
         for j in range(halves):
             f_ref[j, pl.ds(PAD, capacity), :] = first_layer[:, j * 128 : (j + 1) * 128] + vector(0, j)
 
@@ -345,7 +403,7 @@
                 gp_ref[j, pl.ds(PAD + r, TILE), :] = v[8] * left + v[9] * here + v[10] * right
             return carry
 
-        lax.fori_loop(0, tiles, column_taps, 0)
+        lax.fori_loop(0, tiles, column_taps, 0, unroll=UNROLL)
 
         def activate(i, carry):
             r = pl.multiple_of(i * TILE, TILE)
@@ -365,7 +423,7 @@
                 slope_ref[at, lane_at] = slope
             return carry
 
-        lax.fori_loop(0, tiles, activate, 0)
+        lax.fori_loop(0, tiles, activate, 0, unroll=UNROLL)
         act = act_ref[...]
         mix_ref[...] += dot_nt(act, wd_ref[:, at_c])
         dng_ref[:, at_c] = dot_nn(gyt_ref[...], act)
@@ -382,7 +440,7 @@
             return tuple(totals)
 
         zero = jnp.zeros((8, 128), F32)
-        totals = lax.fori_loop(0, tiles, into_conv, (zero,) * halves)
+        totals = lax.fori_loop(0, tiles, into_conv, (zero,) * halves, unroll=UNROLL)
         for j in range(halves):
             put_vector(1, j, column_sum(totals[j]))
 
@@ -408,7 +466,7 @@
                 grads = [fold(d * f) for d in (below, level, above) for f in (left, here, right)]
                 return tuple(a + b for a, b in zip(carry, grads))
 
-            sums = lax.fori_loop(0, tiles, tap_back, (zero,) * 9)
+            sums = lax.fori_loop(0, tiles, tap_back, (zero,) * 9, unroll=UNROLL)
             for k in range(9):
                 put_vector(2 + k, j, column_sum(sums[k]))
 
@@ -426,38 +484,38 @@
                 totals.append(carry[j] + fold(value.astype(F32)))
             return tuple(totals)
 
-        totals = lax.fori_loop(0, tiles, spread_back, (zero,) * halves)
+        totals = lax.fori_loop(0, tiles, spread_back, (zero,) * halves, unroll=UNROLL)
         for j in range(halves):
             put_vector(0, j, column_sum(totals[j]))
         df = df_ref[...]
         upg_ref[:, at_c] = dot_nn(h2t_ref[...], df)
-        dh2_ref[...] += dot_nn(df, wu_ref[at_c, :])
+        dh2_ref[...] += dot_nt(df, wu_ref[:, at_c])
         return carry
 
     lax.fori_loop(0, hidden // CHUNK, chunk_step, 0)
     hg_ref[11:, :] = jnp.zeros((hg_ref.shape[0] - 11, hidden), F32)
 
     def value_of(w, n):
-        up = upg_ref[pl.ds(n * rn, rn), pl.ds(w * 4 * cw, 4 * cw)]
+        down = pl.ds(w * cw, cw)
+        up = [pl.ds(n * rn + e * cw, cw) for e in range(2)]
         return lanes(
-            dng_ref[pl.ds(w * cw, cw), pl.ds(n * width, width)],
-            *[up[e * cw : (e + 1) * cw] for e in range(rn // cw)],
+            dng_ref[down, pl.ds(256 * n, 256)],
+            *[upg_ref[e, pl.ds(128 * w, 128)] for e in up],
+            dng_ref[down, pl.ds(tails + 2 * REST * n, 2 * REST)],
+            *[upg_ref[e, pl.ds(tails + REST * w, REST)] for e in up],
         )
 
     store_pieces(gown_ref, gsend_ref, me, value_of)
 
     def finish(i, carry):
         at = pl.ds(pl.multiple_of(i * 64, 64), 64)
-        occupied = wide_mask(6, at, width)
-        turned_ref[at, :] = (x2_ref[at, :] + mix_ref[at, :] + bias2) * occupied
         gy = gy_ref[at, :].astype(F32)
         grad, normed = dh2_ref[at, :], n2_ref[at, :]
-        dx2_ref[at, :] = gy + normalise_back(grad, normed, r2_ref[at, :], gain2)
+        dx2_ref[at, :] = gy + normalise_back(grad, normed, r2_ref[at, :], mv_ref[8:9, :])
         return tuple(a + column_sum(b) for a, b in zip(carry, (grad * normed, grad, gy)))
 
     zero = jnp.zeros((1, width), F32)
     sums = lax.fori_loop(0, capacity // 64, finish, (zero, zero, zero))
-    mixed_ref[...] = turned_ref[...].T.astype(BF16)
     mg_ref[...] = jnp.zeros_like(mg_ref)
     for k in range(3):
         mg_ref[8 + k : 9 + k, :] = sums[k]
@@ -559,13 +617,17 @@
 
 def token_back_kernel(
     tuned,
-    rows_ref, cols_ref, dx2_ref, dq_ref, dpatch_ref, n1_ref, r1_ref, wq_ref, mv_ref, mg_ref, hg_ref, vk_ref, bp_ref,
-    tg_ref, vown_ref, vsend_ref,
+    dx2_ref, dq_ref, dpatch_ref, n1_ref, r1_ref, chosen_ref, wq_ref, mv_ref, mg_ref, hg_ref, vk_ref, bp_ref,
+    x2_ref, mix_ref, mask_ref,
+    mixed_ref, tg_ref, vown_ref, vsend_ref,
 ):
     me = my_index(tuned)
     capacity, width = dx2_ref.shape
     rn = width // PARTS_N
-    chosen = one_hot(rows_ref, cols_ref, capacity)
+    occupied = mask_ref[6]
+    occupied = lanes(*([occupied] * (width // 128)), occupied[:, : width % 128])
+    mixed_ref[...] = ((x2_ref[...] + mix_ref[...] + mv_ref[10:11, :]) * occupied).T.astype(BF16)
+    chosen = chosen_ref[...]
     high = dpatch_ref[...].astype(BF16)
     low = (dpatch_ref[...] - high.astype(F32)).astype(BF16)
     dh1 = dot_nn(dq_ref[...], wq_ref[...]) + dot_tn(chosen, high) + dot_tn(chosen, low)
@@ -576,9 +638,12 @@
     sums = rows_of(column_sum(dh1 * n1), column_sum(dh1), vk[0:5], bp_ref[...], mg_ref[8:16, :])
     hg = hg_ref[...]
     spare = jnp.zeros((16, 3 * rn), F32)
-    value = [
-        lanes(sums[:, n * rn : (n + 1) * rn], hg[:, n * width : (n + 1) * width], spare) for n in range(PARTS_N)
-    ]
+    value = []
+    for n in range(PARTS_N):
+        parts = []
+        for w in (2 * n, 2 * n + 1):
+            parts += [hg[:, 128 * w : 128 * (w + 1)], hg[:, 1024 + REST * w : 1024 + REST * (w + 1)]]
+        value.append(lanes(sums[:, n * rn : (n + 1) * rn], *parts, spare))
     even = (me & 1) == 0
     for x in range(2):
         slot = x ^ ((me >> 1) & 1)
@@ -622,9 +687,11 @@
 
 def finish_ffn_kernel(a_ref, b_ref, c_ref, d_ref, up_ref, down_ref):
     total = total_of((a_ref, b_ref, c_ref, d_ref))[0]
-    width = down_ref.shape[1]
-    down_ref[...] = total[:, :width]
-    up_ref[...] = rows_of(total[:, width : width + width // 2], total[:, width + width // 2 :])
+    columns = [
+        lanes(total[:, 128 * k : 128 * (k + 1)], total[:, 512 + REST * k : 512 + REST * (k + 1)]) for k in range(4)
+    ]
+    down_ref[...] = lanes(*columns[:2])
+    up_ref[...] = rows_of(*columns[2:])
 
 
 def finish_attend_kernel(a_ref, b_ref, c_ref, d_ref, q_ref, kv_ref, red_ref, proj_ref, vm_ref, vh_ref):
@@ -672,27 +739,32 @@
     piece = (cw, 2 * width)
     vpiece = (16, 2 * width)
 
-    def swap(value, mask):
-        pairs = [(i, i ^ mask) for i in range(wide * narrow)]
+    def swap(value, mask, other=None):
+        masks = (mask, mask if other is None else other)
+        pairs = [(i, i ^ masks[i & 1]) for i in range(wide * narrow)]
         return lax.ppermute(value, ("wide", "narrow"), pairs)
 
+    tokens_f32 = ((capacity, width), F32)
+    tokens_low = ((capacity, width), BF16)
+    x, n1, r1, chosen, live, geo = prepare(img_rows, img_cols, tokens.T)
     if tuned:
-        pack_a, pack_b, pack_v = pack(
+        packed, pack_v = pack(
             (
                 q_weight.T, kv_weight, reduce_weight.T, proj_weight.T, up_weight, down_weight.T,
                 vec_model, vec_hidden,
             ),
             piece, vpiece,
         )
-        near_a = jnp.concatenate([pack_a] + [swap(pack_a, m) for m in (8, 16, 24)], axis=0)
-        vec_pair = jnp.concatenate([pack_v, swap(pack_v, 1)], axis=0)
-        vecs = jnp.concatenate([vec_pair, swap(vec_pair, 2)], axis=0)
-        own_a = jnp.concatenate([near_a] + [swap(near_a, m) for m in (2, 4, 6)], axis=0)
-        pack_b = after(pack_b, near_a)
-        near_b = jnp.concatenate([pack_b] + [swap(pack_b, m) for m in (8, 16, 24)], axis=0)
-        own_a, near_b, vecs = lax.optimization_barrier((own_a, near_b, vecs))
+        line = [swap(packed, m) for m in (8, 16, 24)]
+        vecs = [pack_v] + [swap(pack_v, m) for m in (1, 2, 3)]
+        line = lax.optimization_barrier((*line, x, n1, chosen))[:3]
+        near_a, near_b = (jnp.concatenate([v[k : k + 1] for v in (packed, *line)], axis=0) for k in range(2))
+        half_a = jnp.concatenate([near_a, swap(near_a, 2, 4)], axis=0)
+        half_b = jnp.concatenate([near_b, swap(near_b, 2, 4)], axis=0)
+        own_a = jnp.concatenate([half_a, swap(half_a, 4, 2)], axis=0)
+        own_a, half_b, *vecs = lax.optimization_barrier((own_a, half_b, *vecs))
         oth_a = swap(own_a, 1)
-        plane_b = [swap(near_b, m) for m in (2, 4, 6)]
+        rest_b = swap(half_b, 4, 2)
     else:
         own_a, oth_a, own_b, oth_b, vecs = gather_plain(
             q_weight, kv_weight, reduce_weight, proj_weight, up_weight, down_weight, vec_model, vec_hidden
@@ -700,12 +772,12 @@
 
     square = (width, width)
     (
-        x2, h1, n1, r1, patches, nk, rk, kn, q, kb, vb, p, o, wr, wq, wkv, wp, mv, hv,
+        x2, h1, patches, nk, rk, kn, q, kb, vb, p, o, wr, wq, wkv, wp, mv, hv,
     ) = call(
         functools.partial(attend_kernel, tuned),
-        (img_rows, img_cols, tokens.T, own_a, oth_a, vecs),
+        (x, n1, chosen, live, own_a, oth_a, *vecs),
         (
-            ((capacity, width), F32), ((capacity, width), BF16), ((capacity, width), F32), ((capacity, 1), F32),
+            tokens_f32, tokens_low,
             ((capacity, width), BF16), ((keys, width), F32), ((keys, 1), F32), ((keys, width), BF16),
             ((capacity, width), BF16), ((HEADS * keys, width), BF16), ((HEADS * keys, width), BF16),
             ((capacity, HEADS * keys), F32), ((capacity, width), BF16),
@@ -713,34 +785,39 @@
             ((16, width), F32), ((16, hidden), F32),
         ),
         scratch=(((capacity, HEADS * keys), F32),),
-        scalars=2,
         flops=8 * 10**9,
     )
 
     if tuned:
-        plane_b = lax.optimization_barrier((*plane_b, x2))[:3]
-        own_b = jnp.concatenate([near_b, *plane_b], axis=0)
+        own_b = jnp.concatenate([half_b, after(rest_b, x2)], axis=0)
         oth_b = swap(own_b, 1)
     padded = ((CHUNK // 128, capacity + 2 * PAD, 128), F32)
     halved = ((CHUNK // 128, capacity, 128), F32)
     chunked = ((capacity, CHUNK), F32)
-    mixed, gown_b, gsend_b, dx2, mg, hg = call(
+    n2, r2, h2, h2t, gy, gyt, masks = call(
+        prepare_two_kernel,
+        (geo, cotangent.T, x2, mv),
+        (
+            tokens_f32, ((capacity, 1), F32), tokens_low, ((width, capacity), BF16),
+            tokens_low, ((width, capacity), BF16), ((7, capacity, 128), F32),
+        ),
+        scalars=1,
+        flops=2 * 10**9,
+    )
+    gown_b, gsend_b, mix, dx2, mg, hg = call(
         functools.partial(ffn_kernel, tuned),
-        (img_rows, img_cols, x2, cotangent.T, own_b, oth_b, mv, hv),
+        (geo, n2, r2, h2, h2t, gy, gyt, masks, own_b, oth_b, mv, hv),
         (
-            ((width, capacity), BF16), ((SLOTS,) + piece, BF16), ((SLOTS,) + piece, BF16),
-            ((capacity, width), F32), ((16, width), F32), ((16, hidden), F32),
+            ((SLOTS,) + piece, BF16), ((SLOTS,) + piece, BF16),
+            tokens_f32, tokens_f32, ((16, width), F32), ((16, hidden), F32),
         ),
         scratch=(
-            ((hidden, width), BF16), ((width, hidden), BF16), ((7, capacity, 128), F32),
-            ((capacity, width), F32), ((capacity, 1), F32), ((capacity, width), BF16), ((width, capacity), BF16),
-            ((capacity, width), BF16), ((width, capacity), BF16),
+            ((width, hidden), BF16), ((width, hidden), BF16),
             padded, padded, padded, padded, padded, padded,
             halved, chunked, ((capacity, CHUNK), BF16), halved, ((capacity, CHUNK), BF16), chunked,
-            ((capacity, width), F32), ((capacity, width), F32), ((width, hidden), F32), ((width, hidden), F32),
-            ((capacity, width), F32),
+            tokens_f32, ((width, hidden), F32), ((width, hidden), F32),
         ),
-        scalars=2,
+        scalars=1,
         flops=33 * 10**9,
     )
 
@@ -757,6 +834,7 @@
     )
     four = (4,) + piece
     if tuned:
+        got_b = after(got_b, ds)
         half_b = call(core_sum_kernel, (gown_b, got_b), ((four, BF16),) * 4)
         plane_b = [swap(half_b[k], 2 * k) for k in (1, 2, 3)]
         ds = after(ds, half_b[1])
@@ -774,12 +852,10 @@
         got_a = swap(gsend_a, 1)
         near_b = call(plane_sum_kernel, (half_b[0], *plane_b), (((1,) + piece, BF16),) * 4, flops=2 * 10**10)
         line_b = [swap(near_b[k], 8 * k) for k in (1, 2, 3)]
-    token_grad, vown, vsend = call(
+    mixed, token_grad, vown, vsend = call(
         functools.partial(token_back_kernel, tuned),
-        (img_rows, img_cols, dx2, dq, dpatch, n1, r1, wq, mv, mg, hg, vk, bp),
-        (((width, capacity), BF16), ((2,) + vpiece, BF16), ((2,) + vpiece, BF16)),
-        scalars=2,
-        flops=0,
+        (dx2, dq, dpatch, n1, r1, chosen, wq, mv, mg, hg, vk, bp, x2, mix, masks),
+        (((width, capacity), BF16), ((width, capacity), BF16), ((2,) + vpiece, BF16), ((2,) + vpiece, BF16)),
     )
 
     if not tuned:
@@ -825,17 +901,22 @@
         return split.transpose(0, 3, 2, 1, 4).reshape(PARTS_W, PARTS_N, cw, -1)
 
     def slots(value):
-        value = value.reshape(4, 4, 2, cw, -1).transpose(2, 1, 0, 3, 4)
-        value = value.reshape(2, SLOTS, cw, -1)
-        return value[0], value[1]
+        value = value.reshape(4, 2, 2, 2, cw, -1)
+        even = value[:, :, :, 0].transpose(1, 2, 0, 3, 4)
+        odd = value[:, :, :, 1].transpose(2, 1, 0, 3, 4)
+        return even.reshape(SLOTS, cw, -1), odd.reshape(SLOTS, cw, -1)
 
     a = jnp.concatenate([pieces(reduce, 1), pieces(q, 1), pieces(kv, 2), pieces(proj, 1)], axis=-1)
-    b = jnp.concatenate([pieces(down, 1), pieces(up, 4)], axis=-1)
+    columns = pieces(down, 1).reshape(PARTS_W, PARTS_N, cw, 2, RUN)
+    columns = [columns[..., e, :] for e in range(2)]
+    halves = up.T.reshape(PARTS_N, 2, cw, PARTS_W, RUN).transpose(1, 3, 0, 2, 4)
+    columns += [halves[0], halves[1]]
+    b = jnp.concatenate([c[..., :128] for c in columns] + [c[..., 128:] for c in columns], axis=-1)
     vm = lax.all_gather(vec_model, "narrow", axis=1, tiled=True)
     vh = lax.all_gather(vec_hidden, "narrow", axis=1, tiled=True)
     both = jnp.concatenate([vm.reshape(11, PARTS_N, rn), vh.reshape(11, PARTS_N, width)], axis=-1)
     vecs = jnp.pad(both.transpose(1, 0, 2), ((0, 0), (0, 5), (0, 3 * rn)))
-    return (*slots(a), *slots(b), vecs)
+    return (*slots(a), *slots(b), [vecs[n : n + 1] for n in range(PARTS_N)])
 
 
 def scatter_plain(mesh_shape, width, gown_a, gsend_a, gown_b, gsend_b, vown, vsend):
@@ -859,9 +940,12 @@
     q = natural(a[..., width : width + rn], 1)
     kv = natural(a[..., width + rn : width + 3 * rn], 2)
     proj = natural(a[..., width + 3 * rn :], 1)
-    down = natural(b[..., :width], 1)
-    up = b[..., width:].reshape(PARTS_W, PARTS_N, cw, rn // cw, 4 * cw).transpose(1, 3, 2, 0, 4)
-    up = up.reshape(width, PARTS_W * 4 * cw)
+    columns = [
+        jnp.concatenate([b[..., 128 * k : 128 * (k + 1)], b[..., 512 + REST * k : 512 + REST * (k + 1)]], axis=-1)
+        for k in range(4)
+    ]
+    down = natural(jnp.concatenate(columns[:2], axis=-1), 1)
+    up = jnp.stack(columns[2:]).transpose(2, 0, 3, 1, 4).reshape(width, -1)
     vectors = jnp.stack([vown, vsend], axis=1).reshape(PARTS_N, 16, -1)[:, :11].transpose(1, 0, 2)
     vm = vectors[..., :rn].reshape(11, width)
     vh = vectors[..., rn : rn + width].reshape(11, PARTS_N * width)

time: 114 us -> 102 us (0.89)
  starting transfers between devices: 36.9 us -> 29 us
  Pallas kernels: 46.9 us -> 42.7 us
  other arithmetic: 2.31 us -> 0.07 us
  waiting for transfers between devices: 25.5 us -> 27.7 us
    ppermute x31 -> x27, starting transfers between devices: 36.9 us -> 29 us  [swap(): return lax.ppermute(value, ('wide', 'narrow'), pairs)]
    pallas_call x11 -> x12, Pallas kernels: 45.2 us -> 37.9 us  [call(): pl.pallas_call(kernel, out_shape=[jax.ShapeDtypeStruct(shape, kind) for s...]
    pallas_call x1 -> x2, Pallas kernels: 1.72 us -> 4.82 us  [the longest x1 3.09 us: prepare(): pl.pallas_call(prepare_kernel, out_shape=[jax.ShapeDtypeStruct(shape, kin...]
    concatenate x3 -> x2, other arithmetic: 2.31 us -> 0.07 us  [on_device(): jnp.concatenate([v[k:k + 1] for v in (packed, *line)], axis=0)]
    ppermute x31 -> x27, waiting for transfers between devices: 25.5 us -> 27.7 us  [swap(): return lax.ppermute(value, ('wide', 'narrow'), pairs)]
  transfers between devices with their start and end apart: 31 -> 27, of which waited for: 15 -> 15; matrix products, arithmetic and copies ran while one was open for 3% -> 1% of each run, Pallas kernels for 14% -> 18%
where the time goes in v3:
time: 102 us
  Pallas kernels  42.7 us (42%)
  starting transfers between devices  29 us (28%)
  waiting for transfers between devices  27.7 us (27%)
  local copies, waits for them, and re-layouts  1.2 us (1%)
    pallas_call x12, Pallas kernels, call(): pl.pallas_call(kernel, out_shape=[jax.ShapeDtypeStruct(shape, kind) for s...  37.9 us
    ppermute x27, starting transfers between devices, swap(): return lax.ppermute(value, ('wide', 'narrow'), pairs)  29 us
    ppermute x27, waiting for transfers between devices, swap(): return lax.ppermute(value, ('wide', 'narrow'), pairs)  27.7 us
    pallas_call x1, Pallas kernels, prepare(): pl.pallas_call(prepare_kernel, out_shape=[jax.ShapeDtypeStruct(shape, kin...  3.09 us
  transfers between devices with their start and end apart: 27, of which 15 were waited for; matrix products, arithmetic and copies ran while one was open for 1% of the time, Pallas kernels for 18%

profile of v3, /device:TPU:0, one launch (start us, length us, event | category | flops | bytes accessed | tf_op | source)
XLA Modules:
  0.0 101.7 jit_solution(14170570210750147685)
XLA Ops:
  0.6 1.7 %shard_map.196 = (bf16[2,40,640]{2,1,0:T(8,128)(2,1)}, bf16[1,16,640]{2,1,0:T(8,128)(2,1)}) custom-call(bf16[40,80]{1,0:T(8,128)(2,1)} %bitcast.15, bf16[80,80]{1,0:T(8,128)(2,1)} %refs_1_.1, bf16[40,320]{1,0:T(8,128)(2,1)} %bitcast.13, bf16[40,80]{1,0:T(8,128)(2,1)} %bitcast.16, bf16[80,160]{1,0:T(8,128)(2,1)} %refs_4_.1, bf16[40,320]{1,0:T(8,128)(2,1)} %bitcast.14, ...), custom_call_target="tpu_custom_call" | custom-call | tf_op jit(solution)/shard_map/pallas_call | solution.py:130
  2.4 5.1 %collective-permute-start.2 = (bf16[2,40,640]{2,1,0:T(8,128)(2,1)}, bf16[2,40,640]{2,1,0:T(8,128)(2,1)S(1)}, u32[]{:S(2)}, u32[]{:S(2)}) collective-permute-start(bf16[2,40,640]{2,1,0:T(8,128)(2,1)} %get-tuple-element.106), channel_id=1, source_target_pairs={{0,24},{1,25},{2,26},{3,27},{4,28},{5,29},{6,30},{7,31},{8,16},{9,... | collective-permute-start | bytes 307208 | tf_op jit(solution)/shard_map/ppermute | solution.py:745
  8.1 0.9 fusion
  9.0 3.1 %shard_map.195 = (f32[512,320]{1,0:T(8,128)}, f32[512,320]{1,0:T(8,128)}, f32[512,1]{1,0:T(8,128)}, bf16[512,512]{1,0:T(8,128)(2,1)}, f32[512,128]{1,0:T(8,128)}, /*index=5*/s32[4]{0:T(128)}) custom-call(s32[2]{0:T(128)} %rows_hbm.1, s32[2]{0:T(128)} %cols_hbm.1, bf16[320,512]{1,0:T(8,128)(2,1)} %bitcast.17), custom_call_target="tpu_custom_call" | custom-call | flops 2000000000 | tf_op jit(solution)/shard_map/pallas_call | solution.py:180
  12.1 4.2 %collective-permute-done.1 = bf16[2,40,640]{2,1,0:T(8,128)(2,1)S(1)} collective-permute-done((bf16[2,40,640]{2,1,0:T(8,128)(2,1)}, bf16[2,40,640]{2,1,0:T(8,128)(2,1)S(1)}, u32[]{:S(2)}, u32[]{:S(2)}) %collective-permute-start.1) | collective-permute-done | bytes 102432 | tf_op jit(solution)/shard_map/ppermute | solution.py:745
  16.5 1.6 %collective-permute-start.3 = (bf16[4,40,640]{2,1,0:T(8,128)(2,1)S(1)}, bf16[4,40,640]{2,1,0:T(8,128)(2,1)S(1)}, u32[]{:S(2)}, u32[]{:S(2)}) collective-permute-start(bf16[4,40,640]{2,1,0:T(8,128)(2,1)S(1)} %pad_maximum_fusion), channel_id=1, source_target_pairs={{0,2},{1,5},{2,0},{3,7},{4,6},{5,1},{6,4},{7,3},{8,10},{9,13},{10,... | collective-permute-start | bytes 614408 | tf_op jit(solution)/shard_map/ppermute | solution.py:745
  18.1 4.3 %collective-permute-done.3 = bf16[4,40,640]{2,1,0:T(8,128)(2,1)S(1)} collective-permute-done((bf16[4,40,640]{2,1,0:T(8,128)(2,1)S(1)}, bf16[4,40,640]{2,1,0:T(8,128)(2,1)S(1)}, u32[]{:S(2)}, u32[]{:S(2)}) %collective-permute-start.3) | collective-permute-done | bytes 204832 | tf_op jit(solution)/shard_map/ppermute | solution.py:745
  22.4 1.6 %collective-permute-start.4 = (bf16[8,40,640]{2,1,0:T(8,128)(2,1)S(1)}, bf16[8,40,640]{2,1,0:T(8,128)(2,1)S(1)}, u32[]{:S(2)}, u32[]{:S(2)}) collective-permute-start(bf16[8,40,640]{2,1,0:T(8,128)(2,1)S(1)} %get-tuple-element.192), channel_id=1, source_target_pairs={{0,4},{1,3},{2,6},{3,1},{4,0},{5,7},{6,2},{7,5},{8,12},{9,11},{10,... | collective-permute-start | bytes 1228808 | tf_op jit(solution)/shard_map/ppermute | solution.py:745
  24.0 1.6 %collective-permute-start.5 = (bf16[4,40,640]{2,1,0:T(8,128)(2,1)S(1)}, bf16[4,40,640]{2,1,0:T(8,128)(2,1)S(1)}, u32[]{:S(2)}, u32[]{:S(2)}) collective-permute-start(bf16[4,40,640]{2,1,0:T(8,128)(2,1)S(1)} %pad_maximum_fusion.1), channel_id=1, source_target_pairs={{0,2},{1,5},{2,0},{3,7},{4,6},{5,1},{6,4},{7,3},{8,10},{9,13},{10,... | collective-permute-start | bytes 614408 | tf_op jit(solution)/shard_map/ppermute | solution.py:745
  26.1 1.3 %collective-permute-start.6 = (bf16[1,16,640]{2,1,0:T(8,128)(2,1)S(1)}, bf16[1,16,640]{2,1,0:T(8,128)(2,1)S(1)}, u32[]{:S(2)}, u32[]{:S(2)}) collective-permute-start(bf16[1,16,640]{2,1,0:T(8,128)(2,1)S(1)} %copy-done.4), channel_id=1, source_target_pairs={{0,1},{1,0},{2,3},{3,2},{4,5},{5,4},{6,7},{7,6},{8,9},{9,8},{10,11... | collective-permute-start | bytes 61448 | tf_op jit(solution)/shard_map/ppermute | solution.py:745
  27.4 2.9 %collective-permute-done.5 = bf16[4,40,640]{2,1,0:T(8,128)(2,1)S(1)} collective-permute-done((bf16[4,40,640]{2,1,0:T(8,128)(2,1)S(1)}, bf16[4,40,640]{2,1,0:T(8,128)(2,1)S(1)}, u32[]{:S(2)}, u32[]{:S(2)}) %collective-permute-start.5) | collective-permute-done | bytes 204832 | tf_op jit(solution)/shard_map/ppermute | solution.py:745
  30.4 0.8 collective-permute-done.4
  31.4 1.6 %collective-permute-start.10 = (bf16[8,40,640]{2,1,0:T(8,128)(2,1)S(1)}, bf16[8,40,640]{2,1,0:T(8,128)(2,1)S(1)}, u32[]{:S(2)}, u32[]{:S(2)}) collective-permute-start(bf16[8,40,640]{2,1,0:T(8,128)(2,1)S(1)} %constant_dynamic-update-slice_fusion.11), channel_id=1, source_target_pairs={{0,4},{1,3},{2,6},{3,1},{4,0},{5,7},{6,2},{7,5},{8,12},{9,11},{10,... | collective-permute-start | bytes 1228808 | tf_op jit(solution)/shard_map/ppermute | solution.py:745
  33.8 5.1 %shard_map.197 = (f32[512,320]{1,0:T(8,128)S(1)}, bf16[512,320]{1,0:T(8,128)(2,1)S(1)}, bf16[512,320]{1,0:T(8,128)(2,1)S(1)}, f32[128,320]{1,0:T(8,128)S(1)}, f3...) custom-call(f32[512,320]{1,0:T(8,128)S(1)} %copy-done.5, ...), custom_call_target="tpu_custom_call" | custom-call | flops 8000000000 | tf_op jit(solution)/shard_map/pallas_call | solution.py:713
  39.6 1.6 %shard_map.198 = (f32[512,320]{1,0:T(8,128)S(1)}, f32[512,1]{1,0:T(8,128)S(1)}, bf16[512,320]{1,0:T(8,128)(2,1)S(1)}, bf16[320,512]{1,0:T(8,128)(2,1)S(1)}, bf16...) custom-call(s32[4]{0:T(128)S(1)} %copy-done.7, bf16[320,512]{1,0:T(8,128)(2,1)S(1)} %bitcast.12, ...), custom_call_target="tpu_custom_call" | custom-call | flops 2000000000 | tf_op jit(solution)/shard_map/pallas_call | solution.py:713
  41.9 21.8 %shard_map.199 = (bf16[16,40,640]{2,1,0:T(8,128)(2,1)S(1)}, bf16[16,40,640]{2,1,0:T(8,128)(2,1)S(1)}, f32[512,320]{1,0:T(8,128)S(1)}, f32[512,320]{1,0:T(8,128)S...) custom-call(s32[4]{0:T(128)S(1)} %copy-done.7, f32[512,320]{1,0:T(8,128)S(1)} %get-tuple-element.118.n2_ref, ...), custom_call_target="tpu_custom_call" | custom-call | flops 32999999488 | tf_op jit(solution)/shard_map/pallas_call | solution.py:713
  63.9 2.0 %shard_map.200 = (f32[320,320]{1,0:T(8,128)S(1)}, bf16[512,320]{1,0:T(8,128)(2,1)S(1)}, bf16[512,640]{1,0:T(8,128)(2,1)S(1)}, f32[1,320]{1,0:T(1,128)S(1)}) custom-call(f32[512,320]{1,0:T(8,128)S(1)} %get-tuple-element.128.dx2_ref, bf16[640,320]{1,0:T(8,128)(2,1)S(1)} %get-tuple-element.129.vb_ref, f32[512,640]{1,0:T(8,128)S(1)} %get-tuple-element.130.p_ref, ...), custom_call_target="tpu_custom_call" | custom-call | flops 2500000000 | tf_op jit(solution)/shard_map/pallas_call | solution.py:713
  66.3 1.3 %collective-permute-start.14 = (bf16[4,40,640]{2,1,0:T(8,128)(2,1)S(1)}, bf16[4,40,640]{2,1,0:T(8,128)(2,1)S(1)}, u32[]{:S(2)}, u32[]{:S(2)}) collective-permute-start(bf16[4,40,640]{2,1,0:T(8,128)(2,1)S(1)} %get-tuple-element.163), channel_id=1, source_target_pairs={{0,4},{1,5},{2,6},{3,7},{4,0},{5,1},{6,2},{7,3},{8,12},{9,13},{10,... | collective-permute-start | bytes 614408 | tf_op jit(solution)/shard_map/ppermute | solution.py:745
  68.3 1.5 %collective-permute-start.13 = (bf16[4,40,640]{2,1,0:T(8,128)(2,1)S(1)}, bf16[4,40,640]{2,1,0:T(8,128)(2,1)S(1)}, u32[]{:S(2)}, u32[]{:S(2)}) collective-permute-start(bf16[4,40,640]{2,1,0:T(8,128)(2,1)S(1)} %get-tuple-element.138), channel_id=1, source_target_pairs={{0,2},{1,3},{2,0},{3,1},{4,6},{5,7},{6,4},{7,5},{8,10},{9,11},{10,... | collective-permute-start | bytes 614408 | tf_op jit(solution)/shard_map/ppermute | solution.py:745
  69.9 2.7 %shard_map.202 = (bf16[16,40,640]{2,1,0:T(8,128)(2,1)S(1)}, bf16[16,40,640]{2,1,0:T(8,128)(2,1)S(1)}, bf16[512,320]{1,0:T(8,128)(2,1)S(1)}, f32[512,320]{1,0:T(8,128)S(1)}, f32[8,320]{1,0:T(8,128)S(1)}) custom-call(bf16[512,320]{1,0:T(8,128)(2,1)S(1)} %get-tuple-element.133.dob_ref, bf16[512,640]{1,0:T(8,128)(2,1)S(1)} %get-tuple-element.139.ds_ref, ...), custom_call_target="tpu_custom_call" | custom-call | tf_op jit(solution)/shard_map/pallas_call | solution.py:713
  72.6 2.3 %shard_map.203 = (bf16[320,512]{1,0:T(8,128)(2,1)}, bf16[320,512]{1,0:T(8,128)(2,1)}, bf16[2,16,640]{2,1,0:T(8,128)(2,1)S(1)}, bf16[2,16,640]{2,1,0:T(8,128)(2,1)S(1)}) custom-call(f32[512,320]{1,0:T(8,128)S(1)} %get-tuple-element.128.dx2_ref, bf16[512,320]{1,0:T(8,128)(2,1)S(1)} %get-tuple-element.150.dq_ref, f32[512,320]{1,0:T(8,128)S(1)} %get-tuple-element.151.dpatch_ref, ...), custom_call_target="tpu_custom_call" | custom-call | tf_op jit(solution)/shard_map/pallas_call | solution.py:713
  75.4 2.5 %collective-permute-done.14.c_ref = bf16[4,40,640]{2,1,0:T(8,128)(2,1)S(1)} collective-permute-done((bf16[4,40,640]{2,1,0:T(8,128)(2,1)S(1)}, bf16[4,40,640]{2,1,0:T(8,128)(2,1)S(1)}, u32[]{:S(2)}, u32[]{:S(2)}) %collective-permute-start.14) | collective-permute-done | bytes 204832 | tf_op jit(solution)/shard_map/ppermute | solution.py:745
  78.0 1.2 %collective-permute-done.13.b_ref = bf16[4,40,640]{2,1,0:T(8,128)(2,1)S(1)} collective-permute-done((bf16[4,40,640]{2,1,0:T(8,128)(2,1)S(1)}, bf16[4,40,640]{2,1,0:T(8,128)(2,1)S(1)}, u32[]{:S(2)}, u32[]{:S(2)}) %collective-permute-start.13) | collective-permute-done | bytes 204832 | tf_op jit(solution)/shard_map/ppermute | solution.py:745
  80.3 1.7 %collective-permute-start.19 = (bf16[176,640]{1,0:T(8,128)(2,1)S(1)}, bf16[176,640]{1,0:T(8,128)(2,1)S(1)}, u32[]{:S(2)}, u32[]{:S(2)}) collective-permute-start(bf16[176,640]{1,0:T(8,128)(2,1)S(1)} %get-tuple-element.172), channel_id=1, source_target_pairs={{0,4},{1,5},{2,6},{3,7},{4,0},{5,1},{6,2},{7,3},{8,12},{9,13},{10,... | collective-permute-start | bytes 675848 | tf_op jit(solution)/shard_map/ppermute | solution.py:745
  81.9 1.2 %collective-permute-start.20 = (bf16[176,640]{1,0:T(8,128)(2,1)S(1)}, bf16[176,640]{1,0:T(8,128)(2,1)S(1)}, u32[]{:S(2)}, u32[]{:S(2)}) collective-permute-start(bf16[176,640]{1,0:T(8,128)(2,1)S(1)} %get-tuple-element.173), channel_id=1, source_target_pairs={{0,6},{1,7},{2,4},{3,5},{4,2},{5,3},{6,0},{7,1},{8,14},{9,15},{10,... | collective-permute-start | bytes 675848 | tf_op jit(solution)/shard_map/ppermute | solution.py:745
  83.1 2.7 %collective-permute-start.23 = (bf16[1,40,640]{2,1,0:T(8,128)(2,1)S(1)}, bf16[1,40,640]{2,1,0:T(8,128)(2,1)S(1)}, u32[]{:S(2)}, u32[]{:S(2)}) collective-permute-start(bf16[1,40,640]{2,1,0:T(8,128)(2,1)S(1)} %get-tuple-element.175), channel_id=1, source_target_pairs={{0,24},{1,25},{2,26},{3,27},{4,28},{5,29},{6,30},{7,31},{8,16},{9,... | collective-permute-start | bytes 153608 | tf_op jit(solution)/shard_map/ppermute | solution.py:745
  85.8 2.7 %collective-permute-done.22.c_ref = bf16[1,40,640]{2,1,0:T(8,128)(2,1)S(1)} collective-permute-done((bf16[1,40,640]{2,1,0:T(8,128)(2,1)S(1)}, bf16[1,40,640]{2,1,0:T(8,128)(2,1)S(1)}, u32[]{:S(2)}, u32[]{:S(2)}) %collective-permute-start.22) | collective-permute-done | bytes 51232 | tf_op jit(solution)/shard_map/ppermute | solution.py:745
  89.2 3.4 %collective-permute-done.21.b_ref = bf16[1,40,640]{2,1,0:T(8,128)(2,1)S(1)} collective-permute-done((bf16[1,40,640]{2,1,0:T(8,128)(2,1)S(1)}, bf16[1,40,640]{2,1,0:T(8,128)(2,1)S(1)}, u32[]{:S(2)}, u32[]{:S(2)}) %collective-permute-start.21) | collective-permute-done | bytes 51232 | tf_op jit(solution)/shard_map/ppermute | solution.py:745
  92.8 1.9 %collective-permute-start.25 = (bf16[56,640]{1,0:T(8,128)(2,1)S(1)}, bf16[56,640]{1,0:T(8,128)(2,1)S(1)}, u32[]{:S(2)}, u32[]{:S(2)}) collective-permute-start(bf16[56,640]{1,0:T(8,128)(2,1)S(1)} %get-tuple-element.181), channel_id=1, source_target_pairs={{0,16},{1,17},{2,18},{3,19},{4,20},{5,21},{6,22},{7,23},{8,24},{9,... | collective-permute-start | bytes 215048 | tf_op jit(solution)/shard_map/ppermute | solution.py:745
  94.7 2.4 %collective-permute-start.26 = (bf16[56,640]{1,0:T(8,128)(2,1)S(1)}, bf16[56,640]{1,0:T(8,128)(2,1)S(1)}, u32[]{:S(2)}, u32[]{:S(2)}) collective-permute-start(bf16[56,640]{1,0:T(8,128)(2,1)S(1)} %get-tuple-element.182), channel_id=1, source_target_pairs={{0,24},{1,25},{2,26},{3,27},{4,28},{5,29},{6,30},{7,31},{8,16},{9,... | collective-permute-start | bytes 215048 | tf_op jit(solution)/shard_map/ppermute | solution.py:745
  98.6 2.2 %collective-permute-done.26.d_ref = bf16[56,640]{1,0:T(8,128)(2,1)S(1)} collective-permute-done((bf16[56,640]{1,0:T(8,128)(2,1)S(1)}, bf16[56,640]{1,0:T(8,128)(2,1)S(1)}, u32[]{:S(2)}, u32[]{:S(2)}) %collective-permute-start.26) | collective-permute-done | bytes 71712 | tf_op jit(solution)/shard_map/ppermute | solution.py:745
  100.8 0.9 shard_map.207
  (63 shorter events, 9.1 us)
Async XLA Ops:
  2.4 9.7 %collective-permute-start.2 = (bf16[2,40,640]{2,1,0:T(8,128)(2,1)}, bf16[2,40,640]{2,1,0:T(8,128)(2,1)S(1)}, u32[]{:S(2)}, u32[]{:S(2)}) collective-permute-start(bf16[2,40,640]{2,1,0:T(8,128)(2,1)} %get-tuple-element.106), channel_id=1, source_target_pairs={{0,24},{1,25},{2,26},{3,27},{4,28},{5,29},{6,30},{7,31},{8,16},{9,... | collective-permute-start | bytes 307208 | tf_op jit(solution)/shard_map/ppermute | solution.py:745
  7.5 8.8 %collective-permute-start.1 = (bf16[2,40,640]{2,1,0:T(8,128)(2,1)}, bf16[2,40,640]{2,1,0:T(8,128)(2,1)S(1)}, u32[]{:S(2)}, u32[]{:S(2)}) collective-permute-start(bf16[2,40,640]{2,1,0:T(8,128)(2,1)} %get-tuple-element.106), channel_id=1, source_target_pairs={{0,16},{1,17},{2,18},{3,19},{4,20},{5,21},{6,22},{7,23},{8,24},{9,... | collective-permute-start | bytes 307208 | tf_op jit(solution)/shard_map/ppermute | solution.py:745
  7.5 8.8 %collective-permute-start = (bf16[2,40,640]{2,1,0:T(8,128)(2,1)}, bf16[2,40,640]{2,1,0:T(8,128)(2,1)S(1)}, u32[]{:S(2)}, u32[]{:S(2)}) collective-permute-start(bf16[2,40,640]{2,1,0:T(8,128)(2,1)} %get-tuple-element.106), channel_id=1, source_target_pairs={{0,8},{1,9},{2,10},{3,11},{4,12},{5,13},{6,14},{7,15},{8,0},{9,1},... | collective-permute-start | bytes 307208 | tf_op jit(solution)/shard_map/ppermute | solution.py:745
  12.1 13.5 %copy-start.4 = (bf16[1,16,640]{2,1,0:T(8,128)(2,1)S(1)}, bf16[1,16,640]{2,1,0:T(8,128)(2,1)}, u32[]{:S(2)}) copy-start(bf16[1,16,640]{2,1,0:T(8,128)(2,1)} %get-tuple-element.112.v0_ref) | copy-start | bytes 61444
  16.4 17.3 %copy-start = (f32[512,320]{1,0:T(8,128)S(1)}, f32[512,320]{1,0:T(8,128)}, u32[]{:S(2)}) copy-start(f32[512,320]{1,0:T(8,128)} %get-tuple-element.103.n1_ref) | copy-start | bytes 1966084
  16.4 17.3 %copy-start.1 = (bf16[512,512]{1,0:T(8,128)(2,1)S(1)}, bf16[512,512]{1,0:T(8,128)(2,1)}, u32[]{:S(2)}) copy-start(bf16[512,512]{1,0:T(8,128)(2,1)} %get-tuple-element.104.chosen_ref) | copy-start | bytes 1572868
  16.4 17.3 %copy-start.5 = (f32[512,320]{1,0:T(8,128)S(1)}, f32[512,320]{1,0:T(8,128)}, u32[]{:S(2)}) copy-start(f32[512,320]{1,0:T(8,128)} %get-tuple-element.102.x_ref) | copy-start | bytes 1966084
  16.5 17.3 %copy-start.6 = (f32[512,128]{1,0:T(8,128)S(1)}, f32[512,128]{1,0:T(8,128)}, u32[]{:S(2)}) copy-start(f32[512,128]{1,0:T(8,128)} %get-tuple-element.105.live_ref) | copy-start | bytes 786436
  16.5 5.8 %collective-permute-start.3 = (bf16[4,40,640]{2,1,0:T(8,128)(2,1)S(1)}, bf16[4,40,640]{2,1,0:T(8,128)(2,1)S(1)}, u32[]{:S(2)}, u32[]{:S(2)}) collective-permute-start(bf16[4,40,640]{2,1,0:T(8,128)(2,1)S(1)} %pad_maximum_fusion), channel_id=1, source_target_pairs={{0,2},{1,5},{2,0},{3,7},{4,6},{5,1},{6,4},{7,3},{8,10},{9,13},{10,... | collective-permute-start | bytes 614408 | tf_op jit(solution)/shard_map/ppermute | solution.py:745
  22.4 8.9 %collective-permute-start.4 = (bf16[8,40,640]{2,1,0:T(8,128)(2,1)S(1)}, bf16[8,40,640]{2,1,0:T(8,128)(2,1)S(1)}, u32[]{:S(2)}, u32[]{:S(2)}) collective-permute-start(bf16[8,40,640]{2,1,0:T(8,128)(2,1)S(1)} %get-tuple-element.192), channel_id=1, source_target_pairs={{0,4},{1,3},{2,6},{3,1},{4,0},{5,7},{6,2},{7,5},{8,12},{9,11},{10,... | collective-permute-start | bytes 1228808 | tf_op jit(solution)/shard_map/ppermute | solution.py:745
  24.0 6.4 %collective-permute-start.5 = (bf16[4,40,640]{2,1,0:T(8,128)(2,1)S(1)}, bf16[4,40,640]{2,1,0:T(8,128)(2,1)S(1)}, u32[]{:S(2)}, u32[]{:S(2)}) collective-permute-start(bf16[4,40,640]{2,1,0:T(8,128)(2,1)S(1)} %pad_maximum_fusion.1), channel_id=1, source_target_pairs={{0,2},{1,5},{2,0},{3,7},{4,6},{5,1},{6,4},{7,3},{8,10},{9,13},{10,... | collective-permute-start | bytes 614408 | tf_op jit(solution)/shard_map/ppermute | solution.py:745
  25.6 5.7 %collective-permute-start.8 = (bf16[1,16,640]{2,1,0:T(8,128)(2,1)S(1)}, bf16[1,16,640]{2,1,0:T(8,128)(2,1)S(1)}, u32[]{:S(2)}, u32[]{:S(2)}) collective-permute-start(bf16[1,16,640]{2,1,0:T(8,128)(2,1)S(1)} %copy-done.4), channel_id=1, source_target_pairs={{0,3},{1,2},{2,1},{3,0},{4,7},{5,6},{6,5},{7,4},{8,11},{9,10},{10,... | collective-permute-start | bytes 61448 | tf_op jit(solution)/shard_map/ppermute | solution.py:745
  25.6 5.7 %collective-permute-start.7 = (bf16[1,16,640]{2,1,0:T(8,128)(2,1)S(1)}, bf16[1,16,640]{2,1,0:T(8,128)(2,1)S(1)}, u32[]{:S(2)}, u32[]{:S(2)}) collective-permute-start(bf16[1,16,640]{2,1,0:T(8,128)(2,1)S(1)} %copy-done.4), channel_id=1, source_target_pairs={{0,2},{1,3},{2,0},{3,1},{4,6},{5,7},{6,4},{7,5},{8,10},{9,11},{10,... | collective-permute-start | bytes 61448 | tf_op jit(solution)/shard_map/ppermute | solution.py:745
  26.1 5.2 %collective-permute-start.6 = (bf16[1,16,640]{2,1,0:T(8,128)(2,1)S(1)}, bf16[1,16,640]{2,1,0:T(8,128)(2,1)S(1)}, u32[]{:S(2)}, u32[]{:S(2)}) collective-permute-start(bf16[1,16,640]{2,1,0:T(8,128)(2,1)S(1)} %copy-done.4), channel_id=1, source_target_pairs={{0,1},{1,0},{2,3},{3,2},{4,5},{5,4},{6,7},{7,6},{8,9},{9,8},{10,11... | collective-permute-start | bytes 61448 | tf_op jit(solution)/shard_map/ppermute | solution.py:745
  31.3 2.4 %collective-permute-start.9 = (bf16[16,40,640]{2,1,0:T(8,128)(2,1)S(1)}, bf16[16,40,640]{2,1,0:T(8,128)(2,1)S(1)}, u32[]{:S(2)}, u32[]{:S(2)}) collective-permute-start(bf16[16,40,640]{2,1,0:T(8,128)(2,1)S(1)} %constant_dynamic-update-slice_fusion.5.own_ref), channel_id=1, source_target_pairs={{0,1},{1,0},{2,3},{3,2},{4,5},{5,4},{6,7},{7,6},{8,9},{9,8},{10,11... | collective-permute-start | bytes 2457608 | tf_op jit(solution)/shard_map/ppermute | solution.py:745
  31.4 8.0 %collective-permute-start.10 = (bf16[8,40,640]{2,1,0:T(8,128)(2,1)S(1)}, bf16[8,40,640]{2,1,0:T(8,128)(2,1)S(1)}, u32[]{:S(2)}, u32[]{:S(2)}) collective-permute-start(bf16[8,40,640]{2,1,0:T(8,128)(2,1)S(1)} %constant_dynamic-update-slice_fusion.11), channel_id=1, source_target_pairs={{0,4},{1,3},{2,6},{3,1},{4,0},{5,7},{6,2},{7,5},{8,12},{9,11},{10,... | collective-permute-start | bytes 1228808 | tf_op jit(solution)/shard_map/ppermute | solution.py:745
  39.5 2.4 %collective-permute-start.11 = (bf16[16,40,640]{2,1,0:T(8,128)(2,1)S(1)}, bf16[16,40,640]{2,1,0:T(8,128)(2,1)S(1)}, u32[]{:S(2)}, u32[]{:S(2)}) collective-permute-start(bf16[16,40,640]{2,1,0:T(8,128)(2,1)S(1)} %constant_dynamic-update-slice_fusion.16.own_ref), channel_id=1, source_target_pairs={{0,1},{1,0},{2,3},{3,2},{4,5},{5,4},{6,7},{7,6},{8,9},{9,8},{10,11... | collective-permute-start | bytes 2457608 | tf_op jit(solution)/shard_map/ppermute | solution.py:745
  63.7 2.4 %collective-permute-start.12 = (bf16[16,40,640]{2,1,0:T(8,128)(2,1)S(1)}, bf16[16,40,640]{2,1,0:T(8,128)(2,1)S(1)}, u32[]{:S(2)}, u32[]{:S(2)}) collective-permute-start(bf16[16,40,640]{2,1,0:T(8,128)(2,1)S(1)} %get-tuple-element.136), channel_id=1, source_target_pairs={{0,1},{1,0},{2,3},{3,2},{4,5},{5,4},{6,7},{7,6},{8,9},{9,8},{10,11... | collective-permute-start | bytes 2457608 | tf_op jit(solution)/shard_map/ppermute | solution.py:745
  66.3 11.7 %collective-permute-start.14 = (bf16[4,40,640]{2,1,0:T(8,128)(2,1)S(1)}, bf16[4,40,640]{2,1,0:T(8,128)(2,1)S(1)}, u32[]{:S(2)}, u32[]{:S(2)}) collective-permute-start(bf16[4,40,640]{2,1,0:T(8,128)(2,1)S(1)} %get-tuple-element.163), channel_id=1, source_target_pairs={{0,4},{1,5},{2,6},{3,7},{4,0},{5,1},{6,2},{7,3},{8,12},{9,13},{10,... | collective-permute-start | bytes 614408 | tf_op jit(solution)/shard_map/ppermute | solution.py:745
  67.6 10.4 %collective-permute-start.15 = (bf16[4,40,640]{2,1,0:T(8,128)(2,1)S(1)}, bf16[4,40,640]{2,1,0:T(8,128)(2,1)S(1)}, u32[]{:S(2)}, u32[]{:S(2)}) collective-permute-start(bf16[4,40,640]{2,1,0:T(8,128)(2,1)S(1)} %get-tuple-element.164), channel_id=1, source_target_pairs={{0,6},{1,7},{2,4},{3,5},{4,2},{5,3},{6,0},{7,1},{8,14},{9,15},{10,... | collective-permute-start | bytes 614408 | tf_op jit(solution)/shard_map/ppermute | solution.py:745
  68.3 10.9 %collective-permute-start.13 = (bf16[4,40,640]{2,1,0:T(8,128)(2,1)S(1)}, bf16[4,40,640]{2,1,0:T(8,128)(2,1)S(1)}, u32[]{:S(2)}, u32[]{:S(2)}) collective-permute-start(bf16[4,40,640]{2,1,0:T(8,128)(2,1)S(1)} %get-tuple-element.138), channel_id=1, source_target_pairs={{0,2},{1,3},{2,0},{3,1},{4,6},{5,7},{6,4},{7,5},{8,10},{9,11},{10,... | collective-permute-start | bytes 614408 | tf_op jit(solution)/shard_map/ppermute | solution.py:745
  74.9 4.4 %collective-permute-start.17 = (bf16[2,16,640]{2,1,0:T(8,128)(2,1)S(1)}, bf16[2,16,640]{2,1,0:T(8,128)(2,1)S(1)}, u32[]{:S(2)}, u32[]{:S(2)}) collective-permute-start(bf16[2,16,640]{2,1,0:T(8,128)(2,1)S(1)} %get-tuple-element.169), channel_id=1, source_target_pairs={{0,1},{1,0},{2,3},{3,2},{4,5},{5,4},{6,7},{7,6},{8,9},{9,8},{10,11... | collective-permute-start | bytes 122888 | tf_op jit(solution)/shard_map/ppermute | solution.py:745
  74.9 4.4 %collective-permute-start.16 = (bf16[16,40,640]{2,1,0:T(8,128)(2,1)S(1)}, bf16[16,40,640]{2,1,0:T(8,128)(2,1)S(1)}, u32[]{:S(2)}, u32[]{:S(2)}) collective-permute-start(bf16[16,40,640]{2,1,0:T(8,128)(2,1)S(1)} %get-tuple-element.167), channel_id=1, source_target_pairs={{0,1},{1,0},{2,3},{3,2},{4,5},{5,4},{6,7},{7,6},{8,9},{9,8},{10,11... | collective-permute-start | bytes 2457608 | tf_op jit(solution)/shard_map/ppermute | solution.py:745
  79.5 13.0 %collective-permute-start.18 = (bf16[176,640]{1,0:T(8,128)(2,1)S(1)}, bf16[176,640]{1,0:T(8,128)(2,1)S(1)}, u32[]{:S(2)}, u32[]{:S(2)}) collective-permute-start(bf16[176,640]{1,0:T(8,128)(2,1)S(1)} %get-tuple-element.171), channel_id=1, source_target_pairs={{0,2},{1,3},{2,0},{3,1},{4,6},{5,7},{6,4},{7,5},{8,10},{9,11},{10,... | collective-permute-start | bytes 675848 | tf_op jit(solution)/shard_map/ppermute | solution.py:745
  80.3 12.3 %collective-permute-start.19 = (bf16[176,640]{1,0:T(8,128)(2,1)S(1)}, bf16[176,640]{1,0:T(8,128)(2,1)S(1)}, u32[]{:S(2)}, u32[]{:S(2)}) collective-permute-start(bf16[176,640]{1,0:T(8,128)(2,1)S(1)} %get-tuple-element.172), channel_id=1, source_target_pairs={{0,4},{1,5},{2,6},{3,7},{4,0},{5,1},{6,2},{7,3},{8,12},{9,13},{10,... | collective-permute-start | bytes 675848 | tf_op jit(solution)/shard_map/ppermute | solution.py:745
  81.9 10.6 %collective-permute-start.20 = (bf16[176,640]{1,0:T(8,128)(2,1)S(1)}, bf16[176,640]{1,0:T(8,128)(2,1)S(1)}, u32[]{:S(2)}, u32[]{:S(2)}) collective-permute-start(bf16[176,640]{1,0:T(8,128)(2,1)S(1)} %get-tuple-element.173), channel_id=1, source_target_pairs={{0,6},{1,7},{2,4},{3,5},{4,2},{5,3},{6,0},{7,1},{8,14},{9,15},{10,... | collective-permute-start | bytes 675848 | tf_op jit(solution)/shard_map/ppermute | solution.py:745
  83.1 5.3 %collective-permute-start.22 = (bf16[1,40,640]{2,1,0:T(8,128)(2,1)S(1)}, bf16[1,40,640]{2,1,0:T(8,128)(2,1)S(1)}, u32[]{:S(2)}, u32[]{:S(2)}) collective-permute-start(bf16[1,40,640]{2,1,0:T(8,128)(2,1)S(1)} %get-tuple-element.174), channel_id=1, source_target_pairs={{0,16},{1,17},{2,18},{3,19},{4,20},{5,21},{6,22},{7,23},{8,24},{9,... | collective-permute-start | bytes 153608 | tf_op jit(solution)/shard_map/ppermute | solution.py:745
  83.1 6.1 %collective-permute-start.23 = (bf16[1,40,640]{2,1,0:T(8,128)(2,1)S(1)}, bf16[1,40,640]{2,1,0:T(8,128)(2,1)S(1)}, u32[]{:S(2)}, u32[]{:S(2)}) collective-permute-start(bf16[1,40,640]{2,1,0:T(8,128)(2,1)S(1)} %get-tuple-element.175), channel_id=1, source_target_pairs={{0,24},{1,25},{2,26},{3,27},{4,28},{5,29},{6,30},{7,31},{8,16},{9,... | collective-permute-start | bytes 153608 | tf_op jit(solution)/shard_map/ppermute | solution.py:745
  88.4 4.1 %collective-permute-start.21 = (bf16[1,40,640]{2,1,0:T(8,128)(2,1)S(1)}, bf16[1,40,640]{2,1,0:T(8,128)(2,1)S(1)}, u32[]{:S(2)}, u32[]{:S(2)}) collective-permute-start(bf16[1,40,640]{2,1,0:T(8,128)(2,1)S(1)} %get-tuple-element.165), channel_id=1, source_target_pairs={{0,8},{1,9},{2,10},{3,11},{4,12},{5,13},{6,14},{7,15},{8,0},{9,1},... | collective-permute-start | bytes 153608 | tf_op jit(solution)/shard_map/ppermute | solution.py:745
  92.7 5.9 %collective-permute-start.24 = (bf16[56,640]{1,0:T(8,128)(2,1)S(1)}, bf16[56,640]{1,0:T(8,128)(2,1)S(1)}, u32[]{:S(2)}, u32[]{:S(2)}) collective-permute-start(bf16[56,640]{1,0:T(8,128)(2,1)S(1)} %get-tuple-element.180), channel_id=1, source_target_pairs={{0,8},{1,9},{2,10},{3,11},{4,12},{5,13},{6,14},{7,15},{8,0},{9,1},... | collective-permute-start | bytes 215048 | tf_op jit(solution)/shard_map/ppermute | solution.py:745
  92.8 5.8 %collective-permute-start.25 = (bf16[56,640]{1,0:T(8,128)(2,1)S(1)}, bf16[56,640]{1,0:T(8,128)(2,1)S(1)}, u32[]{:S(2)}, u32[]{:S(2)}) collective-permute-start(bf16[56,640]{1,0:T(8,128)(2,1)S(1)} %get-tuple-element.181), channel_id=1, source_target_pairs={{0,16},{1,17},{2,18},{3,19},{4,20},{5,21},{6,22},{7,23},{8,24},{9,... | collective-permute-start | bytes 215048 | tf_op jit(solution)/shard_map/ppermute | solution.py:745
  94.7 6.1 %collective-permute-start.26 = (bf16[56,640]{1,0:T(8,128)(2,1)S(1)}, bf16[56,640]{1,0:T(8,128)(2,1)S(1)}, u32[]{:S(2)}, u32[]{:S(2)}) collective-permute-start(bf16[56,640]{1,0:T(8,128)(2,1)S(1)} %get-tuple-element.182), channel_id=1, source_target_pairs={{0,24},{1,25},{2,26},{3,27},{4,28},{5,29},{6,30},{7,31},{8,16},{9,... | collective-permute-start | bytes 215048 | tf_op jit(solution)/shard_map/ppermute | solution.py:745
  (3 other events, 14.4 us)

commit v4 on v3

--- a/solution.py
+++ b/solution.py
@@ -20,7 +20,7 @@
 TILE = 32
 CHUNK = 256
 PAD = 40
-UNROLL = 4
+MROWS = 512
 RUN = 160
 REST = RUN - 128
 
@@ -49,11 +49,6 @@
     if not tuned:
         return jnp.int32(0)
     return lax.axis_index("wide") * PARTS_N + lax.axis_index("narrow")
-
-
-def slot_of(device, me):
-    delta = device ^ me
-    return ((delta >> 1) & 3) * 4 + (delta >> 3)
 
 
 def round_slot(device, me):
@@ -64,6 +59,15 @@
     return second * 8 + first * 4 + (delta >> 3)
 
 
+def mixed_slot(device, me):
+    delta = device ^ me
+    plane = [(delta >> 1) & 1, (delta >> 2) & 1]
+    line = [(delta >> 4) & 1, (delta >> 3) & 1]
+    if device & 1:
+        plane = plane[::-1]
+    return plane[1] * 8 + line[1] * 4 + line[0] * 2 + plane[0]
+
+
 def normalise(values):
     centre = values - jnp.mean(values, axis=-1, keepdims=True)
     inverse = lax.rsqrt(jnp.mean(centre * centre, axis=-1, keepdims=True) + EPSILON)
@@ -81,8 +85,8 @@
     return jnp.sum(values, axis=0, keepdims=True)
 
 
-def piece_of(own_ref, other_ref, device, me, first=0, last=5):
-    slot = round_slot(device, me)
+def piece_of(own_ref, other_ref, device, me, first=0, last=5, order=round_slot):
+    slot = order(device, me)
     mine = ((device ^ me) & 1) == 0
     at = pl.ds(128 * first, 128 * (last - first))
     return jnp.where(mine, own_ref[slot, :, at].astype(F32), other_ref[slot, :, at].astype(F32))
@@ -103,7 +107,7 @@
 
 
 def pack_kernel(*refs):
-    sources, (ab_ref, v_ref), held, semaphores = refs[:8], refs[8:10], refs[10:18], refs[18]
+    sources, (a_ref, b_ref, v_ref), held, semaphores = refs[:8], refs[8:11], refs[11:19], refs[19]
     copies = [pltpu.make_async_copy(source, ref, semaphores.at[i]) for i, (source, ref) in enumerate(zip(sources, held))]
     for copy in copies:
         copy.start()
@@ -116,10 +120,10 @@
         return ref[...].astype(F32)
 
     kv = wider(kv_ref).T
-    ab_ref[0] = lanes(wider(red_ref), wider(q_ref), kv[:cw], kv[cw:], wider(proj_ref)).astype(BF16)
+    a_ref[0] = lanes(wider(red_ref), wider(q_ref), kv[:cw], kv[cw:], wider(proj_ref)).astype(BF16)
     up, down = wider(up_ref), wider(down_ref)
     columns = (down[:, :RUN], down[:, RUN:], up[:cw], up[cw:])
-    ab_ref[1] = lanes(*[c[:, :128] for c in columns], *[c[:, 128:] for c in columns]).astype(BF16)
+    b_ref[0] = lanes(*[c[:, :128] for c in columns], *[c[:, 128:] for c in columns]).astype(BF16)
     v_ref[0] = jnp.zeros_like(v_ref[0])
     both = lanes(wider(vm_ref), wider(vh_ref))
     v_ref[0, : both.shape[0], : both.shape[1]] = both.astype(BF16)
@@ -129,9 +133,9 @@
     vmem = pl.BlockSpec(memory_space=pltpu.VMEM)
     return pl.pallas_call(
         pack_kernel,
-        out_shape=[jax.ShapeDtypeStruct(shape, BF16) for shape in ((2,) + piece, (1,) + vpiece)],
+        out_shape=[jax.ShapeDtypeStruct((1,) + shape, BF16) for shape in (piece, piece, vpiece)],
         in_specs=[pl.BlockSpec(memory_space=pl.ANY)] * len(arguments),
-        out_specs=[vmem] * 2,
+        out_specs=[vmem] * 3,
         scratch_shapes=[pltpu.VMEM(v.shape, v.dtype) for v in arguments] + [pltpu.SemaphoreType.DMA((len(arguments),))],
         compiler_params=pltpu.CompilerParams(vmem_limit_bytes=60 * 2**20),
     )(*arguments)
@@ -193,7 +197,7 @@
 
 def attend_kernel(
     tuned,
-    x_ref, n1_ref, chosen_ref, live_ref, own_ref, oth_ref, v0_ref, v1_ref, v2_ref, v3_ref,
+    x_ref, n1_ref, chosen_ref, live_ref, own_ref, oth_ref, vec_ref,
     x2_ref, h1_ref, patch_ref, nk_ref, rk_ref, kn_ref, q_ref, kb_ref, vb_ref,
     p_ref, o_ref, wr_ref, wq_ref, wkv_ref, wp_ref, mv_ref, hv_ref,
     score_ref,
@@ -204,11 +208,7 @@
     keys = capacity // 4
     dim = width // HEADS
 
-    held = [ref[0].astype(F32) for ref in (v0_ref, v1_ref, v2_ref, v3_ref)]
-    odd = (me & 1) == 1
-    held = [jnp.where(odd, held[k ^ 1], held[k]) for k in range(4)]
-    odd = (me & 2) == 2
-    pieces = [jnp.where(odd, held[k ^ 2], held[k]) for k in range(4)]
+    pieces = [vec_ref[n ^ (me & 3)].astype(F32) for n in range(PARTS_N)]
     mv = lanes(*[p[:, :rn] for p in pieces])
     mv_ref[...] = mv
     runs = [p[:, rn + e * RUN : rn + (e + 1) * RUN] for p in pieces for e in range(2)]
@@ -344,7 +344,7 @@
     for pair in range(PARTS_W // 2):
         at = pl.ds(pair * 2 * cw, 2 * cw)
         got = [
-            rows_of(*[piece_of(own_ref, oth_ref, w * PARTS_N + n, me, 0, 5) for w in (2 * pair, 2 * pair + 1)])
+            rows_of(*[piece_of(own_ref, oth_ref, w * PARTS_N + n, me, 0, 5, mixed_slot) for w in (2 * pair, 2 * pair + 1)])
             for n in range(PARTS_N)
         ]
         for n in range(PARTS_N):
@@ -354,7 +354,7 @@
         at = pl.ds(n * rn, rn)
         ends = []
         for w in range(PARTS_W):
-            got = piece_of(own_ref, oth_ref, w * PARTS_N + n, me, 2, 5)
+            got = piece_of(own_ref, oth_ref, w * PARTS_N + n, me, 2, 5, mixed_slot)
             wu_ref[at, pl.ds(128 * w, 128)] = rows_of(got[:, :128], got[:, 128:256]).astype(BF16)
             ends.append(rows_of(got[:, 256 + 2 * REST : 256 + 3 * REST], got[:, 256 + 3 * REST :]))
         wu_ref[at, pl.ds(tails, REST * PARTS_W)] = lanes(*ends).astype(BF16)
@@ -372,19 +372,53 @@
         return jnp.sum(values.reshape(TILE // 8, 8, 128), axis=0)
 
     halves = CHUNK // 128
+    chunks = hidden // CHUNK
+    zero = jnp.zeros((8, 128), F32)
+
+    def columns(c):
+        return pl.ds(pl.multiple_of(c * CHUNK, CHUNK), CHUNK)
+
+    def vector(c, k, j):
+        return hv_ref[k : k + 1, pl.ds(pl.multiple_of(c * CHUNK + j * 128, 128), 128)]
+
+    def put_vector(c, k, j, value):
+        hg_ref[k : k + 1, pl.ds(pl.multiple_of(c * CHUNK + j * 128, 128), 128)] = value
+
+    def first_layer(c, at):
+        value = dot_nn(h2_ref[at, :], wu_ref[:, columns(c)])
+        for j in range(halves):
+            f_ref[j, pl.ds(PAD + at.start, at.size), :] = value[:, j * 128 : (j + 1) * 128] + vector(c, 0, j)
+
+    def act_grad(c, at):
+        da_ref[at, :] = dot_nn(gy_ref[at, :], wd_ref[:, columns(c)])
+
+    def second_layer(c, at):
+        mix_ref[at, :] += dot_nt(act_ref[at, :], wd_ref[:, columns(c)])
+
+    def down_grad(c, at):
+        dng_ref[at, columns(c)] = dot_nn(gyt_ref[at, :], act_ref[...])
+
+    def up_grad(c, at):
+        upg_ref[at, columns(c)] = dot_nn(h2t_ref[at, :], df_ref[...])
+
+    def h2_grad(c, at):
+        dh2_ref[at, :] += dot_nt(df_ref[at, :], wu_ref[:, columns(c)])
+
+    def tasks(product, c, rows, size):
+        return [functools.partial(product, c, pl.ds(r, min(size, rows - r))) for r in range(0, rows, size)]
+
+    def interleave(steps, products):
+        done = 0
+        for i, step in enumerate(steps):
+            step()
+            while done < len(products) and done * len(steps) < (i + 1) * len(products):
+                products[done]()
+                done += 1
 
     def chunk_step(c, carry):
-        at_c = pl.ds(pl.multiple_of(c * CHUNK, CHUNK), CHUNK)
-
-        def vector(k, j):
-            return hv_ref[k : k + 1, pl.ds(pl.multiple_of(c * CHUNK + j * 128, 128), 128)]
-
-        def put_vector(k, j, value):
-            hg_ref[k : k + 1, pl.ds(pl.multiple_of(c * CHUNK + j * 128, 128), 128)] = value
-
-        first_layer = dot_nn(h2_ref[...], wu_ref[:, at_c])
-        for j in range(halves):
-            f_ref[j, pl.ds(PAD, capacity), :] = first_layer[:, j * 128 : (j + 1) * 128] + vector(0, j)
+        before = jnp.maximum(c - 1, 0)
+        following = jnp.minimum(c + 1, chunks - 1)
+        v = [[vector(c, k, j) for k in range(11)] for j in range(halves)]
 
         def taps_of(j, r, at):
             here = f_ref[j, pl.ds(PAD + r, TILE), :]
@@ -392,107 +426,94 @@
             right = f_ref[j, pl.ds(PAD + r + 1, TILE), :] * mask_ref[1, at, :]
             return left, here, right
 
-        def column_taps(i, carry):
-            r = pl.multiple_of(i * TILE, TILE)
+        def column_taps(r, j):
             at = pl.ds(r, TILE)
-            for j in range(halves):
-                left, here, right = taps_of(j, r, at)
-                v = [vector(k, j) for k in range(11)]
-                gm_ref[j, pl.ds(PAD + r, TILE), :] = v[2] * left + v[3] * here + v[4] * right
-                g0_ref[j, at, :] = v[1] + v[5] * left + v[6] * here + v[7] * right
-                gp_ref[j, pl.ds(PAD + r, TILE), :] = v[8] * left + v[9] * here + v[10] * right
-            return carry
-
-        lax.fori_loop(0, tiles, column_taps, 0, unroll=UNROLL)
-
-        def activate(i, carry):
-            r = pl.multiple_of(i * TILE, TILE)
+            left, here, right = taps_of(j, r, at)
+            u = v[j]
+            gm_ref[j, pl.ds(PAD + r, TILE), :] = u[2] * left + u[3] * here + u[4] * right
+            g0_ref[j, at, :] = u[1] + u[5] * left + u[6] * here + u[7] * right
+            gp_ref[j, pl.ds(PAD + r, TILE), :] = u[8] * left + u[9] * here + u[10] * right
+
+        def activate(r, j):
             at = pl.ds(r, TILE)
-            for j in range(halves):
-                conv = (
-                    g0_ref[j, at, :]
-                    + mask_ref[2, at, :] * gm_ref[j, pl.ds(PAD + r - w0, TILE), :]
-                    + mask_ref[3, at, :] * gm_ref[j, pl.ds(PAD + r - w1, TILE), :]
-                    + mask_ref[4, at, :] * gp_ref[j, pl.ds(PAD + r + w0, TILE), :]
-                    + mask_ref[5, at, :] * gp_ref[j, pl.ds(PAD + r + w1, TILE), :]
-                )
-                half = 0.5 * (1.0 + lax.erf(conv * 2.0 ** (-0.5)))
-                lane_at = pl.ds(j * 128, 128)
-                act_ref[at, lane_at] = (conv * half).astype(BF16)
-                slope = half + conv * jnp.exp(-0.5 * conv * conv) * (2.0 * math.pi) ** (-0.5)
-                slope_ref[at, lane_at] = slope
-            return carry
-
-        lax.fori_loop(0, tiles, activate, 0, unroll=UNROLL)
-        act = act_ref[...]
-        mix_ref[...] += dot_nt(act, wd_ref[:, at_c])
-        dng_ref[:, at_c] = dot_nn(gyt_ref[...], act)
-        da_ref[...] = dot_nn(gy_ref[...], wd_ref[:, at_c])
-
-        def into_conv(i, carry):
-            r = pl.multiple_of(i * TILE, TILE)
+            conv = (
+                g0_ref[j, at, :]
+                + mask_ref[2, at, :] * gm_ref[j, pl.ds(PAD + r - w0, TILE), :]
+                + mask_ref[3, at, :] * gm_ref[j, pl.ds(PAD + r - w1, TILE), :]
+                + mask_ref[4, at, :] * gp_ref[j, pl.ds(PAD + r + w0, TILE), :]
+                + mask_ref[5, at, :] * gp_ref[j, pl.ds(PAD + r + w1, TILE), :]
+            )
+            half = 0.5 * (1.0 + lax.erf(conv * 2.0 ** (-0.5)))
+            lane_at = pl.ds(j * 128, 128)
+            act_ref[at, lane_at] = (conv * half).astype(BF16)
+            slope_ref[at, lane_at] = half + conv * jnp.exp(-0.5 * conv * conv) * (2.0 * math.pi) ** (-0.5)
+
+        conv_sums = [zero] * halves
+
+        def into_conv(r, j):
+            at, lane_at = pl.ds(r, TILE), pl.ds(j * 128, 128)
+            value = da_ref[at, lane_at] * slope_ref[at, lane_at]
+            dc_ref[j, pl.ds(PAD + r, TILE), :] = value
+            conv_sums[j] = conv_sums[j] + fold(value)
+
+        tap_sums = [[zero] * 9 for _ in range(halves)]
+
+        def tap_back(r, j):
             at = pl.ds(r, TILE)
-            totals = []
-            for j in range(halves):
-                value = da_ref[at, pl.ds(j * 128, 128)] * slope_ref[at, pl.ds(j * 128, 128)]
-                dc_ref[j, pl.ds(PAD + r, TILE), :] = value
-                totals.append(carry[j] + fold(value))
-            return tuple(totals)
-
-        zero = jnp.zeros((8, 128), F32)
-        totals = lax.fori_loop(0, tiles, into_conv, (zero,) * halves, unroll=UNROLL)
+            left, here, right = taps_of(j, r, at)
+            u = v[j]
+            below = (
+                mask_ref[4, at, :] * dc_ref[j, pl.ds(PAD + r + w0, TILE), :]
+                + mask_ref[5, at, :] * dc_ref[j, pl.ds(PAD + r + w1, TILE), :]
+            )
+            level = dc_ref[j, pl.ds(PAD + r, TILE), :]
+            above = (
+                mask_ref[2, at, :] * dc_ref[j, pl.ds(PAD + r - w0, TILE), :]
+                + mask_ref[3, at, :] * dc_ref[j, pl.ds(PAD + r - w1, TILE), :]
+            )
+            ul_ref[j, pl.ds(PAD + r, TILE), :] = u[2] * below + u[5] * level + u[8] * above
+            u0_ref[j, at, :] = u[3] * below + u[6] * level + u[9] * above
+            ur_ref[j, pl.ds(PAD + r, TILE), :] = u[4] * below + u[7] * level + u[10] * above
+            grads = [fold(d * f) for d in (below, level, above) for f in (left, here, right)]
+            tap_sums[j] = [a + b for a, b in zip(tap_sums[j], grads)]
+
+        up_sums = [zero] * halves
+
+        def spread_back(r, j):
+            at = pl.ds(r, TILE)
+            value = (
+                u0_ref[j, at, :]
+                + mask_ref[0, at, :] * ur_ref[j, pl.ds(PAD + r - 1, TILE), :]
+                + mask_ref[1, at, :] * ul_ref[j, pl.ds(PAD + r + 1, TILE), :]
+            ).astype(BF16)
+            df_ref[at, pl.ds(j * 128, 128)] = value
+            up_sums[j] = up_sums[j] + fold(value.astype(F32))
+
+        def steps(step):
+            return [functools.partial(step, r, j) for j in range(halves) for r in range(0, capacity, TILE)]
+
+        interleave(
+            steps(column_taps) + steps(activate),
+            tasks(act_grad, c, capacity, MROWS) + tasks(up_grad, before, width, MROWS)
+            + tasks(h2_grad, before, capacity, MROWS),
+        )
+        interleave(
+            steps(into_conv) + steps(tap_back),
+            tasks(second_layer, c, capacity, MROWS) + tasks(down_grad, c, width, MROWS),
+        )
+        interleave(steps(spread_back), tasks(first_layer, following, capacity, MROWS))
         for j in range(halves):
-            put_vector(1, j, column_sum(totals[j]))
-
-        for j in range(halves):
-            v = [vector(k, j) for k in range(11)]
-
-            def tap_back(i, carry, j=j, v=v):
-                r = pl.multiple_of(i * TILE, TILE)
-                at = pl.ds(r, TILE)
-                left, here, right = taps_of(j, r, at)
-                below = (
-                    mask_ref[4, at, :] * dc_ref[j, pl.ds(PAD + r + w0, TILE), :]
-                    + mask_ref[5, at, :] * dc_ref[j, pl.ds(PAD + r + w1, TILE), :]
-                )
-                level = dc_ref[j, pl.ds(PAD + r, TILE), :]
-                above = (
-                    mask_ref[2, at, :] * dc_ref[j, pl.ds(PAD + r - w0, TILE), :]
-                    + mask_ref[3, at, :] * dc_ref[j, pl.ds(PAD + r - w1, TILE), :]
-                )
-                ul_ref[j, pl.ds(PAD + r, TILE), :] = v[2] * below + v[5] * level + v[8] * above
-                u0_ref[j, at, :] = v[3] * below + v[6] * level + v[9] * above
-                ur_ref[j, pl.ds(PAD + r, TILE), :] = v[4] * below + v[7] * level + v[10] * above
-                grads = [fold(d * f) for d in (below, level, above) for f in (left, here, right)]
-                return tuple(a + b for a, b in zip(carry, grads))
-
-            sums = lax.fori_loop(0, tiles, tap_back, (zero,) * 9, unroll=UNROLL)
+            put_vector(c, 0, j, column_sum(up_sums[j]))
+            put_vector(c, 1, j, column_sum(conv_sums[j]))
             for k in range(9):
-                put_vector(2 + k, j, column_sum(sums[k]))
-
-        def spread_back(i, carry):
-            r = pl.multiple_of(i * TILE, TILE)
-            at = pl.ds(r, TILE)
-            totals = []
-            for j in range(halves):
-                value = (
-                    u0_ref[j, at, :]
-                    + mask_ref[0, at, :] * ur_ref[j, pl.ds(PAD + r - 1, TILE), :]
-                    + mask_ref[1, at, :] * ul_ref[j, pl.ds(PAD + r + 1, TILE), :]
-                ).astype(BF16)
-                df_ref[at, pl.ds(j * 128, 128)] = value
-                totals.append(carry[j] + fold(value.astype(F32)))
-            return tuple(totals)
-
-        totals = lax.fori_loop(0, tiles, spread_back, (zero,) * halves, unroll=UNROLL)
-        for j in range(halves):
-            put_vector(0, j, column_sum(totals[j]))
-        df = df_ref[...]
-        upg_ref[:, at_c] = dot_nn(h2t_ref[...], df)
-        dh2_ref[...] += dot_nt(df, wu_ref[:, at_c])
+                put_vector(c, 2 + k, j, column_sum(tap_sums[j][k]))
         return carry
 
-    lax.fori_loop(0, hidden // CHUNK, chunk_step, 0)
+    df_ref[...] = jnp.zeros_like(df_ref)
+    first_layer(0, pl.ds(0, capacity))
+    lax.fori_loop(0, chunks, chunk_step, 0)
+    up_grad(chunks - 1, pl.ds(0, width))
+    h2_grad(chunks - 1, pl.ds(0, capacity))
     hg_ref[11:, :] = jnp.zeros((hg_ref.shape[0] - 11, hidden), F32)
 
     def value_of(w, n):
@@ -505,7 +526,7 @@
             *[upg_ref[e, pl.ds(tails + REST * w, REST)] for e in up],
         )
 
-    store_pieces(gown_ref, gsend_ref, me, value_of)
+    store_pieces(gown_ref, gsend_ref, me, value_of, mixed_slot)
 
     def finish(i, carry):
         at = pl.ds(pl.multiple_of(i * 64, 64), 64)
@@ -521,14 +542,14 @@
         mg_ref[8 + k : 9 + k, :] = sums[k]
 
 
-def store_pieces(own_ref, send_ref, me, value_of):
+def store_pieces(own_ref, send_ref, me, value_of, order):
     even = (me & 1) == 0
     for w in range(PARTS_W):
         for x in range(PARTS_N // 2):
             first, second = value_of(w, 2 * x), value_of(w, 2 * x + 1)
-            slot = slot_of(w * PARTS_N + 2 * x, me)
-            own_ref[slot] = jnp.where(even, first, second).astype(BF16)
-            send_ref[slot] = jnp.where(even, second, first).astype(BF16)
+            slot0, slot1 = (order(w * PARTS_N + 2 * x + c, me) for c in range(2))
+            own_ref[jnp.where(even, slot0, slot1)] = jnp.where(even, first, second).astype(BF16)
+            send_ref[jnp.where(even, slot1, slot0)] = jnp.where(even, second, first).astype(BF16)
 
 
 def score_back_kernel(dx2_ref, vb_ref, p_ref, o_ref, wp_ref, gp_ref, dob_ref, ds_ref, bp_ref, dp_ref):
@@ -612,7 +633,20 @@
             gp_ref[at, lane_at],
         )
 
-    store_pieces(gown_ref, gsend_ref, me, value_of)
+    store_pieces(gown_ref, gsend_ref, me, value_of, round_slot)
+
+
+def fold_rows(value, unit):
+    rest = value[8:]
+    beside = lanes(rest[:, : 3 * unit], jnp.zeros((8, 256 - 3 * unit), F32))
+    below = lanes(rest[:, 3 * unit :], jnp.zeros((8, 256 - 2 * unit), F32))
+    return lanes(value[:8], (beside + pltpu.roll(below, 3, 0))[:, : 3 * unit])
+
+
+def unfold_rows(value, unit):
+    beside = lanes(value[:, 5 * unit :], jnp.zeros((8, 256 - 3 * unit), F32))
+    below = pltpu.roll(beside, 5, 0)
+    return rows_of(value[:, : 5 * unit], lanes(beside[:, : 3 * unit], below[:, : 2 * unit]))
 
 
 def token_back_kernel(
@@ -637,13 +671,12 @@
     tg_ref[...] = token_grad.T.astype(BF16)
     sums = rows_of(column_sum(dh1 * n1), column_sum(dh1), vk[0:5], bp_ref[...], mg_ref[8:16, :])
     hg = hg_ref[...]
-    spare = jnp.zeros((16, 3 * rn), F32)
     value = []
     for n in range(PARTS_N):
         parts = []
         for w in (2 * n, 2 * n + 1):
             parts += [hg[:, 128 * w : 128 * (w + 1)], hg[:, 1024 + REST * w : 1024 + REST * (w + 1)]]
-        value.append(lanes(sums[:, n * rn : (n + 1) * rn], *parts, spare))
+        value.append(fold_rows(lanes(sums[:, n * rn : (n + 1) * rn], *parts), rn))
     even = (me & 1) == 0
     for x in range(2):
         slot = x ^ ((me >> 1) & 1)
@@ -658,35 +691,46 @@
     return value
 
 
-def core_sum_kernel(own_ref, got_ref, *out_refs):
+def halve_kernel(keep_ref, got_ref, low_ref, high_ref):
+    half = low_ref.shape[0]
+    low_ref[...] = (keep_ref[:half].astype(F32) + got_ref[:half].astype(F32)).astype(BF16)
+    high_ref[...] = (keep_ref[half:].astype(F32) + got_ref[half:].astype(F32)).astype(BF16)
+
+
+def halve_core_kernel(keep_ref, got_ref, vkeep_ref, vgot_ref, low_ref, vlow_ref, send_ref):
+    half = low_ref.shape[0]
+    low_ref[...] = (keep_ref[:half].astype(F32) + got_ref[:half].astype(F32)).astype(BF16)
+    parts = [keep_ref[half + k].astype(F32) + got_ref[half + k].astype(F32) for k in range(half)]
+    vector = total_of((vkeep_ref, vgot_ref))
+    vlow_ref[...] = vector.astype(BF16)
+    send_ref[...] = rows_of(*parts, vector[0], vector[1]).astype(BF16)
+
+
+def halve_round_kernel(tuned, keep_ref, vkeep_ref, got_ref, low_ref, vlow_ref, send_ref):
+    half, cw = low_ref.shape[:2]
+    rows = vkeep_ref.shape[1]
+    got = got_ref[...].astype(F32)
+    parts = [keep_ref[k].astype(F32) + got[k * cw : (k + 1) * cw] for k in range(2 * half)]
+    for k in range(half):
+        low_ref[k] = parts[k].astype(BF16)
+    got0, got1 = (got[2 * half * cw + k * rows : 2 * half * cw + (k + 1) * rows] for k in range(2))
+    keep0, keep1 = vkeep_ref[0].astype(F32), vkeep_ref[1].astype(F32)
+    even = (my_index(tuned) & 1) == 0
+    low = keep0 + jnp.where(even, got0, got1)
+    vlow_ref[0] = low.astype(BF16)
+    send_ref[...] = rows_of(*parts[half:], jnp.where(even, keep1 + got1, low)).astype(BF16)
+
+
+def quarter_vector_kernel(keep_ref, vkeep_ref, got_ref, *out_refs):
+    cw = keep_ref.shape[1]
+    got = got_ref[...].astype(F32)
+    vector = vkeep_ref[0].astype(F32) + got[4 * cw :]
     for k, ref in enumerate(out_refs):
-        at = slice(4 * k, 4 * k + 4)
-        ref[...] = (own_ref[at].astype(F32) + got_ref[at].astype(F32)).astype(BF16)
-
-
-def core_sum_vector_kernel(own_ref, got_ref, vown_ref, vgot_ref, *out_refs):
-    cw = own_ref.shape[1]
-    vector = [(vown_ref[x].astype(F32) + vgot_ref[x].astype(F32)).astype(BF16) for x in range(2)]
-    for k, ref in enumerate(out_refs):
-        parts = [own_ref[4 * k + j].astype(F32) + got_ref[4 * k + j].astype(F32) for j in range(4)]
-        ref[pl.ds(0, 4 * cw), :] = rows_of(*parts).astype(BF16)
-        ref[pl.ds(4 * cw, vector[0].shape[0]), :] = vector[k & 1]
-
-
-def plane_sum_kernel(a_ref, b_ref, c_ref, d_ref, *out_refs):
-    total = total_of((a_ref, b_ref, c_ref, d_ref)).astype(BF16)
-    for k, ref in enumerate(out_refs):
-        ref[0] = total[k]
-
-
-def plane_sum_vector_kernel(cw, a_ref, b_ref, c_ref, d_ref, *out_refs):
-    total = total_of((a_ref, b_ref, c_ref, d_ref))
-    for k, ref in enumerate(out_refs):
-        ref[...] = rows_of(total[k * cw : (k + 1) * cw], total[4 * cw :]).astype(BF16)
-
-
-def finish_ffn_kernel(a_ref, b_ref, c_ref, d_ref, up_ref, down_ref):
-    total = total_of((a_ref, b_ref, c_ref, d_ref))[0]
+        ref[...] = rows_of(keep_ref[k].astype(F32) + got[k * cw : (k + 1) * cw], vector).astype(BF16)
+
+
+def finish_ffn_kernel(a_ref, b_ref, up_ref, down_ref):
+    total = total_of((a_ref, b_ref))[0]
     columns = [
         lanes(total[:, 128 * k : 128 * (k + 1)], total[:, 512 + REST * k : 512 + REST * (k + 1)]) for k in range(4)
     ]
@@ -703,8 +747,9 @@
     q_ref[...] = unit[0]
     kv_ref[...] = rows_of(unit[1], unit[2]).T
     proj_ref[...] = unit[3]
-    vm_ref[...] = total[cw : cw + vm_ref.shape[0], :rn]
-    vh_ref[...] = total[cw : cw + vh_ref.shape[0], rn : rn + width]
+    vector = unfold_rows(total[cw:], rn)
+    vm_ref[...] = vector[: vm_ref.shape[0], :rn]
+    vh_ref[...] = vector[: vh_ref.shape[0], rn:]
 
 
 def call(kernel, inputs, outputs, scratch=(), scalars=0, limit=40, flops=0, moved=0):
@@ -737,7 +782,7 @@
     cw, rn = width // PARTS_W, width // PARTS_N
     keys = capacity // 4
     piece = (cw, 2 * width)
-    vpiece = (16, 2 * width)
+    vpiece, gpiece = (16, 2 * width), (8, 2 * width)
 
     def swap(value, mask, other=None):
         masks = (mask, mask if other is None else other)
@@ -748,21 +793,23 @@
     tokens_low = ((capacity, width), BF16)
     x, n1, r1, chosen, live, geo = prepare(img_rows, img_cols, tokens.T)
     if tuned:
-        packed, pack_v = pack(
+        pack_a, pack_b, pack_v = pack(
             (
                 q_weight.T, kv_weight, reduce_weight.T, proj_weight.T, up_weight, down_weight.T,
                 vec_model, vec_hidden,
             ),
             piece, vpiece,
         )
-        line = [swap(packed, m) for m in (8, 16, 24)]
-        vecs = [pack_v] + [swap(pack_v, m) for m in (1, 2, 3)]
-        line = lax.optimization_barrier((*line, x, n1, chosen))[:3]
-        near_a, near_b = (jnp.concatenate([v[k : k + 1] for v in (packed, *line)], axis=0) for k in range(2))
-        half_a = jnp.concatenate([near_a, swap(near_a, 2, 4)], axis=0)
-        half_b = jnp.concatenate([near_b, swap(near_b, 2, 4)], axis=0)
-        own_a = jnp.concatenate([half_a, swap(half_a, 4, 2)], axis=0)
-        own_a, half_b, *vecs = lax.optimization_barrier((own_a, half_b, *vecs))
+        def join(*parts):
+            return jnp.concatenate(parts, axis=0)
+
+        line_a = [swap(pack_a, m) for m in (8, 16, 24)]
+        got_b, got_v = swap(pack_b, 2, 4), swap(pack_v, 1)
+        *line_a, got_b, got_v = lax.optimization_barrier((*line_a, got_b, got_v, x, n1, chosen))[:5]
+        buf_a, buf_b, vecs = join(pack_a, *line_a), join(pack_b, got_b), join(pack_v, got_v)
+        buf_a, buf_b = join(buf_a, swap(buf_a, 2, 4)), join(buf_b, swap(buf_b, 16))
+        got = lax.optimization_barrier((swap(buf_a, 4, 2), swap(buf_b, 8), swap(vecs, 2)))
+        own_a, half_b, vecs = (join(v, g) for v, g in zip((buf_a, buf_b, vecs), got))
         oth_a = swap(own_a, 1)
         rest_b = swap(half_b, 4, 2)
     else:
@@ -775,7 +822,7 @@
         x2, h1, patches, nk, rk, kn, q, kb, vb, p, o, wr, wq, wkv, wp, mv, hv,
     ) = call(
         functools.partial(attend_kernel, tuned),
-        (x, n1, chosen, live, own_a, oth_a, *vecs),
+        (x, n1, chosen, live, own_a, oth_a, vecs),
         (
             tokens_f32, tokens_low,
             ((capacity, width), BF16), ((keys, width), F32), ((keys, 1), F32), ((keys, width), BF16),
@@ -832,12 +879,15 @@
         scratch=(((capacity, HEADS * keys), F32),),
         flops=25 * 10**8,
     )
-    four = (4,) + piece
+    def halve(keep, got, flops=0):
+        shape = ((keep.shape[0] // 2,) + piece, BF16)
+        return call(halve_kernel, (keep, got), (shape, shape), flops=flops)
+
     if tuned:
         got_b = after(got_b, ds)
-        half_b = call(core_sum_kernel, (gown_b, got_b), ((four, BF16),) * 4)
-        plane_b = [swap(half_b[k], 2 * k) for k in (1, 2, 3)]
-        ds = after(ds, half_b[1])
+        low_b, high_b = halve(gown_b, got_b)
+        ds = after(ds, high_b)
+        got_b = swap(high_b, 4, 2)
     gown_a, gsend_a, dq, dpatch, vk = call(
         functools.partial(attend_back_kernel, tuned),
         (dob, ds, gp, h1, patches, nk, rk, kn, q, kb, p, wr, wkv, mv),
@@ -850,29 +900,38 @@
     )
     if tuned:
         got_a = swap(gsend_a, 1)
-        near_b = call(plane_sum_kernel, (half_b[0], *plane_b), (((1,) + piece, BF16),) * 4, flops=2 * 10**10)
-        line_b = [swap(near_b[k], 8 * k) for k in (1, 2, 3)]
+        low_b, high_b = halve(low_b, got_b, flops=2 * 10**10)
+        gown_a = after(gown_a, high_b)
     mixed, token_grad, vown, vsend = call(
         functools.partial(token_back_kernel, tuned),
         (dx2, dq, dpatch, n1, r1, chosen, wq, mv, mg, hg, vk, bp, x2, mix, masks),
-        (((width, capacity), BF16), ((width, capacity), BF16), ((2,) + vpiece, BF16), ((2,) + vpiece, BF16)),
+        (((width, capacity), BF16), ((width, capacity), BF16), ((2,) + gpiece, BF16), ((2,) + gpiece, BF16)),
     )
 
     if not tuned:
         grads = scatter_plain(mesh_shape, width, gown_a, gsend_a, gown_b, gsend_b, vown, vsend)
         return (mixed.T, token_grad.T) + grads
 
-    gown_a = after(gown_a, near_b[1])
-    joined = ((4 * cw + 16, 2 * width), BF16)
-    half_a = call(core_sum_vector_kernel, (gown_a, got_a, vown, swap(vsend, 1)), (joined,) * 4)
-    plane_a = [swap(half_a[k], 2 * k) for k in (1, 2, 3)]
-    plane_a = lax.optimization_barrier((*plane_a, *line_b))[:3]
-    near_a = call(
-        functools.partial(plane_sum_vector_kernel, cw), (half_a[0], *plane_a), (((cw + 16, 2 * width), BF16),) * 4
-    )
+    vrows = gpiece[0]
+    low_a, vlow, high_a = call(
+        halve_core_kernel,
+        (gown_a, got_a, vown, swap(vsend, 1)),
+        (((8,) + piece, BF16), ((2,) + gpiece, BF16), ((8 * cw + 2 * vrows, 2 * width), BF16)),
+    )
+    got_a, got_b = lax.optimization_barrier((swap(high_a, 4, 2), swap(high_b, 8)))
+    low_a, vlow, high_a = call(
+        functools.partial(halve_round_kernel, tuned),
+        (low_a, vlow, got_a),
+        (((4,) + piece, BF16), ((1,) + gpiece, BF16), ((4 * cw + vrows, 2 * width), BF16)),
+    )
+    low_b, high_b = halve(low_b, got_b)
+    got_a, got_b = swap(high_a, 2, 4), swap(high_b, 16)
+    near_a = list(call(quarter_vector_kernel, (low_a, vlow, got_a), (((cw + vrows, 2 * width), BF16),) * 4))
+    near_a[1], got_b = lax.optimization_barrier((near_a[1], got_b))
     line_a = [swap(near_a[k], 8 * k) for k in (1, 2, 3)]
+    low_b, high_b = halve(low_b, got_b)
     up_grad, down_grad = call(
-        finish_ffn_kernel, (near_b[0], *line_b), (((rn, 4 * cw), F32), ((cw, width), F32))
+        finish_ffn_kernel, (low_b, swap(high_b, 2, 4)), (((rn, 4 * cw), F32), ((cw, width), F32))
     )
     q_grad, kv_grad, reduce_grad, proj_grad, vm_grad, vh_grad = call(
         finish_attend_kernel,
@@ -900,11 +959,12 @@
         split = turned.reshape(PARTS_W, blocks, cw, PARTS_N, -1)
         return split.transpose(0, 3, 2, 1, 4).reshape(PARTS_W, PARTS_N, cw, -1)
 
-    def slots(value):
-        value = value.reshape(4, 2, 2, 2, cw, -1)
-        even = value[:, :, :, 0].transpose(1, 2, 0, 3, 4)
-        odd = value[:, :, :, 1].transpose(2, 1, 0, 3, 4)
-        return even.reshape(SLOTS, cw, -1), odd.reshape(SLOTS, cw, -1)
+    def slots(value, mixed=False):
+        value = value.reshape(2, 2, 2, 2, 2, cw, -1)
+        orders = ((2, 1, 0, 3), (3, 1, 0, 2)) if mixed else ((2, 3, 0, 1), (3, 2, 0, 1))
+        return tuple(
+            value[:, :, :, :, core].transpose(*order, 4, 5).reshape(SLOTS, cw, -1) for core, order in enumerate(orders)
+        )
 
     a = jnp.concatenate([pieces(reduce, 1), pieces(q, 1), pieces(kv, 2), pieces(proj, 1)], axis=-1)
     columns = pieces(down, 1).reshape(PARTS_W, PARTS_N, cw, 2, RUN)
@@ -916,15 +976,19 @@
     vh = lax.all_gather(vec_hidden, "narrow", axis=1, tiled=True)
     both = jnp.concatenate([vm.reshape(11, PARTS_N, rn), vh.reshape(11, PARTS_N, width)], axis=-1)
     vecs = jnp.pad(both.transpose(1, 0, 2), ((0, 0), (0, 5), (0, 3 * rn)))
-    return (*slots(a), *slots(b), [vecs[n : n + 1] for n in range(PARTS_N)])
+    return (*slots(a), *slots(b, True), vecs)
 
 
 def scatter_plain(mesh_shape, width, gown_a, gsend_a, gown_b, gsend_b, vown, vsend):
     cw, rn = width // PARTS_W, width // PARTS_N
 
-    def devices(own, send):
-        both = jnp.stack([own, send]).reshape(2, 4, 4, cw, -1).transpose(2, 1, 0, 3, 4)
-        return both.reshape(PARTS_W, PARTS_N, cw, -1)
+    def devices(own, send, mixed=False):
+        orders = ((2, 1, 0, 3), (3, 1, 0, 2)) if mixed else ((2, 3, 0, 1), (3, 2, 0, 1))
+        parts = []
+        for value, order in zip((own, send), orders):
+            back = sorted(range(4), key=lambda k: order[k])
+            parts.append(value.reshape(2, 2, 2, 2, cw, -1).transpose(*back, 4, 5))
+        return jnp.stack(parts, axis=4).reshape(PARTS_W, PARTS_N, cw, -1)
 
     def natural(value, blocks):
         split = value.reshape(PARTS_W, PARTS_N, cw, blocks, -1).transpose(0, 3, 2, 1, 4)
@@ -935,7 +999,7 @@
         return lax.psum_scatter(columns, "narrow", scatter_dimension=0, tiled=True).astype(F32)
 
     a = devices(gown_a, gsend_a)
-    b = devices(gown_b, gsend_b)
+    b = devices(gown_b, gsend_b, True)
     reduce = natural(a[..., :width], 1)
     q = natural(a[..., width : width + rn], 1)
     kv = natural(a[..., width + rn : width + 3 * rn], 2)
@@ -946,7 +1010,10 @@
     ]
     down = natural(jnp.concatenate(columns[:2], axis=-1), 1)
     up = jnp.stack(columns[2:]).transpose(2, 0, 3, 1, 4).reshape(width, -1)
-    vectors = jnp.stack([vown, vsend], axis=1).reshape(PARTS_N, 16, -1)[:, :11].transpose(1, 0, 2)
+    vectors = jnp.stack([vown, vsend], axis=1).reshape(PARTS_N, 8, -1)
+    beside = vectors[..., 5 * rn :]
+    beside = jnp.concatenate([beside[:, :3], beside[:, 3:6, : 2 * rn]], axis=-1)
+    vectors = jnp.concatenate([vectors[..., : 5 * rn], beside], axis=1).transpose(1, 0, 2)
     vm = vectors[..., :rn].reshape(11, width)
     vh = vectors[..., rn : rn + width].reshape(11, PARTS_N * width)
 

time: 102 us -> 96.4 us (0.945)
  Pallas kernels: 42.7 us -> 37.9 us
    pallas_call x12 -> x15, Pallas kernels: 37.9 us -> 33.1 us  [call(): pl.pallas_call(kernel, out_shape=[jax.ShapeDtypeStruct(shape, kind) for s...]
    ppermute x27 -> x25, waiting for transfers between devices: 27.7 us -> 27.3 us  [swap(): return lax.ppermute(value, ('wide', 'narrow'), pairs)]
    ppermute x27 -> x25, starting transfers between devices: 29 us -> 29.3 us  [swap(): return lax.ppermute(value, ('wide', 'narrow'), pairs)]
  transfers between devices with their start and end apart: 27 -> 25, of which waited for: 15 -> 12; matrix products, arithmetic and copies ran while one was open for 1% -> 0% of each run, Pallas kernels for 18% -> 19%
where the time goes in v4:
time: 96.4 us; the launch traced here: 96 us
  Pallas kernels  37.9 us (39%)
  starting transfers between devices  29.3 us (30%)
  waiting for transfers between devices  27.3 us (28%)
  between operations  0.98 us (1%)
    pallas_call x15, Pallas kernels, call(): pl.pallas_call(kernel, out_shape=[jax.ShapeDtypeStruct(shape, kind) for s...  33.1 us
    ppermute x25, starting transfers between devices, swap(): return lax.ppermute(value, ('wide', 'narrow'), pairs)  29.3 us
    ppermute x25, waiting for transfers between devices, swap(): return lax.ppermute(value, ('wide', 'narrow'), pairs)  27.3 us
    pallas_call x1, Pallas kernels, prepare(): pl.pallas_call(prepare_kernel, out_shape=[jax.ShapeDtypeStruct(shape, kin...  3.1 us
  transfers between devices with their start and end apart: 25, of which 12 were waited for; matrix products, arithmetic and copies ran while one was open for 0% of the time, Pallas kernels for 19%

profile of v4, /device:TPU:0, one launch (start us, length us, event | category | flops | bytes accessed | tf_op | source)
XLA Modules:
  0.0 96.0 jit_solution(5930714941843507485)
XLA Ops:
  0.6 1.7 %shard_map.196 = (bf16[1,40,640]{2,1,0:T(8,128)(2,1)}, bf16[1,40,640]{2,1,0:T(8,128)(2,1)}, bf16[1,16,640]{2,1,0:T(8,128)(2,1)}) custom-call(bf16[40,80]{1,0:T(8,128)(2,1)} %bitcast.15, bf16[80,80]{1,0:T(8,128)(2,1)} %refs_1_.1, bf16[40,320]{1,0:T(8,128)(2,1)} %bitcast.13, bf16[40,80]{1,0:T(8,128)(2,1)} %bitcast.16, bf16[80,160]{1,0:T(8,128)(2,1)} %refs_4_.1, ...), custom_call_target="tpu_custom_call" | custom-call | tf_op jit(solution)/shard_map/pallas_call | solution.py:134
  2.4 5.1 %collective-permute-start.2 = (bf16[1,40,640]{2,1,0:T(8,128)(2,1)}, bf16[1,40,640]{2,1,0:T(8,128)(2,1)S(1)}, u32[]{:S(2)}, u32[]{:S(2)}) collective-permute-start(bf16[1,40,640]{2,1,0:T(8,128)(2,1)} %get-tuple-element.109), channel_id=1, source_target_pairs={{0,24},{1,25},{2,26},{3,27},{4,28},{5,29},{6,30},{7,31},{8,16},{9,... | collective-permute-start | bytes 153608 | tf_op jit(solution)/shard_map/ppermute | solution.py:790
  8.1 1.6 %collective-permute-start.3 = (bf16[1,40,640]{2,1,0:T(8,128)(2,1)}, bf16[1,40,640]{2,1,0:T(8,128)(2,1)S(1)}, u32[]{:S(2)}, u32[]{:S(2)}) collective-permute-start(bf16[1,40,640]{2,1,0:T(8,128)(2,1)} %get-tuple-element.110), channel_id=1, source_target_pairs={{0,2},{1,5},{2,0},{3,7},{4,6},{5,1},{6,4},{7,3},{8,10},{9,13},{10,... | collective-permute-start | bytes 153608 | tf_op jit(solution)/shard_map/ppermute | solution.py:790
  9.8 3.1 %shard_map.195 = (f32[512,320]{1,0:T(8,128)}, f32[512,320]{1,0:T(8,128)}, f32[512,1]{1,0:T(8,128)}, bf16[512,512]{1,0:T(8,128)(2,1)}, f32[512,128]{1,0:T(8,128)}, /*index=5*/s32[4]{0:T(128)}) custom-call(s32[2]{0:T(128)} %rows_hbm.1, s32[2]{0:T(128)} %cols_hbm.1, bf16[320,512]{1,0:T(8,128)(2,1)} %bitcast.17), custom_call_target="tpu_custom_call" | custom-call | flops 2000000000 | tf_op jit(solution)/shard_map/pallas_call | solution.py:184
  13.0 2.2 %collective-permute-start.7 = (bf16[2,40,640]{2,1,0:T(8,128)(2,1)S(1)}, bf16[2,40,640]{2,1,0:T(8,128)(2,1)S(1)}, u32[]{:S(2)}, u32[]{:S(2)}) collective-permute-start(bf16[2,40,640]{2,1,0:T(8,128)(2,1)S(1)} %pad_maximum_fusion.3), channel_id=1, source_target_pairs={{0,16},{1,17},{2,18},{3,19},{4,20},{5,21},{6,22},{7,23},{8,24},{9,... | collective-permute-start | bytes 307208 | tf_op jit(solution)/shard_map/ppermute | solution.py:790
  15.2 1.2 %collective-permute-start.5 = (bf16[4,40,640]{2,1,0:T(8,128)(2,1)S(1)}, bf16[4,40,640]{2,1,0:T(8,128)(2,1)S(1)}, u32[]{:S(2)}, u32[]{:S(2)}) collective-permute-start(bf16[4,40,640]{2,1,0:T(8,128)(2,1)S(1)} %pad_maximum_fusion.1), channel_id=1, source_target_pairs={{0,2},{1,5},{2,0},{3,7},{4,6},{5,1},{6,4},{7,3},{8,10},{9,13},{10,... | collective-permute-start | bytes 614408 | tf_op jit(solution)/shard_map/ppermute | solution.py:790
  16.5 4.6 %collective-permute-done.5 = bf16[4,40,640]{2,1,0:T(8,128)(2,1)S(1)} collective-permute-done((bf16[4,40,640]{2,1,0:T(8,128)(2,1)S(1)}, bf16[4,40,640]{2,1,0:T(8,128)(2,1)S(1)}, u32[]{:S(2)}, u32[]{:S(2)}) %collective-permute-start.5) | collective-permute-done | bytes 204832 | tf_op jit(solution)/shard_map/ppermute | solution.py:790
  21.1 1.6 %collective-permute-start.6 = (bf16[8,40,640]{2,1,0:T(8,128)(2,1)S(1)}, bf16[8,40,640]{2,1,0:T(8,128)(2,1)S(1)}, u32[]{:S(2)}, u32[]{:S(2)}) collective-permute-start(bf16[8,40,640]{2,1,0:T(8,128)(2,1)S(1)} %get-tuple-element.198), channel_id=1, source_target_pairs={{0,4},{1,3},{2,6},{3,1},{4,0},{5,7},{6,2},{7,5},{8,12},{9,11},{10,... | collective-permute-start | bytes 1228808 | tf_op jit(solution)/shard_map/ppermute | solution.py:790
  22.8 2.1 %collective-permute-start.8 = (bf16[4,40,640]{2,1,0:T(8,128)(2,1)S(1)}, bf16[4,40,640]{2,1,0:T(8,128)(2,1)S(1)}, u32[]{:S(2)}, u32[]{:S(2)}) collective-permute-start(bf16[4,40,640]{2,1,0:T(8,128)(2,1)S(1)} %pad_maximum_fusion.2), channel_id=1, source_target_pairs={{0,8},{1,9},{2,10},{3,11},{4,12},{5,13},{6,14},{7,15},{8,0},{9,1},... | collective-permute-start | bytes 614408 | tf_op jit(solution)/shard_map/ppermute | solution.py:790
  24.9 1.2 %collective-permute-start.9 = (bf16[2,16,640]{2,1,0:T(8,128)(2,1)S(1)}, bf16[2,16,640]{2,1,0:T(8,128)(2,1)S(1)}, u32[]{:S(2)}, u32[]{:S(2)}) collective-permute-start(bf16[2,16,640]{2,1,0:T(8,128)(2,1)S(1)} %pad_maximum_fusion.5), channel_id=1, source_target_pairs={{0,2},{1,3},{2,0},{3,1},{4,6},{5,7},{6,4},{7,5},{8,10},{9,11},{10,... | collective-permute-start | bytes 122888 | tf_op jit(solution)/shard_map/ppermute | solution.py:790
  26.0 2.9 %collective-permute-done.9 = bf16[2,16,640]{2,1,0:T(8,128)(2,1)S(1)} collective-permute-done((bf16[2,16,640]{2,1,0:T(8,128)(2,1)S(1)}, bf16[2,16,640]{2,1,0:T(8,128)(2,1)S(1)}, u32[]{:S(2)}, u32[]{:S(2)}) %collective-permute-start.9) | collective-permute-done | bytes 40992 | tf_op jit(solution)/shard_map/ppermute | solution.py:790
  29.4 1.6 %collective-permute-start.11 = (bf16[8,40,640]{2,1,0:T(8,128)(2,1)S(1)}, bf16[8,40,640]{2,1,0:T(8,128)(2,1)S(1)}, u32[]{:S(2)}, u32[]{:S(2)}) collective-permute-start(bf16[8,40,640]{2,1,0:T(8,128)(2,1)S(1)} %pad_maximum_fusion), channel_id=1, source_target_pairs={{0,4},{1,3},{2,6},{3,1},{4,0},{5,7},{6,2},{7,5},{8,12},{9,11},{10,... | collective-permute-start | bytes 1228808 | tf_op jit(solution)/shard_map/ppermute | solution.py:790
  31.7 5.1 %shard_map.197 = (f32[512,320]{1,0:T(8,128)S(1)}, bf16[512,320]{1,0:T(8,128)(2,1)S(1)}, bf16[512,320]{1,0:T(8,128)(2,1)S(1)}, f32[128,320]{1,0:T(8,128)S(1)}, f3...) custom-call(f32[512,320]{1,0:T(8,128)S(1)} %copy-done.4, ...), custom_call_target="tpu_custom_call" | custom-call | flops 8000000000 | tf_op jit(solution)/shard_map/pallas_call | solution.py:758
  37.6 1.6 %shard_map.198 = (f32[512,320]{1,0:T(8,128)S(1)}, f32[512,1]{1,0:T(8,128)S(1)}, bf16[512,320]{1,0:T(8,128)(2,1)S(1)}, bf16[320,512]{1,0:T(8,128)(2,1)S(1)}, bf16...) custom-call(s32[4]{0:T(128)S(1)} %copy-done.6, bf16[320,512]{1,0:T(8,128)(2,1)S(1)} %bitcast.12, ...), custom_call_target="tpu_custom_call" | custom-call | flops 2000000000 | tf_op jit(solution)/shard_map/pallas_call | solution.py:758
  39.9 16.7 %shard_map.199 = (bf16[16,40,640]{2,1,0:T(8,128)(2,1)S(1)}, bf16[16,40,640]{2,1,0:T(8,128)(2,1)S(1)}, f32[512,320]{1,0:T(8,128)S(1)}, f32[512,320]{1,0:T(8,128)S...) custom-call(s32[4]{0:T(128)S(1)} %copy-done.6, f32[512,320]{1,0:T(8,128)S(1)} %get-tuple-element.121.n2_ref, ...), custom_call_target="tpu_custom_call" | custom-call | flops 32999999488 | tf_op jit(solution)/shard_map/pallas_call | solution.py:758
  56.7 2.2 %shard_map.200 = (f32[320,320]{1,0:T(8,128)S(1)}, bf16[512,320]{1,0:T(8,128)(2,1)S(1)}, bf16[512,640]{1,0:T(8,128)(2,1)S(1)}, f32[1,320]{1,0:T(1,128)S(1)}) custom-call(f32[512,320]{1,0:T(8,128)S(1)} %get-tuple-element.131.dx2_ref, bf16[640,320]{1,0:T(8,128)(2,1)S(1)} %get-tuple-element.132.vb_ref, f32[512,640]{1,0:T(8,128)S(1)} %get-tuple-element.133.p_ref, ...), custom_call_target="tpu_custom_call" | custom-call | flops 2500000000 | tf_op jit(solution)/shard_map/pallas_call | solution.py:758
  59.2 1.9 %collective-permute-start.14 = (bf16[8,40,640]{2,1,0:T(8,128)(2,1)S(1)}, bf16[8,40,640]{2,1,0:T(8,128)(2,1)S(1)}, u32[]{:S(2)}, u32[]{:S(2)}) collective-permute-start(bf16[8,40,640]{2,1,0:T(8,128)(2,1)S(1)} %get-tuple-element.141), channel_id=1, source_target_pairs={{0,4},{1,3},{2,6},{3,1},{4,0},{5,7},{6,2},{7,5},{8,12},{9,11},{10,... | collective-permute-start | bytes 1228808 | tf_op jit(solution)/shard_map/ppermute | solution.py:790
  61.1 2.7 %shard_map.202 = (bf16[16,40,640]{2,1,0:T(8,128)(2,1)S(1)}, bf16[16,40,640]{2,1,0:T(8,128)(2,1)S(1)}, bf16[512,320]{1,0:T(8,128)(2,1)S(1)}, f32[512,320]{1,0:T(8,128)S(1)}, f32[8,320]{1,0:T(8,128)S(1)}) custom-call(bf16[512,320]{1,0:T(8,128)(2,1)S(1)} %get-tuple-element.136.dob_ref, bf16[512,640]{1,0:T(8,128)(2,1)S(1)} %get-tuple-element.142.ds_ref, ...), custom_call_target="tpu_custom_call" | custom-call | tf_op jit(solution)/shard_map/pallas_call | solution.py:758
  63.9 2.3 %shard_map.203 = (bf16[320,512]{1,0:T(8,128)(2,1)}, bf16[320,512]{1,0:T(8,128)(2,1)}, bf16[2,8,640]{2,1,0:T(8,128)(2,1)S(1)}, bf16[2,8,640]{2,1,0:T(8,128)(2,1)S(1)}) custom-call(f32[512,320]{1,0:T(8,128)S(1)} %get-tuple-element.131.dx2_ref, bf16[512,320]{1,0:T(8,128)(2,1)S(1)} %get-tuple-element.153.dq_ref, f32[512,320]{1,0:T(8,128)S(1)} %get-tuple-element.154.dpatch_ref, ...), custom_call_target="tpu_custom_call" | custom-call | tf_op jit(solution)/shard_map/pallas_call | solution.py:758
  67.3 1.3 %collective-permute-done.15.got_ref = bf16[16,40,640]{2,1,0:T(8,128)(2,1)S(1)} collective-permute-done((bf16[16,40,640]{2,1,0:T(8,128)(2,1)S(1)}, bf16[16,40,640]{2,1,0:T(8,128)(2,1)S(1)}, u32[]{:S(2)}, u32[]{:S(2)}) %collective-permute-start.15) | collective-permute-done | bytes 819232 | tf_op jit(solution)/shard_map/ppermute | solution.py:790
  68.8 1.2 %collective-permute-start.17 = (bf16[336,640]{1,0:T(8,128)(2,1)S(1)}, bf16[336,640]{1,0:T(8,128)(2,1)S(1)}, u32[]{:S(2)}, u32[]{:S(2)}) collective-permute-start(bf16[336,640]{1,0:T(8,128)(2,1)S(1)} %get-tuple-element.173), channel_id=1, source_target_pairs={{0,4},{1,3},{2,6},{3,1},{4,0},{5,7},{6,2},{7,5},{8,12},{9,11},{10,... | collective-permute-start | bytes 1290248 | tf_op jit(solution)/shard_map/ppermute | solution.py:790
  70.0 2.0 %collective-permute-start.18 = (bf16[4,40,640]{2,1,0:T(8,128)(2,1)S(1)}, bf16[4,40,640]{2,1,0:T(8,128)(2,1)S(1)}, u32[]{:S(2)}, u32[]{:S(2)}) collective-permute-start(bf16[4,40,640]{2,1,0:T(8,128)(2,1)S(1)} %get-tuple-element.166), channel_id=1, source_target_pairs={{0,8},{1,9},{2,10},{3,11},{4,12},{5,13},{6,14},{7,15},{8,0},{9,1},... | collective-permute-start | bytes 614408 | tf_op jit(solution)/shard_map/ppermute | solution.py:790
  72.0 5.3 %collective-permute-done.18.got_ref = bf16[4,40,640]{2,1,0:T(8,128)(2,1)S(1)} collective-permute-done((bf16[4,40,640]{2,1,0:T(8,128)(2,1)S(1)}, bf16[4,40,640]{2,1,0:T(8,128)(2,1)S(1)}, u32[]{:S(2)}, u32[]{:S(2)}) %collective-permute-start.18) | collective-permute-done | bytes 204832 | tf_op jit(solution)/shard_map/ppermute | solution.py:790
  77.4 0.9 collective-permute-start.19
  78.4 0.8 collective-permute-start.20
  79.2 4.1 %collective-permute-done.19.got_ref = bf16[168,640]{1,0:T(8,128)(2,1)S(1)} collective-permute-done((bf16[168,640]{1,0:T(8,128)(2,1)S(1)}, bf16[168,640]{1,0:T(8,128)(2,1)S(1)}, u32[]{:S(2)}, u32[]{:S(2)}) %collective-permute-start.19) | collective-permute-done | bytes 215072 | tf_op jit(solution)/shard_map/ppermute | solution.py:790
  83.4 2.3 %collective-permute-done.20.got_ref = bf16[2,40,640]{2,1,0:T(8,128)(2,1)S(1)} collective-permute-done((bf16[2,40,640]{2,1,0:T(8,128)(2,1)S(1)}, bf16[2,40,640]{2,1,0:T(8,128)(2,1)S(1)}, u32[]{:S(2)}, u32[]{:S(2)}) %collective-permute-start.20) | collective-permute-done | bytes 102432 | tf_op jit(solution)/shard_map/ppermute | solution.py:790
  86.1 1.6 %collective-permute-start.22 = (bf16[48,640]{1,0:T(8,128)(2,1)S(1)}, bf16[48,640]{1,0:T(8,128)(2,1)S(1)}, u32[]{:S(2)}, u32[]{:S(2)}) collective-permute-start(bf16[48,640]{1,0:T(8,128)(2,1)S(1)} %get-tuple-element.184), channel_id=1, source_target_pairs={{0,16},{1,17},{2,18},{3,19},{4,20},{5,21},{6,22},{7,23},{8,24},{9,... | collective-permute-start | bytes 184328 | tf_op jit(solution)/shard_map/ppermute | solution.py:790
  87.7 2.4 %collective-permute-start.23 = (bf16[48,640]{1,0:T(8,128)(2,1)S(1)}, bf16[48,640]{1,0:T(8,128)(2,1)S(1)}, u32[]{:S(2)}, u32[]{:S(2)}) collective-permute-start(bf16[48,640]{1,0:T(8,128)(2,1)S(1)} %get-tuple-element.185), channel_id=1, source_target_pairs={{0,24},{1,25},{2,26},{3,27},{4,28},{5,29},{6,30},{7,31},{8,16},{9,... | collective-permute-start | bytes 184328 | tf_op jit(solution)/shard_map/ppermute | solution.py:790
  90.2 4.1 %collective-permute-done.24.b_ref = bf16[1,40,640]{2,1,0:T(8,128)(2,1)S(1)} collective-permute-done((bf16[1,40,640]{2,1,0:T(8,128)(2,1)S(1)}, bf16[1,40,640]{2,1,0:T(8,128)(2,1)S(1)}, u32[]{:S(2)}, u32[]{:S(2)}) %collective-permute-start.24) | collective-permute-done | bytes 51232 | tf_op jit(solution)/shard_map/ppermute | solution.py:790
  94.3 0.8 shard_map.211
  95.1 0.9 shard_map.209
  (72 shorter events, 5.9 us)
Async XLA Ops:
  2.4 10.6 %collective-permute-start.2 = (bf16[1,40,640]{2,1,0:T(8,128)(2,1)}, bf16[1,40,640]{2,1,0:T(8,128)(2,1)S(1)}, u32[]{:S(2)}, u32[]{:S(2)}) collective-permute-start(bf16[1,40,640]{2,1,0:T(8,128)(2,1)} %get-tuple-element.109), channel_id=1, source_target_pairs={{0,24},{1,25},{2,26},{3,27},{4,28},{5,29},{6,30},{7,31},{8,16},{9,... | collective-permute-start | bytes 153608 | tf_op jit(solution)/shard_map/ppermute | solution.py:790
  7.5 5.5 %collective-permute-start.1 = (bf16[1,40,640]{2,1,0:T(8,128)(2,1)}, bf16[1,40,640]{2,1,0:T(8,128)(2,1)S(1)}, u32[]{:S(2)}, u32[]{:S(2)}) collective-permute-start(bf16[1,40,640]{2,1,0:T(8,128)(2,1)} %get-tuple-element.109), channel_id=1, source_target_pairs={{0,16},{1,17},{2,18},{3,19},{4,20},{5,21},{6,22},{7,23},{8,24},{9,... | collective-permute-start | bytes 153608 | tf_op jit(solution)/shard_map/ppermute | solution.py:790
  7.5 5.5 %collective-permute-start = (bf16[1,40,640]{2,1,0:T(8,128)(2,1)}, bf16[1,40,640]{2,1,0:T(8,128)(2,1)S(1)}, u32[]{:S(2)}, u32[]{:S(2)}) collective-permute-start(bf16[1,40,640]{2,1,0:T(8,128)(2,1)} %get-tuple-element.109), channel_id=1, source_target_pairs={{0,8},{1,9},{2,10},{3,11},{4,12},{5,13},{6,14},{7,15},{8,0},{9,1},... | collective-permute-start | bytes 153608 | tf_op jit(solution)/shard_map/ppermute | solution.py:790
  8.1 4.8 %collective-permute-start.4 = (bf16[1,16,640]{2,1,0:T(8,128)(2,1)}, bf16[1,16,640]{2,1,0:T(8,128)(2,1)S(1)}, u32[]{:S(2)}, u32[]{:S(2)}) collective-permute-start(bf16[1,16,640]{2,1,0:T(8,128)(2,1)} %get-tuple-element.111), channel_id=1, source_target_pairs={{0,1},{1,0},{2,3},{3,2},{4,5},{5,4},{6,7},{7,6},{8,9},{9,8},{10,11... | collective-permute-start | bytes 61448 | tf_op jit(solution)/shard_map/ppermute | solution.py:790
  8.1 4.8 %collective-permute-start.3 = (bf16[1,40,640]{2,1,0:T(8,128)(2,1)}, bf16[1,40,640]{2,1,0:T(8,128)(2,1)S(1)}, u32[]{:S(2)}, u32[]{:S(2)}) collective-permute-start(bf16[1,40,640]{2,1,0:T(8,128)(2,1)} %get-tuple-element.110), channel_id=1, source_target_pairs={{0,2},{1,5},{2,0},{3,7},{4,6},{5,1},{6,4},{7,3},{8,10},{9,13},{10,... | collective-permute-start | bytes 153608 | tf_op jit(solution)/shard_map/ppermute | solution.py:790
  12.9 12.0 %copy-start.9 = (bf16[1,16,640]{2,1,0:T(8,128)(2,1)S(1)}, bf16[1,16,640]{2,1,0:T(8,128)(2,1)}, u32[]{:S(2)}) copy-start(bf16[1,16,640]{2,1,0:T(8,128)(2,1)} %get-tuple-element.111) | copy-start | bytes 61444
  13.0 9.7 %collective-permute-start.7 = (bf16[2,40,640]{2,1,0:T(8,128)(2,1)S(1)}, bf16[2,40,640]{2,1,0:T(8,128)(2,1)S(1)}, u32[]{:S(2)}, u32[]{:S(2)}) collective-permute-start(bf16[2,40,640]{2,1,0:T(8,128)(2,1)S(1)} %pad_maximum_fusion.3), channel_id=1, source_target_pairs={{0,16},{1,17},{2,18},{3,19},{4,20},{5,21},{6,22},{7,23},{8,24},{9,... | collective-permute-start | bytes 307208 | tf_op jit(solution)/shard_map/ppermute | solution.py:790
  15.2 5.8 %collective-permute-start.5 = (bf16[4,40,640]{2,1,0:T(8,128)(2,1)S(1)}, bf16[4,40,640]{2,1,0:T(8,128)(2,1)S(1)}, u32[]{:S(2)}, u32[]{:S(2)}) collective-permute-start(bf16[4,40,640]{2,1,0:T(8,128)(2,1)S(1)} %pad_maximum_fusion.1), channel_id=1, source_target_pairs={{0,2},{1,5},{2,0},{3,7},{4,6},{5,1},{6,4},{7,3},{8,10},{9,13},{10,... | collective-permute-start | bytes 614408 | tf_op jit(solution)/shard_map/ppermute | solution.py:790
  21.1 10.5 %copy-start = (f32[512,320]{1,0:T(8,128)S(1)}, f32[512,320]{1,0:T(8,128)}, u32[]{:S(2)}) copy-start(f32[512,320]{1,0:T(8,128)} %get-tuple-element.106.n1_ref) | copy-start | bytes 1966084
  21.1 10.5 %copy-start.1 = (bf16[512,512]{1,0:T(8,128)(2,1)S(1)}, bf16[512,512]{1,0:T(8,128)(2,1)}, u32[]{:S(2)}) copy-start(bf16[512,512]{1,0:T(8,128)(2,1)} %get-tuple-element.107.chosen_ref) | copy-start | bytes 1572868
  21.1 10.5 %copy-start.4 = (f32[512,320]{1,0:T(8,128)S(1)}, f32[512,320]{1,0:T(8,128)}, u32[]{:S(2)}) copy-start(f32[512,320]{1,0:T(8,128)} %get-tuple-element.105.x_ref) | copy-start | bytes 1966084
  21.1 10.5 %copy-start.5 = (f32[512,128]{1,0:T(8,128)S(1)}, f32[512,128]{1,0:T(8,128)}, u32[]{:S(2)}) copy-start(f32[512,128]{1,0:T(8,128)} %get-tuple-element.108.live_ref) | copy-start | bytes 786436
  21.1 8.0 %collective-permute-start.6 = (bf16[8,40,640]{2,1,0:T(8,128)(2,1)S(1)}, bf16[8,40,640]{2,1,0:T(8,128)(2,1)S(1)}, u32[]{:S(2)}, u32[]{:S(2)}) collective-permute-start(bf16[8,40,640]{2,1,0:T(8,128)(2,1)S(1)} %get-tuple-element.198), channel_id=1, source_target_pairs={{0,4},{1,3},{2,6},{3,1},{4,0},{5,7},{6,2},{7,5},{8,12},{9,11},{10,... | collective-permute-start | bytes 1228808 | tf_op jit(solution)/shard_map/ppermute | solution.py:790
  22.8 6.2 %collective-permute-start.8 = (bf16[4,40,640]{2,1,0:T(8,128)(2,1)S(1)}, bf16[4,40,640]{2,1,0:T(8,128)(2,1)S(1)}, u32[]{:S(2)}, u32[]{:S(2)}) collective-permute-start(bf16[4,40,640]{2,1,0:T(8,128)(2,1)S(1)} %pad_maximum_fusion.2), channel_id=1, source_target_pairs={{0,8},{1,9},{2,10},{3,11},{4,12},{5,13},{6,14},{7,15},{8,0},{9,1},... | collective-permute-start | bytes 614408 | tf_op jit(solution)/shard_map/ppermute | solution.py:790
  24.9 4.1 %collective-permute-start.9 = (bf16[2,16,640]{2,1,0:T(8,128)(2,1)S(1)}, bf16[2,16,640]{2,1,0:T(8,128)(2,1)S(1)}, u32[]{:S(2)}, u32[]{:S(2)}) collective-permute-start(bf16[2,16,640]{2,1,0:T(8,128)(2,1)S(1)} %pad_maximum_fusion.5), channel_id=1, source_target_pairs={{0,2},{1,3},{2,0},{3,1},{4,6},{5,7},{6,4},{7,5},{8,10},{9,11},{10,... | collective-permute-start | bytes 122888 | tf_op jit(solution)/shard_map/ppermute | solution.py:790
  29.2 2.4 %collective-permute-start.10 = (bf16[16,40,640]{2,1,0:T(8,128)(2,1)S(1)}, bf16[16,40,640]{2,1,0:T(8,128)(2,1)S(1)}, u32[]{:S(2)}, u32[]{:S(2)}) collective-permute-start(bf16[16,40,640]{2,1,0:T(8,128)(2,1)S(1)} %constant_dynamic-update-slice_fusion.5.own_ref), channel_id=1, source_target_pairs={{0,1},{1,0},{2,3},{3,2},{4,5},{5,4},{6,7},{7,6},{8,9},{9,8},{10,11... | collective-permute-start | bytes 2457608 | tf_op jit(solution)/shard_map/ppermute | solution.py:790
  29.4 8.0 %collective-permute-start.11 = (bf16[8,40,640]{2,1,0:T(8,128)(2,1)S(1)}, bf16[8,40,640]{2,1,0:T(8,128)(2,1)S(1)}, u32[]{:S(2)}, u32[]{:S(2)}) collective-permute-start(bf16[8,40,640]{2,1,0:T(8,128)(2,1)S(1)} %pad_maximum_fusion), channel_id=1, source_target_pairs={{0,4},{1,3},{2,6},{3,1},{4,0},{5,7},{6,2},{7,5},{8,12},{9,11},{10,... | collective-permute-start | bytes 1228808 | tf_op jit(solution)/shard_map/ppermute | solution.py:790
  31.6 5.9 %copy-start.3 = (bf16[512,320]{0,1:T(8,128)(2,1)S(1)}, bf16[512,320]{0,1:T(8,128)(2,1)}, u32[]{:S(2)}) copy-start(bf16[512,320]{0,1:T(8,128)(2,1)} %param.13) | copy-start | bytes 983044
  31.6 5.9 %copy-start.6 = (s32[4]{0:T(128)S(1)}, s32[4]{0:T(128)}, u32[]{:S(2)}) copy-start(s32[4]{0:T(128)} %get-tuple-element.104.geo_ref) | copy-start | bytes 52
  37.5 2.4 %collective-permute-start.12 = (bf16[16,40,640]{2,1,0:T(8,128)(2,1)S(1)}, bf16[16,40,640]{2,1,0:T(8,128)(2,1)S(1)}, u32[]{:S(2)}, u32[]{:S(2)}) collective-permute-start(bf16[16,40,640]{2,1,0:T(8,128)(2,1)S(1)} %constant_dynamic-update-slice_fusion.11.own_ref), channel_id=1, source_target_pairs={{0,1},{1,0},{2,3},{3,2},{4,5},{5,4},{6,7},{7,6},{8,9},{9,8},{10,11... | collective-permute-start | bytes 2457608 | tf_op jit(solution)/shard_map/ppermute | solution.py:790
  56.5 2.4 %collective-permute-start.13 = (bf16[16,40,640]{2,1,0:T(8,128)(2,1)S(1)}, bf16[16,40,640]{2,1,0:T(8,128)(2,1)S(1)}, u32[]{:S(2)}, u32[]{:S(2)}) collective-permute-start(bf16[16,40,640]{2,1,0:T(8,128)(2,1)S(1)} %get-tuple-element.139), channel_id=1, source_target_pairs={{0,1},{1,0},{2,3},{3,2},{4,5},{5,4},{6,7},{7,6},{8,9},{9,8},{10,11... | collective-permute-start | bytes 2457608 | tf_op jit(solution)/shard_map/ppermute | solution.py:790
  59.2 8.0 %collective-permute-start.14 = (bf16[8,40,640]{2,1,0:T(8,128)(2,1)S(1)}, bf16[8,40,640]{2,1,0:T(8,128)(2,1)S(1)}, u32[]{:S(2)}, u32[]{:S(2)}) collective-permute-start(bf16[8,40,640]{2,1,0:T(8,128)(2,1)S(1)} %get-tuple-element.141), channel_id=1, source_target_pairs={{0,4},{1,3},{2,6},{3,1},{4,0},{5,7},{6,2},{7,5},{8,12},{9,11},{10,... | collective-permute-start | bytes 1228808 | tf_op jit(solution)/shard_map/ppermute | solution.py:790
  66.1 1.2 %collective-permute-start.16 = (bf16[2,8,640]{2,1,0:T(8,128)(2,1)S(1)}, bf16[2,8,640]{2,1,0:T(8,128)(2,1)S(1)}, u32[]{:S(2)}, u32[]{:S(2)}) collective-permute-start(bf16[2,8,640]{2,1,0:T(8,128)(2,1)S(1)} %get-tuple-element.170), channel_id=1, source_target_pairs={{0,1},{1,0},{2,3},{3,2},{4,5},{5,4},{6,7},{7,6},{8,9},{9,8},{10,11... | collective-permute-start | bytes 61448 | tf_op jit(solution)/shard_map/ppermute | solution.py:790
  66.1 2.5 %collective-permute-start.15 = (bf16[16,40,640]{2,1,0:T(8,128)(2,1)S(1)}, bf16[16,40,640]{2,1,0:T(8,128)(2,1)S(1)}, u32[]{:S(2)}, u32[]{:S(2)}) collective-permute-start(bf16[16,40,640]{2,1,0:T(8,128)(2,1)S(1)} %get-tuple-element.168), channel_id=1, source_target_pairs={{0,1},{1,0},{2,3},{3,2},{4,5},{5,4},{6,7},{7,6},{8,9},{9,8},{10,11... | collective-permute-start | bytes 2457608 | tf_op jit(solution)/shard_map/ppermute | solution.py:790
  68.8 8.5 %collective-permute-start.17 = (bf16[336,640]{1,0:T(8,128)(2,1)S(1)}, bf16[336,640]{1,0:T(8,128)(2,1)S(1)}, u32[]{:S(2)}, u32[]{:S(2)}) collective-permute-start(bf16[336,640]{1,0:T(8,128)(2,1)S(1)} %get-tuple-element.173), channel_id=1, source_target_pairs={{0,4},{1,3},{2,6},{3,1},{4,0},{5,7},{6,2},{7,5},{8,12},{9,11},{10,... | collective-permute-start | bytes 1290248 | tf_op jit(solution)/shard_map/ppermute | solution.py:790
  70.0 7.3 %collective-permute-start.18 = (bf16[4,40,640]{2,1,0:T(8,128)(2,1)S(1)}, bf16[4,40,640]{2,1,0:T(8,128)(2,1)S(1)}, u32[]{:S(2)}, u32[]{:S(2)}) collective-permute-start(bf16[4,40,640]{2,1,0:T(8,128)(2,1)S(1)} %get-tuple-element.166), channel_id=1, source_target_pairs={{0,8},{1,9},{2,10},{3,11},{4,12},{5,13},{6,14},{7,15},{8,0},{9,1},... | collective-permute-start | bytes 614408 | tf_op jit(solution)/shard_map/ppermute | solution.py:790
  77.4 5.9 %collective-permute-start.19 = (bf16[168,640]{1,0:T(8,128)(2,1)S(1)}, bf16[168,640]{1,0:T(8,128)(2,1)S(1)}, u32[]{:S(2)}, u32[]{:S(2)}) collective-permute-start(bf16[168,640]{1,0:T(8,128)(2,1)S(1)} %get-tuple-element.177), channel_id=1, source_target_pairs={{0,2},{1,5},{2,0},{3,7},{4,6},{5,1},{6,4},{7,3},{8,10},{9,13},{10,... | collective-permute-start | bytes 645128 | tf_op jit(solution)/shard_map/ppermute | solution.py:790
  78.4 7.3 %collective-permute-start.20 = (bf16[2,40,640]{2,1,0:T(8,128)(2,1)S(1)}, bf16[2,40,640]{2,1,0:T(8,128)(2,1)S(1)}, u32[]{:S(2)}, u32[]{:S(2)}) collective-permute-start(bf16[2,40,640]{2,1,0:T(8,128)(2,1)S(1)} %get-tuple-element.182), channel_id=1, source_target_pairs={{0,16},{1,17},{2,18},{3,19},{4,20},{5,21},{6,22},{7,23},{8,24},{9,... | collective-permute-start | bytes 307208 | tf_op jit(solution)/shard_map/ppermute | solution.py:790
  85.7 9.4 %collective-permute-start.21 = (bf16[48,640]{1,0:T(8,128)(2,1)S(1)}, bf16[48,640]{1,0:T(8,128)(2,1)S(1)}, u32[]{:S(2)}, u32[]{:S(2)}) collective-permute-start(bf16[48,640]{1,0:T(8,128)(2,1)S(1)} %get-tuple-element.183), channel_id=1, source_target_pairs={{0,8},{1,9},{2,10},{3,11},{4,12},{5,13},{6,14},{7,15},{8,0},{9,1},... | collective-permute-start | bytes 184328 | tf_op jit(solution)/shard_map/ppermute | solution.py:790
  86.1 9.0 %collective-permute-start.22 = (bf16[48,640]{1,0:T(8,128)(2,1)S(1)}, bf16[48,640]{1,0:T(8,128)(2,1)S(1)}, u32[]{:S(2)}, u32[]{:S(2)}) collective-permute-start(bf16[48,640]{1,0:T(8,128)(2,1)S(1)} %get-tuple-element.184), channel_id=1, source_target_pairs={{0,16},{1,17},{2,18},{3,19},{4,20},{5,21},{6,22},{7,23},{8,24},{9,... | collective-permute-start | bytes 184328 | tf_op jit(solution)/shard_map/ppermute | solution.py:790
  87.7 7.4 %collective-permute-start.23 = (bf16[48,640]{1,0:T(8,128)(2,1)S(1)}, bf16[48,640]{1,0:T(8,128)(2,1)S(1)}, u32[]{:S(2)}, u32[]{:S(2)}) collective-permute-start(bf16[48,640]{1,0:T(8,128)(2,1)S(1)} %get-tuple-element.185), channel_id=1, source_target_pairs={{0,24},{1,25},{2,26},{3,27},{4,28},{5,29},{6,30},{7,31},{8,16},{9,... | collective-permute-start | bytes 184328 | tf_op jit(solution)/shard_map/ppermute | solution.py:790
  90.1 4.2 %collective-permute-start.24 = (bf16[1,40,640]{2,1,0:T(8,128)(2,1)S(1)}, bf16[1,40,640]{2,1,0:T(8,128)(2,1)S(1)}, u32[]{:S(2)}, u32[]{:S(2)}) collective-permute-start(bf16[1,40,640]{2,1,0:T(8,128)(2,1)S(1)} %get-tuple-element.193), channel_id=1, source_target_pairs={{0,2},{1,5},{2,0},{3,7},{4,6},{5,1},{6,4},{7,3},{8,10},{9,13},{10,... | collective-permute-start | bytes 153608 | tf_op jit(solution)/shard_map/ppermute | solution.py:790
  (3 other events, 9.1 us)

commit v5 on v4

--- a/solution.py
+++ b/solution.py
@@ -61,11 +61,10 @@
 
 def mixed_slot(device, me):
     delta = device ^ me
-    plane = [(delta >> 1) & 1, (delta >> 2) & 1]
-    line = [(delta >> 4) & 1, (delta >> 3) & 1]
-    if device & 1:
-        plane = plane[::-1]
-    return plane[1] * 8 + line[1] * 4 + line[0] * 2 + plane[0]
+    x, y = (delta >> 1) & 1, (delta >> 2) & 1
+    odd = (device & 1) == 1
+    first, second = jnp.where(odd, y, x), jnp.where(odd, x, y)
+    return second * 8 + ((delta >> 3) & 1) * 4 + ((delta >> 4) & 1) * 2 + first
 
 
 def normalise(values):
@@ -197,9 +196,9 @@
 
 def attend_kernel(
     tuned,
-    x_ref, n1_ref, chosen_ref, live_ref, own_ref, oth_ref, vec_ref,
+    geo_ref, cot_ref, x_ref, n1_ref, chosen_ref, live_ref, own_ref, oth_ref, vec_ref,
     x2_ref, h1_ref, patch_ref, nk_ref, rk_ref, kn_ref, q_ref, kb_ref, vb_ref,
-    p_ref, o_ref, wr_ref, wq_ref, wkv_ref, wp_ref, mv_ref, hv_ref,
+    p_ref, o_ref, wr_ref, wq_ref, wkv_ref, wp_ref, mv_ref, hv_ref, gy_ref, gyt_ref, mask_ref,
     score_ref,
 ):
     me = my_index(tuned)
@@ -268,10 +267,11 @@
             p_ref[at, lane_at] = e / jnp.sum(e, axis=-1, keepdims=True)
         return carry
 
-    lax.fori_loop(0, capacity // 64, soften, 0)
+    lax.fori_loop(0, capacity // 64, soften, 0, unroll=True)
     o = dot_nn(p_ref[...].astype(BF16), vb_ref[...]).astype(BF16)
     o_ref[...] = o
     x2_ref[...] = x_ref[...] + dot_nt(o, wp_ref[...]) + mv[7:8]
+    mask_gradient(geo_ref, cot_ref, gy_ref, gyt_ref, mask_ref)
 
 
 def one_hot(rows_ref, cols_ref, capacity):
@@ -297,16 +297,8 @@
     )
 
 
-def prepare_two_kernel(
-    geo_ref, cot_ref, x2_ref, mv_ref, n2_ref, r2_ref, h2_ref, h2t_ref, gy_ref, gyt_ref, mask_ref
-):
+def mask_gradient(geo_ref, cot_ref, gy_ref, gyt_ref, mask_ref):
     width, capacity = cot_ref.shape
-    normed, inverse = normalise(x2_ref[...])
-    n2_ref[...] = normed
-    r2_ref[...] = inverse
-    h2 = normed * mv_ref[8:9, :] + mv_ref[9:10, :]
-    h2_ref[...] = h2.astype(BF16)
-    h2t_ref[...] = h2.T.astype(BF16)
     area = geo_ref[0] * geo_ref[2] + geo_ref[1] * geo_ref[3]
     position = lax.broadcasted_iota(jnp.int32, (width, capacity), 1)
     gyt = jnp.where(position < area, cot_ref[...].astype(F32), 0.0)
@@ -314,58 +306,83 @@
     gy_ref[...] = gyt.T.astype(BF16)
     first, second, row, col, heights, widths = token_geometry(geo_ref, capacity, 128)
     live = first | second
+    start = lax.broadcasted_iota(jnp.int32, (capacity, 128), 0) // TILE * TILE
+    late = start >= geo_ref[0] * geo_ref[2]
+    early = jnp.logical_not(late)
+    usual = (late & second) | (early & first)
+    apart = second & early
     conditions = (
         live & (col > 0),
         live & (col < widths - 1),
-        first & (row > 0),
-        second & (row > 0),
-        first & (row < heights - 1),
-        second & (row < heights - 1),
+        usual & (row > 0),
+        usual & (row < heights - 1),
+        apart & (row > 0),
+        apart & (row < heights - 1),
         live,
     )
     for k, condition in enumerate(conditions):
         mask_ref[k] = jnp.where(condition, 1.0, 0.0)
 
 
+def place_pieces(ref, core, me, wu_ref, wd_ref):
+    cw = ref.shape[1]
+    rn = 2 * cw
+    tails = 128 * PARTS_W
+    for x in range(PARTS_N // 2):
+        n = 2 * x + core
+        pieces = [ref[mixed_slot(w * PARTS_N + n, me)].astype(F32) for w in range(PARTS_W)]
+        lane_at = pl.ds(pl.multiple_of(256 * n, 256), 256)
+        for pair in range(PARTS_W // 2):
+            value = rows_of(pieces[2 * pair][:, :256], pieces[2 * pair + 1][:, :256])
+            wd_ref[pl.ds(pair * 2 * cw, 2 * cw), lane_at] = value.astype(BF16)
+        at = pl.ds(pl.multiple_of(rn * n, 16), rn)
+        for w, p in enumerate(pieces):
+            wu_ref[at, pl.ds(128 * w, 128)] = rows_of(p[:, 256:384], p[:, 384:512]).astype(BF16)
+        ends = [rows_of(p[:, 512 + 2 * REST : 512 + 3 * REST], p[:, 512 + 3 * REST :]) for p in pieces]
+        wu_ref[at, pl.ds(tails, REST * PARTS_W)] = lanes(*ends).astype(BF16)
+
+
+def prepare_two_kernel(tuned, x2_ref, mv_ref, own_ref, n2_ref, r2_ref, h2_ref, h2t_ref, wu_ref, wd_ref):
+    me = my_index(tuned)
+    place_pieces(own_ref, me & 1, me, wu_ref, wd_ref)
+    normed, inverse = normalise(x2_ref[...])
+    n2_ref[...] = normed
+    r2_ref[...] = inverse
+    h2 = normed * mv_ref[8:9, :] + mv_ref[9:10, :]
+    h2_ref[...] = h2.astype(BF16)
+    h2t_ref[...] = h2.T.astype(BF16)
+
+
 def ffn_kernel(
     tuned,
-    geo_ref, n2_ref, r2_ref, h2_ref, h2t_ref, gy_ref, gyt_ref, mask_ref, own_ref, oth_ref, mv_ref, hv_ref,
-    gown_ref, gsend_ref, mix_ref, dx2_ref, mg_ref, hg_ref,
-    wu_ref, wd_ref, f_ref, gm_ref, gp_ref, dc_ref, ul_ref, ur_ref, g0_ref, slope_ref, act_ref, u0_ref, df_ref, da_ref,
-    dh2_ref, upg_ref, dng_ref,
+    geo_ref, h2_ref, h2t_ref, gy_ref, gyt_ref, mask_ref, own_ref, oth_ref, hv_ref, wu_in_ref, wd_in_ref,
+    gown_ref, gsend_ref, act_ref, dh2_ref, hg_ref, wu_ref, wd_ref,
+    f_ref, gm_ref, gp_ref, dc_ref, ul_ref, ur_ref, g0_ref, slope_ref, u0_ref, df_ref, da_ref,
+    upg_ref, dng_ref,
 ):
     me = my_index(tuned)
-    capacity, width = n2_ref.shape
+    capacity, width = h2_ref.shape
     hidden = hv_ref.shape[1]
     cw, rn = width // PARTS_W, width // PARTS_N
     tiles = capacity // TILE
     tails = 128 * PARTS_W
 
+    place_pieces(oth_ref, 1 - (me & 1), me, wu_ref, wd_ref)
     for pair in range(PARTS_W // 2):
-        at = pl.ds(pair * 2 * cw, 2 * cw)
         got = [
-            rows_of(*[piece_of(own_ref, oth_ref, w * PARTS_N + n, me, 0, 5, mixed_slot) for w in (2 * pair, 2 * pair + 1)])
+            rows_of(*[piece_of(own_ref, oth_ref, w * PARTS_N + n, me, 4, 5, mixed_slot) for w in (2 * pair, 2 * pair + 1)])
             for n in range(PARTS_N)
         ]
-        for n in range(PARTS_N):
-            wd_ref[at, pl.ds(256 * n, 256)] = got[n][:, :256].astype(BF16)
-        wd_ref[at, pl.ds(tails, 2 * REST * PARTS_N)] = lanes(*[g[:, 512 : 512 + 2 * REST] for g in got]).astype(BF16)
-    for n in range(PARTS_N):
-        at = pl.ds(n * rn, rn)
-        ends = []
-        for w in range(PARTS_W):
-            got = piece_of(own_ref, oth_ref, w * PARTS_N + n, me, 2, 5, mixed_slot)
-            wu_ref[at, pl.ds(128 * w, 128)] = rows_of(got[:, :128], got[:, 128:256]).astype(BF16)
-            ends.append(rows_of(got[:, 256 + 2 * REST : 256 + 3 * REST], got[:, 256 + 3 * REST :]))
-        wu_ref[at, pl.ds(tails, REST * PARTS_W)] = lanes(*ends).astype(BF16)
-
-    w0, w1 = geo_ref[2], geo_ref[3]
+        ends = lanes(*[g[:, : 2 * REST] for g in got]).astype(BF16)
+        wd_ref[pl.ds(pair * 2 * cw, 2 * cw), pl.ds(tails, 2 * REST * PARTS_N)] = ends
+
+    area, w0, w1 = geo_ref[0] * geo_ref[2], geo_ref[2], geo_ref[3]
+    split = pl.multiple_of(jnp.minimum(area // TILE, tiles - 1) * TILE, TILE)
 
     for ref in (f_ref, gm_ref, gp_ref, dc_ref, ul_ref, ur_ref):
         ref[:, :PAD, :] = jnp.zeros((CHUNK // 128, PAD, 128), F32)
         ref[:, PAD + capacity :, :] = jnp.zeros((CHUNK // 128, PAD, 128), F32)
 
-    mix_ref[...] = jnp.zeros_like(mix_ref)
     dh2_ref[...] = jnp.zeros_like(dh2_ref)
 
     def fold(values):
@@ -392,11 +409,8 @@
     def act_grad(c, at):
         da_ref[at, :] = dot_nn(gy_ref[at, :], wd_ref[:, columns(c)])
 
-    def second_layer(c, at):
-        mix_ref[at, :] += dot_nt(act_ref[at, :], wd_ref[:, columns(c)])
-
     def down_grad(c, at):
-        dng_ref[at, columns(c)] = dot_nn(gyt_ref[at, :], act_ref[...])
+        dng_ref[at, columns(c)] = dot_nn(gyt_ref[at, :], act_ref[:, columns(c)])
 
     def up_grad(c, at):
         upg_ref[at, columns(c)] = dot_nn(h2t_ref[at, :], df_ref[...])
@@ -420,86 +434,114 @@
         following = jnp.minimum(c + 1, chunks - 1)
         v = [[vector(c, k, j) for k in range(11)] for j in range(halves)]
 
-        def taps_of(j, r, at):
+        def taps_of(j, r, mask_left, mask_right):
             here = f_ref[j, pl.ds(PAD + r, TILE), :]
-            left = f_ref[j, pl.ds(PAD + r - 1, TILE), :] * mask_ref[0, at, :]
-            right = f_ref[j, pl.ds(PAD + r + 1, TILE), :] * mask_ref[1, at, :]
+            left = f_ref[j, pl.ds(PAD + r - 1, TILE), :] * mask_left
+            right = f_ref[j, pl.ds(PAD + r + 1, TILE), :] * mask_right
             return left, here, right
 
-        def column_taps(r, j):
+        def row_length(r):
+            return jnp.where(area > r, w0, w1)
+
+        def column_taps(r):
             at = pl.ds(r, TILE)
-            left, here, right = taps_of(j, r, at)
-            u = v[j]
-            gm_ref[j, pl.ds(PAD + r, TILE), :] = u[2] * left + u[3] * here + u[4] * right
-            g0_ref[j, at, :] = u[1] + u[5] * left + u[6] * here + u[7] * right
-            gp_ref[j, pl.ds(PAD + r, TILE), :] = u[8] * left + u[9] * here + u[10] * right
-
-        def activate(r, j):
+            masks = mask_ref[0, at, :], mask_ref[1, at, :]
+            for j in range(halves):
+                left, here, right = taps_of(j, r, *masks)
+                u = v[j]
+                gm_ref[j, pl.ds(PAD + r, TILE), :] = u[2] * left + u[3] * here + u[4] * right
+                g0_ref[j, at, :] = u[1] + u[5] * left + u[6] * here + u[7] * right
+                gp_ref[j, pl.ds(PAD + r, TILE), :] = u[8] * left + u[9] * here + u[10] * right
+
+        def column_taps_split():
+            at = pl.ds(split, TILE)
+            for j in range(halves):
+                g0_ref[j, at, :] += (
+                    mask_ref[4, at, :] * gm_ref[j, pl.ds(PAD + split - w1, TILE), :]
+                    + mask_ref[5, at, :] * gp_ref[j, pl.ds(PAD + split + w1, TILE), :]
+                )
+
+        def activate(r):
             at = pl.ds(r, TILE)
-            conv = (
-                g0_ref[j, at, :]
-                + mask_ref[2, at, :] * gm_ref[j, pl.ds(PAD + r - w0, TILE), :]
-                + mask_ref[3, at, :] * gm_ref[j, pl.ds(PAD + r - w1, TILE), :]
-                + mask_ref[4, at, :] * gp_ref[j, pl.ds(PAD + r + w0, TILE), :]
-                + mask_ref[5, at, :] * gp_ref[j, pl.ds(PAD + r + w1, TILE), :]
-            )
-            half = 0.5 * (1.0 + lax.erf(conv * 2.0 ** (-0.5)))
-            lane_at = pl.ds(j * 128, 128)
-            act_ref[at, lane_at] = (conv * half).astype(BF16)
-            slope_ref[at, lane_at] = half + conv * jnp.exp(-0.5 * conv * conv) * (2.0 * math.pi) ** (-0.5)
+            length = row_length(r)
+            above, below = mask_ref[2, at, :], mask_ref[3, at, :]
+            for j in range(halves):
+                conv = (
+                    g0_ref[j, at, :]
+                    + above * gm_ref[j, pl.ds(PAD + r - length, TILE), :]
+                    + below * gp_ref[j, pl.ds(PAD + r + length, TILE), :]
+                )
+                half = 0.5 * (1.0 + lax.erf(conv * 2.0 ** (-0.5)))
+                act_ref[at, pl.ds(pl.multiple_of(c * CHUNK + j * 128, 128), 128)] = (conv * half).astype(BF16)
+                slope_ref[at, pl.ds(j * 128, 128)] = half + conv * jnp.exp(-0.5 * conv * conv) * (2.0 * math.pi) ** (-0.5)
 
         conv_sums = [zero] * halves
 
-        def into_conv(r, j):
-            at, lane_at = pl.ds(r, TILE), pl.ds(j * 128, 128)
-            value = da_ref[at, lane_at] * slope_ref[at, lane_at]
-            dc_ref[j, pl.ds(PAD + r, TILE), :] = value
-            conv_sums[j] = conv_sums[j] + fold(value)
+        def into_conv(r):
+            at = pl.ds(r, TILE)
+            for j in range(halves):
+                lane_at = pl.ds(j * 128, 128)
+                value = da_ref[at, lane_at] * slope_ref[at, lane_at]
+                dc_ref[j, pl.ds(PAD + r, TILE), :] = value
+                conv_sums[j] = conv_sums[j] + fold(value)
 
         tap_sums = [[zero] * 9 for _ in range(halves)]
 
-        def tap_back(r, j):
+        def tap_back(r):
             at = pl.ds(r, TILE)
-            left, here, right = taps_of(j, r, at)
-            u = v[j]
-            below = (
-                mask_ref[4, at, :] * dc_ref[j, pl.ds(PAD + r + w0, TILE), :]
-                + mask_ref[5, at, :] * dc_ref[j, pl.ds(PAD + r + w1, TILE), :]
-            )
-            level = dc_ref[j, pl.ds(PAD + r, TILE), :]
-            above = (
-                mask_ref[2, at, :] * dc_ref[j, pl.ds(PAD + r - w0, TILE), :]
-                + mask_ref[3, at, :] * dc_ref[j, pl.ds(PAD + r - w1, TILE), :]
-            )
-            ul_ref[j, pl.ds(PAD + r, TILE), :] = u[2] * below + u[5] * level + u[8] * above
-            u0_ref[j, at, :] = u[3] * below + u[6] * level + u[9] * above
-            ur_ref[j, pl.ds(PAD + r, TILE), :] = u[4] * below + u[7] * level + u[10] * above
-            grads = [fold(d * f) for d in (below, level, above) for f in (left, here, right)]
-            tap_sums[j] = [a + b for a, b in zip(tap_sums[j], grads)]
+            length = row_length(r)
+            masks = [mask_ref[k, at, :] for k in range(4)]
+            for j in range(halves):
+                left, here, right = taps_of(j, r, *masks[:2])
+                u = v[j]
+                below = masks[3] * dc_ref[j, pl.ds(PAD + r + length, TILE), :]
+                level = dc_ref[j, pl.ds(PAD + r, TILE), :]
+                above = masks[2] * dc_ref[j, pl.ds(PAD + r - length, TILE), :]
+                ul_ref[j, pl.ds(PAD + r, TILE), :] = u[2] * below + u[5] * level + u[8] * above
+                u0_ref[j, at, :] = u[3] * below + u[6] * level + u[9] * above
+                ur_ref[j, pl.ds(PAD + r, TILE), :] = u[4] * below + u[7] * level + u[10] * above
+                grads = [fold(d * f) for d in (below, level, above) for f in (left, here, right)]
+                tap_sums[j] = [a + b for a, b in zip(tap_sums[j], grads)]
+
+        def tap_back_split():
+            at, padded = pl.ds(split, TILE), pl.ds(PAD + split, TILE)
+            masks = [mask_ref[k, at, :] for k in (0, 1, 4, 5)]
+            for j in range(halves):
+                left, here, right = taps_of(j, split, *masks[:2])
+                u = v[j]
+                below = masks[3] * dc_ref[j, pl.ds(PAD + split + w1, TILE), :]
+                above = masks[2] * dc_ref[j, pl.ds(PAD + split - w1, TILE), :]
+                ul_ref[j, padded, :] += u[2] * below + u[8] * above
+                u0_ref[j, at, :] += u[3] * below + u[9] * above
+                ur_ref[j, padded, :] += u[4] * below + u[10] * above
+                grads = [fold(d * f) for d in (below, above) for f in (left, here, right)]
+                tap_sums[j] = [a + b for a, b in zip(tap_sums[j], grads[:3] + [zero] * 3 + grads[3:])]
 
         up_sums = [zero] * halves
 
-        def spread_back(r, j):
+        def spread_back(r):
             at = pl.ds(r, TILE)
-            value = (
-                u0_ref[j, at, :]
-                + mask_ref[0, at, :] * ur_ref[j, pl.ds(PAD + r - 1, TILE), :]
-                + mask_ref[1, at, :] * ul_ref[j, pl.ds(PAD + r + 1, TILE), :]
-            ).astype(BF16)
-            df_ref[at, pl.ds(j * 128, 128)] = value
-            up_sums[j] = up_sums[j] + fold(value.astype(F32))
+            mask_left, mask_right = mask_ref[0, at, :], mask_ref[1, at, :]
+            for j in range(halves):
+                value = (
+                    u0_ref[j, at, :]
+                    + mask_left * ur_ref[j, pl.ds(PAD + r - 1, TILE), :]
+                    + mask_right * ul_ref[j, pl.ds(PAD + r + 1, TILE), :]
+                ).astype(BF16)
+                df_ref[at, pl.ds(j * 128, 128)] = value
+                up_sums[j] = up_sums[j] + fold(value.astype(F32))
 
         def steps(step):
-            return [functools.partial(step, r, j) for j in range(halves) for r in range(0, capacity, TILE)]
+            return [functools.partial(step, r) for r in range(0, capacity, TILE)]
 
         interleave(
-            steps(column_taps) + steps(activate),
+            steps(column_taps) + [column_taps_split] + steps(activate),
             tasks(act_grad, c, capacity, MROWS) + tasks(up_grad, before, width, MROWS)
             + tasks(h2_grad, before, capacity, MROWS),
         )
         interleave(
-            steps(into_conv) + steps(tap_back),
-            tasks(second_layer, c, capacity, MROWS) + tasks(down_grad, c, width, MROWS),
+            steps(into_conv) + steps(tap_back) + [tap_back_split],
+            tasks(down_grad, c, width, MROWS),
         )
         interleave(steps(spread_back), tasks(first_layer, following, capacity, MROWS))
         for j in range(halves):
@@ -528,19 +570,6 @@
 
     store_pieces(gown_ref, gsend_ref, me, value_of, mixed_slot)
 
-    def finish(i, carry):
-        at = pl.ds(pl.multiple_of(i * 64, 64), 64)
-        gy = gy_ref[at, :].astype(F32)
-        grad, normed = dh2_ref[at, :], n2_ref[at, :]
-        dx2_ref[at, :] = gy + normalise_back(grad, normed, r2_ref[at, :], mv_ref[8:9, :])
-        return tuple(a + column_sum(b) for a, b in zip(carry, (grad * normed, grad, gy)))
-
-    zero = jnp.zeros((1, width), F32)
-    sums = lax.fori_loop(0, capacity // 64, finish, (zero, zero, zero))
-    mg_ref[...] = jnp.zeros_like(mg_ref)
-    for k in range(3):
-        mg_ref[8 + k : 9 + k, :] = sums[k]
-
 
 def store_pieces(own_ref, send_ref, me, value_of, order):
     even = (me & 1) == 0
@@ -552,9 +581,27 @@
             send_ref[jnp.where(even, slot1, slot0)] = jnp.where(even, second, first).astype(BF16)
 
 
-def score_back_kernel(dx2_ref, vb_ref, p_ref, o_ref, wp_ref, gp_ref, dob_ref, ds_ref, bp_ref, dp_ref):
-    capacity = dx2_ref.shape[0]
+def score_back_kernel(
+    dh2_ref, n2_ref, r2_ref, gy_ref, mv_ref, vb_ref, p_ref, o_ref, wp_ref,
+    gp_ref, dob_ref, ds_ref, bp_ref, dx2_ref, mg_ref,
+    dp_ref,
+):
+    capacity, width = dh2_ref.shape
     keys = capacity // 4
+
+    def norm_back(i, carry):
+        at = pl.ds(pl.multiple_of(i * 64, 64), 64)
+        gy = gy_ref[at, :].astype(F32)
+        grad, normed = dh2_ref[at, :], n2_ref[at, :]
+        dx2_ref[at, :] = gy + normalise_back(grad, normed, r2_ref[at, :], mv_ref[8:9, :])
+        return tuple(a + column_sum(b) for a, b in zip(carry, (grad * normed, grad, gy)))
+
+    zero = jnp.zeros((1, width), F32)
+    sums = lax.fori_loop(0, capacity // 64, norm_back, (zero, zero, zero), unroll=True)
+    mg_ref[...] = jnp.zeros_like(mg_ref)
+    for k in range(3):
+        mg_ref[8 + k : 9 + k, :] = sums[k]
+
     datt = dx2_ref[...].astype(BF16)
     bp_ref[...] = column_sum(datt.astype(F32))
     gp_ref[...] = dot_tn(datt, o_ref[...])
@@ -572,7 +619,7 @@
             ds_ref[at, lane_at] = (p * (dp - row)).astype(BF16)
         return carry
 
-    lax.fori_loop(0, capacity // 64, soften_back, 0)
+    lax.fori_loop(0, capacity // 64, soften_back, 0, unroll=True)
 
 
 def attend_back_kernel(
@@ -636,6 +683,14 @@
     store_pieces(gown_ref, gsend_ref, me, value_of, round_slot)
 
 
+def mixed_kernel(x2_ref, act_ref, wd_ref, mv_ref, mask_ref, mixed_ref):
+    width = x2_ref.shape[1]
+    occupied = mask_ref[6]
+    occupied = lanes(*([occupied] * (width // 128)), occupied[:, : width % 128])
+    mixed = x2_ref[...] + dot_nt(act_ref[...], wd_ref[...]) + mv_ref[10:11, :]
+    mixed_ref[...] = (mixed * occupied).T.astype(BF16)
+
+
 def fold_rows(value, unit):
     rest = value[8:]
     beside = lanes(rest[:, : 3 * unit], jnp.zeros((8, 256 - 3 * unit), F32))
@@ -652,15 +707,11 @@
 def token_back_kernel(
     tuned,
     dx2_ref, dq_ref, dpatch_ref, n1_ref, r1_ref, chosen_ref, wq_ref, mv_ref, mg_ref, hg_ref, vk_ref, bp_ref,
-    x2_ref, mix_ref, mask_ref,
-    mixed_ref, tg_ref, vown_ref, vsend_ref,
+    tg_ref, vown_ref, vsend_ref,
 ):
     me = my_index(tuned)
     capacity, width = dx2_ref.shape
     rn = width // PARTS_N
-    occupied = mask_ref[6]
-    occupied = lanes(*([occupied] * (width // 128)), occupied[:, : width % 128])
-    mixed_ref[...] = ((x2_ref[...] + mix_ref[...] + mv_ref[10:11, :]) * occupied).T.astype(BF16)
     chosen = chosen_ref[...]
     high = dpatch_ref[...].astype(BF16)
     low = (dpatch_ref[...] - high.astype(F32)).astype(BF16)
@@ -729,16 +780,10 @@
         ref[...] = rows_of(keep_ref[k].astype(F32) + got[k * cw : (k + 1) * cw], vector).astype(BF16)
 
 
-def finish_ffn_kernel(a_ref, b_ref, up_ref, down_ref):
-    total = total_of((a_ref, b_ref))[0]
-    columns = [
-        lanes(total[:, 128 * k : 128 * (k + 1)], total[:, 512 + REST * k : 512 + REST * (k + 1)]) for k in range(4)
-    ]
-    down_ref[...] = lanes(*columns[:2])
-    up_ref[...] = rows_of(*columns[2:])
-
-
-def finish_attend_kernel(a_ref, b_ref, c_ref, d_ref, q_ref, kv_ref, red_ref, proj_ref, vm_ref, vh_ref):
+def finish_kernel(
+    a_ref, b_ref, c_ref, d_ref, ffn_ref, ffn_got_ref,
+    q_ref, kv_ref, red_ref, proj_ref, up_ref, down_ref, vm_ref, vh_ref,
+):
     total = total_of((a_ref, b_ref, c_ref, d_ref))
     cw, width = red_ref.shape
     rn = q_ref.shape[1]
@@ -750,9 +795,15 @@
     vector = unfold_rows(total[cw:], rn)
     vm_ref[...] = vector[: vm_ref.shape[0], :rn]
     vh_ref[...] = vector[: vh_ref.shape[0], rn:]
-
-
-def call(kernel, inputs, outputs, scratch=(), scalars=0, limit=40, flops=0, moved=0):
+    total = total_of((ffn_ref, ffn_got_ref))[0]
+    columns = [
+        lanes(total[:, 128 * k : 128 * (k + 1)], total[:, 512 + REST * k : 512 + REST * (k + 1)]) for k in range(4)
+    ]
+    down_ref[...] = lanes(*columns[:2])
+    up_ref[...] = rows_of(*columns[2:])
+
+
+def call(kernel, inputs, outputs, scratch=(), scalars=0, limit=40, flops=0, moved=0, aliases={}):
     vmem = pl.BlockSpec(memory_space=pltpu.VMEM)
     smem = pl.BlockSpec(memory_space=pltpu.SMEM)
     return pl.pallas_call(
@@ -761,6 +812,7 @@
         in_specs=[smem] * scalars + [vmem] * (len(inputs) - scalars),
         out_specs=[vmem] * len(outputs),
         scratch_shapes=[pltpu.VMEM(shape, kind) for shape, kind in scratch],
+        input_output_aliases=aliases,
         compiler_params=pltpu.CompilerParams(vmem_limit_bytes=limit * 2**20),
         cost_estimate=pl.CostEstimate(flops=flops, bytes_accessed=moved, transcendentals=0),
     )(*inputs)
@@ -784,6 +836,9 @@
     piece = (cw, 2 * width)
     vpiece, gpiece = (16, 2 * width), (8, 2 * width)
 
+    def join(*parts):
+        return jnp.concatenate(parts, axis=0)
+
     def swap(value, mask, other=None):
         masks = (mask, mask if other is None else other)
         pairs = [(i, i ^ masks[i & 1]) for i in range(wide * narrow)]
@@ -800,9 +855,6 @@
             ),
             piece, vpiece,
         )
-        def join(*parts):
-            return jnp.concatenate(parts, axis=0)
-
         line_a = [swap(pack_a, m) for m in (8, 16, 24)]
         got_b, got_v = swap(pack_b, 2, 4), swap(pack_v, 1)
         *line_a, got_b, got_v = lax.optimization_barrier((*line_a, got_b, got_v, x, n1, chosen))[:5]
@@ -819,10 +871,10 @@
 
     square = (width, width)
     (
-        x2, h1, patches, nk, rk, kn, q, kb, vb, p, o, wr, wq, wkv, wp, mv, hv,
+        x2, h1, patches, nk, rk, kn, q, kb, vb, p, o, wr, wq, wkv, wp, mv, hv, gy, gyt, masks,
     ) = call(
         functools.partial(attend_kernel, tuned),
-        (x, n1, chosen, live, own_a, oth_a, vecs),
+        (geo, cotangent.T, x, n1, chosen, live, own_a, oth_a, vecs),
         (
             tokens_f32, tokens_low,
             ((capacity, width), BF16), ((keys, width), F32), ((keys, 1), F32), ((keys, width), BF16),
@@ -830,39 +882,41 @@
             ((capacity, HEADS * keys), F32), ((capacity, width), BF16),
             ((4,) + square, BF16), (square, BF16), ((2 * width, width), BF16), (square, BF16),
             ((16, width), F32), ((16, hidden), F32),
+            tokens_low, ((width, capacity), BF16), ((7, capacity, 128), F32),
         ),
         scratch=(((capacity, HEADS * keys), F32),),
+        scalars=1,
         flops=8 * 10**9,
     )
 
     if tuned:
-        own_b = jnp.concatenate([half_b, after(rest_b, x2)], axis=0)
+        own_b = join(half_b, after(rest_b, x2))
         oth_b = swap(own_b, 1)
     padded = ((CHUNK // 128, capacity + 2 * PAD, 128), F32)
     halved = ((CHUNK // 128, capacity, 128), F32)
     chunked = ((capacity, CHUNK), F32)
-    n2, r2, h2, h2t, gy, gyt, masks = call(
-        prepare_two_kernel,
-        (geo, cotangent.T, x2, mv),
+    n2, r2, h2, h2t, wu, wd = call(
+        functools.partial(prepare_two_kernel, tuned),
+        (x2, mv, own_b),
         (
             tokens_f32, ((capacity, 1), F32), tokens_low, ((width, capacity), BF16),
-            tokens_low, ((width, capacity), BF16), ((7, capacity, 128), F32),
+            ((width, hidden), BF16), ((width, hidden), BF16),
         ),
-        scalars=1,
-        flops=2 * 10**9,
-    )
-    gown_b, gsend_b, mix, dx2, mg, hg = call(
+        flops=10**9,
+    )
+    gown_b, gsend_b, act, dh2, hg, wu, wd = call(
         functools.partial(ffn_kernel, tuned),
-        (geo, n2, r2, h2, h2t, gy, gyt, masks, own_b, oth_b, mv, hv),
+        (geo, h2, h2t, gy, gyt, masks, own_b, oth_b, hv, wu, wd),
         (
             ((SLOTS,) + piece, BF16), ((SLOTS,) + piece, BF16),
-            tokens_f32, tokens_f32, ((16, width), F32), ((16, hidden), F32),
+            ((capacity, hidden), BF16), tokens_f32, ((16, hidden), F32),
+            ((width, hidden), BF16), ((width, hidden), BF16),
         ),
+        aliases={9: 5, 10: 6},
         scratch=(
-            ((width, hidden), BF16), ((width, hidden), BF16),
             padded, padded, padded, padded, padded, padded,
-            halved, chunked, ((capacity, CHUNK), BF16), halved, ((capacity, CHUNK), BF16), chunked,
-            tokens_f32, ((width, hidden), F32), ((width, hidden), F32),
+            halved, chunked, halved, ((capacity, CHUNK), BF16), chunked,
+            ((width, hidden), F32), ((width, hidden), F32),
         ),
         scalars=1,
         flops=33 * 10**9,
@@ -870,11 +924,12 @@
 
     if tuned:
         got_b = swap(gsend_b, 1)
-    gp, dob, ds, bp = call(
+    gp, dob, ds, bp, dx2, mg = call(
         score_back_kernel,
-        (dx2, vb, p, o, wp),
+        (dh2, n2, r2, gy, mv, vb, p, o, wp),
         (
             (square, F32), ((capacity, width), BF16), ((capacity, HEADS * keys), BF16), ((1, width), F32),
+            tokens_f32, ((16, width), F32),
         ),
         scratch=(((capacity, HEADS * keys), F32),),
         flops=25 * 10**8,
@@ -900,12 +955,13 @@
     )
     if tuned:
         got_a = swap(gsend_a, 1)
-        low_b, high_b = halve(low_b, got_b, flops=2 * 10**10)
+        low_b, high_b = halve(low_b, got_b, flops=7 * 10**9)
         gown_a = after(gown_a, high_b)
-    mixed, token_grad, vown, vsend = call(
+    (mixed,) = call(mixed_kernel, (x2, act, wd, mv, masks), (((width, capacity), BF16),), flops=10**9)
+    token_grad, vown, vsend = call(
         functools.partial(token_back_kernel, tuned),
-        (dx2, dq, dpatch, n1, r1, chosen, wq, mv, mg, hg, vk, bp, x2, mix, masks),
-        (((width, capacity), BF16), ((width, capacity), BF16), ((2,) + gpiece, BF16), ((2,) + gpiece, BF16)),
+        (dx2, dq, dpatch, n1, r1, chosen, wq, mv, mg, hg, vk, bp),
+        (((width, capacity), BF16), ((2,) + gpiece, BF16), ((2,) + gpiece, BF16)),
     )
 
     if not tuned:
@@ -918,7 +974,7 @@
         (gown_a, got_a, vown, swap(vsend, 1)),
         (((8,) + piece, BF16), ((2,) + gpiece, BF16), ((8 * cw + 2 * vrows, 2 * width), BF16)),
     )
-    got_a, got_b = lax.optimization_barrier((swap(high_a, 4, 2), swap(high_b, 8)))
+    got_a, got_b, mixed = lax.optimization_barrier((swap(high_a, 4, 2), swap(high_b, 8), mixed))
     low_a, vlow, high_a = call(
         functools.partial(halve_round_kernel, tuned),
         (low_a, vlow, got_a),
@@ -927,18 +983,14 @@
     low_b, high_b = halve(low_b, got_b)
     got_a, got_b = swap(high_a, 2, 4), swap(high_b, 16)
     near_a = list(call(quarter_vector_kernel, (low_a, vlow, got_a), (((cw + vrows, 2 * width), BF16),) * 4))
-    near_a[1], got_b = lax.optimization_barrier((near_a[1], got_b))
     line_a = [swap(near_a[k], 8 * k) for k in (1, 2, 3)]
     low_b, high_b = halve(low_b, got_b)
-    up_grad, down_grad = call(
-        finish_ffn_kernel, (low_b, swap(high_b, 2, 4)), (((rn, 4 * cw), F32), ((cw, width), F32))
-    )
-    q_grad, kv_grad, reduce_grad, proj_grad, vm_grad, vh_grad = call(
-        finish_attend_kernel,
-        (near_a[0], *line_a),
+    q_grad, kv_grad, reduce_grad, proj_grad, up_grad, down_grad, vm_grad, vh_grad = call(
+        finish_kernel,
+        (near_a[0], *line_a, low_b, swap(high_b, 2, 4)),
         (
             ((cw, rn), F32), ((rn, 2 * cw), F32), ((cw, width), F32), ((cw, rn), F32),
-            ((11, rn), F32), ((11, width), F32),
+            ((rn, 4 * cw), F32), ((cw, width), F32), ((11, rn), F32), ((11, width), F32),
         ),
     )
     return (

time: 96.4 us -> 88.5 us (0.918)
  waiting for transfers between devices: 27.3 us -> 21.5 us
  Pallas kernels: 37.9 us -> 33.5 us
  starting transfers between devices: 29.3 us -> 31.7 us
    ppermute x25, waiting for transfers between devices: 27.3 us -> 21.5 us  [swap(): return lax.ppermute(value, ('wide', 'narrow'), pairs)]
    pallas_call x15, Pallas kernels: 33.1 us -> 28.7 us  [call(): pl.pallas_call(kernel, out_shape=[jax.ShapeDtypeStruct(shape, kind) for s...]
    ppermute x25, starting transfers between devices: 29.3 us -> 31.7 us  [swap(): return lax.ppermute(value, ('wide', 'narrow'), pairs)]
where the time goes in v5:
time: 88.5 us; the launch traced here: 88.2 us
  Pallas kernels  33.5 us (38%)
  starting transfers between devices  31.7 us (36%)
  waiting for transfers between devices  21.5 us (24%)
  between operations  0.99 us (1%)
    ppermute x25, starting transfers between devices, swap(): return lax.ppermute(value, ('wide', 'narrow'), pairs)  31.7 us
    pallas_call x15, Pallas kernels, call(): pl.pallas_call(kernel, out_shape=[jax.ShapeDtypeStruct(shape, kind) for s...  28.7 us
    ppermute x25, waiting for transfers between devices, swap(): return lax.ppermute(value, ('wide', 'narrow'), pairs)  21.5 us
    pallas_call x1, Pallas kernels, prepare(): pl.pallas_call(prepare_kernel, out_shape=[jax.ShapeDtypeStruct(shape, kin...  3.1 us
  transfers between devices with their start and end apart: 25, of which 12 were waited for; matrix products, arithmetic and copies ran while one was open for 0% of the time, Pallas kernels for 19%

profile of v5, /device:TPU:0, one launch (start us, length us, event | category | flops | bytes accessed | tf_op | source)
XLA Modules:
  0.0 88.2 jit_solution(12895236015787810221)
XLA Ops:
  0.6 1.7 %shard_map.196 = (bf16[1,40,640]{2,1,0:T(8,128)(2,1)}, bf16[1,40,640]{2,1,0:T(8,128)(2,1)}, bf16[1,16,640]{2,1,0:T(8,128)(2,1)}) custom-call(bf16[40,80]{1,0:T(8,128)(2,1)} %bitcast.16, bf16[80,80]{1,0:T(8,128)(2,1)} %refs_1_.1, bf16[40,320]{1,0:T(8,128)(2,1)} %bitcast.14, bf16[40,80]{1,0:T(8,128)(2,1)} %bitcast.17, bf16[80,160]{1,0:T(8,128)(2,1)} %refs_4_.1, ...), custom_call_target="tpu_custom_call" | custom-call | tf_op jit(solution)/shard_map/pallas_call | solution.py:133
  2.4 5.1 %collective-permute-start.2 = (bf16[1,40,640]{2,1,0:T(8,128)(2,1)}, bf16[1,40,640]{2,1,0:T(8,128)(2,1)S(1)}, u32[]{:S(2)}, u32[]{:S(2)}) collective-permute-start(bf16[1,40,640]{2,1,0:T(8,128)(2,1)} %get-tuple-element.111), channel_id=1, source_target_pairs={{0,24},{1,25},{2,26},{3,27},{4,28},{5,29},{6,30},{7,31},{8,16},{9,... | collective-permute-start | bytes 153608 | tf_op jit(solution)/shard_map/ppermute | solution.py:845
  8.1 1.6 %collective-permute-start.3 = (bf16[1,40,640]{2,1,0:T(8,128)(2,1)}, bf16[1,40,640]{2,1,0:T(8,128)(2,1)S(1)}, u32[]{:S(2)}, u32[]{:S(2)}) collective-permute-start(bf16[1,40,640]{2,1,0:T(8,128)(2,1)} %get-tuple-element.112), channel_id=1, source_target_pairs={{0,2},{1,5},{2,0},{3,7},{4,6},{5,1},{6,4},{7,3},{8,10},{9,13},{10,... | collective-permute-start | bytes 153608 | tf_op jit(solution)/shard_map/ppermute | solution.py:845
  9.8 3.1 %shard_map.195 = (f32[512,320]{1,0:T(8,128)}, f32[512,320]{1,0:T(8,128)}, f32[512,1]{1,0:T(8,128)}, bf16[512,512]{1,0:T(8,128)(2,1)}, f32[512,128]{1,0:T(8,128)}, /*index=5*/s32[4]{0:T(128)}) custom-call(s32[2]{0:T(128)} %rows_hbm.1, s32[2]{0:T(128)} %cols_hbm.1, bf16[320,512]{1,0:T(8,128)(2,1)} %bitcast.18), custom_call_target="tpu_custom_call" | custom-call | flops 2000000000 | tf_op jit(solution)/shard_map/pallas_call | solution.py:183
  13.0 2.2 %collective-permute-start.7 = (bf16[2,40,640]{2,1,0:T(8,128)(2,1)S(1)}, bf16[2,40,640]{2,1,0:T(8,128)(2,1)S(1)}, u32[]{:S(2)}, u32[]{:S(2)}) collective-permute-start(bf16[2,40,640]{2,1,0:T(8,128)(2,1)S(1)} %pad_maximum_fusion.3), channel_id=1, source_target_pairs={{0,16},{1,17},{2,18},{3,19},{4,20},{5,21},{6,22},{7,23},{8,24},{9,... | collective-permute-start | bytes 307208 | tf_op jit(solution)/shard_map/ppermute | solution.py:845
  15.2 1.2 %collective-permute-start.5 = (bf16[4,40,640]{2,1,0:T(8,128)(2,1)S(1)}, bf16[4,40,640]{2,1,0:T(8,128)(2,1)S(1)}, u32[]{:S(2)}, u32[]{:S(2)}) collective-permute-start(bf16[4,40,640]{2,1,0:T(8,128)(2,1)S(1)} %pad_maximum_fusion.1), channel_id=1, source_target_pairs={{0,2},{1,5},{2,0},{3,7},{4,6},{5,1},{6,4},{7,3},{8,10},{9,13},{10,... | collective-permute-start | bytes 614408 | tf_op jit(solution)/shard_map/ppermute | solution.py:845
  16.5 4.6 %collective-permute-done.5 = bf16[4,40,640]{2,1,0:T(8,128)(2,1)S(1)} collective-permute-done((bf16[4,40,640]{2,1,0:T(8,128)(2,1)S(1)}, bf16[4,40,640]{2,1,0:T(8,128)(2,1)S(1)}, u32[]{:S(2)}, u32[]{:S(2)}) %collective-permute-start.5) | collective-permute-done | bytes 204832 | tf_op jit(solution)/shard_map/ppermute | solution.py:845
  21.1 1.6 %collective-permute-start.6 = (bf16[8,40,640]{2,1,0:T(8,128)(2,1)S(1)}, bf16[8,40,640]{2,1,0:T(8,128)(2,1)S(1)}, u32[]{:S(2)}, u32[]{:S(2)}) collective-permute-start(bf16[8,40,640]{2,1,0:T(8,128)(2,1)S(1)} %get-tuple-element.202), channel_id=1, source_target_pairs={{0,4},{1,3},{2,6},{3,1},{4,0},{5,7},{6,2},{7,5},{8,12},{9,11},{10,... | collective-permute-start | bytes 1228808 | tf_op jit(solution)/shard_map/ppermute | solution.py:845
  22.7 2.1 %collective-permute-start.8 = (bf16[4,40,640]{2,1,0:T(8,128)(2,1)S(1)}, bf16[4,40,640]{2,1,0:T(8,128)(2,1)S(1)}, u32[]{:S(2)}, u32[]{:S(2)}) collective-permute-start(bf16[4,40,640]{2,1,0:T(8,128)(2,1)S(1)} %pad_maximum_fusion.2), channel_id=1, source_target_pairs={{0,8},{1,9},{2,10},{3,11},{4,12},{5,13},{6,14},{7,15},{8,0},{9,1},... | collective-permute-start | bytes 614408 | tf_op jit(solution)/shard_map/ppermute | solution.py:845
  24.9 1.2 %collective-permute-start.9 = (bf16[2,16,640]{2,1,0:T(8,128)(2,1)S(1)}, bf16[2,16,640]{2,1,0:T(8,128)(2,1)S(1)}, u32[]{:S(2)}, u32[]{:S(2)}) collective-permute-start(bf16[2,16,640]{2,1,0:T(8,128)(2,1)S(1)} %pad_maximum_fusion.5), channel_id=1, source_target_pairs={{0,2},{1,3},{2,0},{3,1},{4,6},{5,7},{6,4},{7,5},{8,10},{9,11},{10,... | collective-permute-start | bytes 122888 | tf_op jit(solution)/shard_map/ppermute | solution.py:845
  26.0 2.9 %collective-permute-done.9 = bf16[2,16,640]{2,1,0:T(8,128)(2,1)S(1)} collective-permute-done((bf16[2,16,640]{2,1,0:T(8,128)(2,1)S(1)}, bf16[2,16,640]{2,1,0:T(8,128)(2,1)S(1)}, u32[]{:S(2)}, u32[]{:S(2)}) %collective-permute-start.9) | collective-permute-done | bytes 40992 | tf_op jit(solution)/shard_map/ppermute | solution.py:845
  29.4 1.6 %collective-permute-start.11 = (bf16[8,40,640]{2,1,0:T(8,128)(2,1)S(1)}, bf16[8,40,640]{2,1,0:T(8,128)(2,1)S(1)}, u32[]{:S(2)}, u32[]{:S(2)}) collective-permute-start(bf16[8,40,640]{2,1,0:T(8,128)(2,1)S(1)} %pad_maximum_fusion), channel_id=1, source_target_pairs={{0,4},{1,3},{2,6},{3,1},{4,0},{5,7},{6,2},{7,5},{8,12},{9,11},{10,... | collective-permute-start | bytes 1228808 | tf_op jit(solution)/shard_map/ppermute | solution.py:845
  31.7 4.8 %shard_map.197 = (f32[512,320]{1,0:T(8,128)S(1)}, bf16[512,320]{1,0:T(8,128)(2,1)S(1)}, bf16[512,320]{1,0:T(8,128)(2,1)S(1)}, f32[128,320]{1,0:T(8,128)S(1)}, f3...) custom-call(s32[4]{0:T(128)S(1)} %copy-done.6, ...), custom_call_target="tpu_custom_call" | custom-call | flops 8000000000 | tf_op jit(solution)/shard_map/pallas_call | solution.py:809
  36.5 1.0 %collective-permute-done.11 = bf16[8,40,640]{2,1,0:T(8,128)(2,1)S(1)} collective-permute-done((bf16[8,40,640]{2,1,0:T(8,128)(2,1)S(1)}, bf16[8,40,640]{2,1,0:T(8,128)(2,1)S(1)}, u32[]{:S(2)}, u32[]{:S(2)}) %collective-permute-start.11) | collective-permute-done | bytes 409632 | tf_op jit(solution)/shard_map/ppermute | solution.py:845
  38.2 1.7 %collective-permute-done.12.oth_ref = bf16[16,40,640]{2,1,0:T(8,128)(2,1)S(1)} collective-permute-done((bf16[16,40,640]{2,1,0:T(8,128)(2,1)S(1)}, bf16[16,40,640]{2,1,0:T(8,128)(2,1)S(1)}, u32[]{:S(2)}, u32[]{:S(2)}) %collective-permute-start.12) | collective-permute-done | bytes 819232 | tf_op jit(solution)/shard_map/ppermute | solution.py:845
  39.9 13.2 %shard_map.199 = (bf16[16,40,640]{2,1,0:T(8,128)(2,1)S(1)}, bf16[16,40,640]{2,1,0:T(8,128)(2,1)S(1)}, bf16[512,1280]{1,0:T(8,128)(2,1)S(1)}, f32[512,320]{1,0:T(...) custom-call(s32[4]{0:T(128)S(1)} %copy-done.6, ...), custom_call_target="tpu_custom_call", output_to_operand_aliasing={{5}: (9, {}), {6}: (10, {})} | custom-call | flops 32999999488 | tf_op jit(solution)/shard_map/pallas_call | solution.py:809
  53.2 1.8 %shard_map.200 = (f32[320,320]{1,0:T(8,128)S(1)}, bf16[512,320]{1,0:T(8,128)(2,1)S(1)}, bf16[512,640]{1,0:T(8,128)(2,1)S(1)}, f32[1,320]{1,0:T(1,128)S(1)}, f32[...) custom-call(f32[512,320]{1,0:T(8,128)S(1)} %get-tuple-element.133.dh2_ref, f32[512,320]{1,0:T(8,128)S(1)} %get-tuple-element.134.n2_ref, ...), custom_call_target="tpu_custom_call" | custom-call | flops 2500000000 | tf_op jit(solution)/shard_map/pallas_call | solution.py:809
  55.6 1.6 %collective-permute-start.14 = (bf16[8,40,640]{2,1,0:T(8,128)(2,1)S(1)}, bf16[8,40,640]{2,1,0:T(8,128)(2,1)S(1)}, u32[]{:S(2)}, u32[]{:S(2)}) collective-permute-start(bf16[8,40,640]{2,1,0:T(8,128)(2,1)S(1)} %get-tuple-element.145), channel_id=1, source_target_pairs={{0,4},{1,3},{2,6},{3,1},{4,0},{5,7},{6,2},{7,5},{8,12},{9,11},{10,... | collective-permute-start | bytes 1228808 | tf_op jit(solution)/shard_map/ppermute | solution.py:845
  57.3 2.8 %shard_map.202 = (bf16[16,40,640]{2,1,0:T(8,128)(2,1)S(1)}, bf16[16,40,640]{2,1,0:T(8,128)(2,1)S(1)}, bf16[512,320]{1,0:T(8,128)(2,1)S(1)}, f32[512,320]{1,0:T(8,128)S(1)}, f32[8,320]{1,0:T(8,128)S(1)}) custom-call(bf16[512,320]{1,0:T(8,128)(2,1)S(1)} %get-tuple-element.140.dob_ref, bf16[512,640]{1,0:T(8,128)(2,1)S(1)} %get-tuple-element.146.ds_ref, ...), custom_call_target="tpu_custom_call" | custom-call | tf_op jit(solution)/shard_map/pallas_call | solution.py:809
  60.1 2.2 %shard_map.204 = (bf16[320,512]{1,0:T(8,128)(2,1)}, bf16[2,8,640]{2,1,0:T(8,128)(2,1)S(1)}, bf16[2,8,640]{2,1,0:T(8,128)(2,1)S(1)}) custom-call(f32[512,320]{1,0:T(8,128)S(1)} %get-tuple-element.162.dx2_ref, bf16[512,320]{1,0:T(8,128)(2,1)S(1)} %get-tuple-element.163.dq_ref, f32[512,320]{1,0:T(8,128)S(1)} %get-tuple-element.164.dpatch_ref, ...), custom_call_target="tpu_custom_call" | custom-call | tf_op jit(solution)/shard_map/pallas_call | solution.py:809
  64.0 1.6 %collective-permute-start.17 = (bf16[336,640]{1,0:T(8,128)(2,1)S(1)}, bf16[336,640]{1,0:T(8,128)(2,1)S(1)}, u32[]{:S(2)}, u32[]{:S(2)}) collective-permute-start(bf16[336,640]{1,0:T(8,128)(2,1)S(1)} %get-tuple-element.173), channel_id=1, source_target_pairs={{0,4},{1,3},{2,6},{3,1},{4,0},{5,7},{6,2},{7,5},{8,12},{9,11},{10,... | collective-permute-start | bytes 1290248 | tf_op jit(solution)/shard_map/ppermute | solution.py:845
  65.7 2.0 %collective-permute-start.18 = (bf16[4,40,640]{2,1,0:T(8,128)(2,1)S(1)}, bf16[4,40,640]{2,1,0:T(8,128)(2,1)S(1)}, u32[]{:S(2)}, u32[]{:S(2)}) collective-permute-start(bf16[4,40,640]{2,1,0:T(8,128)(2,1)S(1)} %get-tuple-element.159), channel_id=1, source_target_pairs={{0,8},{1,9},{2,10},{3,11},{4,12},{5,13},{6,14},{7,15},{8,0},{9,1},... | collective-permute-start | bytes 614408 | tf_op jit(solution)/shard_map/ppermute | solution.py:845
  67.7 1.7 %shard_map.206 = bf16[320,512]{1,0:T(8,128)(2,1)} custom-call(f32[512,320]{1,0:T(8,128)S(1)} %get-tuple-element.121.x2_ref, bf16[512,1280]{1,0:T(8,128)(2,1)S(1)} %get-tuple-element.174.act_ref, bf16[320,1280]{1,0:T(8,128)(2,1)S(1)} %get-tuple-element.175.wd_ref, f32[16,320]{1,0:T(8,128)S(1)} %get-tuple-element.122.mv_ref, ...), custom_call_target="tpu_custom_call" | custom-call | flops 1000000000 | tf_op jit(solution)/shard_map/pallas_call | solution.py:809
  69.4 2.9 %collective-permute-done.18.got_ref = bf16[4,40,640]{2,1,0:T(8,128)(2,1)S(1)} collective-permute-done((bf16[4,40,640]{2,1,0:T(8,128)(2,1)S(1)}, bf16[4,40,640]{2,1,0:T(8,128)(2,1)S(1)}, u32[]{:S(2)}, u32[]{:S(2)}) %collective-permute-start.18) | collective-permute-done | bytes 204832 | tf_op jit(solution)/shard_map/ppermute | solution.py:845
  72.4 1.1 %collective-permute-start.19 = (bf16[168,640]{1,0:T(8,128)(2,1)S(1)}, bf16[168,640]{1,0:T(8,128)(2,1)S(1)}, u32[]{:S(2)}, u32[]{:S(2)}) collective-permute-start(bf16[168,640]{1,0:T(8,128)(2,1)S(1)} %get-tuple-element.183), channel_id=1, source_target_pairs={{0,2},{1,5},{2,0},{3,7},{4,6},{5,1},{6,4},{7,3},{8,10},{9,13},{10,... | collective-permute-start | bytes 645128 | tf_op jit(solution)/shard_map/ppermute | solution.py:845
  73.6 1.6 %collective-permute-start.23 = (bf16[2,40,640]{2,1,0:T(8,128)(2,1)S(1)}, bf16[2,40,640]{2,1,0:T(8,128)(2,1)S(1)}, u32[]{:S(2)}, u32[]{:S(2)}) collective-permute-start(bf16[2,40,640]{2,1,0:T(8,128)(2,1)S(1)} %get-tuple-element.191), channel_id=1, source_target_pairs={{0,16},{1,17},{2,18},{3,19},{4,20},{5,21},{6,22},{7,23},{8,24},{9,... | collective-permute-start | bytes 307208 | tf_op jit(solution)/shard_map/ppermute | solution.py:845
  75.2 3.1 %collective-permute-done.19.got_ref = bf16[168,640]{1,0:T(8,128)(2,1)S(1)} collective-permute-done((bf16[168,640]{1,0:T(8,128)(2,1)S(1)}, bf16[168,640]{1,0:T(8,128)(2,1)S(1)}, u32[]{:S(2)}, u32[]{:S(2)}) %collective-permute-start.19) | collective-permute-done | bytes 215072 | tf_op jit(solution)/shard_map/ppermute | solution.py:845
  78.4 2.1 %collective-permute-start.20 = (bf16[48,640]{1,0:T(8,128)(2,1)S(1)}, bf16[48,640]{1,0:T(8,128)(2,1)S(1)}, u32[]{:S(2)}, u32[]{:S(2)}) collective-permute-start(bf16[48,640]{1,0:T(8,128)(2,1)S(1)} %get-tuple-element.185), channel_id=1, source_target_pairs={{0,8},{1,9},{2,10},{3,11},{4,12},{5,13},{6,14},{7,15},{8,0},{9,1},... | collective-permute-start | bytes 184328 | tf_op jit(solution)/shard_map/ppermute | solution.py:845
  81.2 1.8 %collective-permute-start.22 = (bf16[48,640]{1,0:T(8,128)(2,1)S(1)}, bf16[48,640]{1,0:T(8,128)(2,1)S(1)}, u32[]{:S(2)}, u32[]{:S(2)}) collective-permute-start(bf16[48,640]{1,0:T(8,128)(2,1)S(1)} %get-tuple-element.187), channel_id=1, source_target_pairs={{0,24},{1,25},{2,26},{3,27},{4,28},{5,29},{6,30},{7,31},{8,16},{9,... | collective-permute-start | bytes 184328 | tf_op jit(solution)/shard_map/ppermute | solution.py:845
  83.0 1.0 %collective-permute-start.24 = (bf16[1,40,640]{2,1,0:T(8,128)(2,1)S(1)}, bf16[1,40,640]{2,1,0:T(8,128)(2,1)S(1)}, u32[]{:S(2)}, u32[]{:S(2)}) collective-permute-start(bf16[1,40,640]{2,1,0:T(8,128)(2,1)S(1)} %get-tuple-element.193), channel_id=1, source_target_pairs={{0,2},{1,5},{2,0},{3,7},{4,6},{5,1},{6,4},{7,3},{8,10},{9,13},{10,... | collective-permute-start | bytes 153608 | tf_op jit(solution)/shard_map/ppermute | solution.py:845
  84.0 3.1 %collective-permute-done.24.ffn_got_ref = bf16[1,40,640]{2,1,0:T(8,128)(2,1)S(1)} collective-permute-done((bf16[1,40,640]{2,1,0:T(8,128)(2,1)S(1)}, bf16[1,40,640]{2,1,0:T(8,128)(2,1)S(1)}, u32[]{:S(2)}, u32[]{:S(2)}) %collective-permute-start.24) | collective-permute-done | bytes 51232 | tf_op jit(solution)/shard_map/ppermute | solution.py:845
  87.2 0.9 %shard_map.211 = (f32[40,80]{1,0:T(8,128)}, f32[80,80]{1,0:T(8,128)}, f32[40,320]{1,0:T(8,128)}, f32[40,80]{1,0:T(8,128)}, f32[80,160]{1,0:T(8,128)}, /*index=5*...) custom-call(bf16[48,640]{1,0:T(8,128)(2,1)S(1)} %get-tuple-element.184.a_ref, ...), custom_call_target="tpu_custom_call" | custom-call | tf_op jit(solution)/shard_map/pallas_call | solution.py:809
  (72 shorter events, 6.2 us)
Async XLA Ops:
  2.4 10.6 %collective-permute-start.2 = (bf16[1,40,640]{2,1,0:T(8,128)(2,1)}, bf16[1,40,640]{2,1,0:T(8,128)(2,1)S(1)}, u32[]{:S(2)}, u32[]{:S(2)}) collective-permute-start(bf16[1,40,640]{2,1,0:T(8,128)(2,1)} %get-tuple-element.111), channel_id=1, source_target_pairs={{0,24},{1,25},{2,26},{3,27},{4,28},{5,29},{6,30},{7,31},{8,16},{9,... | collective-permute-start | bytes 153608 | tf_op jit(solution)/shard_map/ppermute | solution.py:845
  7.5 5.5 %collective-permute-start.1 = (bf16[1,40,640]{2,1,0:T(8,128)(2,1)}, bf16[1,40,640]{2,1,0:T(8,128)(2,1)S(1)}, u32[]{:S(2)}, u32[]{:S(2)}) collective-permute-start(bf16[1,40,640]{2,1,0:T(8,128)(2,1)} %get-tuple-element.111), channel_id=1, source_target_pairs={{0,16},{1,17},{2,18},{3,19},{4,20},{5,21},{6,22},{7,23},{8,24},{9,... | collective-permute-start | bytes 153608 | tf_op jit(solution)/shard_map/ppermute | solution.py:845
  7.5 5.5 %collective-permute-start = (bf16[1,40,640]{2,1,0:T(8,128)(2,1)}, bf16[1,40,640]{2,1,0:T(8,128)(2,1)S(1)}, u32[]{:S(2)}, u32[]{:S(2)}) collective-permute-start(bf16[1,40,640]{2,1,0:T(8,128)(2,1)} %get-tuple-element.111), channel_id=1, source_target_pairs={{0,8},{1,9},{2,10},{3,11},{4,12},{5,13},{6,14},{7,15},{8,0},{9,1},... | collective-permute-start | bytes 153608 | tf_op jit(solution)/shard_map/ppermute | solution.py:845
  8.1 4.8 %collective-permute-start.4 = (bf16[1,16,640]{2,1,0:T(8,128)(2,1)}, bf16[1,16,640]{2,1,0:T(8,128)(2,1)S(1)}, u32[]{:S(2)}, u32[]{:S(2)}) collective-permute-start(bf16[1,16,640]{2,1,0:T(8,128)(2,1)} %get-tuple-element.113), channel_id=1, source_target_pairs={{0,1},{1,0},{2,3},{3,2},{4,5},{5,4},{6,7},{7,6},{8,9},{9,8},{10,11... | collective-permute-start | bytes 61448 | tf_op jit(solution)/shard_map/ppermute | solution.py:845
  8.1 4.8 %collective-permute-start.3 = (bf16[1,40,640]{2,1,0:T(8,128)(2,1)}, bf16[1,40,640]{2,1,0:T(8,128)(2,1)S(1)}, u32[]{:S(2)}, u32[]{:S(2)}) collective-permute-start(bf16[1,40,640]{2,1,0:T(8,128)(2,1)} %get-tuple-element.112), channel_id=1, source_target_pairs={{0,2},{1,5},{2,0},{3,7},{4,6},{5,1},{6,4},{7,3},{8,10},{9,13},{10,... | collective-permute-start | bytes 153608 | tf_op jit(solution)/shard_map/ppermute | solution.py:845
  9.8 3.1 %copy-start.8 = (bf16[1,40,640]{2,1,0:T(8,128)(2,1)S(1)}, bf16[1,40,640]{2,1,0:T(8,128)(2,1)}, u32[]{:S(2)}) copy-start(bf16[1,40,640]{2,1,0:T(8,128)(2,1)} %get-tuple-element.111) | copy-start | bytes 153604
  9.8 3.2 %copy-start.7 = (bf16[1,40,640]{2,1,0:T(8,128)(2,1)S(1)}, bf16[1,40,640]{2,1,0:T(8,128)(2,1)}, u32[]{:S(2)}) copy-start(bf16[1,40,640]{2,1,0:T(8,128)(2,1)} %get-tuple-element.112) | copy-start | bytes 153604
  12.9 12.0 %copy-start.9 = (bf16[1,16,640]{2,1,0:T(8,128)(2,1)S(1)}, bf16[1,16,640]{2,1,0:T(8,128)(2,1)}, u32[]{:S(2)}) copy-start(bf16[1,16,640]{2,1,0:T(8,128)(2,1)} %get-tuple-element.113) | copy-start | bytes 61444
  13.0 9.7 %collective-permute-start.7 = (bf16[2,40,640]{2,1,0:T(8,128)(2,1)S(1)}, bf16[2,40,640]{2,1,0:T(8,128)(2,1)S(1)}, u32[]{:S(2)}, u32[]{:S(2)}) collective-permute-start(bf16[2,40,640]{2,1,0:T(8,128)(2,1)S(1)} %pad_maximum_fusion.3), channel_id=1, source_target_pairs={{0,16},{1,17},{2,18},{3,19},{4,20},{5,21},{6,22},{7,23},{8,24},{9,... | collective-permute-start | bytes 307208 | tf_op jit(solution)/shard_map/ppermute | solution.py:845
  15.2 5.8 %collective-permute-start.5 = (bf16[4,40,640]{2,1,0:T(8,128)(2,1)S(1)}, bf16[4,40,640]{2,1,0:T(8,128)(2,1)S(1)}, u32[]{:S(2)}, u32[]{:S(2)}) collective-permute-start(bf16[4,40,640]{2,1,0:T(8,128)(2,1)S(1)} %pad_maximum_fusion.1), channel_id=1, source_target_pairs={{0,2},{1,5},{2,0},{3,7},{4,6},{5,1},{6,4},{7,3},{8,10},{9,13},{10,... | collective-permute-start | bytes 614408 | tf_op jit(solution)/shard_map/ppermute | solution.py:845
  21.1 8.0 %collective-permute-start.6 = (bf16[8,40,640]{2,1,0:T(8,128)(2,1)S(1)}, bf16[8,40,640]{2,1,0:T(8,128)(2,1)S(1)}, u32[]{:S(2)}, u32[]{:S(2)}) collective-permute-start(bf16[8,40,640]{2,1,0:T(8,128)(2,1)S(1)} %get-tuple-element.202), channel_id=1, source_target_pairs={{0,4},{1,3},{2,6},{3,1},{4,0},{5,7},{6,2},{7,5},{8,12},{9,11},{10,... | collective-permute-start | bytes 1228808 | tf_op jit(solution)/shard_map/ppermute | solution.py:845
  22.7 6.2 %collective-permute-start.8 = (bf16[4,40,640]{2,1,0:T(8,128)(2,1)S(1)}, bf16[4,40,640]{2,1,0:T(8,128)(2,1)S(1)}, u32[]{:S(2)}, u32[]{:S(2)}) collective-permute-start(bf16[4,40,640]{2,1,0:T(8,128)(2,1)S(1)} %pad_maximum_fusion.2), channel_id=1, source_target_pairs={{0,8},{1,9},{2,10},{3,11},{4,12},{5,13},{6,14},{7,15},{8,0},{9,1},... | collective-permute-start | bytes 614408 | tf_op jit(solution)/shard_map/ppermute | solution.py:845
  24.8 6.8 %copy-start.5 = (f32[512,128]{1,0:T(8,128)S(1)}, f32[512,128]{1,0:T(8,128)}, u32[]{:S(2)}) copy-start(f32[512,128]{1,0:T(8,128)} %get-tuple-element.110.live_ref) | copy-start | bytes 786436
  24.9 4.1 %collective-permute-start.9 = (bf16[2,16,640]{2,1,0:T(8,128)(2,1)S(1)}, bf16[2,16,640]{2,1,0:T(8,128)(2,1)S(1)}, u32[]{:S(2)}, u32[]{:S(2)}) collective-permute-start(bf16[2,16,640]{2,1,0:T(8,128)(2,1)S(1)} %pad_maximum_fusion.5), channel_id=1, source_target_pairs={{0,2},{1,3},{2,0},{3,1},{4,6},{5,7},{6,4},{7,5},{8,10},{9,11},{10,... | collective-permute-start | bytes 122888 | tf_op jit(solution)/shard_map/ppermute | solution.py:845
  29.1 2.5 %copy-start.4 = (f32[512,320]{1,0:T(8,128)S(1)}, f32[512,320]{1,0:T(8,128)}, u32[]{:S(2)}) copy-start(f32[512,320]{1,0:T(8,128)} %get-tuple-element.107.x_ref) | copy-start | bytes 1966084
  29.2 2.5 %copy-start.6 = (s32[4]{0:T(128)S(1)}, s32[4]{0:T(128)}, u32[]{:S(2)}) copy-start(s32[4]{0:T(128)} %get-tuple-element.106.geo_ref) | copy-start | bytes 52
  29.2 2.4 %collective-permute-start.10 = (bf16[16,40,640]{2,1,0:T(8,128)(2,1)S(1)}, bf16[16,40,640]{2,1,0:T(8,128)(2,1)S(1)}, u32[]{:S(2)}, u32[]{:S(2)}) collective-permute-start(bf16[16,40,640]{2,1,0:T(8,128)(2,1)S(1)} %constant_dynamic-update-slice_fusion.5.own_ref), channel_id=1, source_target_pairs={{0,1},{1,0},{2,3},{3,2},{4,5},{5,4},{6,7},{7,6},{8,9},{9,8},{10,11... | collective-permute-start | bytes 2457608 | tf_op jit(solution)/shard_map/ppermute | solution.py:845
  29.4 8.0 %collective-permute-start.11 = (bf16[8,40,640]{2,1,0:T(8,128)(2,1)S(1)}, bf16[8,40,640]{2,1,0:T(8,128)(2,1)S(1)}, u32[]{:S(2)}, u32[]{:S(2)}) collective-permute-start(bf16[8,40,640]{2,1,0:T(8,128)(2,1)S(1)} %pad_maximum_fusion), channel_id=1, source_target_pairs={{0,4},{1,3},{2,6},{3,1},{4,0},{5,7},{6,2},{7,5},{8,12},{9,11},{10,... | collective-permute-start | bytes 1228808 | tf_op jit(solution)/shard_map/ppermute | solution.py:845
  37.5 2.4 %collective-permute-start.12 = (bf16[16,40,640]{2,1,0:T(8,128)(2,1)S(1)}, bf16[16,40,640]{2,1,0:T(8,128)(2,1)S(1)}, u32[]{:S(2)}, u32[]{:S(2)}) collective-permute-start(bf16[16,40,640]{2,1,0:T(8,128)(2,1)S(1)} %constant_dynamic-update-slice_fusion.11.own_ref), channel_id=1, source_target_pairs={{0,1},{1,0},{2,3},{3,2},{4,5},{5,4},{6,7},{7,6},{8,9},{9,8},{10,11... | collective-permute-start | bytes 2457608 | tf_op jit(solution)/shard_map/ppermute | solution.py:845
  53.0 2.4 %collective-permute-start.13 = (bf16[16,40,640]{2,1,0:T(8,128)(2,1)S(1)}, bf16[16,40,640]{2,1,0:T(8,128)(2,1)S(1)}, u32[]{:S(2)}, u32[]{:S(2)}) collective-permute-start(bf16[16,40,640]{2,1,0:T(8,128)(2,1)S(1)} %get-tuple-element.143), channel_id=1, source_target_pairs={{0,1},{1,0},{2,3},{3,2},{4,5},{5,4},{6,7},{7,6},{8,9},{9,8},{10,11... | collective-permute-start | bytes 2457608 | tf_op jit(solution)/shard_map/ppermute | solution.py:845
  55.6 8.0 %collective-permute-start.14 = (bf16[8,40,640]{2,1,0:T(8,128)(2,1)S(1)}, bf16[8,40,640]{2,1,0:T(8,128)(2,1)S(1)}, u32[]{:S(2)}, u32[]{:S(2)}) collective-permute-start(bf16[8,40,640]{2,1,0:T(8,128)(2,1)S(1)} %get-tuple-element.145), channel_id=1, source_target_pairs={{0,4},{1,3},{2,6},{3,1},{4,0},{5,7},{6,2},{7,5},{8,12},{9,11},{10,... | collective-permute-start | bytes 1228808 | tf_op jit(solution)/shard_map/ppermute | solution.py:845
  57.3 2.8 %copy-start.2 = (f32[512,1]{1,0:T(8,128)S(1)}, f32[512,1]{1,0:T(8,128)}, u32[]{:S(2)}) copy-start(f32[512,1]{1,0:T(8,128)} %get-tuple-element.165.r1_ref) | copy-start | bytes 6148
  60.0 3.7 %collective-permute-start.15 = (bf16[16,40,640]{2,1,0:T(8,128)(2,1)S(1)}, bf16[16,40,640]{2,1,0:T(8,128)(2,1)S(1)}, u32[]{:S(2)}, u32[]{:S(2)}) collective-permute-start(bf16[16,40,640]{2,1,0:T(8,128)(2,1)S(1)} %get-tuple-element.161), channel_id=1, source_target_pairs={{0,1},{1,0},{2,3},{3,2},{4,5},{5,4},{6,7},{7,6},{8,9},{9,8},{10,11... | collective-permute-start | bytes 2457608 | tf_op jit(solution)/shard_map/ppermute | solution.py:845
  62.3 1.4 %collective-permute-start.16 = (bf16[2,8,640]{2,1,0:T(8,128)(2,1)S(1)}, bf16[2,8,640]{2,1,0:T(8,128)(2,1)S(1)}, u32[]{:S(2)}, u32[]{:S(2)}) collective-permute-start(bf16[2,8,640]{2,1,0:T(8,128)(2,1)S(1)} %get-tuple-element.172), channel_id=1, source_target_pairs={{0,1},{1,0},{2,3},{3,2},{4,5},{5,4},{6,7},{7,6},{8,9},{9,8},{10,11... | collective-permute-start | bytes 61448 | tf_op jit(solution)/shard_map/ppermute | solution.py:845
  64.0 8.2 %collective-permute-start.17 = (bf16[336,640]{1,0:T(8,128)(2,1)S(1)}, bf16[336,640]{1,0:T(8,128)(2,1)S(1)}, u32[]{:S(2)}, u32[]{:S(2)}) collective-permute-start(bf16[336,640]{1,0:T(8,128)(2,1)S(1)} %get-tuple-element.173), channel_id=1, source_target_pairs={{0,4},{1,3},{2,6},{3,1},{4,0},{5,7},{6,2},{7,5},{8,12},{9,11},{10,... | collective-permute-start | bytes 1290248 | tf_op jit(solution)/shard_map/ppermute | solution.py:845
  65.7 6.6 %collective-permute-start.18 = (bf16[4,40,640]{2,1,0:T(8,128)(2,1)S(1)}, bf16[4,40,640]{2,1,0:T(8,128)(2,1)S(1)}, u32[]{:S(2)}, u32[]{:S(2)}) collective-permute-start(bf16[4,40,640]{2,1,0:T(8,128)(2,1)S(1)} %get-tuple-element.159), channel_id=1, source_target_pairs={{0,8},{1,9},{2,10},{3,11},{4,12},{5,13},{6,14},{7,15},{8,0},{9,1},... | collective-permute-start | bytes 614408 | tf_op jit(solution)/shard_map/ppermute | solution.py:845
  72.4 5.9 %collective-permute-start.19 = (bf16[168,640]{1,0:T(8,128)(2,1)S(1)}, bf16[168,640]{1,0:T(8,128)(2,1)S(1)}, u32[]{:S(2)}, u32[]{:S(2)}) collective-permute-start(bf16[168,640]{1,0:T(8,128)(2,1)S(1)} %get-tuple-element.183), channel_id=1, source_target_pairs={{0,2},{1,5},{2,0},{3,7},{4,6},{5,1},{6,4},{7,3},{8,10},{9,13},{10,... | collective-permute-start | bytes 645128 | tf_op jit(solution)/shard_map/ppermute | solution.py:845
  73.6 9.4 %collective-permute-start.23 = (bf16[2,40,640]{2,1,0:T(8,128)(2,1)S(1)}, bf16[2,40,640]{2,1,0:T(8,128)(2,1)S(1)}, u32[]{:S(2)}, u32[]{:S(2)}) collective-permute-start(bf16[2,40,640]{2,1,0:T(8,128)(2,1)S(1)} %get-tuple-element.191), channel_id=1, source_target_pairs={{0,16},{1,17},{2,18},{3,19},{4,20},{5,21},{6,22},{7,23},{8,24},{9,... | collective-permute-start | bytes 307208 | tf_op jit(solution)/shard_map/ppermute | solution.py:845
  78.4 8.8 %collective-permute-start.20 = (bf16[48,640]{1,0:T(8,128)(2,1)S(1)}, bf16[48,640]{1,0:T(8,128)(2,1)S(1)}, u32[]{:S(2)}, u32[]{:S(2)}) collective-permute-start(bf16[48,640]{1,0:T(8,128)(2,1)S(1)} %get-tuple-element.185), channel_id=1, source_target_pairs={{0,8},{1,9},{2,10},{3,11},{4,12},{5,13},{6,14},{7,15},{8,0},{9,1},... | collective-permute-start | bytes 184328 | tf_op jit(solution)/shard_map/ppermute | solution.py:845
  80.5 6.7 %collective-permute-start.21 = (bf16[48,640]{1,0:T(8,128)(2,1)S(1)}, bf16[48,640]{1,0:T(8,128)(2,1)S(1)}, u32[]{:S(2)}, u32[]{:S(2)}) collective-permute-start(bf16[48,640]{1,0:T(8,128)(2,1)S(1)} %get-tuple-element.186), channel_id=1, source_target_pairs={{0,16},{1,17},{2,18},{3,19},{4,20},{5,21},{6,22},{7,23},{8,24},{9,... | collective-permute-start | bytes 184328 | tf_op jit(solution)/shard_map/ppermute | solution.py:845
  81.2 6.1 %collective-permute-start.22 = (bf16[48,640]{1,0:T(8,128)(2,1)S(1)}, bf16[48,640]{1,0:T(8,128)(2,1)S(1)}, u32[]{:S(2)}, u32[]{:S(2)}) collective-permute-start(bf16[48,640]{1,0:T(8,128)(2,1)S(1)} %get-tuple-element.187), channel_id=1, source_target_pairs={{0,24},{1,25},{2,26},{3,27},{4,28},{5,29},{6,30},{7,31},{8,16},{9,... | collective-permute-start | bytes 184328 | tf_op jit(solution)/shard_map/ppermute | solution.py:845
  83.0 4.2 %collective-permute-start.24 = (bf16[1,40,640]{2,1,0:T(8,128)(2,1)S(1)}, bf16[1,40,640]{2,1,0:T(8,128)(2,1)S(1)}, u32[]{:S(2)}, u32[]{:S(2)}) collective-permute-start(bf16[1,40,640]{2,1,0:T(8,128)(2,1)S(1)} %get-tuple-element.193), channel_id=1, source_target_pairs={{0,2},{1,5},{2,0},{3,7},{4,6},{5,1},{6,4},{7,3},{8,10},{9,13},{10,... | collective-permute-start | bytes 153608 | tf_op jit(solution)/shard_map/ppermute | solution.py:845
  (3 other events, 7.5 us)

commit v6 on v5

--- a/solution.py
+++ b/solution.py
@@ -350,14 +350,16 @@
     r2_ref[...] = inverse
     h2 = normed * mv_ref[8:9, :] + mv_ref[9:10, :]
     h2_ref[...] = h2.astype(BF16)
-    h2t_ref[...] = h2.T.astype(BF16)
+    width = h2.shape[1]
+    h2t_ref[:width, :] = h2.T.astype(BF16)
+    h2t_ref[width:, :] = jnp.ones((h2t_ref.shape[0] - width, h2.shape[0]), BF16)
 
 
 def ffn_kernel(
     tuned,
     geo_ref, h2_ref, h2t_ref, gy_ref, gyt_ref, mask_ref, own_ref, oth_ref, hv_ref, wu_in_ref, wd_in_ref,
-    gown_ref, gsend_ref, act_ref, dh2_ref, hg_ref, wu_ref, wd_ref,
-    f_ref, gm_ref, gp_ref, dc_ref, ul_ref, ur_ref, g0_ref, slope_ref, u0_ref, df_ref, da_ref,
+    gown_ref, gsend_ref, act_ref, df_ref, hg_ref, wu_ref, wd_ref,
+    f_ref, gm_ref, gp_ref, dc_ref, ul_ref, ur_ref, g0_ref, u0_ref, da_ref,
     upg_ref, dng_ref,
 ):
     me = my_index(tuned)
@@ -380,10 +382,9 @@
     split = pl.multiple_of(jnp.minimum(area // TILE, tiles - 1) * TILE, TILE)
 
     for ref in (f_ref, gm_ref, gp_ref, dc_ref, ul_ref, ur_ref):
-        ref[:, :PAD, :] = jnp.zeros((CHUNK // 128, PAD, 128), F32)
-        ref[:, PAD + capacity :, :] = jnp.zeros((CHUNK // 128, PAD, 128), F32)
-
-    dh2_ref[...] = jnp.zeros_like(dh2_ref)
+        ref[:, :PAD, :] = jnp.zeros((ref.shape[0], PAD, 128), F32)
+        ref[:, PAD + capacity :, :] = jnp.zeros((ref.shape[0], PAD, 128), F32)
+
 
     def fold(values):
         return jnp.sum(values.reshape(TILE // 8, 8, 128), axis=0)
@@ -401,22 +402,11 @@
     def put_vector(c, k, j, value):
         hg_ref[k : k + 1, pl.ds(pl.multiple_of(c * CHUNK + j * 128, 128), 128)] = value
 
-    def first_layer(c, at):
-        value = dot_nn(h2_ref[at, :], wu_ref[:, columns(c)])
-        for j in range(halves):
-            f_ref[j, pl.ds(PAD + at.start, at.size), :] = value[:, j * 128 : (j + 1) * 128] + vector(c, 0, j)
-
     def act_grad(c, at):
         da_ref[at, :] = dot_nn(gy_ref[at, :], wd_ref[:, columns(c)])
 
     def down_grad(c, at):
         dng_ref[at, columns(c)] = dot_nn(gyt_ref[at, :], act_ref[:, columns(c)])
-
-    def up_grad(c, at):
-        upg_ref[at, columns(c)] = dot_nn(h2t_ref[at, :], df_ref[...])
-
-    def h2_grad(c, at):
-        dh2_ref[at, :] += dot_nt(df_ref[at, :], wu_ref[:, columns(c)])
 
     def tasks(product, c, rows, size):
         return [functools.partial(product, c, pl.ds(r, min(size, rows - r))) for r in range(0, rows, size)]
@@ -430,14 +420,12 @@
                 done += 1
 
     def chunk_step(c, carry):
-        before = jnp.maximum(c - 1, 0)
-        following = jnp.minimum(c + 1, chunks - 1)
         v = [[vector(c, k, j) for k in range(11)] for j in range(halves)]
 
         def taps_of(j, r, mask_left, mask_right):
-            here = f_ref[j, pl.ds(PAD + r, TILE), :]
-            left = f_ref[j, pl.ds(PAD + r - 1, TILE), :] * mask_left
-            right = f_ref[j, pl.ds(PAD + r + 1, TILE), :] * mask_right
+            here = f_ref[c * halves + j, pl.ds(PAD + r, TILE), :]
+            left = f_ref[c * halves + j, pl.ds(PAD + r - 1, TILE), :] * mask_left
+            right = f_ref[c * halves + j, pl.ds(PAD + r + 1, TILE), :] * mask_right
             return left, here, right
 
         def row_length(r):
@@ -460,6 +448,8 @@
                     mask_ref[4, at, :] * gm_ref[j, pl.ds(PAD + split - w1, TILE), :]
                     + mask_ref[5, at, :] * gp_ref[j, pl.ds(PAD + split + w1, TILE), :]
                 )
+
+        conv_sums = [zero] * halves
 
         def activate(r):
             at = pl.ds(r, TILE)
@@ -473,15 +463,8 @@
                 )
                 half = 0.5 * (1.0 + lax.erf(conv * 2.0 ** (-0.5)))
                 act_ref[at, pl.ds(pl.multiple_of(c * CHUNK + j * 128, 128), 128)] = (conv * half).astype(BF16)
-                slope_ref[at, pl.ds(j * 128, 128)] = half + conv * jnp.exp(-0.5 * conv * conv) * (2.0 * math.pi) ** (-0.5)
-
-        conv_sums = [zero] * halves
-
-        def into_conv(r):
-            at = pl.ds(r, TILE)
-            for j in range(halves):
-                lane_at = pl.ds(j * 128, 128)
-                value = da_ref[at, lane_at] * slope_ref[at, lane_at]
+                slope = half + conv * ((2.0 * math.pi) ** (-0.5) * jnp.exp2(conv * conv * (-0.5 / math.log(2.0))))
+                value = da_ref[at, pl.ds(j * 128, 128)] * slope
                 dc_ref[j, pl.ds(PAD + r, TILE), :] = value
                 conv_sums[j] = conv_sums[j] + fold(value)
 
@@ -517,8 +500,6 @@
                 grads = [fold(d * f) for d in (below, above) for f in (left, here, right)]
                 tap_sums[j] = [a + b for a, b in zip(tap_sums[j], grads[:3] + [zero] * 3 + grads[3:])]
 
-        up_sums = [zero] * halves
-
         def spread_back(r):
             at = pl.ds(r, TILE)
             mask_left, mask_right = mask_ref[0, at, :], mask_ref[1, at, :]
@@ -528,34 +509,32 @@
                     + mask_left * ur_ref[j, pl.ds(PAD + r - 1, TILE), :]
                     + mask_right * ul_ref[j, pl.ds(PAD + r + 1, TILE), :]
                 ).astype(BF16)
-                df_ref[at, pl.ds(j * 128, 128)] = value
-                up_sums[j] = up_sums[j] + fold(value.astype(F32))
+                df_ref[at, pl.ds(pl.multiple_of(c * CHUNK + j * 128, 128), 128)] = value
 
         def steps(step):
             return [functools.partial(step, r) for r in range(0, capacity, TILE)]
 
+        interleave(steps(column_taps) + [column_taps_split], tasks(act_grad, c, capacity, MROWS))
         interleave(
-            steps(column_taps) + [column_taps_split] + steps(activate),
-            tasks(act_grad, c, capacity, MROWS) + tasks(up_grad, before, width, MROWS)
-            + tasks(h2_grad, before, capacity, MROWS),
+            steps(activate),
+            [],
         )
-        interleave(
-            steps(into_conv) + steps(tap_back) + [tap_back_split],
-            tasks(down_grad, c, width, MROWS),
-        )
-        interleave(steps(spread_back), tasks(first_layer, following, capacity, MROWS))
+        interleave(steps(tap_back) + [tap_back_split], tasks(down_grad, c, width, MROWS))
+        interleave(steps(spread_back), [])
         for j in range(halves):
-            put_vector(c, 0, j, column_sum(up_sums[j]))
             put_vector(c, 1, j, column_sum(conv_sums[j]))
             for k in range(9):
                 put_vector(c, 2 + k, j, column_sum(tap_sums[j][k]))
         return carry
 
-    df_ref[...] = jnp.zeros_like(df_ref)
-    first_layer(0, pl.ds(0, capacity))
+    for c in range(chunks):
+        value = dot_nn(h2_ref[...], wu_ref[:, c * CHUNK : (c + 1) * CHUNK])
+        for j in range(halves):
+            bias = hv_ref[0:1, pl.ds(c * CHUNK + j * 128, 128)]
+            f_ref[c * halves + j, pl.ds(PAD, capacity), :] = value[:, j * 128 : (j + 1) * 128] + bias
     lax.fori_loop(0, chunks, chunk_step, 0)
-    up_grad(chunks - 1, pl.ds(0, width))
-    h2_grad(chunks - 1, pl.ds(0, capacity))
+    upg_ref[...] = dot_nn(h2t_ref[...], df_ref[...])
+    hg_ref[0:1, :] = upg_ref[width : width + 1, :]
     hg_ref[11:, :] = jnp.zeros((hg_ref.shape[0] - 11, hidden), F32)
 
     def value_of(w, n):
@@ -582,12 +561,14 @@
 
 
 def score_back_kernel(
-    dh2_ref, n2_ref, r2_ref, gy_ref, mv_ref, vb_ref, p_ref, o_ref, wp_ref,
+    df_ref, wu_ref, n2_ref, r2_ref, gy_ref, mv_ref, vb_ref, p_ref, o_ref, wp_ref,
     gp_ref, dob_ref, ds_ref, bp_ref, dx2_ref, mg_ref,
-    dp_ref,
+    dp_ref, dh2_ref,
 ):
-    capacity, width = dh2_ref.shape
+    capacity, width = n2_ref.shape
     keys = capacity // 4
+
+    dh2_ref[...] = dot_nt(df_ref[...], wu_ref[...])
 
     def norm_back(i, carry):
         at = pl.ds(pl.multiple_of(i * 64, 64), 64)
@@ -803,7 +784,7 @@
     up_ref[...] = rows_of(*columns[2:])
 
 
-def call(kernel, inputs, outputs, scratch=(), scalars=0, limit=40, flops=0, moved=0, aliases={}):
+def call(kernel, inputs, outputs, scratch=(), scalars=0, limit=24, flops=0, moved=0, aliases={}):
     vmem = pl.BlockSpec(memory_space=pltpu.VMEM)
     smem = pl.BlockSpec(memory_space=pltpu.SMEM)
     return pl.pallas_call(
@@ -864,6 +845,7 @@
         own_a, half_b, vecs = (join(v, g) for v, g in zip((buf_a, buf_b, vecs), got))
         oth_a = swap(own_a, 1)
         rest_b = swap(half_b, 4, 2)
+        oth_half_b = swap(after(half_b, oth_a), 1)
     else:
         own_a, oth_a, own_b, oth_b, vecs = gather_plain(
             q_weight, kv_weight, reduce_weight, proj_weight, up_weight, down_weight, vec_model, vec_hidden
@@ -890,8 +872,9 @@
     )
 
     if tuned:
-        own_b = join(half_b, after(rest_b, x2))
-        oth_b = swap(own_b, 1)
+        rest_b = after(rest_b, x2)
+        own_b = join(half_b, rest_b)
+        oth_b = join(oth_half_b, swap(rest_b, 1))
     padded = ((CHUNK // 128, capacity + 2 * PAD, 128), F32)
     halved = ((CHUNK // 128, capacity, 128), F32)
     chunked = ((capacity, CHUNK), F32)
@@ -899,24 +882,24 @@
         functools.partial(prepare_two_kernel, tuned),
         (x2, mv, own_b),
         (
-            tokens_f32, ((capacity, 1), F32), tokens_low, ((width, capacity), BF16),
+            tokens_f32, ((capacity, 1), F32), tokens_low, ((width + 16, capacity), BF16),
             ((width, hidden), BF16), ((width, hidden), BF16),
         ),
         flops=10**9,
     )
-    gown_b, gsend_b, act, dh2, hg, wu, wd = call(
+    gown_b, gsend_b, act, df, hg, wu, wd = call(
         functools.partial(ffn_kernel, tuned),
         (geo, h2, h2t, gy, gyt, masks, own_b, oth_b, hv, wu, wd),
         (
             ((SLOTS,) + piece, BF16), ((SLOTS,) + piece, BF16),
-            ((capacity, hidden), BF16), tokens_f32, ((16, hidden), F32),
+            ((capacity, hidden), BF16), ((capacity, hidden), BF16), ((16, hidden), F32),
             ((width, hidden), BF16), ((width, hidden), BF16),
         ),
         aliases={9: 5, 10: 6},
         scratch=(
-            padded, padded, padded, padded, padded, padded,
-            halved, chunked, halved, ((capacity, CHUNK), BF16), chunked,
-            ((width, hidden), F32), ((width, hidden), F32),
+            ((hidden // 128, capacity + 2 * PAD, 128), F32), padded, padded, padded, padded, padded,
+            halved, halved, chunked,
+            ((width + 16, hidden), F32), ((width, hidden), F32),
         ),
         scalars=1,
         flops=33 * 10**9,
@@ -926,12 +909,12 @@
         got_b = swap(gsend_b, 1)
     gp, dob, ds, bp, dx2, mg = call(
         score_back_kernel,
-        (dh2, n2, r2, gy, mv, vb, p, o, wp),
+        (df, wu, n2, r2, gy, mv, vb, p, o, wp),
         (
             (square, F32), ((capacity, width), BF16), ((capacity, HEADS * keys), BF16), ((1, width), F32),
             tokens_f32, ((16, width), F32),
         ),
-        scratch=(((capacity, HEADS * keys), F32),),
+        scratch=(((capacity, HEADS * keys), F32), tokens_f32),
         flops=25 * 10**8,
     )
     def halve(keep, got, flops=0):

time: 88.5 us -> 86.6 us (0.979)
  Pallas kernels: 33.5 us -> 32.6 us
  waiting for transfers between devices: 21.5 us -> 20.6 us
    pallas_call x15, Pallas kernels: 28.7 us -> 27.7 us  [call(): pl.pallas_call(kernel, out_shape=[jax.ShapeDtypeStruct(shape, kind) for s...]
    ppermute x25 -> x26, waiting for transfers between devices: 21.5 us -> 20.6 us  [swap(): return lax.ppermute(value, ('wide', 'narrow'), pairs)]
    ppermute x25 -> x26, starting transfers between devices: 31.7 us -> 31.5 us  [swap(): return lax.ppermute(value, ('wide', 'narrow'), pairs)]
  transfers between devices with their start and end apart: 25 -> 26, of which waited for: 12 -> 11; matrix products, arithmetic and copies ran while one was open for 0% -> 0% of each run, Pallas kernels for 19% -> 21%
where the time goes in v6:
time: 86.6 us; the launch traced here: 86.3 us
  Pallas kernels  32.6 us (38%)
  starting transfers between devices  31.5 us (36%)
  waiting for transfers between devices  20.6 us (24%)
  between operations  1 us (1%)
    ppermute x26, starting transfers between devices, swap(): return lax.ppermute(value, ('wide', 'narrow'), pairs)  31.5 us
    pallas_call x15, Pallas kernels, call(): pl.pallas_call(kernel, out_shape=[jax.ShapeDtypeStruct(shape, kind) for s...  27.7 us
    ppermute x26, waiting for transfers between devices, swap(): return lax.ppermute(value, ('wide', 'narrow'), pairs)  20.6 us
    pallas_call x1, Pallas kernels, prepare(): pl.pallas_call(prepare_kernel, out_shape=[jax.ShapeDtypeStruct(shape, kin...  3.1 us
  transfers between devices with their start and end apart: 26, of which 11 were waited for; matrix products, arithmetic and copies ran while one was open for 0% of the time, Pallas kernels for 21%

profile of v6, /device:TPU:0, one launch (start us, length us, event | category | flops | bytes accessed | tf_op | source)
XLA Modules:
  0.0 86.3 jit_solution(4058586148866047066)
XLA Ops:
  0.6 1.7 %shard_map.196 = (bf16[1,40,640]{2,1,0:T(8,128)(2,1)}, bf16[1,40,640]{2,1,0:T(8,128)(2,1)}, bf16[1,16,640]{2,1,0:T(8,128)(2,1)}) custom-call(bf16[40,80]{1,0:T(8,128)(2,1)} %bitcast.16, bf16[80,80]{1,0:T(8,128)(2,1)} %refs_1_.1, bf16[40,320]{1,0:T(8,128)(2,1)} %bitcast.14, bf16[40,80]{1,0:T(8,128)(2,1)} %bitcast.17, bf16[80,160]{1,0:T(8,128)(2,1)} %refs_4_.1, ...), custom_call_target="tpu_custom_call" | custom-call | tf_op jit(solution)/shard_map/pallas_call | solution.py:133
  2.4 5.1 %collective-permute-start.2 = (bf16[1,40,640]{2,1,0:T(8,128)(2,1)}, bf16[1,40,640]{2,1,0:T(8,128)(2,1)S(1)}, u32[]{:S(2)}, u32[]{:S(2)}) collective-permute-start(bf16[1,40,640]{2,1,0:T(8,128)(2,1)} %get-tuple-element.113), channel_id=1, source_target_pairs={{0,24},{1,25},{2,26},{3,27},{4,28},{5,29},{6,30},{7,31},{8,16},{9,... | collective-permute-start | bytes 153608 | tf_op jit(solution)/shard_map/ppermute | solution.py:826
  8.1 1.6 %collective-permute-start.3 = (bf16[1,40,640]{2,1,0:T(8,128)(2,1)}, bf16[1,40,640]{2,1,0:T(8,128)(2,1)S(1)}, u32[]{:S(2)}, u32[]{:S(2)}) collective-permute-start(bf16[1,40,640]{2,1,0:T(8,128)(2,1)} %get-tuple-element.114), channel_id=1, source_target_pairs={{0,2},{1,5},{2,0},{3,7},{4,6},{5,1},{6,4},{7,3},{8,10},{9,13},{10,... | collective-permute-start | bytes 153608 | tf_op jit(solution)/shard_map/ppermute | solution.py:826
  9.8 3.1 %shard_map.195 = (f32[512,320]{1,0:T(8,128)}, f32[512,320]{1,0:T(8,128)}, f32[512,1]{1,0:T(8,128)}, bf16[512,512]{1,0:T(8,128)(2,1)}, f32[512,128]{1,0:T(8,128)}, /*index=5*/s32[4]{0:T(128)}) custom-call(s32[2]{0:T(128)} %rows_hbm.1, s32[2]{0:T(128)} %cols_hbm.1, bf16[320,512]{1,0:T(8,128)(2,1)} %bitcast.18), custom_call_target="tpu_custom_call" | custom-call | flops 2000000000 | tf_op jit(solution)/shard_map/pallas_call | solution.py:183
  13.0 2.2 %collective-permute-start.7 = (bf16[2,40,640]{2,1,0:T(8,128)(2,1)S(1)}, bf16[2,40,640]{2,1,0:T(8,128)(2,1)S(1)}, u32[]{:S(2)}, u32[]{:S(2)}) collective-permute-start(bf16[2,40,640]{2,1,0:T(8,128)(2,1)S(1)} %pad_maximum_fusion.3), channel_id=1, source_target_pairs={{0,16},{1,17},{2,18},{3,19},{4,20},{5,21},{6,22},{7,23},{8,24},{9,... | collective-permute-start | bytes 307208 | tf_op jit(solution)/shard_map/ppermute | solution.py:826
  15.3 1.2 %collective-permute-start.5 = (bf16[4,40,640]{2,1,0:T(8,128)(2,1)S(1)}, bf16[4,40,640]{2,1,0:T(8,128)(2,1)S(1)}, u32[]{:S(2)}, u32[]{:S(2)}) collective-permute-start(bf16[4,40,640]{2,1,0:T(8,128)(2,1)S(1)} %pad_maximum_fusion.1), channel_id=1, source_target_pairs={{0,2},{1,5},{2,0},{3,7},{4,6},{5,1},{6,4},{7,3},{8,10},{9,13},{10,... | collective-permute-start | bytes 614408 | tf_op jit(solution)/shard_map/ppermute | solution.py:826
  16.5 4.6 %collective-permute-done.5 = bf16[4,40,640]{2,1,0:T(8,128)(2,1)S(1)} collective-permute-done((bf16[4,40,640]{2,1,0:T(8,128)(2,1)S(1)}, bf16[4,40,640]{2,1,0:T(8,128)(2,1)S(1)}, u32[]{:S(2)}, u32[]{:S(2)}) %collective-permute-start.5) | collective-permute-done | bytes 204832 | tf_op jit(solution)/shard_map/ppermute | solution.py:826
  21.2 1.6 %collective-permute-start.6 = (bf16[8,40,640]{2,1,0:T(8,128)(2,1)S(1)}, bf16[8,40,640]{2,1,0:T(8,128)(2,1)S(1)}, u32[]{:S(2)}, u32[]{:S(2)}) collective-permute-start(bf16[8,40,640]{2,1,0:T(8,128)(2,1)S(1)} %get-tuple-element.208), channel_id=1, source_target_pairs={{0,4},{1,3},{2,6},{3,1},{4,0},{5,7},{6,2},{7,5},{8,12},{9,11},{10,... | collective-permute-start | bytes 1228808 | tf_op jit(solution)/shard_map/ppermute | solution.py:826
  22.8 2.1 %collective-permute-start.8 = (bf16[4,40,640]{2,1,0:T(8,128)(2,1)S(1)}, bf16[4,40,640]{2,1,0:T(8,128)(2,1)S(1)}, u32[]{:S(2)}, u32[]{:S(2)}) collective-permute-start(bf16[4,40,640]{2,1,0:T(8,128)(2,1)S(1)} %pad_maximum_fusion.2), channel_id=1, source_target_pairs={{0,8},{1,9},{2,10},{3,11},{4,12},{5,13},{6,14},{7,15},{8,0},{9,1},... | collective-permute-start | bytes 614408 | tf_op jit(solution)/shard_map/ppermute | solution.py:826
  24.9 1.2 %collective-permute-start.9 = (bf16[2,16,640]{2,1,0:T(8,128)(2,1)S(1)}, bf16[2,16,640]{2,1,0:T(8,128)(2,1)S(1)}, u32[]{:S(2)}, u32[]{:S(2)}) collective-permute-start(bf16[2,16,640]{2,1,0:T(8,128)(2,1)S(1)} %pad_maximum_fusion.5), channel_id=1, source_target_pairs={{0,2},{1,3},{2,0},{3,1},{4,6},{5,7},{6,4},{7,5},{8,10},{9,11},{10,... | collective-permute-start | bytes 122888 | tf_op jit(solution)/shard_map/ppermute | solution.py:826
  26.1 2.9 %collective-permute-done.9 = bf16[2,16,640]{2,1,0:T(8,128)(2,1)S(1)} collective-permute-done((bf16[2,16,640]{2,1,0:T(8,128)(2,1)S(1)}, bf16[2,16,640]{2,1,0:T(8,128)(2,1)S(1)}, u32[]{:S(2)}, u32[]{:S(2)}) %collective-permute-start.9) | collective-permute-done | bytes 40992 | tf_op jit(solution)/shard_map/ppermute | solution.py:826
  29.5 1.6 %collective-permute-start.11 = (bf16[8,40,640]{2,1,0:T(8,128)(2,1)S(1)}, bf16[8,40,640]{2,1,0:T(8,128)(2,1)S(1)}, u32[]{:S(2)}, u32[]{:S(2)}) collective-permute-start(bf16[8,40,640]{2,1,0:T(8,128)(2,1)S(1)} %get-tuple-element.132), channel_id=1, source_target_pairs={{0,4},{1,3},{2,6},{3,1},{4,0},{5,7},{6,2},{7,5},{8,12},{9,11},{10,... | collective-permute-start | bytes 1228808 | tf_op jit(solution)/shard_map/ppermute | solution.py:826
  31.8 4.8 %shard_map.197 = (f32[512,320]{1,0:T(8,128)S(1)}, bf16[512,320]{1,0:T(8,128)(2,1)S(1)}, bf16[512,320]{1,0:T(8,128)(2,1)S(1)}, f32[128,320]{1,0:T(8,128)S(1)}, f3...) custom-call(s32[4]{0:T(128)S(1)} %copy-done.6, ...), custom_call_target="tpu_custom_call" | custom-call | flops 8000000000 | tf_op jit(solution)/shard_map/pallas_call | solution.py:790
  38.1 1.1 %collective-permute-done.13 = bf16[8,40,640]{2,1,0:T(8,128)(2,1)S(1)} collective-permute-done((bf16[8,40,640]{2,1,0:T(8,128)(2,1)S(1)}, bf16[8,40,640]{2,1,0:T(8,128)(2,1)S(1)}, u32[]{:S(2)}, u32[]{:S(2)}) %collective-permute-start.13) | collective-permute-done | bytes 409632 | tf_op jit(solution)/shard_map/ppermute | solution.py:826
  39.3 11.5 %shard_map.199 = (bf16[16,40,640]{2,1,0:T(8,128)(2,1)S(1)}, bf16[16,40,640]{2,1,0:T(8,128)(2,1)S(1)}, bf16[512,1280]{1,0:T(8,128)(2,1)S(1)}, bf16[512,1280]{1,0:...) custom-call(s32[4]{0:T(128)S(1)} %copy-done.6, ...), custom_call_target="tpu_custom_call", output_to_operand_aliasing={{5}: (9, {}), {6}: (10, {})} | custom-call | flops 32999999488 | tf_op jit(solution)/shard_map/pallas_call | solution.py:790
  51.1 2.5 %shard_map.200 = (f32[320,320]{1,0:T(8,128)S(1)}, bf16[512,320]{1,0:T(8,128)(2,1)S(1)}, bf16[512,640]{1,0:T(8,128)(2,1)S(1)}, f32[1,320]{1,0:T(1,128)S(1)}, f32[...) custom-call(bf16[512,1280]{1,0:T(8,128)(2,1)S(1)} %get-tuple-element.136.df_ref, ...), custom_call_target="tpu_custom_call" | custom-call | flops 2500000000 | tf_op jit(solution)/shard_map/pallas_call | solution.py:790
  53.9 1.5 %collective-permute-start.15 = (bf16[8,40,640]{2,1,0:T(8,128)(2,1)S(1)}, bf16[8,40,640]{2,1,0:T(8,128)(2,1)S(1)}, u32[]{:S(2)}, u32[]{:S(2)}) collective-permute-start(bf16[8,40,640]{2,1,0:T(8,128)(2,1)S(1)} %get-tuple-element.149), channel_id=1, source_target_pairs={{0,4},{1,3},{2,6},{3,1},{4,0},{5,7},{6,2},{7,5},{8,12},{9,11},{10,... | collective-permute-start | bytes 1228808 | tf_op jit(solution)/shard_map/ppermute | solution.py:826
  55.4 2.7 %shard_map.202 = (bf16[16,40,640]{2,1,0:T(8,128)(2,1)S(1)}, bf16[16,40,640]{2,1,0:T(8,128)(2,1)S(1)}, bf16[512,320]{1,0:T(8,128)(2,1)S(1)}, f32[512,320]{1,0:T(8,128)S(1)}, f32[8,320]{1,0:T(8,128)S(1)}) custom-call(bf16[512,320]{1,0:T(8,128)(2,1)S(1)} %get-tuple-element.144.dob_ref, bf16[512,640]{1,0:T(8,128)(2,1)S(1)} %get-tuple-element.150.ds_ref, ...), custom_call_target="tpu_custom_call" | custom-call | tf_op jit(solution)/shard_map/pallas_call | solution.py:790
  58.2 2.2 %shard_map.204 = (bf16[320,512]{1,0:T(8,128)(2,1)}, bf16[2,8,640]{2,1,0:T(8,128)(2,1)S(1)}, bf16[2,8,640]{2,1,0:T(8,128)(2,1)S(1)}) custom-call(f32[512,320]{1,0:T(8,128)S(1)} %get-tuple-element.166.dx2_ref, bf16[512,320]{1,0:T(8,128)(2,1)S(1)} %get-tuple-element.167.dq_ref, f32[512,320]{1,0:T(8,128)S(1)} %get-tuple-element.168.dpatch_ref, ...), custom_call_target="tpu_custom_call" | custom-call | tf_op jit(solution)/shard_map/pallas_call | solution.py:790
  60.9 1.0 %collective-permute-done.15.got_ref = bf16[8,40,640]{2,1,0:T(8,128)(2,1)S(1)} collective-permute-done((bf16[8,40,640]{2,1,0:T(8,128)(2,1)S(1)}, bf16[8,40,640]{2,1,0:T(8,128)(2,1)S(1)}, u32[]{:S(2)}, u32[]{:S(2)}) %collective-permute-start.15) | collective-permute-done | bytes 409632 | tf_op jit(solution)/shard_map/ppermute | solution.py:826
  62.2 1.5 %collective-permute-start.18 = (bf16[336,640]{1,0:T(8,128)(2,1)S(1)}, bf16[336,640]{1,0:T(8,128)(2,1)S(1)}, u32[]{:S(2)}, u32[]{:S(2)}) collective-permute-start(bf16[336,640]{1,0:T(8,128)(2,1)S(1)} %get-tuple-element.177), channel_id=1, source_target_pairs={{0,4},{1,3},{2,6},{3,1},{4,0},{5,7},{6,2},{7,5},{8,12},{9,11},{10,... | collective-permute-start | bytes 1290248 | tf_op jit(solution)/shard_map/ppermute | solution.py:826
  63.7 2.0 %collective-permute-start.19 = (bf16[4,40,640]{2,1,0:T(8,128)(2,1)S(1)}, bf16[4,40,640]{2,1,0:T(8,128)(2,1)S(1)}, u32[]{:S(2)}, u32[]{:S(2)}) collective-permute-start(bf16[4,40,640]{2,1,0:T(8,128)(2,1)S(1)} %get-tuple-element.163), channel_id=1, source_target_pairs={{0,8},{1,9},{2,10},{3,11},{4,12},{5,13},{6,14},{7,15},{8,0},{9,1},... | collective-permute-start | bytes 614408 | tf_op jit(solution)/shard_map/ppermute | solution.py:826
  65.7 1.7 %shard_map.206 = bf16[320,512]{1,0:T(8,128)(2,1)} custom-call(f32[512,320]{1,0:T(8,128)S(1)} %get-tuple-element.123.x2_ref, bf16[512,1280]{1,0:T(8,128)(2,1)S(1)} %get-tuple-element.178.act_ref, bf16[320,1280]{1,0:T(8,128)(2,1)S(1)} %get-tuple-element.179.wd_ref, f32[16,320]{1,0:T(8,128)S(1)} %get-tuple-element.124.mv_ref, ...), custom_call_target="tpu_custom_call" | custom-call | flops 1000000000 | tf_op jit(solution)/shard_map/pallas_call | solution.py:790
  67.4 3.0 %collective-permute-done.19.got_ref = bf16[4,40,640]{2,1,0:T(8,128)(2,1)S(1)} collective-permute-done((bf16[4,40,640]{2,1,0:T(8,128)(2,1)S(1)}, bf16[4,40,640]{2,1,0:T(8,128)(2,1)S(1)}, u32[]{:S(2)}, u32[]{:S(2)}) %collective-permute-start.19) | collective-permute-done | bytes 204832 | tf_op jit(solution)/shard_map/ppermute | solution.py:826
  70.6 1.1 %collective-permute-start.20 = (bf16[168,640]{1,0:T(8,128)(2,1)S(1)}, bf16[168,640]{1,0:T(8,128)(2,1)S(1)}, u32[]{:S(2)}, u32[]{:S(2)}) collective-permute-start(bf16[168,640]{1,0:T(8,128)(2,1)S(1)} %get-tuple-element.187), channel_id=1, source_target_pairs={{0,2},{1,5},{2,0},{3,7},{4,6},{5,1},{6,4},{7,3},{8,10},{9,13},{10,... | collective-permute-start | bytes 645128 | tf_op jit(solution)/shard_map/ppermute | solution.py:826
  71.7 1.5 %collective-permute-start.24 = (bf16[2,40,640]{2,1,0:T(8,128)(2,1)S(1)}, bf16[2,40,640]{2,1,0:T(8,128)(2,1)S(1)}, u32[]{:S(2)}, u32[]{:S(2)}) collective-permute-start(bf16[2,40,640]{2,1,0:T(8,128)(2,1)S(1)} %get-tuple-element.195), channel_id=1, source_target_pairs={{0,16},{1,17},{2,18},{3,19},{4,20},{5,21},{6,22},{7,23},{8,24},{9,... | collective-permute-start | bytes 307208 | tf_op jit(solution)/shard_map/ppermute | solution.py:826
  73.2 3.3 %collective-permute-done.20.got_ref = bf16[168,640]{1,0:T(8,128)(2,1)S(1)} collective-permute-done((bf16[168,640]{1,0:T(8,128)(2,1)S(1)}, bf16[168,640]{1,0:T(8,128)(2,1)S(1)}, u32[]{:S(2)}, u32[]{:S(2)}) %collective-permute-start.20) | collective-permute-done | bytes 215072 | tf_op jit(solution)/shard_map/ppermute | solution.py:826
  76.6 2.0 %collective-permute-start.21 = (bf16[48,640]{1,0:T(8,128)(2,1)S(1)}, bf16[48,640]{1,0:T(8,128)(2,1)S(1)}, u32[]{:S(2)}, u32[]{:S(2)}) collective-permute-start(bf16[48,640]{1,0:T(8,128)(2,1)S(1)} %get-tuple-element.189), channel_id=1, source_target_pairs={{0,8},{1,9},{2,10},{3,11},{4,12},{5,13},{6,14},{7,15},{8,0},{9,1},... | collective-permute-start | bytes 184328 | tf_op jit(solution)/shard_map/ppermute | solution.py:826
  79.3 1.7 %collective-permute-start.23 = (bf16[48,640]{1,0:T(8,128)(2,1)S(1)}, bf16[48,640]{1,0:T(8,128)(2,1)S(1)}, u32[]{:S(2)}, u32[]{:S(2)}) collective-permute-start(bf16[48,640]{1,0:T(8,128)(2,1)S(1)} %get-tuple-element.191), channel_id=1, source_target_pairs={{0,24},{1,25},{2,26},{3,27},{4,28},{5,29},{6,30},{7,31},{8,16},{9,... | collective-permute-start | bytes 184328 | tf_op jit(solution)/shard_map/ppermute | solution.py:826
  81.1 1.2 %collective-permute-start.25 = (bf16[1,40,640]{2,1,0:T(8,128)(2,1)S(1)}, bf16[1,40,640]{2,1,0:T(8,128)(2,1)S(1)}, u32[]{:S(2)}, u32[]{:S(2)}) collective-permute-start(bf16[1,40,640]{2,1,0:T(8,128)(2,1)S(1)} %get-tuple-element.197), channel_id=1, source_target_pairs={{0,2},{1,5},{2,0},{3,7},{4,6},{5,1},{6,4},{7,3},{8,10},{9,13},{10,... | collective-permute-start | bytes 153608 | tf_op jit(solution)/shard_map/ppermute | solution.py:826
  82.2 3.0 %collective-permute-done.25.ffn_got_ref = bf16[1,40,640]{2,1,0:T(8,128)(2,1)S(1)} collective-permute-done((bf16[1,40,640]{2,1,0:T(8,128)(2,1)S(1)}, bf16[1,40,640]{2,1,0:T(8,128)(2,1)S(1)}, u32[]{:S(2)}, u32[]{:S(2)}) %collective-permute-start.25) | collective-permute-done | bytes 51232 | tf_op jit(solution)/shard_map/ppermute | solution.py:826
  85.3 0.9 %shard_map.211 = (f32[40,80]{1,0:T(8,128)}, f32[80,80]{1,0:T(8,128)}, f32[40,320]{1,0:T(8,128)}, f32[40,80]{1,0:T(8,128)}, f32[80,160]{1,0:T(8,128)}, /*index=5*...) custom-call(bf16[48,640]{1,0:T(8,128)(2,1)S(1)} %get-tuple-element.188.a_ref, ...), custom_call_target="tpu_custom_call" | custom-call | tf_op jit(solution)/shard_map/pallas_call | solution.py:790
  (73 shorter events, 6.1 us)
Async XLA Ops:
  2.4 10.6 %collective-permute-start.2 = (bf16[1,40,640]{2,1,0:T(8,128)(2,1)}, bf16[1,40,640]{2,1,0:T(8,128)(2,1)S(1)}, u32[]{:S(2)}, u32[]{:S(2)}) collective-permute-start(bf16[1,40,640]{2,1,0:T(8,128)(2,1)} %get-tuple-element.113), channel_id=1, source_target_pairs={{0,24},{1,25},{2,26},{3,27},{4,28},{5,29},{6,30},{7,31},{8,16},{9,... | collective-permute-start | bytes 153608 | tf_op jit(solution)/shard_map/ppermute | solution.py:826
  7.5 5.5 %collective-permute-start.1 = (bf16[1,40,640]{2,1,0:T(8,128)(2,1)}, bf16[1,40,640]{2,1,0:T(8,128)(2,1)S(1)}, u32[]{:S(2)}, u32[]{:S(2)}) collective-permute-start(bf16[1,40,640]{2,1,0:T(8,128)(2,1)} %get-tuple-element.113), channel_id=1, source_target_pairs={{0,16},{1,17},{2,18},{3,19},{4,20},{5,21},{6,22},{7,23},{8,24},{9,... | collective-permute-start | bytes 153608 | tf_op jit(solution)/shard_map/ppermute | solution.py:826
  7.5 5.5 %collective-permute-start = (bf16[1,40,640]{2,1,0:T(8,128)(2,1)}, bf16[1,40,640]{2,1,0:T(8,128)(2,1)S(1)}, u32[]{:S(2)}, u32[]{:S(2)}) collective-permute-start(bf16[1,40,640]{2,1,0:T(8,128)(2,1)} %get-tuple-element.113), channel_id=1, source_target_pairs={{0,8},{1,9},{2,10},{3,11},{4,12},{5,13},{6,14},{7,15},{8,0},{9,1},... | collective-permute-start | bytes 153608 | tf_op jit(solution)/shard_map/ppermute | solution.py:826
  8.1 4.8 %collective-permute-start.4 = (bf16[1,16,640]{2,1,0:T(8,128)(2,1)}, bf16[1,16,640]{2,1,0:T(8,128)(2,1)S(1)}, u32[]{:S(2)}, u32[]{:S(2)}) collective-permute-start(bf16[1,16,640]{2,1,0:T(8,128)(2,1)} %get-tuple-element.115), channel_id=1, source_target_pairs={{0,1},{1,0},{2,3},{3,2},{4,5},{5,4},{6,7},{7,6},{8,9},{9,8},{10,11... | collective-permute-start | bytes 61448 | tf_op jit(solution)/shard_map/ppermute | solution.py:826
  8.1 4.8 %collective-permute-start.3 = (bf16[1,40,640]{2,1,0:T(8,128)(2,1)}, bf16[1,40,640]{2,1,0:T(8,128)(2,1)S(1)}, u32[]{:S(2)}, u32[]{:S(2)}) collective-permute-start(bf16[1,40,640]{2,1,0:T(8,128)(2,1)} %get-tuple-element.114), channel_id=1, source_target_pairs={{0,2},{1,5},{2,0},{3,7},{4,6},{5,1},{6,4},{7,3},{8,10},{9,13},{10,... | collective-permute-start | bytes 153608 | tf_op jit(solution)/shard_map/ppermute | solution.py:826
  12.9 12.0 %copy-start.9 = (bf16[1,16,640]{2,1,0:T(8,128)(2,1)S(1)}, bf16[1,16,640]{2,1,0:T(8,128)(2,1)}, u32[]{:S(2)}) copy-start(bf16[1,16,640]{2,1,0:T(8,128)(2,1)} %get-tuple-element.115) | copy-start | bytes 61444
  13.0 9.8 %collective-permute-start.7 = (bf16[2,40,640]{2,1,0:T(8,128)(2,1)S(1)}, bf16[2,40,640]{2,1,0:T(8,128)(2,1)S(1)}, u32[]{:S(2)}, u32[]{:S(2)}) collective-permute-start(bf16[2,40,640]{2,1,0:T(8,128)(2,1)S(1)} %pad_maximum_fusion.3), channel_id=1, source_target_pairs={{0,16},{1,17},{2,18},{3,19},{4,20},{5,21},{6,22},{7,23},{8,24},{9,... | collective-permute-start | bytes 307208 | tf_op jit(solution)/shard_map/ppermute | solution.py:826
  15.3 5.8 %collective-permute-start.5 = (bf16[4,40,640]{2,1,0:T(8,128)(2,1)S(1)}, bf16[4,40,640]{2,1,0:T(8,128)(2,1)S(1)}, u32[]{:S(2)}, u32[]{:S(2)}) collective-permute-start(bf16[4,40,640]{2,1,0:T(8,128)(2,1)S(1)} %pad_maximum_fusion.1), channel_id=1, source_target_pairs={{0,2},{1,5},{2,0},{3,7},{4,6},{5,1},{6,4},{7,3},{8,10},{9,13},{10,... | collective-permute-start | bytes 614408 | tf_op jit(solution)/shard_map/ppermute | solution.py:826
  21.1 10.7 %copy-start.5 = (f32[512,128]{1,0:T(8,128)S(1)}, f32[512,128]{1,0:T(8,128)}, u32[]{:S(2)}) copy-start(f32[512,128]{1,0:T(8,128)} %get-tuple-element.112.live_ref) | copy-start | bytes 786436
  21.1 10.7 %copy-start = (f32[512,320]{1,0:T(8,128)S(1)}, f32[512,320]{1,0:T(8,128)}, u32[]{:S(2)}) copy-start(f32[512,320]{1,0:T(8,128)} %get-tuple-element.110.n1_ref) | copy-start | bytes 1966084
  21.1 10.7 %copy-start.1 = (bf16[512,512]{1,0:T(8,128)(2,1)S(1)}, bf16[512,512]{1,0:T(8,128)(2,1)}, u32[]{:S(2)}) copy-start(bf16[512,512]{1,0:T(8,128)(2,1)} %get-tuple-element.111.chosen_ref) | copy-start | bytes 1572868
  21.2 10.7 %copy-start.3 = (bf16[512,320]{0,1:T(8,128)(2,1)S(1)}, bf16[512,320]{0,1:T(8,128)(2,1)}, u32[]{:S(2)}) copy-start(bf16[512,320]{0,1:T(8,128)(2,1)} %param.13) | copy-start | bytes 983044
  21.2 10.6 %copy-start.4 = (f32[512,320]{1,0:T(8,128)S(1)}, f32[512,320]{1,0:T(8,128)}, u32[]{:S(2)}) copy-start(f32[512,320]{1,0:T(8,128)} %get-tuple-element.109.x_ref) | copy-start | bytes 1966084
  21.2 8.0 %collective-permute-start.6 = (bf16[8,40,640]{2,1,0:T(8,128)(2,1)S(1)}, bf16[8,40,640]{2,1,0:T(8,128)(2,1)S(1)}, u32[]{:S(2)}, u32[]{:S(2)}) collective-permute-start(bf16[8,40,640]{2,1,0:T(8,128)(2,1)S(1)} %get-tuple-element.208), channel_id=1, source_target_pairs={{0,4},{1,3},{2,6},{3,1},{4,0},{5,7},{6,2},{7,5},{8,12},{9,11},{10,... | collective-permute-start | bytes 1228808 | tf_op jit(solution)/shard_map/ppermute | solution.py:826
  22.8 6.2 %collective-permute-start.8 = (bf16[4,40,640]{2,1,0:T(8,128)(2,1)S(1)}, bf16[4,40,640]{2,1,0:T(8,128)(2,1)S(1)}, u32[]{:S(2)}, u32[]{:S(2)}) collective-permute-start(bf16[4,40,640]{2,1,0:T(8,128)(2,1)S(1)} %pad_maximum_fusion.2), channel_id=1, source_target_pairs={{0,8},{1,9},{2,10},{3,11},{4,12},{5,13},{6,14},{7,15},{8,0},{9,1},... | collective-permute-start | bytes 614408 | tf_op jit(solution)/shard_map/ppermute | solution.py:826
  24.9 4.1 %collective-permute-start.9 = (bf16[2,16,640]{2,1,0:T(8,128)(2,1)S(1)}, bf16[2,16,640]{2,1,0:T(8,128)(2,1)S(1)}, u32[]{:S(2)}, u32[]{:S(2)}) collective-permute-start(bf16[2,16,640]{2,1,0:T(8,128)(2,1)S(1)} %pad_maximum_fusion.5), channel_id=1, source_target_pairs={{0,2},{1,3},{2,0},{3,1},{4,6},{5,7},{6,4},{7,5},{8,10},{9,11},{10,... | collective-permute-start | bytes 122888 | tf_op jit(solution)/shard_map/ppermute | solution.py:826
  29.3 2.4 %collective-permute-start.10 = (bf16[16,40,640]{2,1,0:T(8,128)(2,1)S(1)}, bf16[16,40,640]{2,1,0:T(8,128)(2,1)S(1)}, u32[]{:S(2)}, u32[]{:S(2)}) collective-permute-start(bf16[16,40,640]{2,1,0:T(8,128)(2,1)S(1)} %constant_dynamic-update-slice_fusion.5.own_ref), channel_id=1, source_target_pairs={{0,1},{1,0},{2,3},{3,2},{4,5},{5,4},{6,7},{7,6},{8,9},{9,8},{10,11... | collective-permute-start | bytes 2457608 | tf_op jit(solution)/shard_map/ppermute | solution.py:826
  29.5 8.0 %collective-permute-start.11 = (bf16[8,40,640]{2,1,0:T(8,128)(2,1)S(1)}, bf16[8,40,640]{2,1,0:T(8,128)(2,1)S(1)}, u32[]{:S(2)}, u32[]{:S(2)}) collective-permute-start(bf16[8,40,640]{2,1,0:T(8,128)(2,1)S(1)} %get-tuple-element.132), channel_id=1, source_target_pairs={{0,4},{1,3},{2,6},{3,1},{4,0},{5,7},{6,2},{7,5},{8,12},{9,11},{10,... | collective-permute-start | bytes 1228808 | tf_op jit(solution)/shard_map/ppermute | solution.py:826
  31.7 6.5 %collective-permute-start.12 = (bf16[8,40,640]{2,1,0:T(8,128)(2,1)S(1)}, bf16[8,40,640]{2,1,0:T(8,128)(2,1)S(1)}, u32[]{:S(2)}, u32[]{:S(2)}) collective-permute-start(bf16[8,40,640]{2,1,0:T(8,128)(2,1)S(1)} %get-tuple-element.132), channel_id=1, source_target_pairs={{0,1},{1,0},{2,3},{3,2},{4,5},{5,4},{6,7},{7,6},{8,9},{9,8},{10,11... | collective-permute-start | bytes 1228808 | tf_op jit(solution)/shard_map/ppermute | solution.py:826
  37.5 1.7 %collective-permute-start.13 = (bf16[8,40,640]{2,1,0:T(8,128)(2,1)S(1)}, bf16[8,40,640]{2,1,0:T(8,128)(2,1)S(1)}, u32[]{:S(2)}, u32[]{:S(2)}) collective-permute-start(bf16[8,40,640]{2,1,0:T(8,128)(2,1)S(1)} %collective-permute-done.11), channel_id=1, source_target_pairs={{0,1},{1,0},{2,3},{3,2},{4,5},{5,4},{6,7},{7,6},{8,9},{9,8},{10,11... | collective-permute-start | bytes 1228808 | tf_op jit(solution)/shard_map/ppermute | solution.py:826
  50.8 2.8 %collective-permute-start.14 = (bf16[16,40,640]{2,1,0:T(8,128)(2,1)S(1)}, bf16[16,40,640]{2,1,0:T(8,128)(2,1)S(1)}, u32[]{:S(2)}, u32[]{:S(2)}) collective-permute-start(bf16[16,40,640]{2,1,0:T(8,128)(2,1)S(1)} %get-tuple-element.147), channel_id=1, source_target_pairs={{0,1},{1,0},{2,3},{3,2},{4,5},{5,4},{6,7},{7,6},{8,9},{9,8},{10,11... | collective-permute-start | bytes 2457608 | tf_op jit(solution)/shard_map/ppermute | solution.py:826
  53.9 8.0 %collective-permute-start.15 = (bf16[8,40,640]{2,1,0:T(8,128)(2,1)S(1)}, bf16[8,40,640]{2,1,0:T(8,128)(2,1)S(1)}, u32[]{:S(2)}, u32[]{:S(2)}) collective-permute-start(bf16[8,40,640]{2,1,0:T(8,128)(2,1)S(1)} %get-tuple-element.149), channel_id=1, source_target_pairs={{0,4},{1,3},{2,6},{3,1},{4,0},{5,7},{6,2},{7,5},{8,12},{9,11},{10,... | collective-permute-start | bytes 1228808 | tf_op jit(solution)/shard_map/ppermute | solution.py:826
  58.1 3.9 %collective-permute-start.16 = (bf16[16,40,640]{2,1,0:T(8,128)(2,1)S(1)}, bf16[16,40,640]{2,1,0:T(8,128)(2,1)S(1)}, u32[]{:S(2)}, u32[]{:S(2)}) collective-permute-start(bf16[16,40,640]{2,1,0:T(8,128)(2,1)S(1)} %get-tuple-element.165), channel_id=1, source_target_pairs={{0,1},{1,0},{2,3},{3,2},{4,5},{5,4},{6,7},{7,6},{8,9},{9,8},{10,11... | collective-permute-start | bytes 2457608 | tf_op jit(solution)/shard_map/ppermute | solution.py:826
  60.4 1.6 %collective-permute-start.17 = (bf16[2,8,640]{2,1,0:T(8,128)(2,1)S(1)}, bf16[2,8,640]{2,1,0:T(8,128)(2,1)S(1)}, u32[]{:S(2)}, u32[]{:S(2)}) collective-permute-start(bf16[2,8,640]{2,1,0:T(8,128)(2,1)S(1)} %get-tuple-element.176), channel_id=1, source_target_pairs={{0,1},{1,0},{2,3},{3,2},{4,5},{5,4},{6,7},{7,6},{8,9},{9,8},{10,11... | collective-permute-start | bytes 61448 | tf_op jit(solution)/shard_map/ppermute | solution.py:826
  62.2 8.2 %collective-permute-start.18 = (bf16[336,640]{1,0:T(8,128)(2,1)S(1)}, bf16[336,640]{1,0:T(8,128)(2,1)S(1)}, u32[]{:S(2)}, u32[]{:S(2)}) collective-permute-start(bf16[336,640]{1,0:T(8,128)(2,1)S(1)} %get-tuple-element.177), channel_id=1, source_target_pairs={{0,4},{1,3},{2,6},{3,1},{4,0},{5,7},{6,2},{7,5},{8,12},{9,11},{10,... | collective-permute-start | bytes 1290248 | tf_op jit(solution)/shard_map/ppermute | solution.py:826
  63.7 6.7 %collective-permute-start.19 = (bf16[4,40,640]{2,1,0:T(8,128)(2,1)S(1)}, bf16[4,40,640]{2,1,0:T(8,128)(2,1)S(1)}, u32[]{:S(2)}, u32[]{:S(2)}) collective-permute-start(bf16[4,40,640]{2,1,0:T(8,128)(2,1)S(1)} %get-tuple-element.163), channel_id=1, source_target_pairs={{0,8},{1,9},{2,10},{3,11},{4,12},{5,13},{6,14},{7,15},{8,0},{9,1},... | collective-permute-start | bytes 614408 | tf_op jit(solution)/shard_map/ppermute | solution.py:826
  70.6 5.9 %collective-permute-start.20 = (bf16[168,640]{1,0:T(8,128)(2,1)S(1)}, bf16[168,640]{1,0:T(8,128)(2,1)S(1)}, u32[]{:S(2)}, u32[]{:S(2)}) collective-permute-start(bf16[168,640]{1,0:T(8,128)(2,1)S(1)} %get-tuple-element.187), channel_id=1, source_target_pairs={{0,2},{1,5},{2,0},{3,7},{4,6},{5,1},{6,4},{7,3},{8,10},{9,13},{10,... | collective-permute-start | bytes 645128 | tf_op jit(solution)/shard_map/ppermute | solution.py:826
  71.7 9.3 %collective-permute-start.24 = (bf16[2,40,640]{2,1,0:T(8,128)(2,1)S(1)}, bf16[2,40,640]{2,1,0:T(8,128)(2,1)S(1)}, u32[]{:S(2)}, u32[]{:S(2)}) collective-permute-start(bf16[2,40,640]{2,1,0:T(8,128)(2,1)S(1)} %get-tuple-element.195), channel_id=1, source_target_pairs={{0,16},{1,17},{2,18},{3,19},{4,20},{5,21},{6,22},{7,23},{8,24},{9,... | collective-permute-start | bytes 307208 | tf_op jit(solution)/shard_map/ppermute | solution.py:826
  76.6 8.7 %collective-permute-start.21 = (bf16[48,640]{1,0:T(8,128)(2,1)S(1)}, bf16[48,640]{1,0:T(8,128)(2,1)S(1)}, u32[]{:S(2)}, u32[]{:S(2)}) collective-permute-start(bf16[48,640]{1,0:T(8,128)(2,1)S(1)} %get-tuple-element.189), channel_id=1, source_target_pairs={{0,8},{1,9},{2,10},{3,11},{4,12},{5,13},{6,14},{7,15},{8,0},{9,1},... | collective-permute-start | bytes 184328 | tf_op jit(solution)/shard_map/ppermute | solution.py:826
  78.6 6.7 %collective-permute-start.22 = (bf16[48,640]{1,0:T(8,128)(2,1)S(1)}, bf16[48,640]{1,0:T(8,128)(2,1)S(1)}, u32[]{:S(2)}, u32[]{:S(2)}) collective-permute-start(bf16[48,640]{1,0:T(8,128)(2,1)S(1)} %get-tuple-element.190), channel_id=1, source_target_pairs={{0,16},{1,17},{2,18},{3,19},{4,20},{5,21},{6,22},{7,23},{8,24},{9,... | collective-permute-start | bytes 184328 | tf_op jit(solution)/shard_map/ppermute | solution.py:826
  79.3 6.0 %collective-permute-start.23 = (bf16[48,640]{1,0:T(8,128)(2,1)S(1)}, bf16[48,640]{1,0:T(8,128)(2,1)S(1)}, u32[]{:S(2)}, u32[]{:S(2)}) collective-permute-start(bf16[48,640]{1,0:T(8,128)(2,1)S(1)} %get-tuple-element.191), channel_id=1, source_target_pairs={{0,24},{1,25},{2,26},{3,27},{4,28},{5,29},{6,30},{7,31},{8,16},{9,... | collective-permute-start | bytes 184328 | tf_op jit(solution)/shard_map/ppermute | solution.py:826
  81.1 4.2 %collective-permute-start.25 = (bf16[1,40,640]{2,1,0:T(8,128)(2,1)S(1)}, bf16[1,40,640]{2,1,0:T(8,128)(2,1)S(1)}, u32[]{:S(2)}, u32[]{:S(2)}) collective-permute-start(bf16[1,40,640]{2,1,0:T(8,128)(2,1)S(1)} %get-tuple-element.197), channel_id=1, source_target_pairs={{0,2},{1,5},{2,0},{3,7},{4,6},{5,1},{6,4},{7,3},{8,10},{9,13},{10,... | collective-permute-start | bytes 153608 | tf_op jit(solution)/shard_map/ppermute | solution.py:826
  (4 other events, 19.7 us)

commit v7 on v6

--- a/solution.py
+++ b/solution.py
@@ -560,14 +560,8 @@
             send_ref[jnp.where(even, slot1, slot0)] = jnp.where(even, second, first).astype(BF16)
 
 
-def score_back_kernel(
-    df_ref, wu_ref, n2_ref, r2_ref, gy_ref, mv_ref, vb_ref, p_ref, o_ref, wp_ref,
-    gp_ref, dob_ref, ds_ref, bp_ref, dx2_ref, mg_ref,
-    dp_ref, dh2_ref,
-):
+def norm_two_back_kernel(df_ref, wu_ref, n2_ref, r2_ref, gy_ref, mv_ref, dx2_ref, mg_ref, dh2_ref):
     capacity, width = n2_ref.shape
-    keys = capacity // 4
-
     dh2_ref[...] = dot_nt(df_ref[...], wu_ref[...])
 
     def norm_back(i, carry):
@@ -583,6 +577,10 @@
     for k in range(3):
         mg_ref[8 + k : 9 + k, :] = sums[k]
 
+
+def score_back_kernel(dx2_ref, vb_ref, p_ref, o_ref, wp_ref, gp_ref, dob_ref, ds_ref, bp_ref, dp_ref):
+    capacity = dx2_ref.shape[0]
+    keys = capacity // 4
     datt = dx2_ref[...].astype(BF16)
     bp_ref[...] = column_sum(datt.astype(F32))
     gp_ref[...] = dot_tn(datt, o_ref[...])
@@ -664,6 +662,11 @@
     store_pieces(gown_ref, gsend_ref, me, value_of, round_slot)
 
 
+def token_grad_kernel(dx2_ref, dh1_ref, n1_ref, r1_ref, mv_ref, tg_ref):
+    value = dx2_ref[...] + normalise_back(dh1_ref[...], n1_ref[...], r1_ref[...], mv_ref[0:1, :])
+    tg_ref[...] = value.T.astype(BF16)
+
+
 def mixed_kernel(x2_ref, act_ref, wd_ref, mv_ref, mask_ref, mixed_ref):
     width = x2_ref.shape[1]
     occupied = mask_ref[6]
@@ -687,11 +690,11 @@
 
 def token_back_kernel(
     tuned,
-    dx2_ref, dq_ref, dpatch_ref, n1_ref, r1_ref, chosen_ref, wq_ref, mv_ref, mg_ref, hg_ref, vk_ref, bp_ref,
-    tg_ref, vown_ref, vsend_ref,
+    dq_ref, dpatch_ref, n1_ref, chosen_ref, wq_ref, mg_ref, hg_ref, vk_ref, bp_ref,
+    dh1_ref, vown_ref, vsend_ref,
 ):
     me = my_index(tuned)
-    capacity, width = dx2_ref.shape
+    width = n1_ref.shape[1]
     rn = width // PARTS_N
     chosen = chosen_ref[...]
     high = dpatch_ref[...].astype(BF16)
@@ -699,8 +702,7 @@
     dh1 = dot_nn(dq_ref[...], wq_ref[...]) + dot_tn(chosen, high) + dot_tn(chosen, low)
     n1 = n1_ref[...]
     vk = vk_ref[...]
-    token_grad = dx2_ref[...] + normalise_back(dh1, n1, r1_ref[...], mv_ref[0:1, :])
-    tg_ref[...] = token_grad.T.astype(BF16)
+    dh1_ref[...] = dh1
     sums = rows_of(column_sum(dh1 * n1), column_sum(dh1), vk[0:5], bp_ref[...], mg_ref[8:16, :])
     hg = hg_ref[...]
     value = []
@@ -727,6 +729,18 @@
     half = low_ref.shape[0]
     low_ref[...] = (keep_ref[:half].astype(F32) + got_ref[:half].astype(F32)).astype(BF16)
     high_ref[...] = (keep_ref[half:].astype(F32) + got_ref[half:].astype(F32)).astype(BF16)
+
+
+def core_high_kernel(own_ref, got_ref, high_ref):
+    half = high_ref.shape[0]
+    high_ref[...] = (own_ref[half:].astype(F32) + got_ref[...].astype(F32)).astype(BF16)
+
+
+def core_low_kernel(own_ref, core_ref, got_ref, low_ref, high_ref):
+    half = low_ref.shape[0]
+    total = own_ref[: 2 * half].astype(F32) + core_ref[...].astype(F32) + got_ref[...].astype(F32)
+    low_ref[...] = total[:half].astype(BF16)
+    high_ref[...] = total[half:].astype(BF16)
 
 
 def halve_core_kernel(keep_ref, got_ref, vkeep_ref, vgot_ref, low_ref, vlow_ref, send_ref):
@@ -905,27 +919,33 @@
         flops=33 * 10**9,
     )
 
+    dx2, mg = call(
+        norm_two_back_kernel,
+        (df, wu, n2, r2, gy, mv),
+        (tokens_f32, ((16, width), F32)),
+        scratch=(tokens_f32,),
+        flops=10**9,
+    )
     if tuned:
-        got_b = swap(gsend_b, 1)
-    gp, dob, ds, bp, dx2, mg = call(
+        core_high, core_low = swap(gsend_b[8:], 1), swap(gsend_b[:8], 1)
+        core_high, dx2 = lax.optimization_barrier((core_high, dx2))
+        (high_b,) = call(core_high_kernel, (gown_b, core_high), (((8,) + piece, BF16),))
+        got_b = swap(high_b, 4, 2)
+        dx2 = after(dx2, high_b)
+    gp, dob, ds, bp = call(
         score_back_kernel,
-        (df, wu, n2, r2, gy, mv, vb, p, o, wp),
+        (dx2, vb, p, o, wp),
         (
             (square, F32), ((capacity, width), BF16), ((capacity, HEADS * keys), BF16), ((1, width), F32),
-            tokens_f32, ((16, width), F32),
         ),
-        scratch=(((capacity, HEADS * keys), F32), tokens_f32),
-        flops=25 * 10**8,
-    )
+        scratch=(((capacity, HEADS * keys), F32),),
+        flops=0,
+    )
+
     def halve(keep, got, flops=0):
         shape = ((keep.shape[0] // 2,) + piece, BF16)
         return call(halve_kernel, (keep, got), (shape, shape), flops=flops)
 
-    if tuned:
-        got_b = after(got_b, ds)
-        low_b, high_b = halve(gown_b, got_b)
-        ds = after(ds, high_b)
-        got_b = swap(high_b, 4, 2)
     gown_a, gsend_a, dq, dpatch, vk = call(
         functools.partial(attend_back_kernel, tuned),
         (dob, ds, gp, h1, patches, nk, rk, kn, q, kb, p, wr, wkv, mv),
@@ -938,14 +958,18 @@
     )
     if tuned:
         got_a = swap(gsend_a, 1)
-        low_b, high_b = halve(low_b, got_b, flops=7 * 10**9)
+        low_b, high_b = call(
+            core_low_kernel, (gown_b, core_low, got_b), (((4,) + piece, BF16),) * 2, flops=7*10**9
+        )
         gown_a = after(gown_a, high_b)
     (mixed,) = call(mixed_kernel, (x2, act, wd, mv, masks), (((width, capacity), BF16),), flops=10**9)
-    token_grad, vown, vsend = call(
+    dh1, vown, vsend = call(
         functools.partial(token_back_kernel, tuned),
-        (dx2, dq, dpatch, n1, r1, chosen, wq, mv, mg, hg, vk, bp),
-        (((width, capacity), BF16), ((2,) + gpiece, BF16), ((2,) + gpiece, BF16)),
-    )
+        (dq, dpatch, n1, chosen, wq, mg, hg, vk, bp),
+        (tokens_f32, ((2,) + gpiece, BF16), ((2,) + gpiece, BF16)),
+    )
+
+    (token_grad,) = call(token_grad_kernel, (dx2, dh1, n1, r1, mv), (((width, capacity), BF16),), flops=10**9)
 
     if not tuned:
         grads = scatter_plain(mesh_shape, width, gown_a, gsend_a, gown_b, gsend_b, vown, vsend)
@@ -957,7 +981,7 @@
         (gown_a, got_a, vown, swap(vsend, 1)),
         (((8,) + piece, BF16), ((2,) + gpiece, BF16), ((8 * cw + 2 * vrows, 2 * width), BF16)),
     )
-    got_a, got_b, mixed = lax.optimization_barrier((swap(high_a, 4, 2), swap(high_b, 8), mixed))
+    got_a, got_b, mixed, token_grad = lax.optimization_barrier((swap(high_a, 4, 2), swap(high_b, 8), mixed, token_grad))
     low_a, vlow, high_a = call(
         functools.partial(halve_round_kernel, tuned),
         (low_a, vlow, got_a),

time: 86.6 us -> 85.9 us (level)
  waiting for transfers between devices: 20.6 us -> 19.7 us
    ppermute x26 -> x27, waiting for transfers between devices: 20.6 us -> 19.7 us  [swap(): return lax.ppermute(value, ('wide', 'narrow'), pairs)]
    pallas_call x15 -> x17, Pallas kernels: 27.7 us -> 27.9 us  [call(): pl.pallas_call(kernel, out_shape=[jax.ShapeDtypeStruct(shape, kind) for s...]
    ppermute x26 -> x27, starting transfers between devices: 31.5 us -> 31.6 us  [swap(): return lax.ppermute(value, ('wide', 'narrow'), pairs)]
  transfers between devices with their start and end apart: 26 -> 27, of which waited for: 11 -> 10; matrix products, arithmetic and copies ran while one was open for 0% -> 0% of each run, Pallas kernels for 21% -> 21%
where the time goes in v7:
time: 85.9 us; the launch traced here: 85.6 us
  Pallas kernels  32.7 us (38%)
  starting transfers between devices  31.6 us (37%)
  waiting for transfers between devices  19.7 us (23%)
  between operations  0.98 us (1%)
    ppermute x27, starting transfers between devices, swap(): return lax.ppermute(value, ('wide', 'narrow'), pairs)  31.6 us
    pallas_call x17, Pallas kernels, call(): pl.pallas_call(kernel, out_shape=[jax.ShapeDtypeStruct(shape, kind) for s...  27.9 us
    ppermute x27, waiting for transfers between devices, swap(): return lax.ppermute(value, ('wide', 'narrow'), pairs)  19.7 us
    pallas_call x1, Pallas kernels, prepare(): pl.pallas_call(prepare_kernel, out_shape=[jax.ShapeDtypeStruct(shape, kin...  3.1 us
  transfers between devices with their start and end apart: 27, of which 10 were waited for; matrix products, arithmetic and copies ran while one was open for 0% of the time, Pallas kernels for 21%

profile of v7, /device:TPU:0, one launch (start us, length us, event | category | flops | bytes accessed | tf_op | source)
XLA Modules:
  0.0 85.6 jit_solution(8616693277590525119)
XLA Ops:
  0.6 1.7 %shard_map.196 = (bf16[1,40,640]{2,1,0:T(8,128)(2,1)}, bf16[1,40,640]{2,1,0:T(8,128)(2,1)}, bf16[1,16,640]{2,1,0:T(8,128)(2,1)}) custom-call(bf16[40,80]{1,0:T(8,128)(2,1)} %bitcast.16, bf16[80,80]{1,0:T(8,128)(2,1)} %refs_1_.1, bf16[40,320]{1,0:T(8,128)(2,1)} %bitcast.14, bf16[40,80]{1,0:T(8,128)(2,1)} %bitcast.17, bf16[80,160]{1,0:T(8,128)(2,1)} %refs_4_.1, ...), custom_call_target="tpu_custom_call" | custom-call | tf_op jit(solution)/shard_map/pallas_call | solution.py:133
  2.4 5.1 %collective-permute-start.2 = (bf16[1,40,640]{2,1,0:T(8,128)(2,1)}, bf16[1,40,640]{2,1,0:T(8,128)(2,1)S(1)}, u32[]{:S(2)}, u32[]{:S(2)}) collective-permute-start(bf16[1,40,640]{2,1,0:T(8,128)(2,1)} %get-tuple-element.113), channel_id=1, source_target_pairs={{0,24},{1,25},{2,26},{3,27},{4,28},{5,29},{6,30},{7,31},{8,16},{9,... | collective-permute-start | bytes 153608 | tf_op jit(solution)/shard_map/ppermute | solution.py:840
  8.1 1.6 %collective-permute-start.3 = (bf16[1,40,640]{2,1,0:T(8,128)(2,1)}, bf16[1,40,640]{2,1,0:T(8,128)(2,1)S(1)}, u32[]{:S(2)}, u32[]{:S(2)}) collective-permute-start(bf16[1,40,640]{2,1,0:T(8,128)(2,1)} %get-tuple-element.114), channel_id=1, source_target_pairs={{0,2},{1,5},{2,0},{3,7},{4,6},{5,1},{6,4},{7,3},{8,10},{9,13},{10,... | collective-permute-start | bytes 153608 | tf_op jit(solution)/shard_map/ppermute | solution.py:840
  9.8 3.1 %shard_map.195 = (f32[512,320]{1,0:T(8,128)}, f32[512,320]{1,0:T(8,128)}, f32[512,1]{1,0:T(8,128)}, bf16[512,512]{1,0:T(8,128)(2,1)}, f32[512,128]{1,0:T(8,128)}, /*index=5*/s32[4]{0:T(128)}) custom-call(s32[2]{0:T(128)} %rows_hbm.1, s32[2]{0:T(128)} %cols_hbm.1, bf16[320,512]{1,0:T(8,128)(2,1)} %bitcast.18), custom_call_target="tpu_custom_call" | custom-call | flops 2000000000 | tf_op jit(solution)/shard_map/pallas_call | solution.py:183
  13.0 2.2 %collective-permute-start.7 = (bf16[2,40,640]{2,1,0:T(8,128)(2,1)S(1)}, bf16[2,40,640]{2,1,0:T(8,128)(2,1)S(1)}, u32[]{:S(2)}, u32[]{:S(2)}) collective-permute-start(bf16[2,40,640]{2,1,0:T(8,128)(2,1)S(1)} %pad_maximum_fusion.3), channel_id=1, source_target_pairs={{0,16},{1,17},{2,18},{3,19},{4,20},{5,21},{6,22},{7,23},{8,24},{9,... | collective-permute-start | bytes 307208 | tf_op jit(solution)/shard_map/ppermute | solution.py:840
  15.3 1.2 %collective-permute-start.5 = (bf16[4,40,640]{2,1,0:T(8,128)(2,1)S(1)}, bf16[4,40,640]{2,1,0:T(8,128)(2,1)S(1)}, u32[]{:S(2)}, u32[]{:S(2)}) collective-permute-start(bf16[4,40,640]{2,1,0:T(8,128)(2,1)S(1)} %pad_maximum_fusion.1), channel_id=1, source_target_pairs={{0,2},{1,5},{2,0},{3,7},{4,6},{5,1},{6,4},{7,3},{8,10},{9,13},{10,... | collective-permute-start | bytes 614408 | tf_op jit(solution)/shard_map/ppermute | solution.py:840
  16.5 4.6 %collective-permute-done.5 = bf16[4,40,640]{2,1,0:T(8,128)(2,1)S(1)} collective-permute-done((bf16[4,40,640]{2,1,0:T(8,128)(2,1)S(1)}, bf16[4,40,640]{2,1,0:T(8,128)(2,1)S(1)}, u32[]{:S(2)}, u32[]{:S(2)}) %collective-permute-start.5) | collective-permute-done | bytes 204832 | tf_op jit(solution)/shard_map/ppermute | solution.py:840
  21.2 1.6 %collective-permute-start.6 = (bf16[8,40,640]{2,1,0:T(8,128)(2,1)S(1)}, bf16[8,40,640]{2,1,0:T(8,128)(2,1)S(1)}, u32[]{:S(2)}, u32[]{:S(2)}) collective-permute-start(bf16[8,40,640]{2,1,0:T(8,128)(2,1)S(1)} %get-tuple-element.210), channel_id=1, source_target_pairs={{0,4},{1,3},{2,6},{3,1},{4,0},{5,7},{6,2},{7,5},{8,12},{9,11},{10,... | collective-permute-start | bytes 1228808 | tf_op jit(solution)/shard_map/ppermute | solution.py:840
  22.8 2.1 %collective-permute-start.8 = (bf16[4,40,640]{2,1,0:T(8,128)(2,1)S(1)}, bf16[4,40,640]{2,1,0:T(8,128)(2,1)S(1)}, u32[]{:S(2)}, u32[]{:S(2)}) collective-permute-start(bf16[4,40,640]{2,1,0:T(8,128)(2,1)S(1)} %pad_maximum_fusion.2), channel_id=1, source_target_pairs={{0,8},{1,9},{2,10},{3,11},{4,12},{5,13},{6,14},{7,15},{8,0},{9,1},... | collective-permute-start | bytes 614408 | tf_op jit(solution)/shard_map/ppermute | solution.py:840
  24.9 1.2 %collective-permute-start.9 = (bf16[2,16,640]{2,1,0:T(8,128)(2,1)S(1)}, bf16[2,16,640]{2,1,0:T(8,128)(2,1)S(1)}, u32[]{:S(2)}, u32[]{:S(2)}) collective-permute-start(bf16[2,16,640]{2,1,0:T(8,128)(2,1)S(1)} %pad_maximum_fusion.5), channel_id=1, source_target_pairs={{0,2},{1,3},{2,0},{3,1},{4,6},{5,7},{6,4},{7,5},{8,10},{9,11},{10,... | collective-permute-start | bytes 122888 | tf_op jit(solution)/shard_map/ppermute | solution.py:840
  26.1 2.9 %collective-permute-done.9 = bf16[2,16,640]{2,1,0:T(8,128)(2,1)S(1)} collective-permute-done((bf16[2,16,640]{2,1,0:T(8,128)(2,1)S(1)}, bf16[2,16,640]{2,1,0:T(8,128)(2,1)S(1)}, u32[]{:S(2)}, u32[]{:S(2)}) %collective-permute-start.9) | collective-permute-done | bytes 40992 | tf_op jit(solution)/shard_map/ppermute | solution.py:840
  29.5 1.6 %collective-permute-start.11 = (bf16[8,40,640]{2,1,0:T(8,128)(2,1)S(1)}, bf16[8,40,640]{2,1,0:T(8,128)(2,1)S(1)}, u32[]{:S(2)}, u32[]{:S(2)}) collective-permute-start(bf16[8,40,640]{2,1,0:T(8,128)(2,1)S(1)} %get-tuple-element.132), channel_id=1, source_target_pairs={{0,4},{1,3},{2,6},{3,1},{4,0},{5,7},{6,2},{7,5},{8,12},{9,11},{10,... | collective-permute-start | bytes 1228808 | tf_op jit(solution)/shard_map/ppermute | solution.py:840
  31.8 4.8 %shard_map.197 = (f32[512,320]{1,0:T(8,128)S(1)}, bf16[512,320]{1,0:T(8,128)(2,1)S(1)}, bf16[512,320]{1,0:T(8,128)(2,1)S(1)}, f32[128,320]{1,0:T(8,128)S(1)}, f3...) custom-call(s32[4]{0:T(128)S(1)} %copy-done.6, ...), custom_call_target="tpu_custom_call" | custom-call | flops 8000000000 | tf_op jit(solution)/shard_map/pallas_call | solution.py:804
  38.1 1.1 %collective-permute-done.13 = bf16[8,40,640]{2,1,0:T(8,128)(2,1)S(1)} collective-permute-done((bf16[8,40,640]{2,1,0:T(8,128)(2,1)S(1)}, bf16[8,40,640]{2,1,0:T(8,128)(2,1)S(1)}, u32[]{:S(2)}, u32[]{:S(2)}) %collective-permute-start.13) | collective-permute-done | bytes 409632 | tf_op jit(solution)/shard_map/ppermute | solution.py:840
  39.3 11.5 %shard_map.199 = (bf16[16,40,640]{2,1,0:T(8,128)(2,1)S(1)}, bf16[16,40,640]{2,1,0:T(8,128)(2,1)S(1)}, bf16[512,1280]{1,0:T(8,128)(2,1)S(1)}, bf16[512,1280]{1,0:...) custom-call(s32[4]{0:T(128)S(1)} %copy-done.6, ...), custom_call_target="tpu_custom_call", output_to_operand_aliasing={{5}: (9, {}), {6}: (10, {})} | custom-call | flops 32999999488 | tf_op jit(solution)/shard_map/pallas_call | solution.py:804
  51.5 1.2 %shard_map.200 = (f32[512,320]{1,0:T(8,128)S(1)}, f32[16,320]{1,0:T(8,128)S(1)}) custom-call(bf16[512,1280]{1,0:T(8,128)(2,1)S(1)} %get-tuple-element.137.df_ref, bf16[320,1280]{1,0:T(8,128)(2,1)S(1)} %get-tuple-element.138.wu_ref, f32[512,320]{1,0:T(8,128)S(1)} %get-tuple-element.139.n2_ref, f32[512,1]{1,0:T(8,128)S(1)} %get-tuple-element.140.r2_ref, ...), custom_call_target="tpu_custom_call" | custom-call | flops 1000000000 | tf_op jit(solution)/shard_map/pallas_call | solution.py:804
  52.8 1.6 %collective-permute-start.16 = (bf16[8,40,640]{2,1,0:T(8,128)(2,1)S(1)}, bf16[8,40,640]{2,1,0:T(8,128)(2,1)S(1)}, u32[]{:S(2)}, u32[]{:S(2)}) collective-permute-start(bf16[8,40,640]{2,1,0:T(8,128)(2,1)S(1)} %shard_map.201), channel_id=1, source_target_pairs={{0,4},{1,3},{2,6},{3,1},{4,0},{5,7},{6,2},{7,5},{8,12},{9,11},{10,... | collective-permute-start | bytes 1228808 | tf_op jit(solution)/shard_map/ppermute | solution.py:840
  54.4 1.2 %shard_map.202 = (f32[320,320]{1,0:T(8,128)S(1)}, bf16[512,320]{1,0:T(8,128)(2,1)S(1)}, bf16[512,640]{1,0:T(8,128)(2,1)S(1)}, f32[1,320]{1,0:T(1,128)S(1)}) custom-call(f32[512,320]{1,0:T(8,128)S(1)} %get-tuple-element.145.dx2_ref, bf16[640,320]{1,0:T(8,128)(2,1)S(1)} %get-tuple-element.146.vb_ref, f32[512,640]{1,0:T(8,128)S(1)} %get-tuple-element.147.p_ref, ...), custom_call_target="tpu_custom_call" | custom-call | tf_op jit(solution)/shard_map/pallas_call | solution.py:804
  55.7 2.8 %shard_map.203 = (bf16[16,40,640]{2,1,0:T(8,128)(2,1)S(1)}, bf16[16,40,640]{2,1,0:T(8,128)(2,1)S(1)}, bf16[512,320]{1,0:T(8,128)(2,1)S(1)}, f32[512,320]{1,0:T(8,128)S(1)}, f32[8,320]{1,0:T(8,128)S(1)}) custom-call(bf16[512,320]{1,0:T(8,128)(2,1)S(1)} %get-tuple-element.150.dob_ref, bf16[512,640]{1,0:T(8,128)(2,1)S(1)} %get-tuple-element.151.ds_ref, ...), custom_call_target="tpu_custom_call" | custom-call | tf_op jit(solution)/shard_map/pallas_call | solution.py:804
  58.5 1.1 %shard_map.205 = (f32[512,320]{1,0:T(8,128)S(1)}, bf16[2,8,640]{2,1,0:T(8,128)(2,1)S(1)}, bf16[2,8,640]{2,1,0:T(8,128)(2,1)S(1)}) custom-call(bf16[512,320]{1,0:T(8,128)(2,1)S(1)} %get-tuple-element.166.dq_ref, f32[512,320]{1,0:T(8,128)S(1)} %get-tuple-element.167.dpatch_ref, f32[512,320]{1,0:T(8,128)S(1)} %copy-done, bf16[512,512]{1,0:T(8,128)(2,1)S(1)} %copy-done.1, ...), custom_call_target="tpu_custom_call" | custom-call | tf_op jit(solution)/shard_map/pallas_call | solution.py:804
  61.3 1.6 %collective-permute-start.19 = (bf16[336,640]{1,0:T(8,128)(2,1)S(1)}, bf16[336,640]{1,0:T(8,128)(2,1)S(1)}, u32[]{:S(2)}, u32[]{:S(2)}) collective-permute-start(bf16[336,640]{1,0:T(8,128)(2,1)S(1)} %get-tuple-element.175), channel_id=1, source_target_pairs={{0,4},{1,3},{2,6},{3,1},{4,0},{5,7},{6,2},{7,5},{8,12},{9,11},{10,... | collective-permute-start | bytes 1290248 | tf_op jit(solution)/shard_map/ppermute | solution.py:840
  62.9 2.0 %collective-permute-start.20 = (bf16[4,40,640]{2,1,0:T(8,128)(2,1)S(1)}, bf16[4,40,640]{2,1,0:T(8,128)(2,1)S(1)}, u32[]{:S(2)}, u32[]{:S(2)}) collective-permute-start(bf16[4,40,640]{2,1,0:T(8,128)(2,1)S(1)} %get-tuple-element.163), channel_id=1, source_target_pairs={{0,8},{1,9},{2,10},{3,11},{4,12},{5,13},{6,14},{7,15},{8,0},{9,1},... | collective-permute-start | bytes 614408 | tf_op jit(solution)/shard_map/ppermute | solution.py:840
  64.9 1.7 %shard_map.207 = bf16[320,512]{1,0:T(8,128)(2,1)} custom-call(f32[512,320]{1,0:T(8,128)S(1)} %get-tuple-element.123.x2_ref, bf16[512,1280]{1,0:T(8,128)(2,1)S(1)} %get-tuple-element.176.act_ref, bf16[320,1280]{1,0:T(8,128)(2,1)S(1)} %get-tuple-element.177.wd_ref, f32[16,320]{1,0:T(8,128)S(1)} %get-tuple-element.124.mv_ref, ...), custom_call_target="tpu_custom_call" | custom-call | flops 1000000000 | tf_op jit(solution)/shard_map/pallas_call | solution.py:804
  66.5 1.4 %shard_map.208 = bf16[320,512]{1,0:T(8,128)(2,1)} custom-call(f32[512,320]{1,0:T(8,128)S(1)} %get-tuple-element.145.dx2_ref, f32[512,320]{1,0:T(8,128)S(1)} %get-tuple-element.178.dh1_ref, f32[512,320]{1,0:T(8,128)S(1)} %copy-done, f32[512,1]{1,0:T(8,128)S(1)} %copy-done.3, f32[16,320]{1,0:T(8,128)S(1)} %get-tuple-element.124.mv_ref), custom_call_target="tpu_custom_call" | custom-call | flops 1000000000 | tf_op jit(solution)/shard_map/pallas_call | solution.py:804
  67.9 2.0 %collective-permute-done.20.got_ref = bf16[4,40,640]{2,1,0:T(8,128)(2,1)S(1)} collective-permute-done((bf16[4,40,640]{2,1,0:T(8,128)(2,1)S(1)}, bf16[4,40,640]{2,1,0:T(8,128)(2,1)S(1)}, u32[]{:S(2)}, u32[]{:S(2)}) %collective-permute-start.20) | collective-permute-done | bytes 204832 | tf_op jit(solution)/shard_map/ppermute | solution.py:840
  70.9 1.4 %collective-permute-start.25 = (bf16[2,40,640]{2,1,0:T(8,128)(2,1)S(1)}, bf16[2,40,640]{2,1,0:T(8,128)(2,1)S(1)}, u32[]{:S(2)}, u32[]{:S(2)}) collective-permute-start(bf16[2,40,640]{2,1,0:T(8,128)(2,1)S(1)} %get-tuple-element.195), channel_id=1, source_target_pairs={{0,16},{1,17},{2,18},{3,19},{4,20},{5,21},{6,22},{7,23},{8,24},{9,... | collective-permute-start | bytes 307208 | tf_op jit(solution)/shard_map/ppermute | solution.py:840
  72.3 3.6 %collective-permute-done.21.got_ref = bf16[168,640]{1,0:T(8,128)(2,1)S(1)} collective-permute-done((bf16[168,640]{1,0:T(8,128)(2,1)S(1)}, bf16[168,640]{1,0:T(8,128)(2,1)S(1)}, u32[]{:S(2)}, u32[]{:S(2)}) %collective-permute-start.21) | collective-permute-done | bytes 215072 | tf_op jit(solution)/shard_map/ppermute | solution.py:840
  76.0 1.8 %collective-permute-start.22 = (bf16[48,640]{1,0:T(8,128)(2,1)S(1)}, bf16[48,640]{1,0:T(8,128)(2,1)S(1)}, u32[]{:S(2)}, u32[]{:S(2)}) collective-permute-start(bf16[48,640]{1,0:T(8,128)(2,1)S(1)} %get-tuple-element.189), channel_id=1, source_target_pairs={{0,8},{1,9},{2,10},{3,11},{4,12},{5,13},{6,14},{7,15},{8,0},{9,1},... | collective-permute-start | bytes 184328 | tf_op jit(solution)/shard_map/ppermute | solution.py:840
  78.5 1.9 %collective-permute-start.24 = (bf16[48,640]{1,0:T(8,128)(2,1)S(1)}, bf16[48,640]{1,0:T(8,128)(2,1)S(1)}, u32[]{:S(2)}, u32[]{:S(2)}) collective-permute-start(bf16[48,640]{1,0:T(8,128)(2,1)S(1)} %get-tuple-element.191), channel_id=1, source_target_pairs={{0,24},{1,25},{2,26},{3,27},{4,28},{5,29},{6,30},{7,31},{8,16},{9,... | collective-permute-start | bytes 184328 | tf_op jit(solution)/shard_map/ppermute | solution.py:840
  80.5 1.0 %collective-permute-start.26 = (bf16[1,40,640]{2,1,0:T(8,128)(2,1)S(1)}, bf16[1,40,640]{2,1,0:T(8,128)(2,1)S(1)}, u32[]{:S(2)}, u32[]{:S(2)}) collective-permute-start(bf16[1,40,640]{2,1,0:T(8,128)(2,1)S(1)} %get-tuple-element.197), channel_id=1, source_target_pairs={{0,2},{1,5},{2,0},{3,7},{4,6},{5,1},{6,4},{7,3},{8,10},{9,13},{10,... | collective-permute-start | bytes 153608 | tf_op jit(solution)/shard_map/ppermute | solution.py:840
  81.4 3.2 %collective-permute-done.26.ffn_got_ref = bf16[1,40,640]{2,1,0:T(8,128)(2,1)S(1)} collective-permute-done((bf16[1,40,640]{2,1,0:T(8,128)(2,1)S(1)}, bf16[1,40,640]{2,1,0:T(8,128)(2,1)S(1)}, u32[]{:S(2)}, u32[]{:S(2)}) %collective-permute-start.26) | collective-permute-done | bytes 51232 | tf_op jit(solution)/shard_map/ppermute | solution.py:840
  84.6 0.9 %shard_map.213 = (f32[40,80]{1,0:T(8,128)}, f32[80,80]{1,0:T(8,128)}, f32[40,320]{1,0:T(8,128)}, f32[40,80]{1,0:T(8,128)}, f32[80,160]{1,0:T(8,128)}, /*index=5*...) custom-call(bf16[48,640]{1,0:T(8,128)(2,1)S(1)} %get-tuple-element.188.a_ref, ...), custom_call_target="tpu_custom_call" | custom-call | tf_op jit(solution)/shard_map/pallas_call | solution.py:804
  (78 shorter events, 8.1 us)
Async XLA Ops:
  2.4 10.6 %collective-permute-start.2 = (bf16[1,40,640]{2,1,0:T(8,128)(2,1)}, bf16[1,40,640]{2,1,0:T(8,128)(2,1)S(1)}, u32[]{:S(2)}, u32[]{:S(2)}) collective-permute-start(bf16[1,40,640]{2,1,0:T(8,128)(2,1)} %get-tuple-element.113), channel_id=1, source_target_pairs={{0,24},{1,25},{2,26},{3,27},{4,28},{5,29},{6,30},{7,31},{8,16},{9,... | collective-permute-start | bytes 153608 | tf_op jit(solution)/shard_map/ppermute | solution.py:840
  7.5 5.5 %collective-permute-start.1 = (bf16[1,40,640]{2,1,0:T(8,128)(2,1)}, bf16[1,40,640]{2,1,0:T(8,128)(2,1)S(1)}, u32[]{:S(2)}, u32[]{:S(2)}) collective-permute-start(bf16[1,40,640]{2,1,0:T(8,128)(2,1)} %get-tuple-element.113), channel_id=1, source_target_pairs={{0,16},{1,17},{2,18},{3,19},{4,20},{5,21},{6,22},{7,23},{8,24},{9,... | collective-permute-start | bytes 153608 | tf_op jit(solution)/shard_map/ppermute | solution.py:840
  7.5 5.5 %collective-permute-start = (bf16[1,40,640]{2,1,0:T(8,128)(2,1)}, bf16[1,40,640]{2,1,0:T(8,128)(2,1)S(1)}, u32[]{:S(2)}, u32[]{:S(2)}) collective-permute-start(bf16[1,40,640]{2,1,0:T(8,128)(2,1)} %get-tuple-element.113), channel_id=1, source_target_pairs={{0,8},{1,9},{2,10},{3,11},{4,12},{5,13},{6,14},{7,15},{8,0},{9,1},... | collective-permute-start | bytes 153608 | tf_op jit(solution)/shard_map/ppermute | solution.py:840
  8.1 4.8 %collective-permute-start.4 = (bf16[1,16,640]{2,1,0:T(8,128)(2,1)}, bf16[1,16,640]{2,1,0:T(8,128)(2,1)S(1)}, u32[]{:S(2)}, u32[]{:S(2)}) collective-permute-start(bf16[1,16,640]{2,1,0:T(8,128)(2,1)} %get-tuple-element.115), channel_id=1, source_target_pairs={{0,1},{1,0},{2,3},{3,2},{4,5},{5,4},{6,7},{7,6},{8,9},{9,8},{10,11... | collective-permute-start | bytes 61448 | tf_op jit(solution)/shard_map/ppermute | solution.py:840
  8.1 4.8 %collective-permute-start.3 = (bf16[1,40,640]{2,1,0:T(8,128)(2,1)}, bf16[1,40,640]{2,1,0:T(8,128)(2,1)S(1)}, u32[]{:S(2)}, u32[]{:S(2)}) collective-permute-start(bf16[1,40,640]{2,1,0:T(8,128)(2,1)} %get-tuple-element.114), channel_id=1, source_target_pairs={{0,2},{1,5},{2,0},{3,7},{4,6},{5,1},{6,4},{7,3},{8,10},{9,13},{10,... | collective-permute-start | bytes 153608 | tf_op jit(solution)/shard_map/ppermute | solution.py:840
  12.9 12.0 %copy-start.9 = (bf16[1,16,640]{2,1,0:T(8,128)(2,1)S(1)}, bf16[1,16,640]{2,1,0:T(8,128)(2,1)}, u32[]{:S(2)}) copy-start(bf16[1,16,640]{2,1,0:T(8,128)(2,1)} %get-tuple-element.115) | copy-start | bytes 61444
  13.0 9.8 %collective-permute-start.7 = (bf16[2,40,640]{2,1,0:T(8,128)(2,1)S(1)}, bf16[2,40,640]{2,1,0:T(8,128)(2,1)S(1)}, u32[]{:S(2)}, u32[]{:S(2)}) collective-permute-start(bf16[2,40,640]{2,1,0:T(8,128)(2,1)S(1)} %pad_maximum_fusion.3), channel_id=1, source_target_pairs={{0,16},{1,17},{2,18},{3,19},{4,20},{5,21},{6,22},{7,23},{8,24},{9,... | collective-permute-start | bytes 307208 | tf_op jit(solution)/shard_map/ppermute | solution.py:840
  15.3 5.8 %collective-permute-start.5 = (bf16[4,40,640]{2,1,0:T(8,128)(2,1)S(1)}, bf16[4,40,640]{2,1,0:T(8,128)(2,1)S(1)}, u32[]{:S(2)}, u32[]{:S(2)}) collective-permute-start(bf16[4,40,640]{2,1,0:T(8,128)(2,1)S(1)} %pad_maximum_fusion.1), channel_id=1, source_target_pairs={{0,2},{1,5},{2,0},{3,7},{4,6},{5,1},{6,4},{7,3},{8,10},{9,13},{10,... | collective-permute-start | bytes 614408 | tf_op jit(solution)/shard_map/ppermute | solution.py:840
  21.1 10.7 %copy-start.5 = (f32[512,128]{1,0:T(8,128)S(1)}, f32[512,128]{1,0:T(8,128)}, u32[]{:S(2)}) copy-start(f32[512,128]{1,0:T(8,128)} %get-tuple-element.112.live_ref) | copy-start | bytes 786436
  21.1 10.7 %copy-start = (f32[512,320]{1,0:T(8,128)S(1)}, f32[512,320]{1,0:T(8,128)}, u32[]{:S(2)}) copy-start(f32[512,320]{1,0:T(8,128)} %get-tuple-element.110.n1_ref) | copy-start | bytes 1966084
  21.1 10.7 %copy-start.1 = (bf16[512,512]{1,0:T(8,128)(2,1)S(1)}, bf16[512,512]{1,0:T(8,128)(2,1)}, u32[]{:S(2)}) copy-start(bf16[512,512]{1,0:T(8,128)(2,1)} %get-tuple-element.111.chosen_ref) | copy-start | bytes 1572868
  21.2 10.7 %copy-start.2 = (bf16[512,320]{0,1:T(8,128)(2,1)S(1)}, bf16[512,320]{0,1:T(8,128)(2,1)}, u32[]{:S(2)}) copy-start(bf16[512,320]{0,1:T(8,128)(2,1)} %param.13) | copy-start | bytes 983044
  21.2 8.0 %collective-permute-start.6 = (bf16[8,40,640]{2,1,0:T(8,128)(2,1)S(1)}, bf16[8,40,640]{2,1,0:T(8,128)(2,1)S(1)}, u32[]{:S(2)}, u32[]{:S(2)}) collective-permute-start(bf16[8,40,640]{2,1,0:T(8,128)(2,1)S(1)} %get-tuple-element.210), channel_id=1, source_target_pairs={{0,4},{1,3},{2,6},{3,1},{4,0},{5,7},{6,2},{7,5},{8,12},{9,11},{10,... | collective-permute-start | bytes 1228808 | tf_op jit(solution)/shard_map/ppermute | solution.py:840
  22.8 6.2 %collective-permute-start.8 = (bf16[4,40,640]{2,1,0:T(8,128)(2,1)S(1)}, bf16[4,40,640]{2,1,0:T(8,128)(2,1)S(1)}, u32[]{:S(2)}, u32[]{:S(2)}) collective-permute-start(bf16[4,40,640]{2,1,0:T(8,128)(2,1)S(1)} %pad_maximum_fusion.2), channel_id=1, source_target_pairs={{0,8},{1,9},{2,10},{3,11},{4,12},{5,13},{6,14},{7,15},{8,0},{9,1},... | collective-permute-start | bytes 614408 | tf_op jit(solution)/shard_map/ppermute | solution.py:840
  24.9 4.1 %collective-permute-start.9 = (bf16[2,16,640]{2,1,0:T(8,128)(2,1)S(1)}, bf16[2,16,640]{2,1,0:T(8,128)(2,1)S(1)}, u32[]{:S(2)}, u32[]{:S(2)}) collective-permute-start(bf16[2,16,640]{2,1,0:T(8,128)(2,1)S(1)} %pad_maximum_fusion.5), channel_id=1, source_target_pairs={{0,2},{1,3},{2,0},{3,1},{4,6},{5,7},{6,4},{7,5},{8,10},{9,11},{10,... | collective-permute-start | bytes 122888 | tf_op jit(solution)/shard_map/ppermute | solution.py:840
  29.3 2.4 %collective-permute-start.10 = (bf16[16,40,640]{2,1,0:T(8,128)(2,1)S(1)}, bf16[16,40,640]{2,1,0:T(8,128)(2,1)S(1)}, u32[]{:S(2)}, u32[]{:S(2)}) collective-permute-start(bf16[16,40,640]{2,1,0:T(8,128)(2,1)S(1)} %constant_dynamic-update-slice_fusion.5.own_ref), channel_id=1, source_target_pairs={{0,1},{1,0},{2,3},{3,2},{4,5},{5,4},{6,7},{7,6},{8,9},{9,8},{10,11... | collective-permute-start | bytes 2457608 | tf_op jit(solution)/shard_map/ppermute | solution.py:840
  29.5 8.0 %collective-permute-start.11 = (bf16[8,40,640]{2,1,0:T(8,128)(2,1)S(1)}, bf16[8,40,640]{2,1,0:T(8,128)(2,1)S(1)}, u32[]{:S(2)}, u32[]{:S(2)}) collective-permute-start(bf16[8,40,640]{2,1,0:T(8,128)(2,1)S(1)} %get-tuple-element.132), channel_id=1, source_target_pairs={{0,4},{1,3},{2,6},{3,1},{4,0},{5,7},{6,2},{7,5},{8,12},{9,11},{10,... | collective-permute-start | bytes 1228808 | tf_op jit(solution)/shard_map/ppermute | solution.py:840
  31.7 6.5 %collective-permute-start.12 = (bf16[8,40,640]{2,1,0:T(8,128)(2,1)S(1)}, bf16[8,40,640]{2,1,0:T(8,128)(2,1)S(1)}, u32[]{:S(2)}, u32[]{:S(2)}) collective-permute-start(bf16[8,40,640]{2,1,0:T(8,128)(2,1)S(1)} %get-tuple-element.132), channel_id=1, source_target_pairs={{0,1},{1,0},{2,3},{3,2},{4,5},{5,4},{6,7},{7,6},{8,9},{9,8},{10,11... | collective-permute-start | bytes 1228808 | tf_op jit(solution)/shard_map/ppermute | solution.py:840
  37.5 1.7 %collective-permute-start.13 = (bf16[8,40,640]{2,1,0:T(8,128)(2,1)S(1)}, bf16[8,40,640]{2,1,0:T(8,128)(2,1)S(1)}, u32[]{:S(2)}, u32[]{:S(2)}) collective-permute-start(bf16[8,40,640]{2,1,0:T(8,128)(2,1)S(1)} %collective-permute-done.11), channel_id=1, source_target_pairs={{0,1},{1,0},{2,3},{3,2},{4,5},{5,4},{6,7},{7,6},{8,9},{9,8},{10,11... | collective-permute-start | bytes 1228808 | tf_op jit(solution)/shard_map/ppermute | solution.py:840
  50.9 1.8 %collective-permute-start.14 = (bf16[8,40,640]{2,1,0:T(8,128)(2,1)S(1)}, bf16[8,40,640]{2,1,0:T(8,128)(2,1)S(1)}, u32[]{:S(2)}, u32[]{:S(2)}) collective-permute-start(bf16[8,40,640]{2,1,0:T(8,128)(2,1)S(1)} %get-tuple-element.207), channel_id=1, source_target_pairs={{0,1},{1,0},{2,3},{3,2},{4,5},{5,4},{6,7},{7,6},{8,9},{9,8},{10,11... | collective-permute-start | bytes 1228808 | tf_op jit(solution)/shard_map/ppermute | solution.py:840
  51.1 9.0 %collective-permute-start.15 = (bf16[8,40,640]{2,1,0:T(8,128)(2,1)S(1)}, bf16[8,40,640]{2,1,0:T(8,128)(2,1)S(1)}, u32[]{:S(2)}, u32[]{:S(2)}) collective-permute-start(bf16[8,40,640]{2,1,0:T(8,128)(2,1)S(1)} %get-tuple-element.206), channel_id=1, source_target_pairs={{0,1},{1,0},{2,3},{3,2},{4,5},{5,4},{6,7},{7,6},{8,9},{9,8},{10,11... | collective-permute-start | bytes 1228808 | tf_op jit(solution)/shard_map/ppermute | solution.py:840
  52.8 8.0 %collective-permute-start.16 = (bf16[8,40,640]{2,1,0:T(8,128)(2,1)S(1)}, bf16[8,40,640]{2,1,0:T(8,128)(2,1)S(1)}, u32[]{:S(2)}, u32[]{:S(2)}) collective-permute-start(bf16[8,40,640]{2,1,0:T(8,128)(2,1)S(1)} %shard_map.201), channel_id=1, source_target_pairs={{0,4},{1,3},{2,6},{3,1},{4,0},{5,7},{6,2},{7,5},{8,12},{9,11},{10,... | collective-permute-start | bytes 1228808 | tf_op jit(solution)/shard_map/ppermute | solution.py:840
  58.5 2.6 %collective-permute-start.17 = (bf16[16,40,640]{2,1,0:T(8,128)(2,1)S(1)}, bf16[16,40,640]{2,1,0:T(8,128)(2,1)S(1)}, u32[]{:S(2)}, u32[]{:S(2)}) collective-permute-start(bf16[16,40,640]{2,1,0:T(8,128)(2,1)S(1)} %get-tuple-element.165), channel_id=1, source_target_pairs={{0,1},{1,0},{2,3},{3,2},{4,5},{5,4},{6,7},{7,6},{8,9},{9,8},{10,11... | collective-permute-start | bytes 2457608 | tf_op jit(solution)/shard_map/ppermute | solution.py:840
  59.6 1.4 %collective-permute-start.18 = (bf16[2,8,640]{2,1,0:T(8,128)(2,1)S(1)}, bf16[2,8,640]{2,1,0:T(8,128)(2,1)S(1)}, u32[]{:S(2)}, u32[]{:S(2)}) collective-permute-start(bf16[2,8,640]{2,1,0:T(8,128)(2,1)S(1)} %get-tuple-element.174), channel_id=1, source_target_pairs={{0,1},{1,0},{2,3},{3,2},{4,5},{5,4},{6,7},{7,6},{8,9},{9,8},{10,11... | collective-permute-start | bytes 61448 | tf_op jit(solution)/shard_map/ppermute | solution.py:840
  61.3 8.6 %collective-permute-start.19 = (bf16[336,640]{1,0:T(8,128)(2,1)S(1)}, bf16[336,640]{1,0:T(8,128)(2,1)S(1)}, u32[]{:S(2)}, u32[]{:S(2)}) collective-permute-start(bf16[336,640]{1,0:T(8,128)(2,1)S(1)} %get-tuple-element.175), channel_id=1, source_target_pairs={{0,4},{1,3},{2,6},{3,1},{4,0},{5,7},{6,2},{7,5},{8,12},{9,11},{10,... | collective-permute-start | bytes 1290248 | tf_op jit(solution)/shard_map/ppermute | solution.py:840
  62.9 7.0 %collective-permute-start.20 = (bf16[4,40,640]{2,1,0:T(8,128)(2,1)S(1)}, bf16[4,40,640]{2,1,0:T(8,128)(2,1)S(1)}, u32[]{:S(2)}, u32[]{:S(2)}) collective-permute-start(bf16[4,40,640]{2,1,0:T(8,128)(2,1)S(1)} %get-tuple-element.163), channel_id=1, source_target_pairs={{0,8},{1,9},{2,10},{3,11},{4,12},{5,13},{6,14},{7,15},{8,0},{9,1},... | collective-permute-start | bytes 614408 | tf_op jit(solution)/shard_map/ppermute | solution.py:840
  70.0 5.9 %collective-permute-start.21 = (bf16[168,640]{1,0:T(8,128)(2,1)S(1)}, bf16[168,640]{1,0:T(8,128)(2,1)S(1)}, u32[]{:S(2)}, u32[]{:S(2)}) collective-permute-start(bf16[168,640]{1,0:T(8,128)(2,1)S(1)} %get-tuple-element.187), channel_id=1, source_target_pairs={{0,2},{1,5},{2,0},{3,7},{4,6},{5,1},{6,4},{7,3},{8,10},{9,13},{10,... | collective-permute-start | bytes 645128 | tf_op jit(solution)/shard_map/ppermute | solution.py:840
  70.9 9.5 %collective-permute-start.25 = (bf16[2,40,640]{2,1,0:T(8,128)(2,1)S(1)}, bf16[2,40,640]{2,1,0:T(8,128)(2,1)S(1)}, u32[]{:S(2)}, u32[]{:S(2)}) collective-permute-start(bf16[2,40,640]{2,1,0:T(8,128)(2,1)S(1)} %get-tuple-element.195), channel_id=1, source_target_pairs={{0,16},{1,17},{2,18},{3,19},{4,20},{5,21},{6,22},{7,23},{8,24},{9,... | collective-permute-start | bytes 307208 | tf_op jit(solution)/shard_map/ppermute | solution.py:840
  76.0 8.7 %collective-permute-start.22 = (bf16[48,640]{1,0:T(8,128)(2,1)S(1)}, bf16[48,640]{1,0:T(8,128)(2,1)S(1)}, u32[]{:S(2)}, u32[]{:S(2)}) collective-permute-start(bf16[48,640]{1,0:T(8,128)(2,1)S(1)} %get-tuple-element.189), channel_id=1, source_target_pairs={{0,8},{1,9},{2,10},{3,11},{4,12},{5,13},{6,14},{7,15},{8,0},{9,1},... | collective-permute-start | bytes 184328 | tf_op jit(solution)/shard_map/ppermute | solution.py:840
  77.8 6.9 %collective-permute-start.23 = (bf16[48,640]{1,0:T(8,128)(2,1)S(1)}, bf16[48,640]{1,0:T(8,128)(2,1)S(1)}, u32[]{:S(2)}, u32[]{:S(2)}) collective-permute-start(bf16[48,640]{1,0:T(8,128)(2,1)S(1)} %get-tuple-element.190), channel_id=1, source_target_pairs={{0,16},{1,17},{2,18},{3,19},{4,20},{5,21},{6,22},{7,23},{8,24},{9,... | collective-permute-start | bytes 184328 | tf_op jit(solution)/shard_map/ppermute | solution.py:840
  78.5 6.1 %collective-permute-start.24 = (bf16[48,640]{1,0:T(8,128)(2,1)S(1)}, bf16[48,640]{1,0:T(8,128)(2,1)S(1)}, u32[]{:S(2)}, u32[]{:S(2)}) collective-permute-start(bf16[48,640]{1,0:T(8,128)(2,1)S(1)} %get-tuple-element.191), channel_id=1, source_target_pairs={{0,24},{1,25},{2,26},{3,27},{4,28},{5,29},{6,30},{7,31},{8,16},{9,... | collective-permute-start | bytes 184328 | tf_op jit(solution)/shard_map/ppermute | solution.py:840
  80.5 4.2 %collective-permute-start.26 = (bf16[1,40,640]{2,1,0:T(8,128)(2,1)S(1)}, bf16[1,40,640]{2,1,0:T(8,128)(2,1)S(1)}, u32[]{:S(2)}, u32[]{:S(2)}) collective-permute-start(bf16[1,40,640]{2,1,0:T(8,128)(2,1)S(1)} %get-tuple-element.197), channel_id=1, source_target_pairs={{0,2},{1,5},{2,0},{3,7},{4,6},{5,1},{6,4},{7,3},{8,10},{9,13},{10,... | collective-permute-start | bytes 153608 | tf_op jit(solution)/shard_map/ppermute | solution.py:840
  (5 other events, 29.2 us)

commit v8 on v7

--- a/solution.py
+++ b/solution.py
@@ -20,7 +20,7 @@
 TILE = 32
 CHUNK = 256
 PAD = 40
-MROWS = 512
+MROWS = 256
 RUN = 160
 REST = RUN - 128
 

time: 85.9 us -> 85.7 us (level)
  no operation moved by 1% of the time
where the time goes in v8:
time: 85.7 us; the launch traced here: 85.3 us
  Pallas kernels  32.6 us (38%)
  starting transfers between devices  31.8 us (37%)
  waiting for transfers between devices  19.4 us (23%)
  between operations  0.98 us (1%)
    ppermute x27, starting transfers between devices, swap(): return lax.ppermute(value, ('wide', 'narrow'), pairs)  31.8 us
    pallas_call x17, Pallas kernels, call(): pl.pallas_call(kernel, out_shape=[jax.ShapeDtypeStruct(shape, kind) for s...  27.8 us
    ppermute x27, waiting for transfers between devices, swap(): return lax.ppermute(value, ('wide', 'narrow'), pairs)  19.4 us
    pallas_call x1, Pallas kernels, prepare(): pl.pallas_call(prepare_kernel, out_shape=[jax.ShapeDtypeStruct(shape, kin...  3.1 us
  transfers between devices with their start and end apart: 27, of which 10 were waited for; matrix products, arithmetic and copies ran while one was open for 0% of the time, Pallas kernels for 21%

profile of v8, /device:TPU:0, one launch (start us, length us, event | category | flops | bytes accessed | tf_op | source)
XLA Modules:
  0.0 85.3 jit_solution(5327351016518347364)
XLA Ops:
  0.6 1.7 %shard_map.196 = (bf16[1,40,640]{2,1,0:T(8,128)(2,1)}, bf16[1,40,640]{2,1,0:T(8,128)(2,1)}, bf16[1,16,640]{2,1,0:T(8,128)(2,1)}) custom-call(bf16[40,80]{1,0:T(8,128)(2,1)} %bitcast.16, bf16[80,80]{1,0:T(8,128)(2,1)} %refs_1_.1, bf16[40,320]{1,0:T(8,128)(2,1)} %bitcast.14, bf16[40,80]{1,0:T(8,128)(2,1)} %bitcast.17, bf16[80,160]{1,0:T(8,128)(2,1)} %refs_4_.1, ...), custom_call_target="tpu_custom_call" | custom-call | tf_op jit(solution)/shard_map/pallas_call | solution.py:133
  2.4 5.1 %collective-permute-start.2 = (bf16[1,40,640]{2,1,0:T(8,128)(2,1)}, bf16[1,40,640]{2,1,0:T(8,128)(2,1)S(1)}, u32[]{:S(2)}, u32[]{:S(2)}) collective-permute-start(bf16[1,40,640]{2,1,0:T(8,128)(2,1)} %get-tuple-element.113), channel_id=1, source_target_pairs={{0,24},{1,25},{2,26},{3,27},{4,28},{5,29},{6,30},{7,31},{8,16},{9,... | collective-permute-start | bytes 153608 | tf_op jit(solution)/shard_map/ppermute | solution.py:840
  8.1 1.6 %collective-permute-start.3 = (bf16[1,40,640]{2,1,0:T(8,128)(2,1)}, bf16[1,40,640]{2,1,0:T(8,128)(2,1)S(1)}, u32[]{:S(2)}, u32[]{:S(2)}) collective-permute-start(bf16[1,40,640]{2,1,0:T(8,128)(2,1)} %get-tuple-element.114), channel_id=1, source_target_pairs={{0,2},{1,5},{2,0},{3,7},{4,6},{5,1},{6,4},{7,3},{8,10},{9,13},{10,... | collective-permute-start | bytes 153608 | tf_op jit(solution)/shard_map/ppermute | solution.py:840
  9.8 3.1 %shard_map.195 = (f32[512,320]{1,0:T(8,128)}, f32[512,320]{1,0:T(8,128)}, f32[512,1]{1,0:T(8,128)}, bf16[512,512]{1,0:T(8,128)(2,1)}, f32[512,128]{1,0:T(8,128)}, /*index=5*/s32[4]{0:T(128)}) custom-call(s32[2]{0:T(128)} %rows_hbm.1, s32[2]{0:T(128)} %cols_hbm.1, bf16[320,512]{1,0:T(8,128)(2,1)} %bitcast.18), custom_call_target="tpu_custom_call" | custom-call | flops 2000000000 | tf_op jit(solution)/shard_map/pallas_call | solution.py:183
  13.0 2.2 %collective-permute-start.7 = (bf16[2,40,640]{2,1,0:T(8,128)(2,1)S(1)}, bf16[2,40,640]{2,1,0:T(8,128)(2,1)S(1)}, u32[]{:S(2)}, u32[]{:S(2)}) collective-permute-start(bf16[2,40,640]{2,1,0:T(8,128)(2,1)S(1)} %pad_maximum_fusion.3), channel_id=1, source_target_pairs={{0,16},{1,17},{2,18},{3,19},{4,20},{5,21},{6,22},{7,23},{8,24},{9,... | collective-permute-start | bytes 307208 | tf_op jit(solution)/shard_map/ppermute | solution.py:840
  15.3 1.2 %collective-permute-start.5 = (bf16[4,40,640]{2,1,0:T(8,128)(2,1)S(1)}, bf16[4,40,640]{2,1,0:T(8,128)(2,1)S(1)}, u32[]{:S(2)}, u32[]{:S(2)}) collective-permute-start(bf16[4,40,640]{2,1,0:T(8,128)(2,1)S(1)} %pad_maximum_fusion.1), channel_id=1, source_target_pairs={{0,2},{1,5},{2,0},{3,7},{4,6},{5,1},{6,4},{7,3},{8,10},{9,13},{10,... | collective-permute-start | bytes 614408 | tf_op jit(solution)/shard_map/ppermute | solution.py:840
  16.5 4.6 %collective-permute-done.5 = bf16[4,40,640]{2,1,0:T(8,128)(2,1)S(1)} collective-permute-done((bf16[4,40,640]{2,1,0:T(8,128)(2,1)S(1)}, bf16[4,40,640]{2,1,0:T(8,128)(2,1)S(1)}, u32[]{:S(2)}, u32[]{:S(2)}) %collective-permute-start.5) | collective-permute-done | bytes 204832 | tf_op jit(solution)/shard_map/ppermute | solution.py:840
  21.2 1.6 %collective-permute-start.6 = (bf16[8,40,640]{2,1,0:T(8,128)(2,1)S(1)}, bf16[8,40,640]{2,1,0:T(8,128)(2,1)S(1)}, u32[]{:S(2)}, u32[]{:S(2)}) collective-permute-start(bf16[8,40,640]{2,1,0:T(8,128)(2,1)S(1)} %get-tuple-element.210), channel_id=1, source_target_pairs={{0,4},{1,3},{2,6},{3,1},{4,0},{5,7},{6,2},{7,5},{8,12},{9,11},{10,... | collective-permute-start | bytes 1228808 | tf_op jit(solution)/shard_map/ppermute | solution.py:840
  22.8 2.1 %collective-permute-start.8 = (bf16[4,40,640]{2,1,0:T(8,128)(2,1)S(1)}, bf16[4,40,640]{2,1,0:T(8,128)(2,1)S(1)}, u32[]{:S(2)}, u32[]{:S(2)}) collective-permute-start(bf16[4,40,640]{2,1,0:T(8,128)(2,1)S(1)} %pad_maximum_fusion.2), channel_id=1, source_target_pairs={{0,8},{1,9},{2,10},{3,11},{4,12},{5,13},{6,14},{7,15},{8,0},{9,1},... | collective-permute-start | bytes 614408 | tf_op jit(solution)/shard_map/ppermute | solution.py:840
  24.9 1.2 %collective-permute-start.9 = (bf16[2,16,640]{2,1,0:T(8,128)(2,1)S(1)}, bf16[2,16,640]{2,1,0:T(8,128)(2,1)S(1)}, u32[]{:S(2)}, u32[]{:S(2)}) collective-permute-start(bf16[2,16,640]{2,1,0:T(8,128)(2,1)S(1)} %pad_maximum_fusion.5), channel_id=1, source_target_pairs={{0,2},{1,3},{2,0},{3,1},{4,6},{5,7},{6,4},{7,5},{8,10},{9,11},{10,... | collective-permute-start | bytes 122888 | tf_op jit(solution)/shard_map/ppermute | solution.py:840
  26.1 2.9 %collective-permute-done.9 = bf16[2,16,640]{2,1,0:T(8,128)(2,1)S(1)} collective-permute-done((bf16[2,16,640]{2,1,0:T(8,128)(2,1)S(1)}, bf16[2,16,640]{2,1,0:T(8,128)(2,1)S(1)}, u32[]{:S(2)}, u32[]{:S(2)}) %collective-permute-start.9) | collective-permute-done | bytes 40992 | tf_op jit(solution)/shard_map/ppermute | solution.py:840
  29.5 1.6 %collective-permute-start.11 = (bf16[8,40,640]{2,1,0:T(8,128)(2,1)S(1)}, bf16[8,40,640]{2,1,0:T(8,128)(2,1)S(1)}, u32[]{:S(2)}, u32[]{:S(2)}) collective-permute-start(bf16[8,40,640]{2,1,0:T(8,128)(2,1)S(1)} %get-tuple-element.132), channel_id=1, source_target_pairs={{0,4},{1,3},{2,6},{3,1},{4,0},{5,7},{6,2},{7,5},{8,12},{9,11},{10,... | collective-permute-start | bytes 1228808 | tf_op jit(solution)/shard_map/ppermute | solution.py:840
  31.8 4.8 %shard_map.197 = (f32[512,320]{1,0:T(8,128)S(1)}, bf16[512,320]{1,0:T(8,128)(2,1)S(1)}, bf16[512,320]{1,0:T(8,128)(2,1)S(1)}, f32[128,320]{1,0:T(8,128)S(1)}, f3...) custom-call(s32[4]{0:T(128)S(1)} %copy-done.6, ...), custom_call_target="tpu_custom_call" | custom-call | flops 8000000000 | tf_op jit(solution)/shard_map/pallas_call | solution.py:804
  38.1 1.1 %collective-permute-done.13 = bf16[8,40,640]{2,1,0:T(8,128)(2,1)S(1)} collective-permute-done((bf16[8,40,640]{2,1,0:T(8,128)(2,1)S(1)}, bf16[8,40,640]{2,1,0:T(8,128)(2,1)S(1)}, u32[]{:S(2)}, u32[]{:S(2)}) %collective-permute-start.13) | collective-permute-done | bytes 409632 | tf_op jit(solution)/shard_map/ppermute | solution.py:840
  39.3 11.4 %shard_map.199 = (bf16[16,40,640]{2,1,0:T(8,128)(2,1)S(1)}, bf16[16,40,640]{2,1,0:T(8,128)(2,1)S(1)}, bf16[512,1280]{1,0:T(8,128)(2,1)S(1)}, bf16[512,1280]{1,0:...) custom-call(s32[4]{0:T(128)S(1)} %copy-done.6, ...), custom_call_target="tpu_custom_call", output_to_operand_aliasing={{5}: (9, {}), {6}: (10, {})} | custom-call | flops 32999999488 | tf_op jit(solution)/shard_map/pallas_call | solution.py:804
  51.3 1.2 %shard_map.200 = (f32[512,320]{1,0:T(8,128)S(1)}, f32[16,320]{1,0:T(8,128)S(1)}) custom-call(bf16[512,1280]{1,0:T(8,128)(2,1)S(1)} %get-tuple-element.137.df_ref, bf16[320,1280]{1,0:T(8,128)(2,1)S(1)} %get-tuple-element.138.wu_ref, f32[512,320]{1,0:T(8,128)S(1)} %get-tuple-element.139.n2_ref, f32[512,1]{1,0:T(8,128)S(1)} %get-tuple-element.140.r2_ref, ...), custom_call_target="tpu_custom_call" | custom-call | flops 1000000000 | tf_op jit(solution)/shard_map/pallas_call | solution.py:804
  52.7 1.6 %collective-permute-start.16 = (bf16[8,40,640]{2,1,0:T(8,128)(2,1)S(1)}, bf16[8,40,640]{2,1,0:T(8,128)(2,1)S(1)}, u32[]{:S(2)}, u32[]{:S(2)}) collective-permute-start(bf16[8,40,640]{2,1,0:T(8,128)(2,1)S(1)} %shard_map.201), channel_id=1, source_target_pairs={{0,4},{1,3},{2,6},{3,1},{4,0},{5,7},{6,2},{7,5},{8,12},{9,11},{10,... | collective-permute-start | bytes 1228808 | tf_op jit(solution)/shard_map/ppermute | solution.py:840
  54.3 1.2 %shard_map.202 = (f32[320,320]{1,0:T(8,128)S(1)}, bf16[512,320]{1,0:T(8,128)(2,1)S(1)}, bf16[512,640]{1,0:T(8,128)(2,1)S(1)}, f32[1,320]{1,0:T(1,128)S(1)}) custom-call(f32[512,320]{1,0:T(8,128)S(1)} %get-tuple-element.145.dx2_ref, bf16[640,320]{1,0:T(8,128)(2,1)S(1)} %get-tuple-element.146.vb_ref, f32[512,640]{1,0:T(8,128)S(1)} %get-tuple-element.147.p_ref, ...), custom_call_target="tpu_custom_call" | custom-call | tf_op jit(solution)/shard_map/pallas_call | solution.py:804
  55.5 2.8 %shard_map.203 = (bf16[16,40,640]{2,1,0:T(8,128)(2,1)S(1)}, bf16[16,40,640]{2,1,0:T(8,128)(2,1)S(1)}, bf16[512,320]{1,0:T(8,128)(2,1)S(1)}, f32[512,320]{1,0:T(8,128)S(1)}, f32[8,320]{1,0:T(8,128)S(1)}) custom-call(bf16[512,320]{1,0:T(8,128)(2,1)S(1)} %get-tuple-element.150.dob_ref, bf16[512,640]{1,0:T(8,128)(2,1)S(1)} %get-tuple-element.151.ds_ref, ...), custom_call_target="tpu_custom_call" | custom-call | tf_op jit(solution)/shard_map/pallas_call | solution.py:804
  58.4 1.1 %shard_map.205 = (f32[512,320]{1,0:T(8,128)S(1)}, bf16[2,8,640]{2,1,0:T(8,128)(2,1)S(1)}, bf16[2,8,640]{2,1,0:T(8,128)(2,1)S(1)}) custom-call(bf16[512,320]{1,0:T(8,128)(2,1)S(1)} %get-tuple-element.166.dq_ref, f32[512,320]{1,0:T(8,128)S(1)} %get-tuple-element.167.dpatch_ref, f32[512,320]{1,0:T(8,128)S(1)} %copy-done, bf16[512,512]{1,0:T(8,128)(2,1)S(1)} %copy-done.1, ...), custom_call_target="tpu_custom_call" | custom-call | tf_op jit(solution)/shard_map/pallas_call | solution.py:804
  61.1 1.6 %collective-permute-start.19 = (bf16[336,640]{1,0:T(8,128)(2,1)S(1)}, bf16[336,640]{1,0:T(8,128)(2,1)S(1)}, u32[]{:S(2)}, u32[]{:S(2)}) collective-permute-start(bf16[336,640]{1,0:T(8,128)(2,1)S(1)} %get-tuple-element.175), channel_id=1, source_target_pairs={{0,4},{1,3},{2,6},{3,1},{4,0},{5,7},{6,2},{7,5},{8,12},{9,11},{10,... | collective-permute-start | bytes 1290248 | tf_op jit(solution)/shard_map/ppermute | solution.py:840
  62.7 2.0 %collective-permute-start.20 = (bf16[4,40,640]{2,1,0:T(8,128)(2,1)S(1)}, bf16[4,40,640]{2,1,0:T(8,128)(2,1)S(1)}, u32[]{:S(2)}, u32[]{:S(2)}) collective-permute-start(bf16[4,40,640]{2,1,0:T(8,128)(2,1)S(1)} %get-tuple-element.163), channel_id=1, source_target_pairs={{0,8},{1,9},{2,10},{3,11},{4,12},{5,13},{6,14},{7,15},{8,0},{9,1},... | collective-permute-start | bytes 614408 | tf_op jit(solution)/shard_map/ppermute | solution.py:840
  64.8 1.7 %shard_map.207 = bf16[320,512]{1,0:T(8,128)(2,1)} custom-call(f32[512,320]{1,0:T(8,128)S(1)} %get-tuple-element.123.x2_ref, bf16[512,1280]{1,0:T(8,128)(2,1)S(1)} %get-tuple-element.176.act_ref, bf16[320,1280]{1,0:T(8,128)(2,1)S(1)} %get-tuple-element.177.wd_ref, f32[16,320]{1,0:T(8,128)S(1)} %get-tuple-element.124.mv_ref, ...), custom_call_target="tpu_custom_call" | custom-call | flops 1000000000 | tf_op jit(solution)/shard_map/pallas_call | solution.py:804
  66.4 1.4 %shard_map.208 = bf16[320,512]{1,0:T(8,128)(2,1)} custom-call(f32[512,320]{1,0:T(8,128)S(1)} %get-tuple-element.145.dx2_ref, f32[512,320]{1,0:T(8,128)S(1)} %get-tuple-element.178.dh1_ref, f32[512,320]{1,0:T(8,128)S(1)} %copy-done, f32[512,1]{1,0:T(8,128)S(1)} %copy-done.3, f32[16,320]{1,0:T(8,128)S(1)} %get-tuple-element.124.mv_ref), custom_call_target="tpu_custom_call" | custom-call | flops 1000000000 | tf_op jit(solution)/shard_map/pallas_call | solution.py:804
  67.8 1.8 %collective-permute-done.20.got_ref = bf16[4,40,640]{2,1,0:T(8,128)(2,1)S(1)} collective-permute-done((bf16[4,40,640]{2,1,0:T(8,128)(2,1)S(1)}, bf16[4,40,640]{2,1,0:T(8,128)(2,1)S(1)}, u32[]{:S(2)}, u32[]{:S(2)}) %collective-permute-start.20) | collective-permute-done | bytes 204832 | tf_op jit(solution)/shard_map/ppermute | solution.py:840
  69.7 1.0 %collective-permute-start.21 = (bf16[168,640]{1,0:T(8,128)(2,1)S(1)}, bf16[168,640]{1,0:T(8,128)(2,1)S(1)}, u32[]{:S(2)}, u32[]{:S(2)}) collective-permute-start(bf16[168,640]{1,0:T(8,128)(2,1)S(1)} %get-tuple-element.187), channel_id=1, source_target_pairs={{0,2},{1,5},{2,0},{3,7},{4,6},{5,1},{6,4},{7,3},{8,10},{9,13},{10,... | collective-permute-start | bytes 645128 | tf_op jit(solution)/shard_map/ppermute | solution.py:840
  70.8 1.4 %collective-permute-start.25 = (bf16[2,40,640]{2,1,0:T(8,128)(2,1)S(1)}, bf16[2,40,640]{2,1,0:T(8,128)(2,1)S(1)}, u32[]{:S(2)}, u32[]{:S(2)}) collective-permute-start(bf16[2,40,640]{2,1,0:T(8,128)(2,1)S(1)} %get-tuple-element.195), channel_id=1, source_target_pairs={{0,16},{1,17},{2,18},{3,19},{4,20},{5,21},{6,22},{7,23},{8,24},{9,... | collective-permute-start | bytes 307208 | tf_op jit(solution)/shard_map/ppermute | solution.py:840
  72.2 3.5 %collective-permute-done.21.got_ref = bf16[168,640]{1,0:T(8,128)(2,1)S(1)} collective-permute-done((bf16[168,640]{1,0:T(8,128)(2,1)S(1)}, bf16[168,640]{1,0:T(8,128)(2,1)S(1)}, u32[]{:S(2)}, u32[]{:S(2)}) %collective-permute-start.21) | collective-permute-done | bytes 215072 | tf_op jit(solution)/shard_map/ppermute | solution.py:840
  75.7 1.9 %collective-permute-start.22 = (bf16[48,640]{1,0:T(8,128)(2,1)S(1)}, bf16[48,640]{1,0:T(8,128)(2,1)S(1)}, u32[]{:S(2)}, u32[]{:S(2)}) collective-permute-start(bf16[48,640]{1,0:T(8,128)(2,1)S(1)} %get-tuple-element.189), channel_id=1, source_target_pairs={{0,8},{1,9},{2,10},{3,11},{4,12},{5,13},{6,14},{7,15},{8,0},{9,1},... | collective-permute-start | bytes 184328 | tf_op jit(solution)/shard_map/ppermute | solution.py:840
  78.2 2.0 %collective-permute-start.24 = (bf16[48,640]{1,0:T(8,128)(2,1)S(1)}, bf16[48,640]{1,0:T(8,128)(2,1)S(1)}, u32[]{:S(2)}, u32[]{:S(2)}) collective-permute-start(bf16[48,640]{1,0:T(8,128)(2,1)S(1)} %get-tuple-element.191), channel_id=1, source_target_pairs={{0,24},{1,25},{2,26},{3,27},{4,28},{5,29},{6,30},{7,31},{8,16},{9,... | collective-permute-start | bytes 184328 | tf_op jit(solution)/shard_map/ppermute | solution.py:840
  80.2 1.0 %collective-permute-start.26 = (bf16[1,40,640]{2,1,0:T(8,128)(2,1)S(1)}, bf16[1,40,640]{2,1,0:T(8,128)(2,1)S(1)}, u32[]{:S(2)}, u32[]{:S(2)}) collective-permute-start(bf16[1,40,640]{2,1,0:T(8,128)(2,1)S(1)} %get-tuple-element.197), channel_id=1, source_target_pairs={{0,2},{1,5},{2,0},{3,7},{4,6},{5,1},{6,4},{7,3},{8,10},{9,13},{10,... | collective-permute-start | bytes 153608 | tf_op jit(solution)/shard_map/ppermute | solution.py:840
  81.2 3.2 %collective-permute-done.26.ffn_got_ref = bf16[1,40,640]{2,1,0:T(8,128)(2,1)S(1)} collective-permute-done((bf16[1,40,640]{2,1,0:T(8,128)(2,1)S(1)}, bf16[1,40,640]{2,1,0:T(8,128)(2,1)S(1)}, u32[]{:S(2)}, u32[]{:S(2)}) %collective-permute-start.26) | collective-permute-done | bytes 51232 | tf_op jit(solution)/shard_map/ppermute | solution.py:840
  (78 shorter events, 8.0 us)
Async XLA Ops:
  2.4 10.6 %collective-permute-start.2 = (bf16[1,40,640]{2,1,0:T(8,128)(2,1)}, bf16[1,40,640]{2,1,0:T(8,128)(2,1)S(1)}, u32[]{:S(2)}, u32[]{:S(2)}) collective-permute-start(bf16[1,40,640]{2,1,0:T(8,128)(2,1)} %get-tuple-element.113), channel_id=1, source_target_pairs={{0,24},{1,25},{2,26},{3,27},{4,28},{5,29},{6,30},{7,31},{8,16},{9,... | collective-permute-start | bytes 153608 | tf_op jit(solution)/shard_map/ppermute | solution.py:840
  7.5 5.5 %collective-permute-start.1 = (bf16[1,40,640]{2,1,0:T(8,128)(2,1)}, bf16[1,40,640]{2,1,0:T(8,128)(2,1)S(1)}, u32[]{:S(2)}, u32[]{:S(2)}) collective-permute-start(bf16[1,40,640]{2,1,0:T(8,128)(2,1)} %get-tuple-element.113), channel_id=1, source_target_pairs={{0,16},{1,17},{2,18},{3,19},{4,20},{5,21},{6,22},{7,23},{8,24},{9,... | collective-permute-start | bytes 153608 | tf_op jit(solution)/shard_map/ppermute | solution.py:840
  7.5 5.5 %collective-permute-start = (bf16[1,40,640]{2,1,0:T(8,128)(2,1)}, bf16[1,40,640]{2,1,0:T(8,128)(2,1)S(1)}, u32[]{:S(2)}, u32[]{:S(2)}) collective-permute-start(bf16[1,40,640]{2,1,0:T(8,128)(2,1)} %get-tuple-element.113), channel_id=1, source_target_pairs={{0,8},{1,9},{2,10},{3,11},{4,12},{5,13},{6,14},{7,15},{8,0},{9,1},... | collective-permute-start | bytes 153608 | tf_op jit(solution)/shard_map/ppermute | solution.py:840
  8.1 4.8 %collective-permute-start.4 = (bf16[1,16,640]{2,1,0:T(8,128)(2,1)}, bf16[1,16,640]{2,1,0:T(8,128)(2,1)S(1)}, u32[]{:S(2)}, u32[]{:S(2)}) collective-permute-start(bf16[1,16,640]{2,1,0:T(8,128)(2,1)} %get-tuple-element.115), channel_id=1, source_target_pairs={{0,1},{1,0},{2,3},{3,2},{4,5},{5,4},{6,7},{7,6},{8,9},{9,8},{10,11... | collective-permute-start | bytes 61448 | tf_op jit(solution)/shard_map/ppermute | solution.py:840
  8.1 4.8 %collective-permute-start.3 = (bf16[1,40,640]{2,1,0:T(8,128)(2,1)}, bf16[1,40,640]{2,1,0:T(8,128)(2,1)S(1)}, u32[]{:S(2)}, u32[]{:S(2)}) collective-permute-start(bf16[1,40,640]{2,1,0:T(8,128)(2,1)} %get-tuple-element.114), channel_id=1, source_target_pairs={{0,2},{1,5},{2,0},{3,7},{4,6},{5,1},{6,4},{7,3},{8,10},{9,13},{10,... | collective-permute-start | bytes 153608 | tf_op jit(solution)/shard_map/ppermute | solution.py:840
  12.9 12.0 %copy-start.9 = (bf16[1,16,640]{2,1,0:T(8,128)(2,1)S(1)}, bf16[1,16,640]{2,1,0:T(8,128)(2,1)}, u32[]{:S(2)}) copy-start(bf16[1,16,640]{2,1,0:T(8,128)(2,1)} %get-tuple-element.115) | copy-start | bytes 61444
  13.0 9.8 %collective-permute-start.7 = (bf16[2,40,640]{2,1,0:T(8,128)(2,1)S(1)}, bf16[2,40,640]{2,1,0:T(8,128)(2,1)S(1)}, u32[]{:S(2)}, u32[]{:S(2)}) collective-permute-start(bf16[2,40,640]{2,1,0:T(8,128)(2,1)S(1)} %pad_maximum_fusion.3), channel_id=1, source_target_pairs={{0,16},{1,17},{2,18},{3,19},{4,20},{5,21},{6,22},{7,23},{8,24},{9,... | collective-permute-start | bytes 307208 | tf_op jit(solution)/shard_map/ppermute | solution.py:840
  15.3 5.8 %collective-permute-start.5 = (bf16[4,40,640]{2,1,0:T(8,128)(2,1)S(1)}, bf16[4,40,640]{2,1,0:T(8,128)(2,1)S(1)}, u32[]{:S(2)}, u32[]{:S(2)}) collective-permute-start(bf16[4,40,640]{2,1,0:T(8,128)(2,1)S(1)} %pad_maximum_fusion.1), channel_id=1, source_target_pairs={{0,2},{1,5},{2,0},{3,7},{4,6},{5,1},{6,4},{7,3},{8,10},{9,13},{10,... | collective-permute-start | bytes 614408 | tf_op jit(solution)/shard_map/ppermute | solution.py:840
  21.1 10.7 %copy-start.5 = (f32[512,128]{1,0:T(8,128)S(1)}, f32[512,128]{1,0:T(8,128)}, u32[]{:S(2)}) copy-start(f32[512,128]{1,0:T(8,128)} %get-tuple-element.112.live_ref) | copy-start | bytes 786436
  21.1 10.7 %copy-start = (f32[512,320]{1,0:T(8,128)S(1)}, f32[512,320]{1,0:T(8,128)}, u32[]{:S(2)}) copy-start(f32[512,320]{1,0:T(8,128)} %get-tuple-element.110.n1_ref) | copy-start | bytes 1966084
  21.1 10.7 %copy-start.1 = (bf16[512,512]{1,0:T(8,128)(2,1)S(1)}, bf16[512,512]{1,0:T(8,128)(2,1)}, u32[]{:S(2)}) copy-start(bf16[512,512]{1,0:T(8,128)(2,1)} %get-tuple-element.111.chosen_ref) | copy-start | bytes 1572868
  21.2 10.7 %copy-start.2 = (bf16[512,320]{0,1:T(8,128)(2,1)S(1)}, bf16[512,320]{0,1:T(8,128)(2,1)}, u32[]{:S(2)}) copy-start(bf16[512,320]{0,1:T(8,128)(2,1)} %param.13) | copy-start | bytes 983044
  21.2 8.0 %collective-permute-start.6 = (bf16[8,40,640]{2,1,0:T(8,128)(2,1)S(1)}, bf16[8,40,640]{2,1,0:T(8,128)(2,1)S(1)}, u32[]{:S(2)}, u32[]{:S(2)}) collective-permute-start(bf16[8,40,640]{2,1,0:T(8,128)(2,1)S(1)} %get-tuple-element.210), channel_id=1, source_target_pairs={{0,4},{1,3},{2,6},{3,1},{4,0},{5,7},{6,2},{7,5},{8,12},{9,11},{10,... | collective-permute-start | bytes 1228808 | tf_op jit(solution)/shard_map/ppermute | solution.py:840
  22.8 6.2 %collective-permute-start.8 = (bf16[4,40,640]{2,1,0:T(8,128)(2,1)S(1)}, bf16[4,40,640]{2,1,0:T(8,128)(2,1)S(1)}, u32[]{:S(2)}, u32[]{:S(2)}) collective-permute-start(bf16[4,40,640]{2,1,0:T(8,128)(2,1)S(1)} %pad_maximum_fusion.2), channel_id=1, source_target_pairs={{0,8},{1,9},{2,10},{3,11},{4,12},{5,13},{6,14},{7,15},{8,0},{9,1},... | collective-permute-start | bytes 614408 | tf_op jit(solution)/shard_map/ppermute | solution.py:840
  24.9 4.1 %collective-permute-start.9 = (bf16[2,16,640]{2,1,0:T(8,128)(2,1)S(1)}, bf16[2,16,640]{2,1,0:T(8,128)(2,1)S(1)}, u32[]{:S(2)}, u32[]{:S(2)}) collective-permute-start(bf16[2,16,640]{2,1,0:T(8,128)(2,1)S(1)} %pad_maximum_fusion.5), channel_id=1, source_target_pairs={{0,2},{1,3},{2,0},{3,1},{4,6},{5,7},{6,4},{7,5},{8,10},{9,11},{10,... | collective-permute-start | bytes 122888 | tf_op jit(solution)/shard_map/ppermute | solution.py:840
  29.3 2.4 %collective-permute-start.10 = (bf16[16,40,640]{2,1,0:T(8,128)(2,1)S(1)}, bf16[16,40,640]{2,1,0:T(8,128)(2,1)S(1)}, u32[]{:S(2)}, u32[]{:S(2)}) collective-permute-start(bf16[16,40,640]{2,1,0:T(8,128)(2,1)S(1)} %constant_dynamic-update-slice_fusion.5.own_ref), channel_id=1, source_target_pairs={{0,1},{1,0},{2,3},{3,2},{4,5},{5,4},{6,7},{7,6},{8,9},{9,8},{10,11... | collective-permute-start | bytes 2457608 | tf_op jit(solution)/shard_map/ppermute | solution.py:840
  29.5 8.0 %collective-permute-start.11 = (bf16[8,40,640]{2,1,0:T(8,128)(2,1)S(1)}, bf16[8,40,640]{2,1,0:T(8,128)(2,1)S(1)}, u32[]{:S(2)}, u32[]{:S(2)}) collective-permute-start(bf16[8,40,640]{2,1,0:T(8,128)(2,1)S(1)} %get-tuple-element.132), channel_id=1, source_target_pairs={{0,4},{1,3},{2,6},{3,1},{4,0},{5,7},{6,2},{7,5},{8,12},{9,11},{10,... | collective-permute-start | bytes 1228808 | tf_op jit(solution)/shard_map/ppermute | solution.py:840
  31.7 6.5 %collective-permute-start.12 = (bf16[8,40,640]{2,1,0:T(8,128)(2,1)S(1)}, bf16[8,40,640]{2,1,0:T(8,128)(2,1)S(1)}, u32[]{:S(2)}, u32[]{:S(2)}) collective-permute-start(bf16[8,40,640]{2,1,0:T(8,128)(2,1)S(1)} %get-tuple-element.132), channel_id=1, source_target_pairs={{0,1},{1,0},{2,3},{3,2},{4,5},{5,4},{6,7},{7,6},{8,9},{9,8},{10,11... | collective-permute-start | bytes 1228808 | tf_op jit(solution)/shard_map/ppermute | solution.py:840
  37.5 1.7 %collective-permute-start.13 = (bf16[8,40,640]{2,1,0:T(8,128)(2,1)S(1)}, bf16[8,40,640]{2,1,0:T(8,128)(2,1)S(1)}, u32[]{:S(2)}, u32[]{:S(2)}) collective-permute-start(bf16[8,40,640]{2,1,0:T(8,128)(2,1)S(1)} %collective-permute-done.11), channel_id=1, source_target_pairs={{0,1},{1,0},{2,3},{3,2},{4,5},{5,4},{6,7},{7,6},{8,9},{9,8},{10,11... | collective-permute-start | bytes 1228808 | tf_op jit(solution)/shard_map/ppermute | solution.py:840
  50.8 1.8 %collective-permute-start.14 = (bf16[8,40,640]{2,1,0:T(8,128)(2,1)S(1)}, bf16[8,40,640]{2,1,0:T(8,128)(2,1)S(1)}, u32[]{:S(2)}, u32[]{:S(2)}) collective-permute-start(bf16[8,40,640]{2,1,0:T(8,128)(2,1)S(1)} %get-tuple-element.207), channel_id=1, source_target_pairs={{0,1},{1,0},{2,3},{3,2},{4,5},{5,4},{6,7},{7,6},{8,9},{9,8},{10,11... | collective-permute-start | bytes 1228808 | tf_op jit(solution)/shard_map/ppermute | solution.py:840
  50.9 9.1 %collective-permute-start.15 = (bf16[8,40,640]{2,1,0:T(8,128)(2,1)S(1)}, bf16[8,40,640]{2,1,0:T(8,128)(2,1)S(1)}, u32[]{:S(2)}, u32[]{:S(2)}) collective-permute-start(bf16[8,40,640]{2,1,0:T(8,128)(2,1)S(1)} %get-tuple-element.206), channel_id=1, source_target_pairs={{0,1},{1,0},{2,3},{3,2},{4,5},{5,4},{6,7},{7,6},{8,9},{9,8},{10,11... | collective-permute-start | bytes 1228808 | tf_op jit(solution)/shard_map/ppermute | solution.py:840
  52.7 8.0 %collective-permute-start.16 = (bf16[8,40,640]{2,1,0:T(8,128)(2,1)S(1)}, bf16[8,40,640]{2,1,0:T(8,128)(2,1)S(1)}, u32[]{:S(2)}, u32[]{:S(2)}) collective-permute-start(bf16[8,40,640]{2,1,0:T(8,128)(2,1)S(1)} %shard_map.201), channel_id=1, source_target_pairs={{0,4},{1,3},{2,6},{3,1},{4,0},{5,7},{6,2},{7,5},{8,12},{9,11},{10,... | collective-permute-start | bytes 1228808 | tf_op jit(solution)/shard_map/ppermute | solution.py:840
  58.3 2.6 %collective-permute-start.17 = (bf16[16,40,640]{2,1,0:T(8,128)(2,1)S(1)}, bf16[16,40,640]{2,1,0:T(8,128)(2,1)S(1)}, u32[]{:S(2)}, u32[]{:S(2)}) collective-permute-start(bf16[16,40,640]{2,1,0:T(8,128)(2,1)S(1)} %get-tuple-element.165), channel_id=1, source_target_pairs={{0,1},{1,0},{2,3},{3,2},{4,5},{5,4},{6,7},{7,6},{8,9},{9,8},{10,11... | collective-permute-start | bytes 2457608 | tf_op jit(solution)/shard_map/ppermute | solution.py:840
  59.5 1.4 %collective-permute-start.18 = (bf16[2,8,640]{2,1,0:T(8,128)(2,1)S(1)}, bf16[2,8,640]{2,1,0:T(8,128)(2,1)S(1)}, u32[]{:S(2)}, u32[]{:S(2)}) collective-permute-start(bf16[2,8,640]{2,1,0:T(8,128)(2,1)S(1)} %get-tuple-element.174), channel_id=1, source_target_pairs={{0,1},{1,0},{2,3},{3,2},{4,5},{5,4},{6,7},{7,6},{8,9},{9,8},{10,11... | collective-permute-start | bytes 61448 | tf_op jit(solution)/shard_map/ppermute | solution.py:840
  61.1 8.5 %collective-permute-start.19 = (bf16[336,640]{1,0:T(8,128)(2,1)S(1)}, bf16[336,640]{1,0:T(8,128)(2,1)S(1)}, u32[]{:S(2)}, u32[]{:S(2)}) collective-permute-start(bf16[336,640]{1,0:T(8,128)(2,1)S(1)} %get-tuple-element.175), channel_id=1, source_target_pairs={{0,4},{1,3},{2,6},{3,1},{4,0},{5,7},{6,2},{7,5},{8,12},{9,11},{10,... | collective-permute-start | bytes 1290248 | tf_op jit(solution)/shard_map/ppermute | solution.py:840
  62.7 6.9 %collective-permute-start.20 = (bf16[4,40,640]{2,1,0:T(8,128)(2,1)S(1)}, bf16[4,40,640]{2,1,0:T(8,128)(2,1)S(1)}, u32[]{:S(2)}, u32[]{:S(2)}) collective-permute-start(bf16[4,40,640]{2,1,0:T(8,128)(2,1)S(1)} %get-tuple-element.163), channel_id=1, source_target_pairs={{0,8},{1,9},{2,10},{3,11},{4,12},{5,13},{6,14},{7,15},{8,0},{9,1},... | collective-permute-start | bytes 614408 | tf_op jit(solution)/shard_map/ppermute | solution.py:840
  69.7 5.9 %collective-permute-start.21 = (bf16[168,640]{1,0:T(8,128)(2,1)S(1)}, bf16[168,640]{1,0:T(8,128)(2,1)S(1)}, u32[]{:S(2)}, u32[]{:S(2)}) collective-permute-start(bf16[168,640]{1,0:T(8,128)(2,1)S(1)} %get-tuple-element.187), channel_id=1, source_target_pairs={{0,2},{1,5},{2,0},{3,7},{4,6},{5,1},{6,4},{7,3},{8,10},{9,13},{10,... | collective-permute-start | bytes 645128 | tf_op jit(solution)/shard_map/ppermute | solution.py:840
  70.8 9.4 %collective-permute-start.25 = (bf16[2,40,640]{2,1,0:T(8,128)(2,1)S(1)}, bf16[2,40,640]{2,1,0:T(8,128)(2,1)S(1)}, u32[]{:S(2)}, u32[]{:S(2)}) collective-permute-start(bf16[2,40,640]{2,1,0:T(8,128)(2,1)S(1)} %get-tuple-element.195), channel_id=1, source_target_pairs={{0,16},{1,17},{2,18},{3,19},{4,20},{5,21},{6,22},{7,23},{8,24},{9,... | collective-permute-start | bytes 307208 | tf_op jit(solution)/shard_map/ppermute | solution.py:840
  75.7 8.7 %collective-permute-start.22 = (bf16[48,640]{1,0:T(8,128)(2,1)S(1)}, bf16[48,640]{1,0:T(8,128)(2,1)S(1)}, u32[]{:S(2)}, u32[]{:S(2)}) collective-permute-start(bf16[48,640]{1,0:T(8,128)(2,1)S(1)} %get-tuple-element.189), channel_id=1, source_target_pairs={{0,8},{1,9},{2,10},{3,11},{4,12},{5,13},{6,14},{7,15},{8,0},{9,1},... | collective-permute-start | bytes 184328 | tf_op jit(solution)/shard_map/ppermute | solution.py:840
  77.6 6.8 %collective-permute-start.23 = (bf16[48,640]{1,0:T(8,128)(2,1)S(1)}, bf16[48,640]{1,0:T(8,128)(2,1)S(1)}, u32[]{:S(2)}, u32[]{:S(2)}) collective-permute-start(bf16[48,640]{1,0:T(8,128)(2,1)S(1)} %get-tuple-element.190), channel_id=1, source_target_pairs={{0,16},{1,17},{2,18},{3,19},{4,20},{5,21},{6,22},{7,23},{8,24},{9,... | collective-permute-start | bytes 184328 | tf_op jit(solution)/shard_map/ppermute | solution.py:840
  78.2 6.2 %collective-permute-start.24 = (bf16[48,640]{1,0:T(8,128)(2,1)S(1)}, bf16[48,640]{1,0:T(8,128)(2,1)S(1)}, u32[]{:S(2)}, u32[]{:S(2)}) collective-permute-start(bf16[48,640]{1,0:T(8,128)(2,1)S(1)} %get-tuple-element.191), channel_id=1, source_target_pairs={{0,24},{1,25},{2,26},{3,27},{4,28},{5,29},{6,30},{7,31},{8,16},{9,... | collective-permute-start | bytes 184328 | tf_op jit(solution)/shard_map/ppermute | solution.py:840
  80.2 4.2 %collective-permute-start.26 = (bf16[1,40,640]{2,1,0:T(8,128)(2,1)S(1)}, bf16[1,40,640]{2,1,0:T(8,128)(2,1)S(1)}, u32[]{:S(2)}, u32[]{:S(2)}) collective-permute-start(bf16[1,40,640]{2,1,0:T(8,128)(2,1)S(1)} %get-tuple-element.197), channel_id=1, source_target_pairs={{0,2},{1,5},{2,0},{3,7},{4,6},{5,1},{6,4},{7,3},{8,10},{9,13},{10,... | collective-permute-start | bytes 153608 | tf_op jit(solution)/shard_map/ppermute | solution.py:840
  (5 other events, 29.2 us)

commit v9 on v8

--- a/solution.py
+++ b/solution.py
@@ -150,17 +150,12 @@
     ]
     for copy in copies:
         copy.start()
-    for copy in copies:
+    for copy in copies[:2]:
         copy.wait()
     capacity = tok_ref.shape[1]
     for j in range(2):
         geo_ref[j] = rows_ref[j]
         geo_ref[2 + j] = cols_ref[j]
-    tokens = tok_ref[...].astype(F32).T
-    x_ref[...] = tokens
-    normed, inverse = normalise(tokens)
-    n1_ref[...] = normed
-    r1_ref[...] = inverse
     chosen_ref[...] = one_hot(rows_ref, cols_ref, capacity)
     area0, area1 = rows_ref[0] * cols_ref[0], rows_ref[1] * cols_ref[1]
     quarter0, quarter1 = area0 // 4, area1 // 4
@@ -170,6 +165,12 @@
         (token >= area0) & (token < area0 + area1) & (key >= quarter0) & (key < quarter0 + quarter1)
     )
     live_ref[...] = jnp.where(live, 1.0, 0.0)
+    copies[2].wait()
+    tokens = tok_ref[...].astype(F32).T
+    x_ref[...] = tokens
+    normed, inverse = normalise(tokens)
+    n1_ref[...] = normed
+    r1_ref[...] = inverse
 
 
 def prepare(img_rows, img_cols, tokens):

time: 85.7 us -> 85.7 us (level)
  no operation moved by 1% of the time
where the time goes in v9:
time: 85.7 us; the launch traced here: 85.4 us
  Pallas kernels  32.5 us (38%)
  starting transfers between devices  31.7 us (37%)
  waiting for transfers between devices  19.5 us (23%)
  between operations  0.99 us (1%)
    ppermute x27, starting transfers between devices, swap(): return lax.ppermute(value, ('wide', 'narrow'), pairs)  31.7 us
    pallas_call x17, Pallas kernels, call(): pl.pallas_call(kernel, out_shape=[jax.ShapeDtypeStruct(shape, kind) for s...  27.8 us
    ppermute x27, waiting for transfers between devices, swap(): return lax.ppermute(value, ('wide', 'narrow'), pairs)  19.5 us
    pallas_call x1, Pallas kernels, prepare(): pl.pallas_call(prepare_kernel, out_shape=[jax.ShapeDtypeStruct(shape, kin...  3.02 us
  transfers between devices with their start and end apart: 27, of which 10 were waited for; matrix products, arithmetic and copies ran while one was open for 0% of the time, Pallas kernels for 21%

profile of v9, /device:TPU:0, one launch (start us, length us, event | category | flops | bytes accessed | tf_op | source)
XLA Modules:
  0.0 85.4 jit_solution(1895403758571963526)
XLA Ops:
  0.6 1.7 %shard_map.196 = (bf16[1,40,640]{2,1,0:T(8,128)(2,1)}, bf16[1,40,640]{2,1,0:T(8,128)(2,1)}, bf16[1,16,640]{2,1,0:T(8,128)(2,1)}) custom-call(bf16[40,80]{1,0:T(8,128)(2,1)} %bitcast.16, bf16[80,80]{1,0:T(8,128)(2,1)} %refs_1_.1, bf16[40,320]{1,0:T(8,128)(2,1)} %bitcast.14, bf16[40,80]{1,0:T(8,128)(2,1)} %bitcast.17, bf16[80,160]{1,0:T(8,128)(2,1)} %refs_4_.1, ...), custom_call_target="tpu_custom_call" | custom-call | tf_op jit(solution)/shard_map/pallas_call | solution.py:133
  2.4 5.1 %collective-permute-start.2 = (bf16[1,40,640]{2,1,0:T(8,128)(2,1)}, bf16[1,40,640]{2,1,0:T(8,128)(2,1)S(1)}, u32[]{:S(2)}, u32[]{:S(2)}) collective-permute-start(bf16[1,40,640]{2,1,0:T(8,128)(2,1)} %get-tuple-element.113), channel_id=1, source_target_pairs={{0,24},{1,25},{2,26},{3,27},{4,28},{5,29},{6,30},{7,31},{8,16},{9,... | collective-permute-start | bytes 153608 | tf_op jit(solution)/shard_map/ppermute | solution.py:841
  8.1 1.6 %collective-permute-start.3 = (bf16[1,40,640]{2,1,0:T(8,128)(2,1)}, bf16[1,40,640]{2,1,0:T(8,128)(2,1)S(1)}, u32[]{:S(2)}, u32[]{:S(2)}) collective-permute-start(bf16[1,40,640]{2,1,0:T(8,128)(2,1)} %get-tuple-element.114), channel_id=1, source_target_pairs={{0,2},{1,5},{2,0},{3,7},{4,6},{5,1},{6,4},{7,3},{8,10},{9,13},{10,... | collective-permute-start | bytes 153608 | tf_op jit(solution)/shard_map/ppermute | solution.py:841
  9.8 3.0 %shard_map.195 = (f32[512,320]{1,0:T(8,128)}, f32[512,320]{1,0:T(8,128)}, f32[512,1]{1,0:T(8,128)}, bf16[512,512]{1,0:T(8,128)(2,1)}, f32[512,128]{1,0:T(8,128)}, /*index=5*/s32[4]{0:T(128)}) custom-call(s32[2]{0:T(128)} %rows_hbm.1, s32[2]{0:T(128)} %cols_hbm.1, bf16[320,512]{1,0:T(8,128)(2,1)} %bitcast.18), custom_call_target="tpu_custom_call" | custom-call | flops 2000000000 | tf_op jit(solution)/shard_map/pallas_call | solution.py:184
  12.9 2.2 %collective-permute-start.7 = (bf16[2,40,640]{2,1,0:T(8,128)(2,1)S(1)}, bf16[2,40,640]{2,1,0:T(8,128)(2,1)S(1)}, u32[]{:S(2)}, u32[]{:S(2)}) collective-permute-start(bf16[2,40,640]{2,1,0:T(8,128)(2,1)S(1)} %pad_maximum_fusion.3), channel_id=1, source_target_pairs={{0,16},{1,17},{2,18},{3,19},{4,20},{5,21},{6,22},{7,23},{8,24},{9,... | collective-permute-start | bytes 307208 | tf_op jit(solution)/shard_map/ppermute | solution.py:841
  15.2 1.3 %collective-permute-start.5 = (bf16[4,40,640]{2,1,0:T(8,128)(2,1)S(1)}, bf16[4,40,640]{2,1,0:T(8,128)(2,1)S(1)}, u32[]{:S(2)}, u32[]{:S(2)}) collective-permute-start(bf16[4,40,640]{2,1,0:T(8,128)(2,1)S(1)} %pad_maximum_fusion.1), channel_id=1, source_target_pairs={{0,2},{1,5},{2,0},{3,7},{4,6},{5,1},{6,4},{7,3},{8,10},{9,13},{10,... | collective-permute-start | bytes 614408 | tf_op jit(solution)/shard_map/ppermute | solution.py:841
  16.5 4.5 %collective-permute-done.5 = bf16[4,40,640]{2,1,0:T(8,128)(2,1)S(1)} collective-permute-done((bf16[4,40,640]{2,1,0:T(8,128)(2,1)S(1)}, bf16[4,40,640]{2,1,0:T(8,128)(2,1)S(1)}, u32[]{:S(2)}, u32[]{:S(2)}) %collective-permute-start.5) | collective-permute-done | bytes 204832 | tf_op jit(solution)/shard_map/ppermute | solution.py:841
  21.1 1.6 %collective-permute-start.6 = (bf16[8,40,640]{2,1,0:T(8,128)(2,1)S(1)}, bf16[8,40,640]{2,1,0:T(8,128)(2,1)S(1)}, u32[]{:S(2)}, u32[]{:S(2)}) collective-permute-start(bf16[8,40,640]{2,1,0:T(8,128)(2,1)S(1)} %get-tuple-element.210), channel_id=1, source_target_pairs={{0,4},{1,3},{2,6},{3,1},{4,0},{5,7},{6,2},{7,5},{8,12},{9,11},{10,... | collective-permute-start | bytes 1228808 | tf_op jit(solution)/shard_map/ppermute | solution.py:841
  22.7 2.1 %collective-permute-start.8 = (bf16[4,40,640]{2,1,0:T(8,128)(2,1)S(1)}, bf16[4,40,640]{2,1,0:T(8,128)(2,1)S(1)}, u32[]{:S(2)}, u32[]{:S(2)}) collective-permute-start(bf16[4,40,640]{2,1,0:T(8,128)(2,1)S(1)} %pad_maximum_fusion.2), channel_id=1, source_target_pairs={{0,8},{1,9},{2,10},{3,11},{4,12},{5,13},{6,14},{7,15},{8,0},{9,1},... | collective-permute-start | bytes 614408 | tf_op jit(solution)/shard_map/ppermute | solution.py:841
  24.8 1.3 %collective-permute-start.9 = (bf16[2,16,640]{2,1,0:T(8,128)(2,1)S(1)}, bf16[2,16,640]{2,1,0:T(8,128)(2,1)S(1)}, u32[]{:S(2)}, u32[]{:S(2)}) collective-permute-start(bf16[2,16,640]{2,1,0:T(8,128)(2,1)S(1)} %pad_maximum_fusion.5), channel_id=1, source_target_pairs={{0,2},{1,3},{2,0},{3,1},{4,6},{5,7},{6,4},{7,5},{8,10},{9,11},{10,... | collective-permute-start | bytes 122888 | tf_op jit(solution)/shard_map/ppermute | solution.py:841
  26.1 2.8 %collective-permute-done.9 = bf16[2,16,640]{2,1,0:T(8,128)(2,1)S(1)} collective-permute-done((bf16[2,16,640]{2,1,0:T(8,128)(2,1)S(1)}, bf16[2,16,640]{2,1,0:T(8,128)(2,1)S(1)}, u32[]{:S(2)}, u32[]{:S(2)}) %collective-permute-start.9) | collective-permute-done | bytes 40992 | tf_op jit(solution)/shard_map/ppermute | solution.py:841
  29.4 1.6 %collective-permute-start.11 = (bf16[8,40,640]{2,1,0:T(8,128)(2,1)S(1)}, bf16[8,40,640]{2,1,0:T(8,128)(2,1)S(1)}, u32[]{:S(2)}, u32[]{:S(2)}) collective-permute-start(bf16[8,40,640]{2,1,0:T(8,128)(2,1)S(1)} %get-tuple-element.132), channel_id=1, source_target_pairs={{0,4},{1,3},{2,6},{3,1},{4,0},{5,7},{6,2},{7,5},{8,12},{9,11},{10,... | collective-permute-start | bytes 1228808 | tf_op jit(solution)/shard_map/ppermute | solution.py:841
  31.8 4.8 %shard_map.197 = (f32[512,320]{1,0:T(8,128)S(1)}, bf16[512,320]{1,0:T(8,128)(2,1)S(1)}, bf16[512,320]{1,0:T(8,128)(2,1)S(1)}, f32[128,320]{1,0:T(8,128)S(1)}, f3...) custom-call(s32[4]{0:T(128)S(1)} %copy-done.6, ...), custom_call_target="tpu_custom_call" | custom-call | flops 8000000000 | tf_op jit(solution)/shard_map/pallas_call | solution.py:805
  38.1 1.1 %collective-permute-done.13 = bf16[8,40,640]{2,1,0:T(8,128)(2,1)S(1)} collective-permute-done((bf16[8,40,640]{2,1,0:T(8,128)(2,1)S(1)}, bf16[8,40,640]{2,1,0:T(8,128)(2,1)S(1)}, u32[]{:S(2)}, u32[]{:S(2)}) %collective-permute-start.13) | collective-permute-done | bytes 409632 | tf_op jit(solution)/shard_map/ppermute | solution.py:841
  39.2 11.4 %shard_map.199 = (bf16[16,40,640]{2,1,0:T(8,128)(2,1)S(1)}, bf16[16,40,640]{2,1,0:T(8,128)(2,1)S(1)}, bf16[512,1280]{1,0:T(8,128)(2,1)S(1)}, bf16[512,1280]{1,0:...) custom-call(s32[4]{0:T(128)S(1)} %copy-done.6, ...), custom_call_target="tpu_custom_call", output_to_operand_aliasing={{5}: (9, {}), {6}: (10, {})} | custom-call | flops 32999999488 | tf_op jit(solution)/shard_map/pallas_call | solution.py:805
  51.3 1.2 %shard_map.200 = (f32[512,320]{1,0:T(8,128)S(1)}, f32[16,320]{1,0:T(8,128)S(1)}) custom-call(bf16[512,1280]{1,0:T(8,128)(2,1)S(1)} %get-tuple-element.137.df_ref, bf16[320,1280]{1,0:T(8,128)(2,1)S(1)} %get-tuple-element.138.wu_ref, f32[512,320]{1,0:T(8,128)S(1)} %get-tuple-element.139.n2_ref, f32[512,1]{1,0:T(8,128)S(1)} %get-tuple-element.140.r2_ref, ...), custom_call_target="tpu_custom_call" | custom-call | flops 1000000000 | tf_op jit(solution)/shard_map/pallas_call | solution.py:805
  52.6 1.5 %collective-permute-start.16 = (bf16[8,40,640]{2,1,0:T(8,128)(2,1)S(1)}, bf16[8,40,640]{2,1,0:T(8,128)(2,1)S(1)}, u32[]{:S(2)}, u32[]{:S(2)}) collective-permute-start(bf16[8,40,640]{2,1,0:T(8,128)(2,1)S(1)} %shard_map.201), channel_id=1, source_target_pairs={{0,4},{1,3},{2,6},{3,1},{4,0},{5,7},{6,2},{7,5},{8,12},{9,11},{10,... | collective-permute-start | bytes 1228808 | tf_op jit(solution)/shard_map/ppermute | solution.py:841
  54.1 1.2 %shard_map.202 = (f32[320,320]{1,0:T(8,128)S(1)}, bf16[512,320]{1,0:T(8,128)(2,1)S(1)}, bf16[512,640]{1,0:T(8,128)(2,1)S(1)}, f32[1,320]{1,0:T(1,128)S(1)}) custom-call(f32[512,320]{1,0:T(8,128)S(1)} %get-tuple-element.145.dx2_ref, bf16[640,320]{1,0:T(8,128)(2,1)S(1)} %get-tuple-element.146.vb_ref, f32[512,640]{1,0:T(8,128)S(1)} %get-tuple-element.147.p_ref, ...), custom_call_target="tpu_custom_call" | custom-call | tf_op jit(solution)/shard_map/pallas_call | solution.py:805
  55.4 2.8 %shard_map.203 = (bf16[16,40,640]{2,1,0:T(8,128)(2,1)S(1)}, bf16[16,40,640]{2,1,0:T(8,128)(2,1)S(1)}, bf16[512,320]{1,0:T(8,128)(2,1)S(1)}, f32[512,320]{1,0:T(8,128)S(1)}, f32[8,320]{1,0:T(8,128)S(1)}) custom-call(bf16[512,320]{1,0:T(8,128)(2,1)S(1)} %get-tuple-element.150.dob_ref, bf16[512,640]{1,0:T(8,128)(2,1)S(1)} %get-tuple-element.151.ds_ref, ...), custom_call_target="tpu_custom_call" | custom-call | tf_op jit(solution)/shard_map/pallas_call | solution.py:805
  58.2 1.1 %shard_map.205 = (f32[512,320]{1,0:T(8,128)S(1)}, bf16[2,8,640]{2,1,0:T(8,128)(2,1)S(1)}, bf16[2,8,640]{2,1,0:T(8,128)(2,1)S(1)}) custom-call(bf16[512,320]{1,0:T(8,128)(2,1)S(1)} %get-tuple-element.166.dq_ref, f32[512,320]{1,0:T(8,128)S(1)} %get-tuple-element.167.dpatch_ref, f32[512,320]{1,0:T(8,128)S(1)} %copy-done, bf16[512,512]{1,0:T(8,128)(2,1)S(1)} %copy-done.1, ...), custom_call_target="tpu_custom_call" | custom-call | tf_op jit(solution)/shard_map/pallas_call | solution.py:805
  61.0 1.5 %collective-permute-start.19 = (bf16[336,640]{1,0:T(8,128)(2,1)S(1)}, bf16[336,640]{1,0:T(8,128)(2,1)S(1)}, u32[]{:S(2)}, u32[]{:S(2)}) collective-permute-start(bf16[336,640]{1,0:T(8,128)(2,1)S(1)} %get-tuple-element.175), channel_id=1, source_target_pairs={{0,4},{1,3},{2,6},{3,1},{4,0},{5,7},{6,2},{7,5},{8,12},{9,11},{10,... | collective-permute-start | bytes 1290248 | tf_op jit(solution)/shard_map/ppermute | solution.py:841
  62.6 2.1 %collective-permute-start.20 = (bf16[4,40,640]{2,1,0:T(8,128)(2,1)S(1)}, bf16[4,40,640]{2,1,0:T(8,128)(2,1)S(1)}, u32[]{:S(2)}, u32[]{:S(2)}) collective-permute-start(bf16[4,40,640]{2,1,0:T(8,128)(2,1)S(1)} %get-tuple-element.163), channel_id=1, source_target_pairs={{0,8},{1,9},{2,10},{3,11},{4,12},{5,13},{6,14},{7,15},{8,0},{9,1},... | collective-permute-start | bytes 614408 | tf_op jit(solution)/shard_map/ppermute | solution.py:841
  64.7 1.7 %shard_map.207 = bf16[320,512]{1,0:T(8,128)(2,1)} custom-call(f32[512,320]{1,0:T(8,128)S(1)} %get-tuple-element.123.x2_ref, bf16[512,1280]{1,0:T(8,128)(2,1)S(1)} %get-tuple-element.176.act_ref, bf16[320,1280]{1,0:T(8,128)(2,1)S(1)} %get-tuple-element.177.wd_ref, f32[16,320]{1,0:T(8,128)S(1)} %get-tuple-element.124.mv_ref, ...), custom_call_target="tpu_custom_call" | custom-call | flops 1000000000 | tf_op jit(solution)/shard_map/pallas_call | solution.py:805
  66.4 1.4 %shard_map.208 = bf16[320,512]{1,0:T(8,128)(2,1)} custom-call(f32[512,320]{1,0:T(8,128)S(1)} %get-tuple-element.145.dx2_ref, f32[512,320]{1,0:T(8,128)S(1)} %get-tuple-element.178.dh1_ref, f32[512,320]{1,0:T(8,128)S(1)} %copy-done, f32[512,1]{1,0:T(8,128)S(1)} %copy-done.3, f32[16,320]{1,0:T(8,128)S(1)} %get-tuple-element.124.mv_ref), custom_call_target="tpu_custom_call" | custom-call | flops 1000000000 | tf_op jit(solution)/shard_map/pallas_call | solution.py:805
  67.7 1.9 %collective-permute-done.20.got_ref = bf16[4,40,640]{2,1,0:T(8,128)(2,1)S(1)} collective-permute-done((bf16[4,40,640]{2,1,0:T(8,128)(2,1)S(1)}, bf16[4,40,640]{2,1,0:T(8,128)(2,1)S(1)}, u32[]{:S(2)}, u32[]{:S(2)}) %collective-permute-start.20) | collective-permute-done | bytes 204832 | tf_op jit(solution)/shard_map/ppermute | solution.py:841
  70.7 1.4 %collective-permute-start.25 = (bf16[2,40,640]{2,1,0:T(8,128)(2,1)S(1)}, bf16[2,40,640]{2,1,0:T(8,128)(2,1)S(1)}, u32[]{:S(2)}, u32[]{:S(2)}) collective-permute-start(bf16[2,40,640]{2,1,0:T(8,128)(2,1)S(1)} %get-tuple-element.195), channel_id=1, source_target_pairs={{0,16},{1,17},{2,18},{3,19},{4,20},{5,21},{6,22},{7,23},{8,24},{9,... | collective-permute-start | bytes 307208 | tf_op jit(solution)/shard_map/ppermute | solution.py:841
  72.1 3.6 %collective-permute-done.21.got_ref = bf16[168,640]{1,0:T(8,128)(2,1)S(1)} collective-permute-done((bf16[168,640]{1,0:T(8,128)(2,1)S(1)}, bf16[168,640]{1,0:T(8,128)(2,1)S(1)}, u32[]{:S(2)}, u32[]{:S(2)}) %collective-permute-start.21) | collective-permute-done | bytes 215072 | tf_op jit(solution)/shard_map/ppermute | solution.py:841
  75.7 1.8 %collective-permute-start.22 = (bf16[48,640]{1,0:T(8,128)(2,1)S(1)}, bf16[48,640]{1,0:T(8,128)(2,1)S(1)}, u32[]{:S(2)}, u32[]{:S(2)}) collective-permute-start(bf16[48,640]{1,0:T(8,128)(2,1)S(1)} %get-tuple-element.189), channel_id=1, source_target_pairs={{0,8},{1,9},{2,10},{3,11},{4,12},{5,13},{6,14},{7,15},{8,0},{9,1},... | collective-permute-start | bytes 184328 | tf_op jit(solution)/shard_map/ppermute | solution.py:841
  78.2 2.0 %collective-permute-start.24 = (bf16[48,640]{1,0:T(8,128)(2,1)S(1)}, bf16[48,640]{1,0:T(8,128)(2,1)S(1)}, u32[]{:S(2)}, u32[]{:S(2)}) collective-permute-start(bf16[48,640]{1,0:T(8,128)(2,1)S(1)} %get-tuple-element.191), channel_id=1, source_target_pairs={{0,24},{1,25},{2,26},{3,27},{4,28},{5,29},{6,30},{7,31},{8,16},{9,... | collective-permute-start | bytes 184328 | tf_op jit(solution)/shard_map/ppermute | solution.py:841
  80.2 1.0 %collective-permute-start.26 = (bf16[1,40,640]{2,1,0:T(8,128)(2,1)S(1)}, bf16[1,40,640]{2,1,0:T(8,128)(2,1)S(1)}, u32[]{:S(2)}, u32[]{:S(2)}) collective-permute-start(bf16[1,40,640]{2,1,0:T(8,128)(2,1)S(1)} %get-tuple-element.197), channel_id=1, source_target_pairs={{0,2},{1,5},{2,0},{3,7},{4,6},{5,1},{6,4},{7,3},{8,10},{9,13},{10,... | collective-permute-start | bytes 153608 | tf_op jit(solution)/shard_map/ppermute | solution.py:841
  81.2 3.2 %collective-permute-done.26.ffn_got_ref = bf16[1,40,640]{2,1,0:T(8,128)(2,1)S(1)} collective-permute-done((bf16[1,40,640]{2,1,0:T(8,128)(2,1)S(1)}, bf16[1,40,640]{2,1,0:T(8,128)(2,1)S(1)}, u32[]{:S(2)}, u32[]{:S(2)}) %collective-permute-start.26) | collective-permute-done | bytes 51232 | tf_op jit(solution)/shard_map/ppermute | solution.py:841
  84.4 0.9 %shard_map.213 = (f32[40,80]{1,0:T(8,128)}, f32[80,80]{1,0:T(8,128)}, f32[40,320]{1,0:T(8,128)}, f32[40,80]{1,0:T(8,128)}, f32[80,160]{1,0:T(8,128)}, /*index=5*...) custom-call(bf16[48,640]{1,0:T(8,128)(2,1)S(1)} %get-tuple-element.188.a_ref, ...), custom_call_target="tpu_custom_call" | custom-call | tf_op jit(solution)/shard_map/pallas_call | solution.py:805
  (78 shorter events, 8.1 us)
Async XLA Ops:
  2.4 10.5 %collective-permute-start.2 = (bf16[1,40,640]{2,1,0:T(8,128)(2,1)}, bf16[1,40,640]{2,1,0:T(8,128)(2,1)S(1)}, u32[]{:S(2)}, u32[]{:S(2)}) collective-permute-start(bf16[1,40,640]{2,1,0:T(8,128)(2,1)} %get-tuple-element.113), channel_id=1, source_target_pairs={{0,24},{1,25},{2,26},{3,27},{4,28},{5,29},{6,30},{7,31},{8,16},{9,... | collective-permute-start | bytes 153608 | tf_op jit(solution)/shard_map/ppermute | solution.py:841
  7.5 5.4 %collective-permute-start.1 = (bf16[1,40,640]{2,1,0:T(8,128)(2,1)}, bf16[1,40,640]{2,1,0:T(8,128)(2,1)S(1)}, u32[]{:S(2)}, u32[]{:S(2)}) collective-permute-start(bf16[1,40,640]{2,1,0:T(8,128)(2,1)} %get-tuple-element.113), channel_id=1, source_target_pairs={{0,16},{1,17},{2,18},{3,19},{4,20},{5,21},{6,22},{7,23},{8,24},{9,... | collective-permute-start | bytes 153608 | tf_op jit(solution)/shard_map/ppermute | solution.py:841
  7.5 5.4 %collective-permute-start = (bf16[1,40,640]{2,1,0:T(8,128)(2,1)}, bf16[1,40,640]{2,1,0:T(8,128)(2,1)S(1)}, u32[]{:S(2)}, u32[]{:S(2)}) collective-permute-start(bf16[1,40,640]{2,1,0:T(8,128)(2,1)} %get-tuple-element.113), channel_id=1, source_target_pairs={{0,8},{1,9},{2,10},{3,11},{4,12},{5,13},{6,14},{7,15},{8,0},{9,1},... | collective-permute-start | bytes 153608 | tf_op jit(solution)/shard_map/ppermute | solution.py:841
  8.1 4.7 %collective-permute-start.4 = (bf16[1,16,640]{2,1,0:T(8,128)(2,1)}, bf16[1,16,640]{2,1,0:T(8,128)(2,1)S(1)}, u32[]{:S(2)}, u32[]{:S(2)}) collective-permute-start(bf16[1,16,640]{2,1,0:T(8,128)(2,1)} %get-tuple-element.115), channel_id=1, source_target_pairs={{0,1},{1,0},{2,3},{3,2},{4,5},{5,4},{6,7},{7,6},{8,9},{9,8},{10,11... | collective-permute-start | bytes 61448 | tf_op jit(solution)/shard_map/ppermute | solution.py:841
  8.1 4.7 %collective-permute-start.3 = (bf16[1,40,640]{2,1,0:T(8,128)(2,1)}, bf16[1,40,640]{2,1,0:T(8,128)(2,1)S(1)}, u32[]{:S(2)}, u32[]{:S(2)}) collective-permute-start(bf16[1,40,640]{2,1,0:T(8,128)(2,1)} %get-tuple-element.114), channel_id=1, source_target_pairs={{0,2},{1,5},{2,0},{3,7},{4,6},{5,1},{6,4},{7,3},{8,10},{9,13},{10,... | collective-permute-start | bytes 153608 | tf_op jit(solution)/shard_map/ppermute | solution.py:841
  12.8 12.0 %copy-start.9 = (bf16[1,16,640]{2,1,0:T(8,128)(2,1)S(1)}, bf16[1,16,640]{2,1,0:T(8,128)(2,1)}, u32[]{:S(2)}) copy-start(bf16[1,16,640]{2,1,0:T(8,128)(2,1)} %get-tuple-element.115) | copy-start | bytes 61444
  12.9 9.8 %collective-permute-start.7 = (bf16[2,40,640]{2,1,0:T(8,128)(2,1)S(1)}, bf16[2,40,640]{2,1,0:T(8,128)(2,1)S(1)}, u32[]{:S(2)}, u32[]{:S(2)}) collective-permute-start(bf16[2,40,640]{2,1,0:T(8,128)(2,1)S(1)} %pad_maximum_fusion.3), channel_id=1, source_target_pairs={{0,16},{1,17},{2,18},{3,19},{4,20},{5,21},{6,22},{7,23},{8,24},{9,... | collective-permute-start | bytes 307208 | tf_op jit(solution)/shard_map/ppermute | solution.py:841
  15.2 5.8 %collective-permute-start.5 = (bf16[4,40,640]{2,1,0:T(8,128)(2,1)S(1)}, bf16[4,40,640]{2,1,0:T(8,128)(2,1)S(1)}, u32[]{:S(2)}, u32[]{:S(2)}) collective-permute-start(bf16[4,40,640]{2,1,0:T(8,128)(2,1)S(1)} %pad_maximum_fusion.1), channel_id=1, source_target_pairs={{0,2},{1,5},{2,0},{3,7},{4,6},{5,1},{6,4},{7,3},{8,10},{9,13},{10,... | collective-permute-start | bytes 614408 | tf_op jit(solution)/shard_map/ppermute | solution.py:841
  21.0 10.7 %copy-start.5 = (f32[512,128]{1,0:T(8,128)S(1)}, f32[512,128]{1,0:T(8,128)}, u32[]{:S(2)}) copy-start(f32[512,128]{1,0:T(8,128)} %get-tuple-element.112.live_ref) | copy-start | bytes 786436
  21.1 10.7 %copy-start = (f32[512,320]{1,0:T(8,128)S(1)}, f32[512,320]{1,0:T(8,128)}, u32[]{:S(2)}) copy-start(f32[512,320]{1,0:T(8,128)} %get-tuple-element.110.n1_ref) | copy-start | bytes 1966084
  21.1 10.7 %copy-start.1 = (bf16[512,512]{1,0:T(8,128)(2,1)S(1)}, bf16[512,512]{1,0:T(8,128)(2,1)}, u32[]{:S(2)}) copy-start(bf16[512,512]{1,0:T(8,128)(2,1)} %get-tuple-element.111.chosen_ref) | copy-start | bytes 1572868
  21.1 10.7 %copy-start.2 = (bf16[512,320]{0,1:T(8,128)(2,1)S(1)}, bf16[512,320]{0,1:T(8,128)(2,1)}, u32[]{:S(2)}) copy-start(bf16[512,320]{0,1:T(8,128)(2,1)} %param.13) | copy-start | bytes 983044
  21.1 8.0 %collective-permute-start.6 = (bf16[8,40,640]{2,1,0:T(8,128)(2,1)S(1)}, bf16[8,40,640]{2,1,0:T(8,128)(2,1)S(1)}, u32[]{:S(2)}, u32[]{:S(2)}) collective-permute-start(bf16[8,40,640]{2,1,0:T(8,128)(2,1)S(1)} %get-tuple-element.210), channel_id=1, source_target_pairs={{0,4},{1,3},{2,6},{3,1},{4,0},{5,7},{6,2},{7,5},{8,12},{9,11},{10,... | collective-permute-start | bytes 1228808 | tf_op jit(solution)/shard_map/ppermute | solution.py:841
  22.7 6.2 %collective-permute-start.8 = (bf16[4,40,640]{2,1,0:T(8,128)(2,1)S(1)}, bf16[4,40,640]{2,1,0:T(8,128)(2,1)S(1)}, u32[]{:S(2)}, u32[]{:S(2)}) collective-permute-start(bf16[4,40,640]{2,1,0:T(8,128)(2,1)S(1)} %pad_maximum_fusion.2), channel_id=1, source_target_pairs={{0,8},{1,9},{2,10},{3,11},{4,12},{5,13},{6,14},{7,15},{8,0},{9,1},... | collective-permute-start | bytes 614408 | tf_op jit(solution)/shard_map/ppermute | solution.py:841
  24.8 4.1 %collective-permute-start.9 = (bf16[2,16,640]{2,1,0:T(8,128)(2,1)S(1)}, bf16[2,16,640]{2,1,0:T(8,128)(2,1)S(1)}, u32[]{:S(2)}, u32[]{:S(2)}) collective-permute-start(bf16[2,16,640]{2,1,0:T(8,128)(2,1)S(1)} %pad_maximum_fusion.5), channel_id=1, source_target_pairs={{0,2},{1,3},{2,0},{3,1},{4,6},{5,7},{6,4},{7,5},{8,10},{9,11},{10,... | collective-permute-start | bytes 122888 | tf_op jit(solution)/shard_map/ppermute | solution.py:841
  29.2 2.4 %collective-permute-start.10 = (bf16[16,40,640]{2,1,0:T(8,128)(2,1)S(1)}, bf16[16,40,640]{2,1,0:T(8,128)(2,1)S(1)}, u32[]{:S(2)}, u32[]{:S(2)}) collective-permute-start(bf16[16,40,640]{2,1,0:T(8,128)(2,1)S(1)} %constant_dynamic-update-slice_fusion.5.own_ref), channel_id=1, source_target_pairs={{0,1},{1,0},{2,3},{3,2},{4,5},{5,4},{6,7},{7,6},{8,9},{9,8},{10,11... | collective-permute-start | bytes 2457608 | tf_op jit(solution)/shard_map/ppermute | solution.py:841
  29.4 8.0 %collective-permute-start.11 = (bf16[8,40,640]{2,1,0:T(8,128)(2,1)S(1)}, bf16[8,40,640]{2,1,0:T(8,128)(2,1)S(1)}, u32[]{:S(2)}, u32[]{:S(2)}) collective-permute-start(bf16[8,40,640]{2,1,0:T(8,128)(2,1)S(1)} %get-tuple-element.132), channel_id=1, source_target_pairs={{0,4},{1,3},{2,6},{3,1},{4,0},{5,7},{6,2},{7,5},{8,12},{9,11},{10,... | collective-permute-start | bytes 1228808 | tf_op jit(solution)/shard_map/ppermute | solution.py:841
  31.6 6.5 %collective-permute-start.12 = (bf16[8,40,640]{2,1,0:T(8,128)(2,1)S(1)}, bf16[8,40,640]{2,1,0:T(8,128)(2,1)S(1)}, u32[]{:S(2)}, u32[]{:S(2)}) collective-permute-start(bf16[8,40,640]{2,1,0:T(8,128)(2,1)S(1)} %get-tuple-element.132), channel_id=1, source_target_pairs={{0,1},{1,0},{2,3},{3,2},{4,5},{5,4},{6,7},{7,6},{8,9},{9,8},{10,11... | collective-permute-start | bytes 1228808 | tf_op jit(solution)/shard_map/ppermute | solution.py:841
  37.4 1.7 %collective-permute-start.13 = (bf16[8,40,640]{2,1,0:T(8,128)(2,1)S(1)}, bf16[8,40,640]{2,1,0:T(8,128)(2,1)S(1)}, u32[]{:S(2)}, u32[]{:S(2)}) collective-permute-start(bf16[8,40,640]{2,1,0:T(8,128)(2,1)S(1)} %collective-permute-done.11), channel_id=1, source_target_pairs={{0,1},{1,0},{2,3},{3,2},{4,5},{5,4},{6,7},{7,6},{8,9},{9,8},{10,11... | collective-permute-start | bytes 1228808 | tf_op jit(solution)/shard_map/ppermute | solution.py:841
  50.7 1.8 %collective-permute-start.14 = (bf16[8,40,640]{2,1,0:T(8,128)(2,1)S(1)}, bf16[8,40,640]{2,1,0:T(8,128)(2,1)S(1)}, u32[]{:S(2)}, u32[]{:S(2)}) collective-permute-start(bf16[8,40,640]{2,1,0:T(8,128)(2,1)S(1)} %get-tuple-element.207), channel_id=1, source_target_pairs={{0,1},{1,0},{2,3},{3,2},{4,5},{5,4},{6,7},{7,6},{8,9},{9,8},{10,11... | collective-permute-start | bytes 1228808 | tf_op jit(solution)/shard_map/ppermute | solution.py:841
  50.9 9.0 %collective-permute-start.15 = (bf16[8,40,640]{2,1,0:T(8,128)(2,1)S(1)}, bf16[8,40,640]{2,1,0:T(8,128)(2,1)S(1)}, u32[]{:S(2)}, u32[]{:S(2)}) collective-permute-start(bf16[8,40,640]{2,1,0:T(8,128)(2,1)S(1)} %get-tuple-element.206), channel_id=1, source_target_pairs={{0,1},{1,0},{2,3},{3,2},{4,5},{5,4},{6,7},{7,6},{8,9},{9,8},{10,11... | collective-permute-start | bytes 1228808 | tf_op jit(solution)/shard_map/ppermute | solution.py:841
  52.6 8.0 %collective-permute-start.16 = (bf16[8,40,640]{2,1,0:T(8,128)(2,1)S(1)}, bf16[8,40,640]{2,1,0:T(8,128)(2,1)S(1)}, u32[]{:S(2)}, u32[]{:S(2)}) collective-permute-start(bf16[8,40,640]{2,1,0:T(8,128)(2,1)S(1)} %shard_map.201), channel_id=1, source_target_pairs={{0,4},{1,3},{2,6},{3,1},{4,0},{5,7},{6,2},{7,5},{8,12},{9,11},{10,... | collective-permute-start | bytes 1228808 | tf_op jit(solution)/shard_map/ppermute | solution.py:841
  58.1 2.6 %collective-permute-start.17 = (bf16[16,40,640]{2,1,0:T(8,128)(2,1)S(1)}, bf16[16,40,640]{2,1,0:T(8,128)(2,1)S(1)}, u32[]{:S(2)}, u32[]{:S(2)}) collective-permute-start(bf16[16,40,640]{2,1,0:T(8,128)(2,1)S(1)} %get-tuple-element.165), channel_id=1, source_target_pairs={{0,1},{1,0},{2,3},{3,2},{4,5},{5,4},{6,7},{7,6},{8,9},{9,8},{10,11... | collective-permute-start | bytes 2457608 | tf_op jit(solution)/shard_map/ppermute | solution.py:841
  59.3 1.5 %collective-permute-start.18 = (bf16[2,8,640]{2,1,0:T(8,128)(2,1)S(1)}, bf16[2,8,640]{2,1,0:T(8,128)(2,1)S(1)}, u32[]{:S(2)}, u32[]{:S(2)}) collective-permute-start(bf16[2,8,640]{2,1,0:T(8,128)(2,1)S(1)} %get-tuple-element.174), channel_id=1, source_target_pairs={{0,1},{1,0},{2,3},{3,2},{4,5},{5,4},{6,7},{7,6},{8,9},{9,8},{10,11... | collective-permute-start | bytes 61448 | tf_op jit(solution)/shard_map/ppermute | solution.py:841
  61.0 8.6 %collective-permute-start.19 = (bf16[336,640]{1,0:T(8,128)(2,1)S(1)}, bf16[336,640]{1,0:T(8,128)(2,1)S(1)}, u32[]{:S(2)}, u32[]{:S(2)}) collective-permute-start(bf16[336,640]{1,0:T(8,128)(2,1)S(1)} %get-tuple-element.175), channel_id=1, source_target_pairs={{0,4},{1,3},{2,6},{3,1},{4,0},{5,7},{6,2},{7,5},{8,12},{9,11},{10,... | collective-permute-start | bytes 1290248 | tf_op jit(solution)/shard_map/ppermute | solution.py:841
  62.6 7.1 %collective-permute-start.20 = (bf16[4,40,640]{2,1,0:T(8,128)(2,1)S(1)}, bf16[4,40,640]{2,1,0:T(8,128)(2,1)S(1)}, u32[]{:S(2)}, u32[]{:S(2)}) collective-permute-start(bf16[4,40,640]{2,1,0:T(8,128)(2,1)S(1)} %get-tuple-element.163), channel_id=1, source_target_pairs={{0,8},{1,9},{2,10},{3,11},{4,12},{5,13},{6,14},{7,15},{8,0},{9,1},... | collective-permute-start | bytes 614408 | tf_op jit(solution)/shard_map/ppermute | solution.py:841
  69.7 5.9 %collective-permute-start.21 = (bf16[168,640]{1,0:T(8,128)(2,1)S(1)}, bf16[168,640]{1,0:T(8,128)(2,1)S(1)}, u32[]{:S(2)}, u32[]{:S(2)}) collective-permute-start(bf16[168,640]{1,0:T(8,128)(2,1)S(1)} %get-tuple-element.187), channel_id=1, source_target_pairs={{0,2},{1,5},{2,0},{3,7},{4,6},{5,1},{6,4},{7,3},{8,10},{9,13},{10,... | collective-permute-start | bytes 645128 | tf_op jit(solution)/shard_map/ppermute | solution.py:841
  70.7 9.5 %collective-permute-start.25 = (bf16[2,40,640]{2,1,0:T(8,128)(2,1)S(1)}, bf16[2,40,640]{2,1,0:T(8,128)(2,1)S(1)}, u32[]{:S(2)}, u32[]{:S(2)}) collective-permute-start(bf16[2,40,640]{2,1,0:T(8,128)(2,1)S(1)} %get-tuple-element.195), channel_id=1, source_target_pairs={{0,16},{1,17},{2,18},{3,19},{4,20},{5,21},{6,22},{7,23},{8,24},{9,... | collective-permute-start | bytes 307208 | tf_op jit(solution)/shard_map/ppermute | solution.py:841
  75.7 8.7 %collective-permute-start.22 = (bf16[48,640]{1,0:T(8,128)(2,1)S(1)}, bf16[48,640]{1,0:T(8,128)(2,1)S(1)}, u32[]{:S(2)}, u32[]{:S(2)}) collective-permute-start(bf16[48,640]{1,0:T(8,128)(2,1)S(1)} %get-tuple-element.189), channel_id=1, source_target_pairs={{0,8},{1,9},{2,10},{3,11},{4,12},{5,13},{6,14},{7,15},{8,0},{9,1},... | collective-permute-start | bytes 184328 | tf_op jit(solution)/shard_map/ppermute | solution.py:841
  77.6 6.9 %collective-permute-start.23 = (bf16[48,640]{1,0:T(8,128)(2,1)S(1)}, bf16[48,640]{1,0:T(8,128)(2,1)S(1)}, u32[]{:S(2)}, u32[]{:S(2)}) collective-permute-start(bf16[48,640]{1,0:T(8,128)(2,1)S(1)} %get-tuple-element.190), channel_id=1, source_target_pairs={{0,16},{1,17},{2,18},{3,19},{4,20},{5,21},{6,22},{7,23},{8,24},{9,... | collective-permute-start | bytes 184328 | tf_op jit(solution)/shard_map/ppermute | solution.py:841
  78.2 6.2 %collective-permute-start.24 = (bf16[48,640]{1,0:T(8,128)(2,1)S(1)}, bf16[48,640]{1,0:T(8,128)(2,1)S(1)}, u32[]{:S(2)}, u32[]{:S(2)}) collective-permute-start(bf16[48,640]{1,0:T(8,128)(2,1)S(1)} %get-tuple-element.191), channel_id=1, source_target_pairs={{0,24},{1,25},{2,26},{3,27},{4,28},{5,29},{6,30},{7,31},{8,16},{9,... | collective-permute-start | bytes 184328 | tf_op jit(solution)/shard_map/ppermute | solution.py:841
  80.2 4.2 %collective-permute-start.26 = (bf16[1,40,640]{2,1,0:T(8,128)(2,1)S(1)}, bf16[1,40,640]{2,1,0:T(8,128)(2,1)S(1)}, u32[]{:S(2)}, u32[]{:S(2)}) collective-permute-start(bf16[1,40,640]{2,1,0:T(8,128)(2,1)S(1)} %get-tuple-element.197), channel_id=1, source_target_pairs={{0,2},{1,5},{2,0},{3,7},{4,6},{5,1},{6,4},{7,3},{8,10},{9,13},{10,... | collective-permute-start | bytes 153608 | tf_op jit(solution)/shard_map/ppermute | solution.py:841
  (5 other events, 29.0 us)
